TPU v7x, 128 devices: a whole 4x4x4 slice. The times are simulated.
128 devices in a mesh: clip: 8 (over y, z_lo), seq: 16 (over z_hi, x, core).
Axes of the slice: x: 4, y: 4, z: 4 (z_hi: 2, z_lo: 2; z = z_hi * 2 + z_lo), core: 2. Of those that a mesh axis runs over, the one named last changes fastest.
Arguments:
- features: bfloat16 [8, 16, 32, 32, 256], P('clip', None, 'seq'), may hold values from -53 to 53
- first_conv: bfloat16 [3, 3, 3, 256, 256], replicated, may hold values from -0.078125 to 0.078125
- second_conv: bfloat16 [3, 3, 3, 256, 256], replicated, may hold values from -0.078125 to 0.078125
- out_conv: bfloat16 [3, 3, 3, 256, 16], replicated, may hold values from -0.078125 to 0.078125
- norm_gains: float32 [3, 256], replicated, may hold values from 0.25 to 1.75
- norm_shifts: float32 [3, 256], replicated, may hold values from -3 to 3
- embed_weight: bfloat16 [64, 3072], replicated, may hold values from -0.75 to 0.75
- embed_bias: float32 [3072], replicated, may hold values from -5 to 5
- mod_shift: float32 [8, 3072], P('clip'), may hold values from -3 to 3
- mod_scale: float32 [8, 3072], P('clip'), may hold values from -3 to 3
- qkv_weight: bfloat16 [4608, 3072], P(('clip', 'seq')), may hold values from -0.8 to 0.8
Outputs:
- latent: float32 [8, 16, 32, 32, 16], P('clip', None, 'seq')
- frame_heads: bfloat16 [8, 16, 256, 1536], P('clip', 'seq')
All inputs are finite; a program needn't handle non-finite values.
Results may differ from a plain program's by a relative error of at most 0.012.
Values may be sent and summed in bfloat16 or wider, within the bound.
No kernel may reach another device: no remote copies, remote signals or barrier semaphores. Data moves between devices by JAX's collectives and lax.ppermute only.
A program may use at most 192 MiB of HBM per device.

v0:
```python
import functools
import math

import jax
import jax.numpy as jnp
from jax import lax
from jax.experimental import pallas as pl
from jax.experimental.pallas import tpu as pltpu
from jax.sharding import PartitionSpec as P

C = 256
GROUPS = 32
LAT = 16
D = 3072
HEADS = 12
HDIM = 128
FRAMES = 16
HALF = 16
ROW = FRAMES * 2 * HALF
CELLS = 2 * ROW
SEQ = 16
CLIPS = 8
QROWS = 36
QPAD = 48
EPS = 1e-06
F32 = jnp.float32
BF16 = jnp.bfloat16
VMEM = pl.BlockSpec(memory_space=pltpu.VMEM)
SMEM = pl.BlockSpec(memory_space=pltpu.SMEM)
ANY = pl.BlockSpec(memory_space=pl.ANY)


def nt_dot(a, b):
    return lax.dot_general(a, b, (((1,), (1,)), ((), ())), preferred_element_type=F32)


def dot(a, b):
    return jnp.dot(a, b, preferred_element_type=F32)


def exact_dot(rows, zero_one):
    high = rows.astype(BF16).astype(F32)
    rest = rows - high
    mid = rest.astype(BF16).astype(F32)
    low = rest - mid
    parts = jnp.concatenate([high, mid, low, jnp.zeros_like(low)], axis=0).astype(BF16)
    out = dot(parts, zero_one)
    return out[0:8] + out[8:16] + out[16:24]


def iota(shape, dim):
    return lax.broadcasted_iota(jnp.int32, shape, dim)


def one_hot(cond):
    return jnp.where(cond, 1.0, 0.0).astype(BF16)


def rows8(first, second=None):
    n = first.shape[1]
    row = iota((8, n), 0)
    out = jnp.where(row == 0, jnp.broadcast_to(first, (8, n)), 0.0)
    if second is not None:
        out = jnp.where(row == 1, jnp.broadcast_to(second, (8, n)), out)
    return out


def write_stats(cells, stats_ref):
    count = cells.shape[0]
    mean_c = jnp.sum(cells, axis=0, keepdims=True) * (1.0 / count)
    same = one_hot((iota((C, C), 0) >> 3) == (iota((C, C), 1) >> 3))
    mean_g = exact_dot(rows8(mean_c), same)[0:1] * (1.0 / 8)
    off = cells - mean_c
    square_c = jnp.sum(off * off, axis=0, keepdims=True)
    gap = mean_c - mean_g
    square_c = square_c + count * (gap * gap)
    lane = iota((C, 128), 1)
    pick = one_hot((iota((C, 128), 0) >> 3) == (lane & 31))
    both = exact_dot(rows8(mean_c * (1.0 / 8), square_c), pick)
    row = jnp.where(iota((1, 128), 1) < GROUPS, both[0:1], both[1:2])
    stats_ref[...] = jnp.broadcast_to(row[None], (SEQ, 1, 128))


def read_stats(stats_ref, count):
    each = stats_ref[...].reshape(SEQ, 128)
    lane = iota((1, 128), 1)
    mean = jnp.sum(each, axis=0, keepdims=True) * (1.0 / SEQ)
    off = each - mean
    between = jnp.sum(off * off, axis=0, keepdims=True) * (8.0 * count)
    within = mean * SEQ
    total = jnp.where(lane < GROUPS, between, jnp.where(lane < 2 * GROUPS, within, 0.0))
    mean = jnp.where(lane < GROUPS, mean, 0.0)
    spread = one_hot((iota((128, C), 0) & 31) == (iota((128, C), 1) >> 3))
    both = exact_dot(rows8(mean, total), spread)
    return both[0:1], lax.rsqrt(both[1:2] * (1.0 / (8.0 * count * SEQ)) + EPS)


def split_kernel(feat_ref, f0_ref, f1_ref, stats_ref, wide):
    cells = feat_ref[...].astype(F32).reshape(CELLS, C)
    for side in range(2):
        wide[side] = cells[:, side * 128 : (side + 1) * 128]
    for frame in range(FRAMES):
        for row, out in ((0, f0_ref), (1, f1_ref)):
            for parity in range(2):
                base = (frame * 2 + row) * 32 + parity
                at = (frame * 2 + parity) * HALF
                for side in range(2):
                    part = wide[side, pl.ds(base, HALF, stride=2)]
                    out[at : at + HALF, side * 128 : (side + 1) * 128] = part.astype(BF16)
    write_stats(cells, stats_ref)


def fill_window(place_ref, stats_ref, rows, gain, shift, window):
    mean, rstd = read_stats(stats_ref, CELLS)
    gain = rstd * gain * 0.5
    shift = shift * 0.5
    place = place_ref[0]
    top_on = jnp.where(place > 0, 1.0, 0.0).astype(F32)
    low_on = jnp.where(place < SEQ - 1, 1.0, 0.0).astype(F32)
    window[:, 0:2] = jnp.zeros((4, 2, 4, HALF, C), BF16)
    step = 4
    n = step * HALF
    pair = iota((n, C), 0) & (HALF - 1)
    for row, source in enumerate(rows):
        for frame in range(0, FRAMES, step):
            x = source[frame * 32 : (frame + step) * 32].astype(F32)
            half = (x - mean) * gain + shift
            act = half + half * jnp.tanh(half)
            if row == 0:
                act = act * top_on
            if row == 3:
                act = act * low_on
            act = act.reshape(step, 2, HALF, C)
            even = act[:, 0].reshape(n, C)
            odd = act[:, 1].reshape(n, C)
            odd_before = jnp.where(pair == 0, 0.0, pltpu.roll(odd, 1, 0))
            even_after = jnp.where(pair == HALF - 1, 0.0, pltpu.roll(even, n - 1, 0))
            for plane, part in enumerate((odd_before, even, odd, even_after)):
                window[row, 2 + frame : 2 + frame + step, plane] = part.astype(BF16).reshape(
                    step, HALF, C
                )


def convolve(window, weight):
    total = None
    for tap in range(27):
        p, q, r = tap // 9, tap // 3 % 3, tap % 3
        cells = window[q : q + 2, p : p + FRAMES, r : r + 2].reshape(CELLS, C)
        term = dot(cells, weight[tap])
        total = term if total is None else total + term
    return total


def first_kernel(
    place_ref, stats_ref, top_ref, f0_ref, f1_ref, low_ref, gain_ref, shift_ref, weight_hbm,
    hidden_ref, h0_ref, h1_ref, stats_out, window, weight, sem,
):
    copy = pltpu.make_async_copy(weight_hbm, weight, sem)
    copy.start()
    rows = (top_ref, f0_ref, f1_ref, low_ref)
    fill_window(place_ref, stats_ref, rows, gain_ref[0:1], shift_ref[0:1], window)
    copy.wait()
    hidden = convolve(window, weight)
    hidden_ref[...] = hidden
    h0_ref[...] = hidden[:ROW].astype(BF16)
    h1_ref[...] = hidden[ROW:].astype(BF16)
    write_stats(hidden, stats_out)


def second_kernel(
    place_ref, stats_ref, top_ref, hidden_ref, low_ref, f0_ref, f1_ref, gain_ref, shift_ref, weight_hbm,
    b0_ref, b1_ref, stats_out, window, weight, sem,
):
    copy = pltpu.make_async_copy(weight_hbm, weight, sem)
    copy.start()
    rows = (top_ref, hidden_ref.at[0:ROW], hidden_ref.at[ROW:CELLS], low_ref)
    fill_window(place_ref, stats_ref, rows, gain_ref[1:2], shift_ref[1:2], window)
    copy.wait()
    added = convolve(window, weight)
    b0 = (added[:ROW] + f0_ref[...].astype(F32)).astype(BF16)
    b1 = (added[ROW:] + f1_ref[...].astype(F32)).astype(BF16)
    b0_ref[...] = b0
    b1_ref[...] = b1
    write_stats(jnp.concatenate([b0, b1], axis=0).astype(F32), stats_out)


def third_kernel(
    place_ref, stats_ref, top_ref, b0_ref, b1_ref, low_ref, gain_ref, shift_ref, weight_ref, embed_ref, bias_ref,
    latent_ref, tokens_ref, window,
):
    rows = (top_ref, b0_ref, b1_ref, low_ref)
    fill_window(place_ref, stats_ref, rows, gain_ref[2:3], shift_ref[2:3], window)
    latent = convolve(window, weight_ref).reshape(2, FRAMES, 2, HALF, LAT)
    n = FRAMES * HALF
    patches = jnp.concatenate(
        [latent[dh, :, dw].reshape(n, LAT) for dh in range(2) for dw in range(2)], axis=1
    )
    latent_ref[...] = patches
    rounded = patches.astype(BF16)
    embedded = dot(jnp.concatenate([rounded, rounded], axis=1), embed_ref[...]) + bias_ref[0:1]
    spread = jnp.sum(embedded * embedded, axis=1, keepdims=True) * (1.0 / D)
    rstd = lax.rsqrt(spread + EPS)
    high = rstd.astype(BF16).astype(F32)
    lane = iota((n, 128), 1)
    wide = jnp.concatenate([rounded.astype(F32) * rstd, jnp.zeros((n, 64), F32)], axis=1)
    wide = jnp.where((lane == 64) | (lane == 65), high, wide)
    wide = jnp.where((lane == 66) | (lane == 67), 1.0, wide)
    wide = jnp.where(lane == 68, rstd - high, wide)
    tokens_ref[...] = wide.astype(BF16)


def embed_kernel(embed_ref, bias_ref, embed_out, bias_out):
    embed = embed_ref[...].astype(F32)
    embed = embed - jnp.mean(embed, axis=1, keepdims=True)
    high = embed.astype(BF16)
    embed_out[0:64] = high
    embed_out[64:128] = (embed - high.astype(F32)).astype(BF16)
    bias = bias_ref[...]
    bias_out[...] = jnp.broadcast_to(bias - jnp.mean(bias, axis=1, keepdims=True), (8, D))


def fold_kernel(near_ref, far_refs, embed_ref, bias_ref, scale_ref, shift_ref, out_ref):
    scale = 1.0 + scale_ref[...]
    embed = (embed_ref[0:64].astype(F32) + embed_ref[64:128].astype(F32)) * scale
    row = iota((16, D), 0)
    ends = jnp.where(row == 0, bias_ref[0:1] * scale, jnp.where(row == 1, shift_ref[...], 0.0))
    every = jnp.concatenate([embed, ends], axis=0)
    high = every.astype(BF16).astype(F32)
    gap = jnp.zeros((48, D), F32)
    both = jnp.concatenate([high, gap, every - high, gap], axis=0).astype(BF16)
    lane = iota((QROWS, 128), 1)
    blocks = [near_ref.at[i] for i in range(2)] + [far.at[i] for far in far_refs for i in range(2)]
    for i, block in enumerate(blocks):
        out = nt_dot(block[...], both)
        out = out[:, 0:128] + out[:, 128:256]
        bias, shift = out[:, 64:65], out[:, 65:66]
        bias_high = bias.astype(BF16).astype(F32)
        shift_high = shift.astype(BF16).astype(F32)
        out = jnp.where((lane == 64) | (lane == 68), bias_high, out)
        out = jnp.where(lane == 65, bias - bias_high, out)
        out = jnp.where(lane == 66, shift_high, out)
        out = jnp.where(lane == 67, shift - shift_high, out)
        out_ref[i] = jnp.concatenate([out, jnp.zeros((QPAD - QROWS, 128), F32)], axis=0).astype(BF16)


def sort_kernel(place_ref, near_ref, far_ref, out_ref, wide):
    seq, clip = place_ref[0], place_ref[1]
    for j in range(SEQ):
        source = (near_ref, far_ref)[j & 1]
        for k in range(CLIPS):
            block = source[j >> 1, k].astype(F32)
            at = ((clip ^ k) * SEQ + (seq ^ j)) * QROWS
            wide[pl.ds(at, QROWS)] = block[:QROWS]
    out_ref[...] = wide[...].astype(BF16)


def attend_kernel(place_ref, near_ref, far_ref, fold_ref, out_ref, queries, mixed):
    seq = place_ref[0]
    blocks = [(near_ref, far_ref)[j & 1].at[j >> 1] for j in range(SEQ)]
    mine = pl.ds(pl.multiple_of(seq * HALF, HALF), HALF)
    tokens = jnp.concatenate([block[mine] for block in blocks], axis=0)
    wide = HEADS * HDIM
    scaled = (nt_dot(tokens, fold_ref[0:wide]) * (1.0 / math.sqrt(HDIM))).astype(BF16)
    for head in range(HEADS):
        cols = slice(head * HDIM, (head + 1) * HDIM)
        keyed = dot(scaled[:, cols], fold_ref[wide + head * HDIM : wide + (head + 1) * HDIM])
        queries[:, head] = keyed.astype(BF16).reshape(SEQ, HALF, 128)
    n = HEADS * HALF
    keys = FRAMES * HALF
    off = (iota((n, keys), 0) & (HALF - 1)) != (iota((n, keys), 1) & (HALF - 1))
    bar = jnp.where(off, -jnp.inf, 0.0)
    for j, block in enumerate(blocks):
        scores = nt_dot(queries[j].reshape(n, 128), block[...]) + bar
        raised = jnp.exp(scores - jnp.max(scores, axis=1, keepdims=True))
        mix = dot(raised.astype(BF16), block[...])
        mix = mix * (1.0 / mix[:, 66:67])
        mixed[:, j * HALF : (j + 1) * HALF] = mix.astype(BF16).reshape(HEADS, HALF, 128)
    for head in range(HEADS):
        cols = slice(head * HDIM, (head + 1) * HDIM)
        at = 2 * wide + head * HDIM
        out = nt_dot(mixed[head], fold_ref[at : at + HDIM]).astype(BF16)
        for j in range(SEQ):
            rows = pl.ds(pl.multiple_of((seq ^ j) * HALF, HALF), HALF)
            out_ref[rows, cols] = out[j * HALF : (j + 1) * HALF]


def shape(*dims, dtype=BF16):
    return jax.ShapeDtypeStruct(dims, dtype)


def call(body, outs, ins, scratch=(), flops=0, moved=0, limit=32):
    return pl.pallas_call(
        body,
        out_shape=outs,
        in_specs=ins,
        out_specs=jax.tree.map(lambda _: VMEM, outs),
        scratch_shapes=list(scratch),
        compiler_params=pltpu.CompilerParams(vmem_limit_bytes=limit << 20),
        cost_estimate=pl.CostEstimate(flops=flops, bytes_accessed=moved, transcendentals=0),
        name=body.__name__ if hasattr(body, "__name__") else None,
    )


def swap(values, axis, bits, count):
    return lax.ppermute(values, axis, [(i, i ^ bits) for i in range(count)])


def neighbours(low_row, high_row):
    top = lax.ppermute(high_row, "seq", [(i, i + 1) for i in range(SEQ - 1)])
    low = lax.ppermute(low_row, "seq", [(i + 1, i) for i in range(SEQ - 1)])
    return top, low


def exchange(stats):
    return lax.all_to_all(stats, "seq", 0, 0, tiled=True)


def gather_seq(block):
    pair = jnp.stack([block, swap(block, "seq", 8, SEQ)])
    others = [swap(pair, "seq", bits, SEQ) for bits in (2, 4, 6)]
    near = jnp.stack([pair] + others, axis=1).reshape((8,) + block.shape)
    return near, swap(near, "seq", 1, SEQ)


WINDOW = pltpu.VMEM((4, FRAMES + 2, 4, HALF, C), BF16)
WEIGHT = pltpu.VMEM((27, C, C), BF16)
CONV_FLOPS = 2 * CELLS * 27 * C * C


def shards(
    features,
    first_conv,
    second_conv,
    out_conv,
    norm_gains,
    norm_shifts,
    embed_weight,
    embed_bias,
    mod_shift,
    mod_scale,
    qkv_weight,
):
    place = jnp.stack([lax.axis_index("seq"), lax.axis_index("clip")]).astype(jnp.int32)
    row = shape(ROW, C)
    stats = shape(SEQ, 1, 128, dtype=F32)

    near_rows = jnp.stack([qkv_weight, swap(qkv_weight, "clip", 1, CLIPS)])
    far_rows = [swap(near_rows, "clip", bits, CLIPS) for bits in (2, 4, 6)]

    f0, f1, stats0 = call(
        split_kernel, [row, row, stats], [VMEM], [pltpu.VMEM((2, CELLS, 128), F32)], 0, 1 << 20
    )(features.reshape(FRAMES, 2, 32, C))
    top, low = neighbours(f0, f1)
    stats0 = exchange(stats0)
    hidden, h0, h1, stats1 = call(
        first_kernel,
        [shape(CELLS, C, dtype=F32), row, row, stats],
        [SMEM] + [VMEM] * 7 + [ANY],
        [WINDOW, WEIGHT, pltpu.SemaphoreType.DMA],
        CONV_FLOPS,
        5 << 20,
    )(place, stats0, top, f0, f1, low, norm_gains, norm_shifts, first_conv.reshape(27, C, C))
    top, low = neighbours(h0, h1)
    stats1 = exchange(stats1)
    b0, b1, stats2 = call(
        second_kernel,
        [row, row, stats],
        [SMEM] + [VMEM] * 8 + [ANY],
        [WINDOW, WEIGHT, pltpu.SemaphoreType.DMA],
        CONV_FLOPS,
        6 << 20,
    )(place, stats1, top, hidden, low, f0, f1, norm_gains, norm_shifts, second_conv.reshape(27, C, C))
    top, low = neighbours(b0, b1)

    embed, bias = call(embed_kernel, [shape(128, D), shape(8, D, dtype=F32)], [VMEM] * 2)(
        embed_weight, embed_bias.reshape(1, D)
    )
    folded = call(
        lambda near, a, b, c, *rest: fold_kernel(near, (a, b, c), *rest),
        shape(CLIPS, QPAD, 128),
        [VMEM] * 8,
    )(near_rows, *far_rows, embed, bias, mod_scale, mod_shift)
    fold_near, fold_far = gather_seq(folded)

    stats2 = exchange(stats2)
    patches, tokens = call(
        third_kernel,
        [shape(FRAMES * HALF, 4 * LAT, dtype=F32), shape(FRAMES * HALF, 128)],
        [SMEM] + [VMEM] * 10,
        [WINDOW],
        CONV_FLOPS // 2,
        4 << 20,
    )(
        place, stats2, top, b0, b1, low, norm_gains, norm_shifts, out_conv.reshape(27, C, LAT), embed, bias
    )
    token_near, token_far = gather_seq(tokens)
    sorted_rows = call(
        sort_kernel,
        shape(3 * HEADS * HDIM, 128),
        [SMEM] + [VMEM] * 2,
        [pltpu.VMEM((3 * HEADS * HDIM, 128), F32)],
    )(place, fold_near, fold_far)
    frame_heads = call(
        attend_kernel,
        shape(SEQ * HALF, HEADS * HDIM),
        [SMEM] + [VMEM] * 3,
        [pltpu.VMEM((SEQ, HEADS, HALF, 128), BF16), pltpu.VMEM((HEADS, SEQ * HALF, 128), BF16)],
    )(place, token_near, token_far, sorted_rows)
    latent = patches.reshape(FRAMES, HALF, 2, 2, LAT).transpose(0, 2, 1, 3, 4)
    return (
        latent.reshape(1, FRAMES, 2, 2 * HALF, LAT),
        frame_heads.reshape(1, 1, SEQ * HALF, HEADS * HDIM),
    )


def solution(mesh):
    placed = (
        P("clip", None, "seq", None, None),
        P(),
        P(),
        P(),
        P(),
        P(),
        P(),
        P(),
        P("clip", None),
        P("clip", None),
        P(("clip", "seq"), None),
    )
    return jax.shard_map(
        shards,
        mesh=mesh,
        in_specs=placed,
        out_specs=(P("clip", None, "seq", None, None), P("clip", "seq", None, None)),
        check_vma=False,
    )
```

profile of v0, /device:TPU:1, one launch (start us, length us, event | category | flops | bytes accessed | tf_op | source)
XLA Modules:
  0.0 130.4 jit_solution(7355320794920097219)
XLA Ops:
  2.9 4.5 %collective-permute-start = (bf16[512,256]{1,0:T(8,128)(2,1)S(1)}, bf16[512,256]{1,0:T(8,128)(2,1)S(1)}, u32[]{:S(2)}, u32[]{:S(2)}) collective-permute-start(bf16[512,256]{1,0:T(8,128)(2,1)S(1)} %get-tuple-element.17.f1_ref), channel_id=1, source_target_pairs={{0,1},{1,2},{2,3},{3,4},{4,5},{5,6},{6,7},{7,8},{8,9},{9,10},{10,1... | collective-permute-start | bytes 786440 | tf_op jit(solution)/shard_map/ppermute | solution.py:309
  7.4 1.9 %collective-permute-start.1 = (bf16[512,256]{1,0:T(8,128)(2,1)S(1)}, bf16[512,256]{1,0:T(8,128)(2,1)S(1)}, u32[]{:S(2)}, u32[]{:S(2)}) collective-permute-start(bf16[512,256]{1,0:T(8,128)(2,1)S(1)} %get-tuple-element.18.f0_ref), channel_id=1, source_target_pairs={{1,0},{2,1},{3,2},{4,3},{5,4},{6,5},{7,6},{8,7},{9,8},{10,9},{11,1... | collective-permute-start | bytes 786440 | tf_op jit(solution)/shard_map/ppermute | solution.py:310
  9.4 9.4 %all-to-all-start = ((f32[16,1,128]{2,1,0:T(1,128)}), f32[16,1,128]{2,1,0:T(1,128)S(1)}, u32[]{:S(2)}, u32[]{:S(2)}) async-start(f32[16,1,128]{2,1,0:T(1,128)} %get-tuple-element.16), calls=%async_computation | async-start | bytes 16384 | tf_op jit(solution)/shard_map/all_to_all | solution.py:315
  19.6 6.1 %all-to-all-done.stats_ref = f32[16,1,128]{2,1,0:T(1,128)S(1)} async-done(((f32[16,1,128]{2,1,0:T(1,128)}), f32[16,1,128]{2,1,0:T(1,128)S(1)}, u32[]{:S(2)}, u32[]{:S(2)}) %all-to-all-start) | async-done | bytes 8224 | tf_op jit(solution)/shard_map/all_to_all | solution.py:315
  25.7 2.0 %copy-done.5 = bf16[3,3,3,256,256]{4,3,2,1,0:T(8,128)(2,1)S(1)} copy-done((bf16[3,3,3,256,256]{4,3,2,1,0:T(8,128)(2,1)S(1)}, bf16[3,3,3,256,256]{4,3,2,1,0:T(8,128)(2,1)}, u32[]{:S(2)}) %copy-start.5) | copy-done | bytes 3538968
  29.1 6.0 %first_kernel.1 = (f32[1024,256]{1,0:T(8,128)S(1)}, bf16[512,256]{1,0:T(8,128)(2,1)S(1)}, bf16[512,256]{1,0:T(8,128)(2,1)S(1)}, f32[16,1,128]{2,1,0:T(1,128)S(1)}) custom-call(s32[2]{0:T(128)S(1)} %pad_add_fusion.place_ref, f32[16,1,128]{2,1,0:T(1,128)S(1)} %all-to-all-done.stats_ref, bf16[512,256]{1,0:T(8,128)(2,1)S(1)} %collective-permute-done.top_ref, ...), custom_call_target="tpu_custom_call" | custom-call | flops 3623878656 | bytes 5242880 | tf_op jit(solution)/shard_map/first_kernel/pallas_call | solution.py:355
  35.1 2.7 %collective-permute-start.2 = (bf16[512,256]{1,0:T(8,128)(2,1)S(1)}, bf16[512,256]{1,0:T(8,128)(2,1)S(1)}, u32[]{:S(2)}, u32[]{:S(2)}) collective-permute-start(bf16[512,256]{1,0:T(8,128)(2,1)S(1)} %get-tuple-element.20), channel_id=1, source_target_pairs={{0,1},{1,2},{2,3},{3,4},{4,5},{5,6},{6,7},{7,8},{8,9},{9,10},{10,1... | collective-permute-start | bytes 786440 | tf_op jit(solution)/shard_map/ppermute | solution.py:309
  37.8 1.9 %collective-permute-start.3 = (bf16[512,256]{1,0:T(8,128)(2,1)S(1)}, bf16[512,256]{1,0:T(8,128)(2,1)S(1)}, u32[]{:S(2)}, u32[]{:S(2)}) collective-permute-start(bf16[512,256]{1,0:T(8,128)(2,1)S(1)} %get-tuple-element.22), channel_id=1, source_target_pairs={{1,0},{2,1},{3,2},{4,3},{5,4},{6,5},{7,6},{8,7},{9,8},{10,9},{11,1... | collective-permute-start | bytes 786440 | tf_op jit(solution)/shard_map/ppermute | solution.py:310
  41.2 2.6 %collective-permute-start.13 = (bf16[2,36,3072]{2,1,0:T(8,128)(2,1)S(1)}, bf16[2,36,3072]{2,1,0:T(8,128)(2,1)S(1)}, u32[]{:S(2)}, u32[]{:S(2)}) collective-permute-start(bf16[2,36,3072]{2,1,0:T(8,128)(2,1)S(1)} %pad_maximum_fusion.2.near), channel_id=1, source_target_pairs={{0,64},{16,80},{32,96},{48,112},{64,0},{80,16},{96,32},{112,48},{1... | collective-permute-start | bytes 1327112 | tf_op jit(solution)/shard_map/ppermute | solution.py:305
  43.8 14.6 %all_to_all.15.stats_ref = f32[16,1,128]{2,1,0:T(1,128)S(1)} all-to-all(f32[16,1,128]{2,1,0:T(1,128)S(1)} %get-tuple-element.19), channel_id=1, replica_groups=mesh['clip'=8,'seq'=16] {'seq'}, dimensions={0} | all-to-all | bytes 16384 | tf_op jit(solution)/shard_map/all_to_all | solution.py:315
  58.5 6.6 %second_kernel.1 = (bf16[512,256]{1,0:T(8,128)(2,1)S(1)}, bf16[512,256]{1,0:T(8,128)(2,1)S(1)}, f32[16,1,128]{2,1,0:T(1,128)}) custom-call(s32[2]{0:T(128)S(1)} %pad_add_fusion.place_ref, f32[16,1,128]{2,1,0:T(1,128)S(1)} %all_to_all.15.stats_ref, bf16[512,256]{1,0:T(8,128)(2,1)S(1)} %collective-permute-done.2.top_ref, ...), custom_call_target="tpu_custom_call" | custom-call | flops 3623878656 | bytes 6291456 | tf_op jit(solution)/shard_map/second_kernel/pallas_call | solution.py:365
  65.1 2.7 %collective-permute-start.4 = (bf16[512,256]{1,0:T(8,128)(2,1)S(1)}, bf16[512,256]{1,0:T(8,128)(2,1)}, u32[]{:S(2)}, u32[]{:S(2)}) collective-permute-start(bf16[512,256]{1,0:T(8,128)(2,1)S(1)} %get-tuple-element.24.b1_ref), channel_id=1, source_target_pairs={{0,1},{1,2},{2,3},{3,4},{4,5},{5,6},{6,7},{7,8},{8,9},{9,10},{10,1... | collective-permute-start | bytes 786440 | tf_op jit(solution)/shard_map/ppermute | solution.py:309
  67.9 2.3 %collective-permute-start.5 = (bf16[512,256]{1,0:T(8,128)(2,1)S(1)}, bf16[512,256]{1,0:T(8,128)(2,1)}, u32[]{:S(2)}, u32[]{:S(2)}) collective-permute-start(bf16[512,256]{1,0:T(8,128)(2,1)S(1)} %get-tuple-element.25.b0_ref), channel_id=1, source_target_pairs={{1,0},{2,1},{3,2},{4,3},{5,4},{6,5},{7,6},{8,7},{9,8},{10,9},{11,1... | collective-permute-start | bytes 786440 | tf_op jit(solution)/shard_map/ppermute | solution.py:310
  70.5 3.3 %_lambda_.1 = bf16[8,48,128]{2,1,0:T(8,128)(2,1)S(1)} custom-call(bf16[2,36,3072]{2,1,0:T(8,128)(2,1)S(1)} %pad_maximum_fusion.2.near, bf16[2,36,3072]{2,1,0:T(8,128)(2,1)S(1)} %collective-permute-done.12.a, bf16[2,36,3072]{2,1,0:T(8,128)(2,1)S(1)} %collective-permute-done.13.b, bf16[2,36,3072]{2,1,0:T(8,128)(2,1)S(1)} %collective-permute-done.14.c, ...), custom_call_target="tpu_custom_call" | custom-call | tf_op jit(solution)/shard_map/<lambda>/pallas_call | solution.py:378
  74.0 5.0 %collective-permute-done.15 = bf16[8,48,128]{2,1,0:T(8,128)(2,1)S(1)} collective-permute-done((bf16[8,48,128]{2,1,0:T(8,128)(2,1)S(1)}, bf16[8,48,128]{2,1,0:T(8,128)(2,1)S(1)}, u32[]{:S(2)}, u32[]{:S(2)}) %collective-permute-start.15) | collective-permute-done | bytes 98336 | tf_op jit(solution)/shard_map/ppermute | solution.py:305
  79.7 5.0 %collective-permute-start.18 = (bf16[2,8,48,128]{3,2,1,0:T(8,128)(2,1)}, bf16[2,8,48,128]{3,2,1,0:T(8,128)(2,1)}, u32[]{:S(2)}, u32[]{:S(2)}) collective-permute-start(bf16[2,8,48,128]{3,2,1,0:T(8,128)(2,1)} %get-tuple-element.33), channel_id=1, source_target_pairs={{0,6},{1,7},{2,4},{3,5},{4,2},{5,3},{6,0},{7,1},{8,14},{9,15},{10,... | collective-permute-start | bytes 589832 | tf_op jit(solution)/shard_map/ppermute | solution.py:305
  85.3 6.4 %all-to-all-start.2 = ((f32[16,1,128]{2,1,0:T(1,128)}), f32[16,1,128]{2,1,0:T(1,128)S(1)}, u32[]{:S(2)}, u32[]{:S(2)}) async-start(f32[16,1,128]{2,1,0:T(1,128)} %get-tuple-element.23), calls=%async_computation.2 | async-start | bytes 16384 | tf_op jit(solution)/shard_map/all_to_all | solution.py:315
  91.7 1.8 %copy.17 = bf16[3,3,3,256,16]{4,3,2,1,0:T(8,128)(2,1)S(1)} copy(bf16[3,3,3,256,16]{3,4,2,1,0:T(8,128)(2,1)} %param.14) | data formatting | bytes 442368 | tf_op args[3]
  93.5 5.2 %all-to-all-done.2.stats_ref = f32[16,1,128]{2,1,0:T(1,128)S(1)} async-done(((f32[16,1,128]{2,1,0:T(1,128)}), f32[16,1,128]{2,1,0:T(1,128)S(1)}, u32[]{:S(2)}, u32[]{:S(2)}) %all-to-all-start.2) | async-done | bytes 8224 | tf_op jit(solution)/shard_map/all_to_all | solution.py:315
  98.7 6.6 %third_kernel.1 = (f32[256,64]{1,0:T(8,128)S(1)}, bf16[256,128]{1,0:T(8,128)(2,1)S(1)}) custom-call(s32[2]{0:T(128)S(1)} %pad_add_fusion.place_ref, f32[16,1,128]{2,1,0:T(1,128)S(1)} %all-to-all-done.2.stats_ref, bf16[512,256]{1,0:T(8,128)(2,1)} %collective-permute-done.4.top_ref, bf16[512,256]{1,0:T(8,128)(2,1)S(1)} %get-tuple-element.25.b0_ref, ...), custom_call_target="tpu_custom_call" | custom-call | flops 1811939328 | bytes 4194304 | tf_op jit(solution)/shard_map/third_kernel/pallas_call | solution.py:386
  113.4 3.5 %collective-permute-done.9 = bf16[2,256,128]{2,1,0:T(8,128)(2,1)S(1)} collective-permute-done((bf16[2,256,128]{2,1,0:T(8,128)(2,1)S(1)}, bf16[2,256,128]{2,1,0:T(8,128)(2,1)S(1)}, u32[]{:S(2)}, u32[]{:S(2)}) %collective-permute-start.9) | collective-permute-done | bytes 131104 | tf_op jit(solution)/shard_map/ppermute | solution.py:305
  117.7 3.1 %collective-permute-start.10 = (bf16[8,256,128]{2,1,0:T(8,128)(2,1)S(1)}, bf16[8,256,128]{2,1,0:T(8,128)(2,1)S(1)}, u32[]{:S(2)}, u32[]{:S(2)}) collective-permute-start(bf16[8,256,128]{2,1,0:T(8,128)(2,1)S(1)} %bitcast.32), channel_id=1, source_target_pairs={{0,1},{1,0},{2,3},{3,2},{4,5},{5,4},{6,7},{7,6},{8,9},{9,8},{10,11... | collective-permute-start | bytes 1572872 | tf_op jit(solution)/shard_map/ppermute | solution.py:305
  122.4 2.0 %copy.22 = f32[1,16,2,32,16]{3,4,2,1,0:T(8,128)} copy(f32[1,16,2,32,16]{4,1,3,2,0:T(8,128)} %bitcast.42) | data formatting | bytes 131072
  125.2 5.2 %attend_kernel.1 = bf16[256,1536]{1,0:T(8,128)(2,1)} custom-call(s32[2]{0:T(128)S(1)} %pad_add_fusion.place_ref, bf16[8,256,128]{2,1,0:T(8,128)(2,1)S(1)} %bitcast.33, bf16[8,256,128]{2,1,0:T(8,128)(2,1)S(1)} %collective-permute-done.10.far_ref, bf16[4608,128]{1,0:T(8,128)(2,1)S(1)} %sort_kernel.1.fold_ref), custom_call_target="tpu_custom_call" | custom-call | tf_op jit(solution)/shard_map/attend_kernel/pallas_call | solution.py:403
  (68 shorter events, 19.0 us)
Async XLA Ops:
  2.9 22.8 %collective-permute-start = (bf16[512,256]{1,0:T(8,128)(2,1)S(1)}, bf16[512,256]{1,0:T(8,128)(2,1)S(1)}, u32[]{:S(2)}, u32[]{:S(2)}) collective-permute-start(bf16[512,256]{1,0:T(8,128)(2,1)S(1)} %get-tuple-element.17.f1_ref), channel_id=1, source_target_pairs={{0,1},{1,2},{2,3},{3,4},{4,5},{5,6},{6,7},{7,8},{8,9},{9,10},{10,1... | collective-permute-start | bytes 786440 | tf_op jit(solution)/shard_map/ppermute | solution.py:309
  7.4 18.3 %collective-permute-start.1 = (bf16[512,256]{1,0:T(8,128)(2,1)S(1)}, bf16[512,256]{1,0:T(8,128)(2,1)S(1)}, u32[]{:S(2)}, u32[]{:S(2)}) collective-permute-start(bf16[512,256]{1,0:T(8,128)(2,1)S(1)} %get-tuple-element.18.f0_ref), channel_id=1, source_target_pairs={{1,0},{2,1},{3,2},{4,3},{5,4},{6,5},{7,6},{8,7},{9,8},{10,9},{11,1... | collective-permute-start | bytes 786440 | tf_op jit(solution)/shard_map/ppermute | solution.py:310
  9.4 16.3 %all-to-all-start = ((f32[16,1,128]{2,1,0:T(1,128)}), f32[16,1,128]{2,1,0:T(1,128)S(1)}, u32[]{:S(2)}, u32[]{:S(2)}) async-start(f32[16,1,128]{2,1,0:T(1,128)} %get-tuple-element.16), calls=%async_computation | async-start | bytes 16384 | tf_op jit(solution)/shard_map/all_to_all | solution.py:315
  18.8 21.0 %collective-permute-start.11 = (bf16[36,3072]{1,0:T(8,128)(2,1)}, bf16[36,3072]{1,0:T(8,128)(2,1)S(1)}, u32[]{:S(2)}, u32[]{:S(2)}) collective-permute-start(bf16[36,3072]{1,0:T(8,128)(2,1)} %param.21), channel_id=1, source_target_pairs={{0,16},{16,0},{32,48},{48,32},{64,80},{80,64},{96,112},{112,96},{1... | collective-permute-start | bytes 663560 | tf_op jit(solution)/shard_map/ppermute | solution.py:305
  35.1 23.4 %collective-permute-start.2 = (bf16[512,256]{1,0:T(8,128)(2,1)S(1)}, bf16[512,256]{1,0:T(8,128)(2,1)S(1)}, u32[]{:S(2)}, u32[]{:S(2)}) collective-permute-start(bf16[512,256]{1,0:T(8,128)(2,1)S(1)} %get-tuple-element.20), channel_id=1, source_target_pairs={{0,1},{1,2},{2,3},{3,4},{4,5},{5,6},{6,7},{7,8},{8,9},{9,10},{10,1... | collective-permute-start | bytes 786440 | tf_op jit(solution)/shard_map/ppermute | solution.py:309
  37.8 20.6 %collective-permute-start.3 = (bf16[512,256]{1,0:T(8,128)(2,1)S(1)}, bf16[512,256]{1,0:T(8,128)(2,1)S(1)}, u32[]{:S(2)}, u32[]{:S(2)}) collective-permute-start(bf16[512,256]{1,0:T(8,128)(2,1)S(1)} %get-tuple-element.22), channel_id=1, source_target_pairs={{1,0},{2,1},{3,2},{4,3},{5,4},{6,5},{7,6},{8,7},{9,8},{10,9},{11,1... | collective-permute-start | bytes 786440 | tf_op jit(solution)/shard_map/ppermute | solution.py:310
  39.8 30.7 %collective-permute-start.12 = (bf16[2,36,3072]{2,1,0:T(8,128)(2,1)S(1)}, bf16[2,36,3072]{2,1,0:T(8,128)(2,1)S(1)}, u32[]{:S(2)}, u32[]{:S(2)}) collective-permute-start(bf16[2,36,3072]{2,1,0:T(8,128)(2,1)S(1)} %pad_maximum_fusion.2.near), channel_id=1, source_target_pairs={{0,32},{16,48},{32,0},{48,16},{64,96},{80,112},{96,64},{112,80},{1... | collective-permute-start | bytes 1327112 | tf_op jit(solution)/shard_map/ppermute | solution.py:305
  41.2 29.3 %collective-permute-start.13 = (bf16[2,36,3072]{2,1,0:T(8,128)(2,1)S(1)}, bf16[2,36,3072]{2,1,0:T(8,128)(2,1)S(1)}, u32[]{:S(2)}, u32[]{:S(2)}) collective-permute-start(bf16[2,36,3072]{2,1,0:T(8,128)(2,1)S(1)} %pad_maximum_fusion.2.near), channel_id=1, source_target_pairs={{0,64},{16,80},{32,96},{48,112},{64,0},{80,16},{96,32},{112,48},{1... | collective-permute-start | bytes 1327112 | tf_op jit(solution)/shard_map/ppermute | solution.py:305
  43.8 26.7 %collective-permute-start.14 = (bf16[2,36,3072]{2,1,0:T(8,128)(2,1)S(1)}, bf16[2,36,3072]{2,1,0:T(8,128)(2,1)S(1)}, u32[]{:S(2)}, u32[]{:S(2)}) collective-permute-start(bf16[2,36,3072]{2,1,0:T(8,128)(2,1)S(1)} %pad_maximum_fusion.2.near), channel_id=1, source_target_pairs={{0,96},{16,112},{32,64},{48,80},{64,32},{80,48},{96,0},{112,16},{1... | collective-permute-start | bytes 1327112 | tf_op jit(solution)/shard_map/ppermute | solution.py:305
  65.1 33.6 %copy-start.8 = (f32[3,256]{1,0:T(4,128)S(1)}, f32[3,256]{1,0:T(4,128)}, u32[]{:S(2)}) copy-start(f32[3,256]{1,0:T(4,128)} %gain_ref.5) | copy-start | bytes 9220
  65.1 33.6 %copy-start.10 = (f32[3,256]{1,0:T(4,128)S(1)}, f32[3,256]{1,0:T(4,128)}, u32[]{:S(2)}) copy-start(f32[3,256]{1,0:T(4,128)} %shift_ref.5) | copy-start | bytes 9220
  65.1 33.6 %collective-permute-start.4 = (bf16[512,256]{1,0:T(8,128)(2,1)S(1)}, bf16[512,256]{1,0:T(8,128)(2,1)}, u32[]{:S(2)}, u32[]{:S(2)}) collective-permute-start(bf16[512,256]{1,0:T(8,128)(2,1)S(1)} %get-tuple-element.24.b1_ref), channel_id=1, source_target_pairs={{0,1},{1,2},{2,3},{3,4},{4,5},{5,6},{6,7},{7,8},{8,9},{9,10},{10,1... | collective-permute-start | bytes 786440 | tf_op jit(solution)/shard_map/ppermute | solution.py:309
  67.9 30.8 %collective-permute-start.5 = (bf16[512,256]{1,0:T(8,128)(2,1)S(1)}, bf16[512,256]{1,0:T(8,128)(2,1)}, u32[]{:S(2)}, u32[]{:S(2)}) collective-permute-start(bf16[512,256]{1,0:T(8,128)(2,1)S(1)} %get-tuple-element.25.b0_ref), channel_id=1, source_target_pairs={{1,0},{2,1},{3,2},{4,3},{5,4},{6,5},{7,6},{8,7},{9,8},{10,9},{11,1... | collective-permute-start | bytes 786440 | tf_op jit(solution)/shard_map/ppermute | solution.py:310
  73.9 5.1 %collective-permute-start.15 = (bf16[8,48,128]{2,1,0:T(8,128)(2,1)S(1)}, bf16[8,48,128]{2,1,0:T(8,128)(2,1)S(1)}, u32[]{:S(2)}, u32[]{:S(2)}) collective-permute-start(bf16[8,48,128]{2,1,0:T(8,128)(2,1)S(1)} %_lambda_.1), channel_id=1, source_target_pairs={{0,8},{1,9},{2,10},{3,11},{4,12},{5,13},{6,14},{7,15},{8,0},{9,1},... | collective-permute-start | bytes 294920 | tf_op jit(solution)/shard_map/ppermute | solution.py:305
  79.7 27.1 %collective-permute-start.18 = (bf16[2,8,48,128]{3,2,1,0:T(8,128)(2,1)}, bf16[2,8,48,128]{3,2,1,0:T(8,128)(2,1)}, u32[]{:S(2)}, u32[]{:S(2)}) collective-permute-start(bf16[2,8,48,128]{3,2,1,0:T(8,128)(2,1)} %get-tuple-element.33), channel_id=1, source_target_pairs={{0,6},{1,7},{2,4},{3,5},{4,2},{5,3},{6,0},{7,1},{8,14},{9,15},{10,... | collective-permute-start | bytes 589832 | tf_op jit(solution)/shard_map/ppermute | solution.py:305
  84.7 22.1 %collective-permute-start.17 = (bf16[2,8,48,128]{3,2,1,0:T(8,128)(2,1)}, bf16[2,8,48,128]{3,2,1,0:T(8,128)(2,1)}, u32[]{:S(2)}, u32[]{:S(2)}) collective-permute-start(bf16[2,8,48,128]{3,2,1,0:T(8,128)(2,1)} %get-tuple-element.33), channel_id=1, source_target_pairs={{0,4},{1,5},{2,6},{3,7},{4,0},{5,1},{6,2},{7,3},{8,12},{9,13},{10,... | collective-permute-start | bytes 589832 | tf_op jit(solution)/shard_map/ppermute | solution.py:305
  84.7 22.1 %collective-permute-start.16 = (bf16[2,8,48,128]{3,2,1,0:T(8,128)(2,1)}, bf16[2,8,48,128]{3,2,1,0:T(8,128)(2,1)}, u32[]{:S(2)}, u32[]{:S(2)}) collective-permute-start(bf16[2,8,48,128]{3,2,1,0:T(8,128)(2,1)} %get-tuple-element.33), channel_id=1, source_target_pairs={{0,2},{1,3},{2,0},{3,1},{4,6},{5,7},{6,4},{7,5},{8,10},{9,11},{10,... | collective-permute-start | bytes 589832 | tf_op jit(solution)/shard_map/ppermute | solution.py:305
  85.3 13.4 %all-to-all-start.2 = ((f32[16,1,128]{2,1,0:T(1,128)}), f32[16,1,128]{2,1,0:T(1,128)S(1)}, u32[]{:S(2)}, u32[]{:S(2)}) async-start(f32[16,1,128]{2,1,0:T(1,128)} %get-tuple-element.23), calls=%async_computation.2 | async-start | bytes 16384 | tf_op jit(solution)/shard_map/all_to_all | solution.py:315
  105.3 4.7 %collective-permute-start.6 = (bf16[256,128]{1,0:T(8,128)(2,1)S(1)}, bf16[256,128]{1,0:T(8,128)(2,1)S(1)}, u32[]{:S(2)}, u32[]{:S(2)}) collective-permute-start(bf16[256,128]{1,0:T(8,128)(2,1)S(1)} %get-tuple-element.29), channel_id=1, source_target_pairs={{0,8},{1,9},{2,10},{3,11},{4,12},{5,13},{6,14},{7,15},{8,0},{9,1},... | collective-permute-start | bytes 196616 | tf_op jit(solution)/shard_map/ppermute | solution.py:305
  108.1 16.3 %collective-permute-start.19 = (bf16[8,8,48,128]{3,2,1,0:T(8,128)(2,1)S(1)}, bf16[8,8,48,128]{3,2,1,0:T(8,128)(2,1)S(1)}, u32[]{:S(2)}, u32[]{:S(2)}) collective-permute-start(bf16[8,8,48,128]{3,2,1,0:T(8,128)(2,1)S(1)} %bitcast.30), channel_id=1, source_target_pairs={{0,1},{1,0},{2,3},{3,2},{4,5},{5,4},{6,7},{7,6},{8,9},{9,8},{10,11... | collective-permute-start | bytes 2359304 | tf_op jit(solution)/shard_map/ppermute | solution.py:305
  110.1 6.9 %collective-permute-start.9 = (bf16[2,256,128]{2,1,0:T(8,128)(2,1)S(1)}, bf16[2,256,128]{2,1,0:T(8,128)(2,1)S(1)}, u32[]{:S(2)}, u32[]{:S(2)}) collective-permute-start(bf16[2,256,128]{2,1,0:T(8,128)(2,1)S(1)} %get-tuple-element.35), channel_id=1, source_target_pairs={{0,6},{1,7},{2,4},{3,5},{4,2},{5,3},{6,0},{7,1},{8,14},{9,15},{10,... | collective-permute-start | bytes 393224 | tf_op jit(solution)/shard_map/ppermute | solution.py:305
  111.0 5.9 %collective-permute-start.8 = (bf16[2,256,128]{2,1,0:T(8,128)(2,1)S(1)}, bf16[2,256,128]{2,1,0:T(8,128)(2,1)S(1)}, u32[]{:S(2)}, u32[]{:S(2)}) collective-permute-start(bf16[2,256,128]{2,1,0:T(8,128)(2,1)S(1)} %get-tuple-element.35), channel_id=1, source_target_pairs={{0,4},{1,5},{2,6},{3,7},{4,0},{5,1},{6,2},{7,3},{8,12},{9,13},{10,... | collective-permute-start | bytes 393224 | tf_op jit(solution)/shard_map/ppermute | solution.py:305
  112.2 5.4 %collective-permute-start.7 = (bf16[2,256,128]{2,1,0:T(8,128)(2,1)S(1)}, bf16[2,256,128]{2,1,0:T(8,128)(2,1)S(1)}, u32[]{:S(2)}, u32[]{:S(2)}) collective-permute-start(bf16[2,256,128]{2,1,0:T(8,128)(2,1)S(1)} %get-tuple-element.35), channel_id=1, source_target_pairs={{0,2},{1,3},{2,0},{3,1},{4,6},{5,7},{6,4},{7,5},{8,10},{9,11},{10,... | collective-permute-start | bytes 393224 | tf_op jit(solution)/shard_map/ppermute | solution.py:305
  117.7 7.5 %collective-permute-start.10 = (bf16[8,256,128]{2,1,0:T(8,128)(2,1)S(1)}, bf16[8,256,128]{2,1,0:T(8,128)(2,1)S(1)}, u32[]{:S(2)}, u32[]{:S(2)}) collective-permute-start(bf16[8,256,128]{2,1,0:T(8,128)(2,1)S(1)} %bitcast.32), channel_id=1, source_target_pairs={{0,1},{1,0},{2,3},{3,2},{4,5},{5,4},{6,7},{7,6},{8,9},{9,8},{10,11... | collective-permute-start | bytes 1572872 | tf_op jit(solution)/shard_map/ppermute | solution.py:305
  (11 other events, 100.1 us)
where the time goes:
time: 131 us; the launch traced here: 130 us
  starting transfers between devices  51.2 us (39%)
  Pallas kernels  30.2 us (23%)
  waiting for transfers between devices  21.5 us (16%)
  blocking collectives  14.6 us (11%)
  local copies, waits for them, and re-layouts  9.8 us (7%)
  other arithmetic  2.2 us (2%)
    ppermute x14, starting transfers between devices, swap(): return lax.ppermute(values, axis, [(i, i ^ bits) for i in range(count)])  19.3 us
    all_to_all x2, starting transfers between devices, exchange(): return lax.all_to_all(stats, 'seq', 0, 0, tiled=True)  15.8 us
    all_to_all x1, blocking collectives, exchange(): return lax.all_to_all(stats, 'seq', 0, 0, tiled=True)  14.6 us
    all_to_all x2, waiting for transfers between devices, exchange(): return lax.all_to_all(stats, 'seq', 0, 0, tiled=True)  11.3 us
    ppermute x14, waiting for transfers between devices, swap(): return lax.ppermute(values, axis, [(i, i ^ bits) for i in range(count)])  10.2 us
    ppermute x3, starting transfers between devices, neighbours(): top = lax.ppermute(high_row, 'seq', [(i, i + 1) for i in range(SEQ - 1)])  9.99 us
    unnamed x28, local copies, waits for them, and re-layouts  8.2 us
    pallas_call x1, Pallas kernels, shards(): call(third_kernel, [shape(FRAMES * HALF, 4 * LAT, dtype=F32), shape(FRAME...  6.62 us
  transfers between devices with their start and end apart: 22, of which 6 were waited for; matrix products, arithmetic and copies ran while one was open for 6% of the time, Pallas kernels for 18%

commit v1 on v0

--- a/solution.py
+++ b/solution.py
@@ -141,26 +141,36 @@
                 )
 
 
-def convolve(window, weight):
+def convolve(window, weight, copies):
     total = None
-    for tap in range(27):
-        p, q, r = tap // 9, tap // 3 % 3, tap % 3
-        cells = window[q : q + 2, p : p + FRAMES, r : r + 2].reshape(CELLS, C)
-        term = dot(cells, weight[tap])
-        total = term if total is None else total + term
+    for p in range(3):
+        copies[p].wait()
+        for q in range(3):
+            for r in range(3):
+                cells = window[q : q + 2, p : p + FRAMES, r : r + 2].reshape(CELLS, C)
+                term = dot(cells, weight[9 * p + 3 * q + r])
+                total = term if total is None else total + term
     return total
+
+
+def start_weights(source, weight, sems):
+    copies = [
+        pltpu.make_async_copy(source.at[9 * p : 9 * p + 9], weight.at[9 * p : 9 * p + 9], sems.at[p])
+        for p in range(3)
+    ]
+    for copy in copies:
+        copy.start()
+    return copies
 
 
 def first_kernel(
     place_ref, stats_ref, top_ref, f0_ref, f1_ref, low_ref, gain_ref, shift_ref, weight_hbm,
-    hidden_ref, h0_ref, h1_ref, stats_out, window, weight, sem,
+    hidden_ref, h0_ref, h1_ref, stats_out, window, weight, sems,
 ):
-    copy = pltpu.make_async_copy(weight_hbm, weight, sem)
-    copy.start()
+    copies = start_weights(weight_hbm, weight, sems)
     rows = (top_ref, f0_ref, f1_ref, low_ref)
     fill_window(place_ref, stats_ref, rows, gain_ref[0:1], shift_ref[0:1], window)
-    copy.wait()
-    hidden = convolve(window, weight)
+    hidden = convolve(window, weight, copies)
     hidden_ref[...] = hidden
     h0_ref[...] = hidden[:ROW].astype(BF16)
     h1_ref[...] = hidden[ROW:].astype(BF16)
@@ -169,14 +179,12 @@
 
 def second_kernel(
     place_ref, stats_ref, top_ref, hidden_ref, low_ref, f0_ref, f1_ref, gain_ref, shift_ref, weight_hbm,
-    b0_ref, b1_ref, stats_out, window, weight, sem,
+    b0_ref, b1_ref, stats_out, window, weight, sems,
 ):
-    copy = pltpu.make_async_copy(weight_hbm, weight, sem)
-    copy.start()
+    copies = start_weights(weight_hbm, weight, sems)
     rows = (top_ref, hidden_ref.at[0:ROW], hidden_ref.at[ROW:CELLS], low_ref)
     fill_window(place_ref, stats_ref, rows, gain_ref[1:2], shift_ref[1:2], window)
-    copy.wait()
-    added = convolve(window, weight)
+    added = convolve(window, weight, copies)
     b0 = (added[:ROW] + f0_ref[...].astype(F32)).astype(BF16)
     b1 = (added[ROW:] + f1_ref[...].astype(F32)).astype(BF16)
     b0_ref[...] = b0
@@ -184,29 +192,56 @@
     write_stats(jnp.concatenate([b0, b1], axis=0).astype(F32), stats_out)
 
 
+def column_to_row(column):
+    square = jnp.broadcast_to(column, (128, 128))
+    return jnp.sum(jnp.where(iota((128, 128), 0) == iota((128, 128), 1), square, 0.0), axis=0, keepdims=True)
+
+
 def third_kernel(
     place_ref, stats_ref, top_ref, b0_ref, b1_ref, low_ref, gain_ref, shift_ref, weight_ref, embed_ref, bias_ref,
-    latent_ref, tokens_ref, window,
+    own_ref, other_ref, patches_ref, parcel_ref, window, weight,
 ):
+    n = FRAMES * HALF
+    for p in range(3):
+        for row in range(4):
+            for plane in range(4):
+                block = (p * 4 + row) * 4 + plane
+                for dh in range(2):
+                    for dw in range(2):
+                        at = (2 * dh + dw) * LAT
+                        q, r = row - dh, plane - dw
+                        if 0 <= q < 3 and 0 <= r < 3:
+                            weight[block, at : at + LAT] = weight_ref[9 * p + 3 * q + r]
+                        else:
+                            weight[block, at : at + LAT] = jnp.zeros((LAT, C), BF16)
     rows = (top_ref, b0_ref, b1_ref, low_ref)
     fill_window(place_ref, stats_ref, rows, gain_ref[2:3], shift_ref[2:3], window)
-    latent = convolve(window, weight_ref).reshape(2, FRAMES, 2, HALF, LAT)
-    n = FRAMES * HALF
-    patches = jnp.concatenate(
-        [latent[dh, :, dw].reshape(n, LAT) for dh in range(2) for dw in range(2)], axis=1
-    )
-    latent_ref[...] = patches
+    patches = None
+    for p in range(3):
+        for row in range(4):
+            for plane in range(4):
+                cells = window[row, p : p + FRAMES, plane].reshape(n, C)
+                term = nt_dot(cells, weight[(p * 4 + row) * 4 + plane])
+                patches = term if patches is None else patches + term
+    patches_ref[...] = patches
     rounded = patches.astype(BF16)
     embedded = dot(jnp.concatenate([rounded, rounded], axis=1), embed_ref[...]) + bias_ref[0:1]
     spread = jnp.sum(embedded * embedded, axis=1, keepdims=True) * (1.0 / D)
     rstd = lax.rsqrt(spread + EPS)
-    high = rstd.astype(BF16).astype(F32)
-    lane = iota((n, 128), 1)
-    wide = jnp.concatenate([rounded.astype(F32) * rstd, jnp.zeros((n, 64), F32)], axis=1)
-    wide = jnp.where((lane == 64) | (lane == 65), high, wide)
-    wide = jnp.where((lane == 66) | (lane == 67), 1.0, wide)
-    wide = jnp.where(lane == 68, rstd - high, wide)
-    tokens_ref[...] = wide.astype(BF16)
+    scaled = (rounded.astype(F32) * rstd).reshape(FRAMES, 2, 8, 64)
+    rstd = jnp.broadcast_to(rstd, (n, 128)).reshape(FRAMES, 2, 8, 128)
+    both = jnp.concatenate([scaled[:, side].reshape(128, 64) for side in range(2)], axis=1)
+    parcel_ref[0:128] = both.astype(BF16)
+    line = iota((16, 128), 0)
+    lines = jnp.where(line == 4, 1.0, 0.0)
+    for side in range(2):
+        each = column_to_row(rstd[:, side].reshape(128, 128)[:, 0:1])
+        high = each.astype(BF16).astype(F32)
+        lines = jnp.where(line == 2 * side, high, lines)
+        lines = jnp.where(line == 2 * side + 1, each - high, lines)
+    parcel_ref[128:144] = lines.astype(BF16)
+    parcel_ref[144:288] = own_ref[...]
+    parcel_ref[288:432] = other_ref[...]
 
 
 def embed_kernel(embed_ref, bias_ref, embed_out, bias_out):
@@ -219,69 +254,137 @@
     bias_out[...] = jnp.broadcast_to(bias - jnp.mean(bias, axis=1, keepdims=True), (8, D))
 
 
-def fold_kernel(near_ref, far_refs, embed_ref, bias_ref, scale_ref, shift_ref, out_ref):
-    scale = 1.0 + scale_ref[...]
-    embed = (embed_ref[0:64].astype(F32) + embed_ref[64:128].astype(F32)) * scale
-    row = iota((16, D), 0)
-    ends = jnp.where(row == 0, bias_ref[0:1] * scale, jnp.where(row == 1, shift_ref[...], 0.0))
-    every = jnp.concatenate([embed, ends], axis=0)
-    high = every.astype(BF16).astype(F32)
-    gap = jnp.zeros((48, D), F32)
-    both = jnp.concatenate([high, gap, every - high, gap], axis=0).astype(BF16)
-    lane = iota((QROWS, 128), 1)
-    blocks = [near_ref.at[i] for i in range(2)] + [far.at[i] for far in far_refs for i in range(2)]
-    for i, block in enumerate(blocks):
-        out = nt_dot(block[...], both)
-        out = out[:, 0:128] + out[:, 128:256]
-        bias, shift = out[:, 64:65], out[:, 65:66]
+def fold_kernel(
+    w0_ref, w1_ref, w2_ref, w3_ref, embed_ref, bias_ref, scale_ref, shift_ref, mods_ref,
+    own_ref, other_ref, stacked, wide,
+):
+    for i, block in enumerate((w0_ref, w1_ref, w2_ref, w3_ref)):
+        stacked[i * QPAD : i * QPAD + QROWS] = block[...]
+        stacked[i * QPAD + QROWS : (i + 1) * QPAD] = jnp.zeros((QPAD - QROWS, D), BF16)
+    embed = embed_ref[0:64].astype(F32) + embed_ref[64:128].astype(F32)
+    row = iota((64, D), 0)
+    sides = []
+    for scale, shift in (
+        (scale_ref[...], shift_ref[...]),
+        (mods_ref[0:1], mods_ref[1:2]),
+    ):
+        scale = 1.0 + scale
+        bias = bias_ref[0:1] * scale
         bias_high = bias.astype(BF16).astype(F32)
         shift_high = shift.astype(BF16).astype(F32)
-        out = jnp.where((lane == 64) | (lane == 68), bias_high, out)
-        out = jnp.where(lane == 65, bias - bias_high, out)
-        out = jnp.where(lane == 66, shift_high, out)
-        out = jnp.where(lane == 67, shift - shift_high, out)
-        out_ref[i] = jnp.concatenate([out, jnp.zeros((QPAD - QROWS, 128), F32)], axis=0).astype(BF16)
-
-
-def sort_kernel(place_ref, near_ref, far_ref, out_ref, wide):
+        ends = jnp.where(row == 0, bias_high, jnp.where(row == 1, bias - bias_high, 0.0))
+        ends = jnp.where(row == 2, shift_high, jnp.where(row == 3, shift - shift_high, ends))
+        sides += [embed * scale, ends]
+    every = jnp.concatenate(sides, axis=0).astype(BF16)
+    out = nt_dot(stacked[...], every)
+    lane = iota((4 * QPAD, 128), 1)
+    for side, target in enumerate((own_ref, other_ref)):
+        part = out[:, side * 128 : (side + 1) * 128]
+        bias = part[:, 64:65] + part[:, 65:66]
+        shift = part[:, 66:67] + part[:, 67:68]
+        bias_high = bias.astype(BF16).astype(F32)
+        shift_high = shift.astype(BF16).astype(F32)
+        part = jnp.where((lane == 64) | (lane == 68), bias_high, part)
+        part = jnp.where(lane == 65, bias - bias_high, part)
+        part = jnp.where(lane == 66, shift_high, part)
+        part = jnp.where(lane == 67, shift - shift_high, part)
+        for i in range(4):
+            wide[i * QROWS : (i + 1) * QROWS] = part[i * QPAD : i * QPAD + QROWS]
+        target[...] = wide[...].astype(BF16)
+
+
+WIDE = HEADS * HDIM
+
+
+def sort_kernel(place_ref, near_ref, far_ref, plain_ref, turned_ref, keys_ref, loose, wide):
     seq, clip = place_ref[0], place_ref[1]
     for j in range(SEQ):
         source = (near_ref, far_ref)[j & 1]
+        loose[j] = source[j >> 1, 144:432].astype(F32)
         for k in range(CLIPS):
-            block = source[j >> 1, k].astype(F32)
-            at = ((clip ^ k) * SEQ + (seq ^ j)) * QROWS
-            wide[pl.ds(at, QROWS)] = block[:QROWS]
-    out_ref[...] = wide[...].astype(BF16)
-
-
-def attend_kernel(place_ref, near_ref, far_ref, fold_ref, out_ref, queries, mixed):
+            at = ((clip ^ (2 * (k & 3) + (k >> 2))) * SEQ + (seq ^ j)) * QROWS
+            wide[pl.ds(at, QROWS)] = loose[j, k * QROWS : (k + 1) * QROWS]
+    lane = iota((WIDE, 128), 1)
+    for part in range(3):
+        rows = wide[part * WIDE : (part + 1) * WIDE]
+        if part != 1:
+            at = part // 2 * WIDE
+            plain_ref[at : at + WIDE] = rows.astype(BF16)
+            turned_ref[at : at + WIDE] = pltpu.roll(rows, 64, 1).astype(BF16)
+        else:
+            bias = rows[:, 64:65] + rows[:, 65:66]
+            shift = rows[:, 66:67] + rows[:, 67:68]
+            left = jnp.where(lane < 64, rows, 0.0)
+            keys_ref[:, 0:128] = left.astype(BF16)
+            keys_ref[:, 256:384] = pltpu.roll(left, 64, 1).astype(BF16)
+            for side in range(2):
+                extra = jnp.where((lane == 2 * side) | (lane == 2 * side + 1), bias, 0.0)
+                extra = jnp.where(lane == 4, shift, extra)
+                keys_ref[:, 256 * side + 128 : 256 * side + 256] = extra.astype(BF16)
+
+
+def attend_kernel(place_ref, near_ref, far_ref, plain_ref, turned_ref, keys_ref, out_ref, queries, mixed):
     seq = place_ref[0]
     blocks = [(near_ref, far_ref)[j & 1].at[j >> 1] for j in range(SEQ)]
-    mine = pl.ds(pl.multiple_of(seq * HALF, HALF), HALF)
-    tokens = jnp.concatenate([block[mine] for block in blocks], axis=0)
-    wide = HEADS * HDIM
-    scaled = (nt_dot(tokens, fold_ref[0:wide]) * (1.0 / math.sqrt(HDIM))).astype(BF16)
+    tables = (plain_ref, turned_ref)
+    lane = iota((128, 128), 1)
+    pick = one_hot(iota((8, 128), 1) == iota((8, 128), 0) + seq * 8)
+    twin = pl.ds(pl.multiple_of((seq >> 1) * 16, 16), 16)
+    tokens, scales = [], []
+    for block in blocks:
+        pair = block[twin].astype(F32)
+        tokens.append(jnp.where((seq & 1) == 1, pair[8:16], pair[0:8]))
+        scales.append(nt_dot(pick, block[128:144]))
+    tokens = jnp.concatenate(tokens, axis=0)
+    scales = jnp.concatenate(scales, axis=0)
+    asked = []
+    for side in range(2):
+        high, low = scales[:, 2 * side : 2 * side + 1], scales[:, 2 * side + 1 : 2 * side + 2]
+        spot = lane - 64 * (1 - side)
+        own = jnp.where((lane >> 6) == side, tokens, 0.0)
+        own = jnp.where((spot == 0) | (spot == 1), high, own)
+        own = jnp.where((spot == 2) | (spot == 3), 1.0, own)
+        own = jnp.where(spot == 4, low, own).astype(BF16)
+        asked.append((nt_dot(own, tables[side][0:WIDE]) * (1.0 / math.sqrt(HDIM))).astype(BF16))
     for head in range(HEADS):
         cols = slice(head * HDIM, (head + 1) * HDIM)
-        keyed = dot(scaled[:, cols], fold_ref[wide + head * HDIM : wide + (head + 1) * HDIM])
-        queries[:, head] = keyed.astype(BF16).reshape(SEQ, HALF, 128)
+        keyed = [
+            dot(asked[side][:, cols], keys_ref[cols, 256 * side : 256 * side + 256]).reshape(SEQ, 8, 256)
+            for side in range(2)
+        ]
+        queries[:, head] = jnp.concatenate(keyed, axis=1).astype(BF16)
     n = HEADS * HALF
-    keys = FRAMES * HALF
-    off = (iota((n, keys), 0) & (HALF - 1)) != (iota((n, keys), 1) & (HALF - 1))
+    off = (iota((n, 128), 0) & 7) != (iota((n, 128), 1) & 7)
     bar = jnp.where(off, -jnp.inf, 0.0)
+    lane = iota((n, 128), 1)
+    side = (iota((n, 128), 0) >> 3) & 1
+    mine = (lane >> 6) == side
+    spot = lane - 64 * (1 - side)
+    right = side[:, 0:1] == 1
     for j, block in enumerate(blocks):
-        scores = nt_dot(queries[j].reshape(n, 128), block[...]) + bar
-        raised = jnp.exp(scores - jnp.max(scores, axis=1, keepdims=True))
-        mix = dot(raised.astype(BF16), block[...])
-        mix = mix * (1.0 / mix[:, 66:67])
-        mixed[:, j * HALF : (j + 1) * HALF] = mix.astype(BF16).reshape(HEADS, HALF, 128)
+        query = queries[j].reshape(n, 256)
+        scores = nt_dot(query[:, 0:128], block[0:128]) + dot(query[:, 128:144], block[128:144]) + bar
+        raised = jnp.exp(scores - jnp.max(scores, axis=1, keepdims=True)).astype(BF16)
+        mix = dot(raised, block[0:128])
+        ends = nt_dot(raised, block[128:144])
+        inverse = 1.0 / ends[:, 4:5]
+        scale = jnp.where(right, ends[:, 2:3] + ends[:, 3:4], ends[:, 0:1] + ends[:, 1:2]) * inverse
+        high = scale.astype(BF16).astype(F32)
+        mix = jnp.where(mine, mix * inverse, 0.0)
+        mix = jnp.where((spot == 0) | (spot == 1), high, mix)
+        mix = jnp.where((spot == 2) | (spot == 3), 1.0, mix)
+        mix = jnp.where(spot == 4, scale - high, mix).reshape(HEADS, 2, 8, 128)
+        for at in range(2):
+            mixed[at, :, j * 8 : (j + 1) * 8] = mix[:, at]
     for head in range(HEADS):
         cols = slice(head * HDIM, (head + 1) * HDIM)
-        at = 2 * wide + head * HDIM
-        out = nt_dot(mixed[head], fold_ref[at : at + HDIM]).astype(BF16)
+        rows = slice(WIDE + head * HDIM, WIDE + (head + 1) * HDIM)
+        out = [
+            nt_dot(mixed[at, head].astype(BF16), tables[at][rows]).reshape(SEQ, 8, HDIM) for at in range(2)
+        ]
+        out = jnp.concatenate(out, axis=1).astype(BF16)
         for j in range(SEQ):
-            rows = pl.ds(pl.multiple_of((seq ^ j) * HALF, HALF), HALF)
-            out_ref[rows, cols] = out[j * HALF : (j + 1) * HALF]
+            out_ref[pl.ds(pl.multiple_of((seq ^ j) * HALF, HALF), HALF), cols] = out[j]
 
 
 def shape(*dims, dtype=BF16):
@@ -315,15 +418,18 @@
     return lax.all_to_all(stats, "seq", 0, 0, tiled=True)
 
 
-def gather_seq(block):
-    pair = jnp.stack([block, swap(block, "seq", 8, SEQ)])
+def gather_seq(block, beside):
+    over = swap(block, "seq", 8, SEQ)
+    over, beside = lax.optimization_barrier((over, beside))
+    pair = jnp.stack([block, over])
     others = [swap(pair, "seq", bits, SEQ) for bits in (2, 4, 6)]
     near = jnp.stack([pair] + others, axis=1).reshape((8,) + block.shape)
-    return near, swap(near, "seq", 1, SEQ)
+    return near, swap(near, "seq", 1, SEQ), beside
 
 
 WINDOW = pltpu.VMEM((4, FRAMES + 2, 4, HALF, C), BF16)
 WEIGHT = pltpu.VMEM((27, C, C), BF16)
+SEMS = pltpu.SemaphoreType.DMA((3,))
 CONV_FLOPS = 2 * CELLS * 27 * C * C
 
 
@@ -343,9 +449,10 @@
     place = jnp.stack([lax.axis_index("seq"), lax.axis_index("clip")]).astype(jnp.int32)
     row = shape(ROW, C)
     stats = shape(SEQ, 1, 128, dtype=F32)
-
-    near_rows = jnp.stack([qkv_weight, swap(qkv_weight, "clip", 1, CLIPS)])
-    far_rows = [swap(near_rows, "clip", bits, CLIPS) for bits in (2, 4, 6)]
+    taps = 27
+
+    rows = [qkv_weight] + [swap(qkv_weight, "clip", bits, CLIPS) for bits in (2, 4, 6)]
+    mods = swap(jnp.concatenate([mod_scale, mod_shift], axis=0), "clip", 1, CLIPS)
 
     f0, f1, stats0 = call(
         split_kernel, [row, row, stats], [VMEM], [pltpu.VMEM((2, CELLS, 128), F32)], 0, 1 << 20
@@ -356,61 +463,64 @@
         first_kernel,
         [shape(CELLS, C, dtype=F32), row, row, stats],
         [SMEM] + [VMEM] * 7 + [ANY],
-        [WINDOW, WEIGHT, pltpu.SemaphoreType.DMA],
+        [WINDOW, WEIGHT, SEMS],
         CONV_FLOPS,
         5 << 20,
-    )(place, stats0, top, f0, f1, low, norm_gains, norm_shifts, first_conv.reshape(27, C, C))
+        56,
+    )(place, stats0, top, f0, f1, low, norm_gains, norm_shifts, first_conv.reshape(taps, C, C))
     top, low = neighbours(h0, h1)
+
+    embed, bias = call(embed_kernel, [shape(128, D), shape(8, D, dtype=F32)], [VMEM] * 2)(
+        embed_weight, embed_bias.reshape(1, D)
+    )
+    folded = shape(4 * QROWS, 128)
+    own, other = call(
+        fold_kernel,
+        [folded, folded],
+        [VMEM] * 9,
+        [pltpu.VMEM((4 * QPAD, D), BF16), pltpu.VMEM((4 * QROWS, 128), F32)],
+    )(*rows, embed, bias, mod_scale, mod_shift, mods)
     stats1 = exchange(stats1)
+    stats1, own, other = lax.optimization_barrier((stats1, own, other))
+    other = swap(other, "clip", 1, CLIPS)
+
     b0, b1, stats2 = call(
         second_kernel,
         [row, row, stats],
         [SMEM] + [VMEM] * 8 + [ANY],
-        [WINDOW, WEIGHT, pltpu.SemaphoreType.DMA],
+        [WINDOW, WEIGHT, SEMS],
         CONV_FLOPS,
         6 << 20,
-    )(place, stats1, top, hidden, low, f0, f1, norm_gains, norm_shifts, second_conv.reshape(27, C, C))
+    )(place, stats1, top, hidden, low, f0, f1, norm_gains, norm_shifts, second_conv.reshape(taps, C, C))
     top, low = neighbours(b0, b1)
-
-    embed, bias = call(embed_kernel, [shape(128, D), shape(8, D, dtype=F32)], [VMEM] * 2)(
-        embed_weight, embed_bias.reshape(1, D)
-    )
-    folded = call(
-        lambda near, a, b, c, *rest: fold_kernel(near, (a, b, c), *rest),
-        shape(CLIPS, QPAD, 128),
-        [VMEM] * 8,
-    )(near_rows, *far_rows, embed, bias, mod_scale, mod_shift)
-    fold_near, fold_far = gather_seq(folded)
-
     stats2 = exchange(stats2)
-    patches, tokens = call(
+    patches, parcel = call(
         third_kernel,
-        [shape(FRAMES * HALF, 4 * LAT, dtype=F32), shape(FRAMES * HALF, 128)],
-        [SMEM] + [VMEM] * 10,
-        [WINDOW],
+        [shape(FRAMES * HALF, 4 * LAT, dtype=F32), shape(432, 128)],
+        [SMEM] + [VMEM] * 12,
+        [WINDOW, pltpu.VMEM((48, 4 * LAT, C), BF16)],
         CONV_FLOPS // 2,
         4 << 20,
     )(
-        place, stats2, top, b0, b1, low, norm_gains, norm_shifts, out_conv.reshape(27, C, LAT), embed, bias
+        place, stats2, top, b0, b1, low, norm_gains, norm_shifts,
+        out_conv.transpose(0, 1, 2, 4, 3).reshape(taps, LAT, C), embed, bias, own, other,
     )
-    token_near, token_far = gather_seq(tokens)
-    sorted_rows = call(
+    latent = patches.reshape(FRAMES, HALF, 2, 2, LAT).transpose(0, 2, 1, 3, 4)
+    latent = latent.reshape(1, FRAMES, 2, 2 * HALF, LAT)
+    near, far, latent = gather_seq(parcel, latent)
+    plain, turned, keys = call(
         sort_kernel,
-        shape(3 * HEADS * HDIM, 128),
+        [shape(2 * WIDE, 128), shape(2 * WIDE, 128), shape(WIDE, 512)],
         [SMEM] + [VMEM] * 2,
-        [pltpu.VMEM((3 * HEADS * HDIM, 128), F32)],
-    )(place, fold_near, fold_far)
+        [pltpu.VMEM((SEQ, 8 * QROWS, 128), F32), pltpu.VMEM((3 * WIDE, 128), F32)],
+    )(place, near, far)
     frame_heads = call(
         attend_kernel,
-        shape(SEQ * HALF, HEADS * HDIM),
-        [SMEM] + [VMEM] * 3,
-        [pltpu.VMEM((SEQ, HEADS, HALF, 128), BF16), pltpu.VMEM((HEADS, SEQ * HALF, 128), BF16)],
-    )(place, token_near, token_far, sorted_rows)
-    latent = patches.reshape(FRAMES, HALF, 2, 2, LAT).transpose(0, 2, 1, 3, 4)
-    return (
-        latent.reshape(1, FRAMES, 2, 2 * HALF, LAT),
-        frame_heads.reshape(1, 1, SEQ * HALF, HEADS * HDIM),
-    )
+        shape(SEQ * HALF, WIDE),
+        [SMEM] + [VMEM] * 5,
+        [pltpu.VMEM((SEQ, HEADS, HALF, 256), BF16), pltpu.VMEM((2, HEADS, 128, 128), F32)],
+    )(place, near, far, plain, turned, keys)
+    return (latent, frame_heads.reshape(1, 1, SEQ * HALF, WIDE))
 
 
 def solution(mesh):

time: 131 us -> 135 us (1.031)
  blocking collectives: 14.6 us -> 0 us
  waiting for transfers between devices: 21.5 us -> 35.8 us
  Pallas kernels: 30.2 us -> 36.7 us
  other arithmetic: 2.2 us -> 0.77 us
    all_to_all x1 -> x0, blocking collectives: 14.6 us -> none  [exchange(): return lax.all_to_all(stats, 'seq', 0, 0, tiled=True)]
    ppermute x14 -> x10, waiting for transfers between devices: 10.2 us -> 18 us  [swap(): return lax.ppermute(values, axis, [(i, i ^ bits) for i in range(count)])]
    all_to_all x2 -> x3, starting transfers between devices: 15.8 us -> 22.9 us  [exchange(): return lax.all_to_all(stats, 'seq', 0, 0, tiled=True)]
    ppermute x14 -> x10, starting transfers between devices: 19.3 us -> 12.6 us  [swap(): return lax.ppermute(values, axis, [(i, i ^ bits) for i in range(count)])]
    all_to_all x2 -> x3, waiting for transfers between devices: 11.3 us -> 17.8 us  [exchange(): return lax.all_to_all(stats, 'seq', 0, 0, tiled=True)]
    pallas_call x1, Pallas kernels: 5.96 us -> 10.1 us  [shards(): call(first_kernel, [shape(CELLS, C, dtype=F32), row, row, stats], [SMEM]...]
    pallas_call x1, Pallas kernels: 6.61 us -> 9.44 us  [shards(): call(second_kernel, [row, row, stats], [SMEM] + [VMEM] * 8 + [ANY], [WIND...]
    another operation x4 -> x2, other arithmetic: 2.07 us -> 0.14 us  [gather_seq(): near = jnp.stack([pair] + others, axis=1).reshape((8,) + block.shape)]
  transfers between devices with their start and end apart: 22 -> 19, of which waited for: 6 -> 10; matrix products, arithmetic and copies ran while one was open for 6% -> 2% of each run, Pallas kernels for 18% -> 1%
where the time goes in v1:
time: 135 us; the launch traced here: 134 us
  starting transfers between devices  51.2 us (38%)
  Pallas kernels  36.7 us (27%)
  waiting for transfers between devices  35.8 us (27%)
  local copies, waits for them, and re-layouts  8.77 us (6%)
    all_to_all x3, starting transfers between devices, exchange(): return lax.all_to_all(stats, 'seq', 0, 0, tiled=True)  22.9 us
    ppermute x10, waiting for transfers between devices, swap(): return lax.ppermute(values, axis, [(i, i ^ bits) for i in range(count)])  18 us
    all_to_all x3, waiting for transfers between devices, exchange(): return lax.all_to_all(stats, 'seq', 0, 0, tiled=True)  17.8 us
    ppermute x10, starting transfers between devices, swap(): return lax.ppermute(values, axis, [(i, i ^ bits) for i in range(count)])  12.6 us
    pallas_call x1, Pallas kernels, shards(): call(first_kernel, [shape(CELLS, C, dtype=F32), row, row, stats], [SMEM]...  10.1 us
    ppermute x3, starting transfers between devices, neighbours(): top = lax.ppermute(high_row, 'seq', [(i, i + 1) for i in range(SEQ - 1)])  9.85 us
    pallas_call x1, Pallas kernels, shards(): call(second_kernel, [row, row, stats], [SMEM] + [VMEM] * 8 + [ANY], [WIND...  9.44 us
    pallas_call x1, Pallas kernels, shards(): call(attend_kernel, shape(SEQ * HALF, WIDE), [SMEM] + [VMEM] * 5, [pltpu....  8.83 us
  transfers between devices with their start and end apart: 19, of which 10 were waited for; matrix products, arithmetic and copies ran while one was open for 2% of the time, Pallas kernels for 1%

profile of v1, /device:TPU:1, one launch (start us, length us, event | category | flops | bytes accessed | tf_op | source)
XLA Modules:
  0.0 134.1 jit_solution(15799467138004622303)
XLA Ops:
  2.9 4.5 %collective-permute-start = (bf16[512,256]{1,0:T(8,128)(2,1)S(1)}, bf16[512,256]{1,0:T(8,128)(2,1)S(1)}, u32[]{:S(2)}, u32[]{:S(2)}) collective-permute-start(bf16[512,256]{1,0:T(8,128)(2,1)S(1)} %get-tuple-element.27.f1_ref), channel_id=1, source_target_pairs={{0,1},{1,2},{2,3},{3,4},{4,5},{5,6},{6,7},{7,8},{8,9},{9,10},{10,1... | collective-permute-start | bytes 786440 | tf_op jit(solution)/shard_map/ppermute | solution.py:412
  7.4 1.9 %collective-permute-start.1 = (bf16[512,256]{1,0:T(8,128)(2,1)S(1)}, bf16[512,256]{1,0:T(8,128)(2,1)S(1)}, u32[]{:S(2)}, u32[]{:S(2)}) collective-permute-start(bf16[512,256]{1,0:T(8,128)(2,1)S(1)} %get-tuple-element.28.f0_ref), channel_id=1, source_target_pairs={{1,0},{2,1},{3,2},{4,3},{5,4},{6,5},{7,6},{8,7},{9,8},{10,9},{11,1... | collective-permute-start | bytes 786440 | tf_op jit(solution)/shard_map/ppermute | solution.py:413
  9.4 9.4 %all-to-all-start = ((f32[16,1,128]{2,1,0:T(1,128)}), f32[16,1,128]{2,1,0:T(1,128)S(1)}, u32[]{:S(2)}, u32[]{:S(2)}) async-start(f32[16,1,128]{2,1,0:T(1,128)} %get-tuple-element.26), calls=%async_computation | async-start | bytes 16384 | tf_op jit(solution)/shard_map/all_to_all | solution.py:418
  19.4 6.3 %all-to-all-done.stats_ref = f32[16,1,128]{2,1,0:T(1,128)S(1)} async-done(((f32[16,1,128]{2,1,0:T(1,128)}), f32[16,1,128]{2,1,0:T(1,128)S(1)}, u32[]{:S(2)}, u32[]{:S(2)}) %all-to-all-start) | async-done | bytes 8224 | tf_op jit(solution)/shard_map/all_to_all | solution.py:418
  26.6 10.1 %first_kernel.1 = (f32[1024,256]{1,0:T(8,128)}, bf16[512,256]{1,0:T(8,128)(2,1)}, bf16[512,256]{1,0:T(8,128)(2,1)}, f32[16,1,128]{2,1,0:T(1,128)}) custom-call(s32[2]{0:T(128)} %pad_add_fusion.place_ref, f32[16,1,128]{2,1,0:T(1,128)} %copy-done.16, bf16[512,256]{1,0:T(8,128)(2,1)} %copy-done.17, bf16[512,256]{1,0:T(8,128)(2,1)} %copy-done.8, ...), custom_call_target="tpu_custom_call" | custom-call | flops 3623878656 | bytes 5242880 | tf_op jit(solution)/shard_map/first_kernel/pallas_call | solution.py:462
  36.7 2.8 %collective-permute-start.6 = (bf16[512,256]{1,0:T(8,128)(2,1)}, bf16[512,256]{1,0:T(8,128)(2,1)S(1)}, u32[]{:S(2)}, u32[]{:S(2)}) collective-permute-start(bf16[512,256]{1,0:T(8,128)(2,1)} %get-tuple-element.35), channel_id=1, source_target_pairs={{0,1},{1,2},{2,3},{3,4},{4,5},{5,6},{6,7},{7,8},{8,9},{9,10},{10,1... | collective-permute-start | bytes 786440 | tf_op jit(solution)/shard_map/ppermute | solution.py:412
  39.4 1.9 %collective-permute-start.7 = (bf16[512,256]{1,0:T(8,128)(2,1)}, bf16[512,256]{1,0:T(8,128)(2,1)S(1)}, u32[]{:S(2)}, u32[]{:S(2)}) collective-permute-start(bf16[512,256]{1,0:T(8,128)(2,1)} %get-tuple-element.37), channel_id=1, source_target_pairs={{1,0},{2,1},{3,2},{4,3},{5,4},{6,5},{7,6},{8,7},{9,8},{10,9},{11,1... | collective-permute-start | bytes 786440 | tf_op jit(solution)/shard_map/ppermute | solution.py:413
  42.2 2.9 %collective-permute-start.3 = (bf16[36,3072]{1,0:T(8,128)(2,1)S(1)}, bf16[36,3072]{1,0:T(8,128)(2,1)S(1)}, u32[]{:S(2)}, u32[]{:S(2)}) collective-permute-start(bf16[36,3072]{1,0:T(8,128)(2,1)S(1)} %copy-done.2), channel_id=1, source_target_pairs={{0,64},{16,80},{32,96},{48,112},{64,0},{80,16},{96,32},{112,48},{1... | collective-permute-start | bytes 663560 | tf_op jit(solution)/shard_map/ppermute | solution.py:408
  47.1 2.7 %collective-permute-start.4 = (bf16[36,3072]{1,0:T(8,128)(2,1)S(1)}, bf16[36,3072]{1,0:T(8,128)(2,1)S(1)}, u32[]{:S(2)}, u32[]{:S(2)}) collective-permute-start(bf16[36,3072]{1,0:T(8,128)(2,1)S(1)} %copy-done.2), channel_id=1, source_target_pairs={{0,96},{16,112},{32,64},{48,80},{64,32},{80,48},{96,0},{112,16},{1... | collective-permute-start | bytes 663560 | tf_op jit(solution)/shard_map/ppermute | solution.py:408
  49.8 5.6 %all-to-all-start.1 = ((f32[16,1,128]{2,1,0:T(1,128)}), f32[16,1,128]{2,1,0:T(1,128)S(1)}, u32[]{:S(2)}, u32[]{:S(2)}) async-start(f32[16,1,128]{2,1,0:T(1,128)} %get-tuple-element.29), calls=%async_computation.1 | async-start | bytes 16384 | tf_op jit(solution)/shard_map/all_to_all | solution.py:418
  57.8 4.5 %all-to-all-done.1.stats_ref = f32[16,1,128]{2,1,0:T(1,128)S(1)} async-done(((f32[16,1,128]{2,1,0:T(1,128)}), f32[16,1,128]{2,1,0:T(1,128)S(1)}, u32[]{:S(2)}, u32[]{:S(2)}) %all-to-all-start.1) | async-done | bytes 8224 | tf_op jit(solution)/shard_map/all_to_all | solution.py:418
  62.4 2.0 %copy-done.7 = bf16[3,3,3,256,256]{4,3,2,1,0:T(8,128)(2,1)S(1)} copy-done((bf16[3,3,3,256,256]{4,3,2,1,0:T(8,128)(2,1)S(1)}, bf16[3,3,3,256,256]{4,3,2,1,0:T(8,128)(2,1)}, u32[]{:S(2)}) %copy-start.7) | copy-done | bytes 3538968
  67.5 9.4 %second_kernel.1 = (bf16[512,256]{1,0:T(8,128)(2,1)S(1)}, bf16[512,256]{1,0:T(8,128)(2,1)S(1)}, f32[16,1,128]{2,1,0:T(1,128)}) custom-call(s32[2]{0:T(128)S(1)} %copy-done.6, f32[16,1,128]{2,1,0:T(1,128)S(1)} %all-to-all-done.1.stats_ref, bf16[512,256]{1,0:T(8,128)(2,1)S(1)} %collective-permute-done.6.top_ref, f32[1024,256]{1,0:T(8,128)S(1)} %copy-done.15, ...), custom_call_target="tpu_custom_call" | custom-call | flops 3623878656 | bytes 6291456 | tf_op jit(solution)/shard_map/second_kernel/pallas_call | solution.py:487
  77.0 2.6 %collective-permute-start.8 = (bf16[512,256]{1,0:T(8,128)(2,1)S(1)}, bf16[512,256]{1,0:T(8,128)(2,1)S(1)}, u32[]{:S(2)}, u32[]{:S(2)}) collective-permute-start(bf16[512,256]{1,0:T(8,128)(2,1)S(1)} %get-tuple-element.39.b1_ref), channel_id=1, source_target_pairs={{0,1},{1,2},{2,3},{3,4},{4,5},{5,6},{6,7},{7,8},{8,9},{9,10},{10,1... | collective-permute-start | bytes 786440 | tf_op jit(solution)/shard_map/ppermute | solution.py:412
  79.6 1.9 %collective-permute-start.9 = (bf16[512,256]{1,0:T(8,128)(2,1)S(1)}, bf16[512,256]{1,0:T(8,128)(2,1)S(1)}, u32[]{:S(2)}, u32[]{:S(2)}) collective-permute-start(bf16[512,256]{1,0:T(8,128)(2,1)S(1)} %get-tuple-element.40.b0_ref), channel_id=1, source_target_pairs={{1,0},{2,1},{3,2},{4,3},{5,4},{6,5},{7,6},{8,7},{9,8},{10,9},{11,1... | collective-permute-start | bytes 786440 | tf_op jit(solution)/shard_map/ppermute | solution.py:413
  82.5 7.9 %all-to-all-start.2 = ((f32[16,1,128]{2,1,0:T(1,128)}), f32[16,1,128]{2,1,0:T(1,128)S(1)}, u32[]{:S(2)}, u32[]{:S(2)}) async-start(f32[16,1,128]{2,1,0:T(1,128)} %get-tuple-element.38), calls=%async_computation.2 | async-start | bytes 16384 | tf_op jit(solution)/shard_map/all_to_all | solution.py:418
  90.4 6.9 %all-to-all-done.2.stats_ref = f32[16,1,128]{2,1,0:T(1,128)S(1)} async-done(((f32[16,1,128]{2,1,0:T(1,128)}), f32[16,1,128]{2,1,0:T(1,128)S(1)}, u32[]{:S(2)}, u32[]{:S(2)}) %all-to-all-start.2) | async-done | bytes 8224 | tf_op jit(solution)/shard_map/all_to_all | solution.py:418
  97.4 4.1 %third_kernel.1 = (f32[256,64]{1,0:T(8,128)S(1)}, bf16[432,128]{1,0:T(8,128)(2,1)S(1)}) custom-call(s32[2]{0:T(128)S(1)} %copy-done.6, f32[16,1,128]{2,1,0:T(1,128)S(1)} %all-to-all-done.2.stats_ref, bf16[512,256]{1,0:T(8,128)(2,1)S(1)} %collective-permute-done.8.top_ref, bf16[512,256]{1,0:T(8,128)(2,1)S(1)} %get-tuple-element.40.b0_ref, ...), custom_call_target="tpu_custom_call" | custom-call | flops 1811939328 | bytes 4194304 | tf_op jit(solution)/shard_map/third_kernel/pallas_call | solution.py:497
  102.6 4.4 %collective-permute-done.11 = bf16[432,128]{1,0:T(8,128)(2,1)S(1)} collective-permute-done((bf16[432,128]{1,0:T(8,128)(2,1)S(1)}, bf16[432,128]{1,0:T(8,128)(2,1)S(1)}, u32[]{:S(2)}, u32[]{:S(2)}) %collective-permute-start.11) | collective-permute-done | bytes 110624 | tf_op jit(solution)/shard_map/ppermute | solution.py:408
  110.4 3.6 %collective-permute-done.13 = bf16[2,432,128]{2,1,0:T(8,128)(2,1)S(1)} collective-permute-done((bf16[2,432,128]{2,1,0:T(8,128)(2,1)S(1)}, bf16[2,432,128]{2,1,0:T(8,128)(2,1)S(1)}, u32[]{:S(2)}, u32[]{:S(2)}) %collective-permute-start.13) | collective-permute-done | bytes 221216 | tf_op jit(solution)/shard_map/ppermute | solution.py:408
  114.0 3.3 %collective-permute-done.12 = bf16[2,432,128]{2,1,0:T(8,128)(2,1)S(1)} collective-permute-done((bf16[2,432,128]{2,1,0:T(8,128)(2,1)S(1)}, bf16[2,432,128]{2,1,0:T(8,128)(2,1)S(1)}, u32[]{:S(2)}, u32[]{:S(2)}) %collective-permute-start.12) | collective-permute-done | bytes 221216 | tf_op jit(solution)/shard_map/ppermute | solution.py:408
  117.3 2.9 %collective-permute-done.14 = bf16[2,432,128]{2,1,0:T(8,128)(2,1)S(1)} collective-permute-done((bf16[2,432,128]{2,1,0:T(8,128)(2,1)S(1)}, bf16[2,432,128]{2,1,0:T(8,128)(2,1)S(1)}, u32[]{:S(2)}, u32[]{:S(2)}) %collective-permute-start.14) | collective-permute-done | bytes 221216 | tf_op jit(solution)/shard_map/ppermute | solution.py:408
  123.5 1.8 %sort_kernel.1 = (bf16[3072,128]{1,0:T(8,128)(2,1)S(1)}, bf16[3072,128]{1,0:T(8,128)(2,1)S(1)}, bf16[1536,512]{1,0:T(8,128)(2,1)S(1)}) custom-call(s32[2]{0:T(128)S(1)} %copy-done.6, bf16[8,432,128]{2,1,0:T(8,128)(2,1)S(1)} %bitcast.23, bf16[8,432,128]{2,1,0:T(8,128)(2,1)S(1)} %collective-permute-done.15.far_ref), custom_call_target="tpu_custom_call" | custom-call | tf_op jit(solution)/shard_map/sort_kernel/pallas_call | solution.py:511
  125.3 8.8 %attend_kernel.1 = bf16[256,1536]{1,0:T(8,128)(2,1)} custom-call(s32[2]{0:T(128)S(1)} %copy-done.6, bf16[8,432,128]{2,1,0:T(8,128)(2,1)S(1)} %bitcast.24, bf16[8,432,128]{2,1,0:T(8,128)(2,1)S(1)} %collective-permute-done.15.far_ref, bf16[3072,128]{1,0:T(8,128)(2,1)S(1)} %get-tuple-element.47.plain_ref, bf16[3072,128]{1,0:T(8,128)(2,1)S(1)} %get-tuple-element.48.turned_ref, ...), custom_call_target="tpu_custom_call" | custom-call | tf_op jit(solution)/shard_map/attend_kernel/pallas_call | solution.py:517
  (69 shorter events, 20.8 us)
Async XLA Ops:
  2.9 22.8 %collective-permute-start = (bf16[512,256]{1,0:T(8,128)(2,1)S(1)}, bf16[512,256]{1,0:T(8,128)(2,1)S(1)}, u32[]{:S(2)}, u32[]{:S(2)}) collective-permute-start(bf16[512,256]{1,0:T(8,128)(2,1)S(1)} %get-tuple-element.27.f1_ref), channel_id=1, source_target_pairs={{0,1},{1,2},{2,3},{3,4},{4,5},{5,6},{6,7},{7,8},{8,9},{9,10},{10,1... | collective-permute-start | bytes 786440 | tf_op jit(solution)/shard_map/ppermute | solution.py:412
  7.4 18.3 %collective-permute-start.1 = (bf16[512,256]{1,0:T(8,128)(2,1)S(1)}, bf16[512,256]{1,0:T(8,128)(2,1)S(1)}, u32[]{:S(2)}, u32[]{:S(2)}) collective-permute-start(bf16[512,256]{1,0:T(8,128)(2,1)S(1)} %get-tuple-element.28.f0_ref), channel_id=1, source_target_pairs={{1,0},{2,1},{3,2},{4,3},{5,4},{6,5},{7,6},{8,7},{9,8},{10,9},{11,1... | collective-permute-start | bytes 786440 | tf_op jit(solution)/shard_map/ppermute | solution.py:413
  9.4 16.3 %all-to-all-start = ((f32[16,1,128]{2,1,0:T(1,128)}), f32[16,1,128]{2,1,0:T(1,128)S(1)}, u32[]{:S(2)}, u32[]{:S(2)}) async-start(f32[16,1,128]{2,1,0:T(1,128)} %get-tuple-element.26), calls=%async_computation | async-start | bytes 16384 | tf_op jit(solution)/shard_map/all_to_all | solution.py:418
  26.5 28.8 %copy-start.5 = (f32[3072]{0:T(1024)S(1)}, f32[3072]{0:T(1024)}, u32[]{:S(2)}) copy-start(f32[3072]{0:T(1024)} %param.18) | copy-start | bytes 36868
  26.6 35.8 %copy-start.6 = (s32[2]{0:T(128)S(1)}, s32[2]{0:T(128)}, u32[]{:S(2)}) copy-start(s32[2]{0:T(128)} %pad_add_fusion.place_ref) | copy-start | bytes 28
  26.6 35.8 %copy-start.13 = (f32[3,256]{1,0:T(4,128)S(1)}, f32[3,256]{1,0:T(4,128)}, u32[]{:S(2)}) copy-start(f32[3,256]{1,0:T(4,128)} %gain_ref.5) | copy-start | bytes 9220
  26.6 35.8 %copy-start.14 = (f32[3,256]{1,0:T(4,128)S(1)}, f32[3,256]{1,0:T(4,128)}, u32[]{:S(2)}) copy-start(f32[3,256]{1,0:T(4,128)} %shift_ref.7) | copy-start | bytes 9220
  36.7 25.7 %collective-permute-start.6 = (bf16[512,256]{1,0:T(8,128)(2,1)}, bf16[512,256]{1,0:T(8,128)(2,1)S(1)}, u32[]{:S(2)}, u32[]{:S(2)}) collective-permute-start(bf16[512,256]{1,0:T(8,128)(2,1)} %get-tuple-element.35), channel_id=1, source_target_pairs={{0,1},{1,2},{2,3},{3,4},{4,5},{5,6},{6,7},{7,8},{8,9},{9,10},{10,1... | collective-permute-start | bytes 786440 | tf_op jit(solution)/shard_map/ppermute | solution.py:412
  39.4 22.9 %collective-permute-start.7 = (bf16[512,256]{1,0:T(8,128)(2,1)}, bf16[512,256]{1,0:T(8,128)(2,1)S(1)}, u32[]{:S(2)}, u32[]{:S(2)}) collective-permute-start(bf16[512,256]{1,0:T(8,128)(2,1)} %get-tuple-element.37), channel_id=1, source_target_pairs={{1,0},{2,1},{3,2},{4,3},{5,4},{6,5},{7,6},{8,7},{9,8},{10,9},{11,1... | collective-permute-start | bytes 786440 | tf_op jit(solution)/shard_map/ppermute | solution.py:413
  41.4 5.6 %collective-permute-start.5 = (f32[2,3072]{1,0:T(2,128)S(1)}, f32[2,3072]{1,0:T(2,128)S(1)}, u32[]{:S(2)}, u32[]{:S(2)}) collective-permute-start(f32[2,3072]{1,0:T(2,128)S(1)} %pad_maximum_fusion.2), channel_id=1, source_target_pairs={{0,16},{16,0},{32,48},{48,32},{64,80},{80,64},{96,112},{112,96},{1... | collective-permute-start | bytes 73736 | tf_op jit(solution)/shard_map/ppermute | solution.py:408
  42.2 13.5 %collective-permute-start.3 = (bf16[36,3072]{1,0:T(8,128)(2,1)S(1)}, bf16[36,3072]{1,0:T(8,128)(2,1)S(1)}, u32[]{:S(2)}, u32[]{:S(2)}) collective-permute-start(bf16[36,3072]{1,0:T(8,128)(2,1)S(1)} %copy-done.2), channel_id=1, source_target_pairs={{0,64},{16,80},{32,96},{48,112},{64,0},{80,16},{96,32},{112,48},{1... | collective-permute-start | bytes 663560 | tf_op jit(solution)/shard_map/ppermute | solution.py:408
  45.2 11.8 %collective-permute-start.2 = (bf16[36,3072]{1,0:T(8,128)(2,1)S(1)}, bf16[36,3072]{1,0:T(8,128)(2,1)S(1)}, u32[]{:S(2)}, u32[]{:S(2)}) collective-permute-start(bf16[36,3072]{1,0:T(8,128)(2,1)S(1)} %copy-done.2), channel_id=1, source_target_pairs={{0,32},{16,48},{32,0},{48,16},{64,96},{80,112},{96,64},{112,80},{1... | collective-permute-start | bytes 663560 | tf_op jit(solution)/shard_map/ppermute | solution.py:408
  47.1 9.9 %collective-permute-start.4 = (bf16[36,3072]{1,0:T(8,128)(2,1)S(1)}, bf16[36,3072]{1,0:T(8,128)(2,1)S(1)}, u32[]{:S(2)}, u32[]{:S(2)}) collective-permute-start(bf16[36,3072]{1,0:T(8,128)(2,1)S(1)} %copy-done.2), channel_id=1, source_target_pairs={{0,96},{16,112},{32,64},{48,80},{64,32},{80,48},{96,0},{112,16},{1... | collective-permute-start | bytes 663560 | tf_op jit(solution)/shard_map/ppermute | solution.py:408
  49.8 12.6 %all-to-all-start.1 = ((f32[16,1,128]{2,1,0:T(1,128)}), f32[16,1,128]{2,1,0:T(1,128)S(1)}, u32[]{:S(2)}, u32[]{:S(2)}) async-start(f32[16,1,128]{2,1,0:T(1,128)} %get-tuple-element.29), calls=%async_computation.1 | async-start | bytes 16384 | tf_op jit(solution)/shard_map/all_to_all | solution.py:418
  67.5 29.8 %copy-start.12 = (bf16[3,3,3,256,16]{3,4,2,1,0:T(8,128)(2,1)S(1)}, bf16[3,3,3,256,16]{3,4,2,1,0:T(8,128)(2,1)}, u32[]{:S(2)}) copy-start(bf16[3,3,3,256,16]{3,4,2,1,0:T(8,128)(2,1)} %param.14) | copy-start | bytes 663556
  77.0 20.4 %collective-permute-start.8 = (bf16[512,256]{1,0:T(8,128)(2,1)S(1)}, bf16[512,256]{1,0:T(8,128)(2,1)S(1)}, u32[]{:S(2)}, u32[]{:S(2)}) collective-permute-start(bf16[512,256]{1,0:T(8,128)(2,1)S(1)} %get-tuple-element.39.b1_ref), channel_id=1, source_target_pairs={{0,1},{1,2},{2,3},{3,4},{4,5},{5,6},{6,7},{7,8},{8,9},{9,10},{10,1... | collective-permute-start | bytes 786440 | tf_op jit(solution)/shard_map/ppermute | solution.py:412
  79.6 17.8 %collective-permute-start.9 = (bf16[512,256]{1,0:T(8,128)(2,1)S(1)}, bf16[512,256]{1,0:T(8,128)(2,1)S(1)}, u32[]{:S(2)}, u32[]{:S(2)}) collective-permute-start(bf16[512,256]{1,0:T(8,128)(2,1)S(1)} %get-tuple-element.40.b0_ref), channel_id=1, source_target_pairs={{1,0},{2,1},{3,2},{4,3},{5,4},{6,5},{7,6},{8,7},{9,8},{10,9},{11,1... | collective-permute-start | bytes 786440 | tf_op jit(solution)/shard_map/ppermute | solution.py:413
  81.5 8.9 %collective-permute-start.10 = (bf16[144,128]{1,0:T(8,128)(2,1)S(1)}, bf16[144,128]{1,0:T(8,128)(2,1)S(1)}, u32[]{:S(2)}, u32[]{:S(2)}) collective-permute-start(bf16[144,128]{1,0:T(8,128)(2,1)S(1)} %get-tuple-element.42), channel_id=1, source_target_pairs={{0,16},{16,0},{32,48},{48,32},{64,80},{80,64},{96,112},{112,96},{1... | collective-permute-start | bytes 110600 | tf_op jit(solution)/shard_map/ppermute | solution.py:408
  82.5 14.8 %all-to-all-start.2 = ((f32[16,1,128]{2,1,0:T(1,128)}), f32[16,1,128]{2,1,0:T(1,128)S(1)}, u32[]{:S(2)}, u32[]{:S(2)}) async-start(f32[16,1,128]{2,1,0:T(1,128)} %get-tuple-element.38), calls=%async_computation.2 | async-start | bytes 16384 | tf_op jit(solution)/shard_map/all_to_all | solution.py:418
  101.5 5.5 %collective-permute-start.11 = (bf16[432,128]{1,0:T(8,128)(2,1)S(1)}, bf16[432,128]{1,0:T(8,128)(2,1)S(1)}, u32[]{:S(2)}, u32[]{:S(2)}) collective-permute-start(bf16[432,128]{1,0:T(8,128)(2,1)S(1)} %get-tuple-element.43), channel_id=1, source_target_pairs={{0,8},{1,9},{2,10},{3,11},{4,12},{5,13},{6,14},{7,15},{8,0},{9,1},... | collective-permute-start | bytes 331784 | tf_op jit(solution)/shard_map/ppermute | solution.py:408
  107.0 7.0 %collective-permute-start.13 = (bf16[2,432,128]{2,1,0:T(8,128)(2,1)S(1)}, bf16[2,432,128]{2,1,0:T(8,128)(2,1)S(1)}, u32[]{:S(2)}, u32[]{:S(2)}) collective-permute-start(bf16[2,432,128]{2,1,0:T(8,128)(2,1)S(1)} %get-tuple-element.53), channel_id=1, source_target_pairs={{0,4},{1,5},{2,6},{3,7},{4,0},{5,1},{6,2},{7,3},{8,12},{9,13},{10,... | collective-permute-start | bytes 663560 | tf_op jit(solution)/shard_map/ppermute | solution.py:408
  108.0 9.3 %collective-permute-start.12 = (bf16[2,432,128]{2,1,0:T(8,128)(2,1)S(1)}, bf16[2,432,128]{2,1,0:T(8,128)(2,1)S(1)}, u32[]{:S(2)}, u32[]{:S(2)}) collective-permute-start(bf16[2,432,128]{2,1,0:T(8,128)(2,1)S(1)} %get-tuple-element.53), channel_id=1, source_target_pairs={{0,2},{1,3},{2,0},{3,1},{4,6},{5,7},{6,4},{7,5},{8,10},{9,11},{10,... | collective-permute-start | bytes 663560 | tf_op jit(solution)/shard_map/ppermute | solution.py:408
  108.6 11.6 %collective-permute-start.14 = (bf16[2,432,128]{2,1,0:T(8,128)(2,1)S(1)}, bf16[2,432,128]{2,1,0:T(8,128)(2,1)S(1)}, u32[]{:S(2)}, u32[]{:S(2)}) collective-permute-start(bf16[2,432,128]{2,1,0:T(8,128)(2,1)S(1)} %get-tuple-element.53), channel_id=1, source_target_pairs={{0,6},{1,7},{2,4},{3,5},{4,2},{5,3},{6,0},{7,1},{8,14},{9,15},{10,... | collective-permute-start | bytes 663560 | tf_op jit(solution)/shard_map/ppermute | solution.py:408
  120.4 3.1 %collective-permute-start.15 = (bf16[8,432,128]{2,1,0:T(8,128)(2,1)S(1)}, bf16[8,432,128]{2,1,0:T(8,128)(2,1)S(1)}, u32[]{:S(2)}, u32[]{:S(2)}) collective-permute-start(bf16[8,432,128]{2,1,0:T(8,128)(2,1)S(1)} %bitcast.22), channel_id=1, source_target_pairs={{0,1},{1,0},{2,3},{3,2},{4,5},{5,4},{6,7},{7,6},{8,9},{9,8},{10,11... | collective-permute-start | bytes 2654216 | tf_op jit(solution)/shard_map/ppermute | solution.py:408
  (14 other events, 128.1 us)

commit v2 on v1

v2 whole, which is shorter than its diff:
```python
import functools
import math

import jax
import jax.numpy as jnp
from jax import lax
from jax.experimental import pallas as pl
from jax.experimental.pallas import tpu as pltpu
from jax.sharding import PartitionSpec as P

C = 256
GROUPS = 32
LAT = 16
D = 3072
HEADS = 12
HDIM = 128
FRAMES = 16
HALF = 16
ROW = FRAMES * 2 * HALF
CELLS = 2 * ROW
SEQ = 16
CLIPS = 8
QROWS = 36
QPAD = 48
EPS = 1e-06
F32 = jnp.float32
BF16 = jnp.bfloat16
VMEM = pl.BlockSpec(memory_space=pltpu.VMEM)
SMEM = pl.BlockSpec(memory_space=pltpu.SMEM)
HBM = pl.BlockSpec(memory_space=pltpu.HBM)
DMA = pltpu.SemaphoreType.DMA


def nt_dot(a, b):
    return lax.dot_general(a, b, (((1,), (1,)), ((), ())), preferred_element_type=F32)


def dot(a, b):
    return jnp.dot(a, b, preferred_element_type=F32)


def exact_dot(rows, zero_one):
    high = rows.astype(BF16).astype(F32)
    rest = rows - high
    mid = rest.astype(BF16).astype(F32)
    low = rest - mid
    parts = jnp.concatenate([high, mid, low, jnp.zeros_like(low)], axis=0).astype(BF16)
    out = dot(parts, zero_one)
    return out[0:8] + out[8:16] + out[16:24]


def iota(shape, dim):
    return lax.broadcasted_iota(jnp.int32, shape, dim)


def one_hot(cond):
    return jnp.where(cond, 1.0, 0.0).astype(BF16)


def rows8(first, second=None):
    n = first.shape[1]
    row = iota((8, n), 0)
    out = jnp.where(row == 0, jnp.broadcast_to(first, (8, n)), 0.0)
    if second is not None:
        out = jnp.where(row == 1, jnp.broadcast_to(second, (8, n)), out)
    return out


def write_stats(cells, stats_ref):
    count = cells.shape[0]
    mean_c = jnp.sum(cells, axis=0, keepdims=True) * (1.0 / count)
    same = one_hot((iota((C, C), 0) >> 3) == (iota((C, C), 1) >> 3))
    mean_g = exact_dot(rows8(mean_c), same)[0:1] * (1.0 / 8)
    off = cells - mean_c
    square_c = jnp.sum(off * off, axis=0, keepdims=True)
    gap = mean_c - mean_g
    square_c = square_c + count * (gap * gap)
    lane = iota((C, 128), 1)
    pick = one_hot((iota((C, 128), 0) >> 3) == (lane & 31))
    both = exact_dot(rows8(mean_c * (1.0 / 8), square_c), pick)
    row = jnp.where(iota((1, 128), 1) < GROUPS, both[0:1], both[1:2])
    stats_ref[...] = jnp.broadcast_to(row[None], (SEQ, 1, 128))


def read_stats(stats_ref, count):
    each = stats_ref[...].reshape(SEQ, 128)
    lane = iota((1, 128), 1)
    mean = jnp.sum(each, axis=0, keepdims=True) * (1.0 / SEQ)
    off = each - mean
    between = jnp.sum(off * off, axis=0, keepdims=True) * (8.0 * count)
    within = mean * SEQ
    total = jnp.where(lane < GROUPS, between, jnp.where(lane < 2 * GROUPS, within, 0.0))
    mean = jnp.where(lane < GROUPS, mean, 0.0)
    spread = one_hot((iota((128, C), 0) & 31) == (iota((128, C), 1) >> 3))
    both = exact_dot(rows8(mean, total), spread)
    return both[0:1], lax.rsqrt(both[1:2] * (1.0 / (8.0 * count * SEQ)) + EPS)


def own_rows(place_ref, rows_ref, near_ref, far_ref):
    odd = place_ref[0] & 1
    near_ref[...] = rows_ref[pl.ds(pl.multiple_of((1 - odd) * ROW, ROW), ROW)].astype(BF16)
    far_ref[...] = rows_ref[pl.ds(pl.multiple_of(odd * ROW, ROW), ROW)].astype(BF16)


def split_kernel(
    place_ref, feat_hbm, gain_hbm, shift_hbm, scale_hbm, mod_hbm,
    rows_ref, near_ref, far_ref, stats_ref, norms_ref, mods_ref,
    feat_ref, gain_ref, shift_ref, scale_ref, mod_ref, wide, sems,
):
    sources = (feat_hbm, gain_hbm, shift_hbm, scale_hbm, mod_hbm)
    targets = (feat_ref, gain_ref, shift_ref, scale_ref, mod_ref)
    copies = [pltpu.make_async_copy(a, b, sems.at[i]) for i, (a, b) in enumerate(zip(sources, targets))]
    for copy in copies:
        copy.start()
    for copy in copies:
        copy.wait()
    norms_ref[0:3] = gain_ref[...]
    norms_ref[4:7] = shift_ref[...]
    mods_ref[0:1] = scale_ref[...]
    mods_ref[1:2] = mod_ref[...]
    cells = feat_ref[...].astype(F32).reshape(CELLS, C)
    for side in range(2):
        wide[side] = cells[:, side * 128 : (side + 1) * 128]
    for frame in range(FRAMES):
        for row in range(2):
            for parity in range(2):
                base = (frame * 2 + row) * 32 + parity
                at = row * ROW + (frame * 2 + parity) * HALF
                for side in range(2):
                    part = wide[side, pl.ds(base, HALF, stride=2)]
                    rows_ref[at : at + HALF, side * 128 : (side + 1) * 128] = part.astype(BF16)
    own_rows(place_ref, rows_ref, near_ref, far_ref)
    write_stats(cells, stats_ref)


def fill_window(place_ref, stats_ref, rows_ref, near_ref, far_ref, norms_ref, layer, window, centers=None, load=None):
    mean, rstd = read_stats(stats_ref, CELLS)
    gain = rstd * norms_ref[layer : layer + 1] * 0.5
    shift = norms_ref[4 + layer : 5 + layer] * 0.5
    place = place_ref[0]
    odd = place & 1
    near_at = 3 * (1 - odd)
    far_on = jnp.where((place > 0) & (place < SEQ - 1), 1.0, 0.0).astype(F32)
    window[:, 0:2] = jnp.zeros((4, 2, 4, HALF, C), BF16)
    step = 4
    n = step * HALF
    pair = iota((n, C), 0) & (HALF - 1)
    level = -mean
    levels = [level] * 4 if centers is None else [center + level for center in centers]
    sources = (
        (near_at, near_ref),
        (3 - near_at, far_ref),
        (1, rows_ref.at[0:ROW]),
        (2, rows_ref.at[ROW:CELLS]),
    )
    for which, (row, source) in enumerate(sources):
        if which == 2 and load is not None:
            load.wait()
        for frame in range(0, FRAMES, step):
            x = source[frame * 32 : (frame + step) * 32].astype(F32)
            half = (x + levels[which]) * gain + shift
            act = half + half * jnp.tanh(half)
            if which == 1:
                act = act * far_on
            act = act.reshape(step, 2, HALF, C)
            even = act[:, 0].reshape(n, C)
            odd_ones = act[:, 1].reshape(n, C)
            odd_before = jnp.where(pair == 0, 0.0, pltpu.roll(odd_ones, 1, 0))
            even_after = jnp.where(pair == HALF - 1, 0.0, pltpu.roll(even, n - 1, 0))
            for plane, part in enumerate((odd_before, even, odd_ones, even_after)):
                window[row, 2 + frame : 2 + frame + step, plane] = part.astype(BF16).reshape(
                    step, HALF, C
                )


def convolve(window, weight):
    total = None
    for tap in range(27):
        p, q, r = tap // 9, tap // 3 % 3, tap % 3
        cells = window[q : q + 2, p : p + FRAMES, r : r + 2].reshape(CELLS, C)
        term = dot(cells, weight[tap])
        total = term if total is None else total + term
    return total


def first_kernel(
    place_ref, stats_ref, rows_ref, near_ref, far_ref, norms_ref, weight_hbm,
    hidden_hbm, center_ref, near_out, far_out, stats_out, window, weight, hidden_ref, sems,
):
    copy = pltpu.make_async_copy(weight_hbm, weight, sems.at[0])
    copy.start()
    fill_window(place_ref, stats_ref, rows_ref, near_ref, far_ref, norms_ref, 0, window)
    copy.wait()
    hidden = convolve(window, weight)
    center = jnp.sum(hidden, axis=0, keepdims=True) * (1.0 / CELLS)
    hidden_ref[...] = (hidden - center).astype(BF16)
    copy = pltpu.make_async_copy(hidden_ref, hidden_hbm, sems.at[1])
    copy.start()
    center_ref[...] = jnp.broadcast_to(center, (8, C))
    high = center.astype(BF16).astype(F32)
    mid = (center - high).astype(BF16).astype(F32)
    line = iota((16, C), 0)
    terms = jnp.where(line == 0, high, jnp.where(line == 1, mid, jnp.where(line == 2, center - high - mid, 0.0)))
    own_rows(place_ref, hidden_ref, near_out.at[0:ROW], far_out.at[0:ROW])
    near_out[ROW : ROW + 16] = terms.astype(BF16)
    far_out[ROW : ROW + 16] = terms.astype(BF16)
    write_stats(hidden, stats_out)
    copy.wait()


def second_kernel(
    place_ref, stats_ref, hidden_hbm, center_ref, near_ref, far_ref, norms_ref, feat_ref, weight_hbm,
    block_ref, near_out, far_out, stats_out, window, weight, hidden_ref, sems,
):
    load = pltpu.make_async_copy(hidden_hbm, hidden_ref, sems.at[1])
    load.start()
    copy = pltpu.make_async_copy(weight_hbm, weight, sems.at[0])
    copy.start()
    own = center_ref[0:1]
    centers = [jnp.sum(ref[ROW : ROW + 16].astype(F32), axis=0, keepdims=True) for ref in (near_ref, far_ref)]
    centers += [own, own]
    fill_window(place_ref, stats_ref, hidden_ref, near_ref, far_ref, norms_ref, 1, window, centers, load)
    copy.wait()
    block = (convolve(window, weight) + feat_ref[...].astype(F32)).astype(BF16)
    block_ref[...] = block
    own_rows(place_ref, block_ref, near_out, far_out)
    write_stats(block.astype(F32), stats_out)


def column_to_row(column):
    square = jnp.broadcast_to(column, (128, 128))
    return jnp.sum(jnp.where(iota((128, 128), 0) == iota((128, 128), 1), square, 0.0), axis=0, keepdims=True)


def third_kernel(
    place_ref, stats_ref, rows_ref, near_ref, far_ref, norms_ref, weight_ref, embed_ref, bias_ref,
    own_ref, other_ref, patches_ref, parcel_ref, window, weight,
):
    n = FRAMES * HALF
    for p in range(3):
        for row in range(4):
            for plane in range(4):
                block = (p * 4 + row) * 4 + plane
                for dh in range(2):
                    for dw in range(2):
                        at = (2 * dh + dw) * LAT
                        q, r = row - dh, plane - dw
                        if 0 <= q < 3 and 0 <= r < 3:
                            weight[block, at : at + LAT] = weight_ref[9 * p + 3 * q + r]
                        else:
                            weight[block, at : at + LAT] = jnp.zeros((LAT, C), BF16)
    fill_window(place_ref, stats_ref, rows_ref, near_ref, far_ref, norms_ref, 2, window)
    patches = None
    for p in range(3):
        for row in range(4):
            for plane in range(4):
                cells = window[row, p : p + FRAMES, plane].reshape(n, C)
                term = nt_dot(cells, weight[(p * 4 + row) * 4 + plane])
                patches = term if patches is None else patches + term
    patches_ref[...] = patches
    rounded = patches.astype(BF16)
    embedded = dot(jnp.concatenate([rounded, rounded], axis=1), embed_ref[...]) + bias_ref[0:1]
    spread = jnp.sum(embedded * embedded, axis=1, keepdims=True) * (1.0 / D)
    rstd = lax.rsqrt(spread + EPS)
    scaled = (rounded.astype(F32) * rstd).reshape(FRAMES, 2, 8, 64)
    rstd = jnp.broadcast_to(rstd, (n, 128)).reshape(FRAMES, 2, 8, 128)
    both = jnp.concatenate([scaled[:, side].reshape(128, 64) for side in range(2)], axis=1)
    parcel_ref[0:128] = both.astype(BF16)
    line = iota((16, 128), 0)
    lines = jnp.where(line == 4, 1.0, 0.0)
    for side in range(2):
        each = column_to_row(rstd[:, side].reshape(128, 128)[:, 0:1])
        high = each.astype(BF16).astype(F32)
        lines = jnp.where(line == 2 * side, high, lines)
        lines = jnp.where(line == 2 * side + 1, each - high, lines)
    parcel_ref[128:144] = lines.astype(BF16)
    parcel_ref[144:288] = own_ref[...]
    parcel_ref[288:432] = other_ref[...]


def embed_kernel(embed_ref, bias_ref, embed_out, bias_out):
    embed = embed_ref[...].astype(F32)
    embed = embed - jnp.mean(embed, axis=1, keepdims=True)
    high = embed.astype(BF16)
    embed_out[0:64] = high
    embed_out[64:128] = (embed - high.astype(F32)).astype(BF16)
    bias = bias_ref[...]
    bias_out[...] = jnp.broadcast_to(bias - jnp.mean(bias, axis=1, keepdims=True), (8, D))


def fold_kernel(
    here_ref, there_ref, embed_ref, bias_ref, own_mods_ref, mods_ref, own_ref, other_ref, stacked, wide,
):
    for i in range(4):
        stacked[i * QPAD : i * QPAD + QROWS] = (here_ref, there_ref)[i >> 1][i & 1]
        stacked[i * QPAD + QROWS : (i + 1) * QPAD] = jnp.zeros((QPAD - QROWS, D), BF16)
    embed = embed_ref[0:64].astype(F32) + embed_ref[64:128].astype(F32)
    row = iota((64, D), 0)
    sides = []
    for mod_ref in (own_mods_ref, mods_ref):
        scale, shift = 1.0 + mod_ref[0:1], mod_ref[1:2]
        bias = bias_ref[0:1] * scale
        bias_high = bias.astype(BF16).astype(F32)
        shift_high = shift.astype(BF16).astype(F32)
        ends = jnp.where(row == 0, bias_high, jnp.where(row == 1, bias - bias_high, 0.0))
        ends = jnp.where(row == 2, shift_high, jnp.where(row == 3, shift - shift_high, ends))
        sides += [embed * scale, ends]
    every = jnp.concatenate(sides, axis=0).astype(BF16)
    out = nt_dot(stacked[...], every)
    lane = iota((4 * QPAD, 128), 1)
    for side, target in enumerate((own_ref, other_ref)):
        part = out[:, side * 128 : (side + 1) * 128]
        bias = part[:, 64:65] + part[:, 65:66]
        shift = part[:, 66:67] + part[:, 67:68]
        bias_high = bias.astype(BF16).astype(F32)
        shift_high = shift.astype(BF16).astype(F32)
        part = jnp.where((lane == 64) | (lane == 68), bias_high, part)
        part = jnp.where(lane == 65, bias - bias_high, part)
        part = jnp.where(lane == 66, shift_high, part)
        part = jnp.where(lane == 67, shift - shift_high, part)
        for i in range(4):
            wide[i * QROWS : (i + 1) * QROWS] = part[i * QPAD : i * QPAD + QROWS]
        target[...] = wide[...].astype(BF16)


WIDE = HEADS * HDIM


def sort_kernel(place_ref, clip_ref, near_ref, far_ref, asks_ref, keys_ref, values_ref, loose, wide):
    seq, clip = place_ref[0], clip_ref[0]
    for j in range(SEQ):
        source = (near_ref, far_ref)[j & 1]
        loose[j] = source[j >> 1, 144:432].astype(F32)
        for k in range(CLIPS):
            at = ((clip ^ (2 * (k & 3) + (k >> 2))) * SEQ + (seq ^ j)) * QROWS
            wide[pl.ds(at, QROWS)] = loose[j, k * QROWS : (k + 1) * QROWS]
    lane = iota((WIDE, 128), 1)
    rows = wide[0:WIDE]
    asks_ref[:, 0:128] = rows.astype(BF16)
    asks_ref[:, 128:256] = pltpu.roll(rows, 64, 1).astype(BF16)
    for part, target in ((1, keys_ref), (2, values_ref)):
        rows = wide[part * WIDE : (part + 1) * WIDE]
        bias = rows[:, 64:65] + rows[:, 65:66]
        shift = rows[:, 66:67] + rows[:, 67:68]
        left = jnp.where(lane < 64, rows, 0.0)
        target[:, 0:128] = left.astype(BF16)
        target[:, 256:384] = pltpu.roll(left, 64, 1).astype(BF16)
        for side in range(2):
            extra = jnp.where((lane == 2 * side) | (lane == 2 * side + 1), bias, 0.0)
            extra = jnp.where(lane == 4, shift, extra)
            target[:, 256 * side + 128 : 256 * side + 256] = extra.astype(BF16)


def attend_kernel(place_ref, near_ref, far_ref, asks_ref, keys_ref, values_ref, out_ref, queries, mixed, scores, weights):
    seq = place_ref[0]
    blocks = [(near_ref, far_ref)[j & 1].at[j >> 1] for j in range(SEQ)]
    lane = iota((128, 128), 1)
    pick = one_hot(iota((8, 128), 1) == iota((8, 128), 0) + seq * 8)
    twin = pl.ds(pl.multiple_of((seq >> 1) * 16, 16), 16)
    tokens, scales = [], []
    for block in blocks:
        pair = block[twin].astype(F32)
        tokens.append(jnp.where((seq & 1) == 1, pair[8:16], pair[0:8]))
        scales.append(nt_dot(pick, block[128:144]))
    tokens = jnp.concatenate(tokens, axis=0)
    scales = jnp.concatenate(scales, axis=0)
    asked = []
    for side in range(2):
        high, low = scales[:, 2 * side : 2 * side + 1], scales[:, 2 * side + 1 : 2 * side + 2]
        spot = lane - 64 * (1 - side)
        own = jnp.where((lane >> 6) == side, tokens, 0.0)
        own = jnp.where((spot == 0) | (spot == 1), high, own)
        own = jnp.where((spot == 2) | (spot == 3), 1.0, own)
        own = jnp.where(spot == 4, low, own).astype(BF16)
        asked.append((nt_dot(own, asks_ref[:, 128 * side : 128 * side + 128]) * (1.0 / math.sqrt(HDIM))).astype(BF16))
    for head in range(HEADS):
        cols = slice(head * HDIM, (head + 1) * HDIM)
        keyed = [
            dot(asked[side][:, cols], keys_ref[cols, 256 * side : 256 * side + 256]).reshape(SEQ, 8, 256)
            for side in range(2)
        ]
        queries[:, head] = jnp.concatenate(keyed, axis=1).astype(BF16)
    n = HEADS * HALF
    same = jnp.where(iota((8, n), 0) == (iota((8, n), 1) & 7), 1.0, 0.0)
    for j, block in enumerate(blocks):
        query = queries[j].reshape(n, 256)
        ends = lax.dot_general(block[128:144], query[:, 128:144], (((0,), (1,)), ((), ())), preferred_element_type=F32)
        scores[j] = nt_dot(block[0:128], query[:, 0:128]) + ends
    for j in range(SEQ):
        each = scores[j].reshape(FRAMES, 8, n)
        raised = jnp.exp(each - jnp.max(each, axis=0, keepdims=True))
        shares = raised * (same / jnp.sum(raised, axis=0))
        weights[j] = jnp.transpose(shares.astype(BF16).reshape(128, n))
    for j, block in enumerate(blocks):
        mix = dot(weights[j], block[0:128]).reshape(HEADS, 2, 8, 128)
        ends = nt_dot(weights[j], block[128:144]).reshape(HEADS, 2, 8, 16)
        for side in range(2):
            mixed[side, :, j * 8 : (j + 1) * 8, 0:128] = mix[:, side]
            mixed[side, :, j * 8 : (j + 1) * 8, 128:144] = ends[:, side]
    for head in range(HEADS):
        cols = slice(head * HDIM, (head + 1) * HDIM)
        out = []
        for side in range(2):
            part = nt_dot(mixed[side, head, :, 0:128].astype(BF16), values_ref[cols, 256 * side : 256 * side + 128])
            at = 256 * side + 128
            part = part + nt_dot(mixed[side, head, :, 128:144].astype(BF16), values_ref[cols, at : at + 16])
            out.append(part.reshape(SEQ, 8, HDIM))
        out = jnp.concatenate(out, axis=1).astype(BF16)
        for j in range(SEQ):
            out_ref[pl.ds(pl.multiple_of((seq ^ j) * HALF, HALF), HALF), cols] = out[j]


def shape(*dims, dtype=BF16):
    return jax.ShapeDtypeStruct(dims, dtype)


def call(body, outs, ins, scratch=(), flops=0, moved=0, limit=32, first_out=VMEM):
    outs = list(outs) if isinstance(outs, list) else outs
    if first_out is HBM:
        outs[0] = pltpu.HBM(outs[0].shape, outs[0].dtype)
    kernel = pl.pallas_call(
        body,
        out_shape=outs,
        in_specs=ins,
        out_specs=[first_out] + [VMEM] * (len(outs) - 1) if isinstance(outs, list) else VMEM,
        scratch_shapes=list(scratch),
        compiler_params=pltpu.CompilerParams(vmem_limit_bytes=limit << 20),
        cost_estimate=pl.CostEstimate(flops=flops, bytes_accessed=moved, transcendentals=0),
        name=body.__name__,
    )

    def run(*args):
        return kernel(
            *(pltpu.with_memory_space_constraint(x, pltpu.HBM) if spec is HBM else x for x, spec in zip(args, ins))
        )

    return run


def swap(values, axis, bits, count):
    return lax.ppermute(values, axis, [(i, i ^ bits) for i in range(count)])


CHIP_PAIRS = [(i, i ^ 1) for i in range(SEQ)]
NEXT_PAIRS = [(i, (i + 1 if i & 1 else i - 1) % SEQ) for i in range(SEQ)]


def neighbours(near, far):
    far = lax.ppermute(far, "seq", NEXT_PAIRS)
    return lax.ppermute(near, "seq", CHIP_PAIRS), far


def exchange(stats):
    return lax.all_to_all(stats, "seq", 0, 0, tiled=True)


def gather_seq(block, beside):
    over = swap(block, "seq", 8, SEQ)
    over, beside = lax.optimization_barrier((over, beside))
    pair = jnp.stack([block, over])
    others = [swap(pair, "seq", bits, SEQ) for bits in (2, 4, 6)]
    near = jnp.stack([pair] + others, axis=1).reshape((8,) + block.shape)
    return near, swap(near, "seq", 1, SEQ), beside


WINDOW = pltpu.VMEM((4, FRAMES + 2, 4, HALF, C), BF16)
WEIGHT = pltpu.VMEM((27, C, C), BF16)
CONV_FLOPS = 2 * CELLS * 27 * C * C


def shards(
    features,
    first_conv,
    second_conv,
    out_conv,
    norm_gains,
    norm_shifts,
    embed_weight,
    embed_bias,
    mod_shift,
    mod_scale,
    qkv_weight,
):
    place = lax.axis_index("seq").astype(jnp.int32).reshape(1)
    clip = lax.axis_index("clip").astype(jnp.int32).reshape(1)
    row = shape(ROW, C)
    stats = shape(SEQ, 1, 128, dtype=F32)
    taps = 27

    beside = swap(qkv_weight, "clip", 2, CLIPS)
    cells = shape(CELLS, C)
    long_row = shape(ROW + 16, C)
    rows_f, near, far, stats0, norms, own_mods = call(
        split_kernel,
        [cells, row, row, stats, shape(8, C, dtype=F32), shape(2, D, dtype=F32)],
        [SMEM] + [HBM] * 5,
        [
            pltpu.VMEM((FRAMES, 2, 32, C), BF16),
            pltpu.VMEM((3, C), F32),
            pltpu.VMEM((3, C), F32),
            pltpu.VMEM((1, D), F32),
            pltpu.VMEM((1, D), F32),
            pltpu.VMEM((2, CELLS, 128), F32),
            DMA((5,)),
        ],
        0,
        1 << 20,
    )(place, features.reshape(FRAMES, 2, 32, C), norm_gains, norm_shifts, mod_scale, mod_shift)
    near, far = neighbours(near, far)
    mods = swap(own_mods, "clip", 1, CLIPS)
    stats0 = exchange(stats0)
    stats0, mods, beside = lax.optimization_barrier((stats0, mods, beside))
    here = jnp.stack([qkv_weight, beside])
    there = swap(here, "clip", 4, CLIPS)
    hidden, center, near_h, far_h, stats1 = call(
        first_kernel,
        [cells, shape(8, C, dtype=F32), long_row, long_row, stats],
        [SMEM] + [VMEM] * 5 + [HBM],
        [WINDOW, WEIGHT, pltpu.VMEM((CELLS, C), BF16), DMA((2,))],
        CONV_FLOPS,
        5 << 20,
        first_out=HBM,
    )(place, stats0, rows_f, near, far, norms, first_conv.reshape(taps, C, C))
    near, far = neighbours(near_h, far_h)

    embed, bias = call(embed_kernel, [shape(128, D), shape(8, D, dtype=F32)], [VMEM] * 2)(
        embed_weight, embed_bias.reshape(1, D)
    )
    folded = shape(4 * QROWS, 128)
    own, other = call(
        fold_kernel,
        [folded, folded],
        [VMEM] * 6,
        [pltpu.VMEM((4 * QPAD, D), BF16), pltpu.VMEM((4 * QROWS, 128), F32)],
    )(here, there, embed, bias, own_mods, mods)
    stats1 = exchange(stats1)
    stats1, own, other = lax.optimization_barrier((stats1, own, other))
    other = swap(other, "clip", 1, CLIPS)

    block, near_b, far_b, stats2 = call(
        second_kernel,
        [cells, row, row, stats],
        [SMEM, VMEM, HBM] + [VMEM] * 5 + [HBM],
        [WINDOW, WEIGHT, pltpu.VMEM((CELLS, C), BF16), DMA((2,))],
        CONV_FLOPS,
        6 << 20,
    )(place, stats1, hidden, center, near, far, norms, rows_f, second_conv.reshape(taps, C, C))
    near, far = neighbours(near_b, far_b)
    stats2 = exchange(stats2)
    patches, parcel = call(
        third_kernel,
        [shape(FRAMES * HALF, 4 * LAT, dtype=F32), shape(432, 128)],
        [SMEM] + [VMEM] * 10,
        [WINDOW, pltpu.VMEM((48, 4 * LAT, C), BF16)],
        CONV_FLOPS // 2,
        4 << 20,
    )(
        place, stats2, block, near, far, norms,
        out_conv.transpose(0, 1, 2, 4, 3).reshape(taps, LAT, C), embed, bias, own, other,
    )
    latent = patches.reshape(FRAMES, HALF, 2, 2, LAT).transpose(0, 2, 1, 3, 4)
    latent = latent.reshape(1, FRAMES, 2, 2 * HALF, LAT)
    near, far, latent = gather_seq(parcel, latent)
    asks, keys, values = call(
        sort_kernel,
        [shape(WIDE, 256), shape(WIDE, 512), shape(WIDE, 512)],
        [SMEM] * 2 + [VMEM] * 2,
        [pltpu.VMEM((SEQ, 8 * QROWS, 128), F32), pltpu.VMEM((3 * WIDE, 128), F32)],
    )(place, clip, near, far)
    frame_heads = call(
        attend_kernel,
        shape(SEQ * HALF, WIDE),
        [SMEM] + [VMEM] * 5,
        [
            pltpu.VMEM((SEQ, HEADS, HALF, 256), BF16),
            pltpu.VMEM((2, HEADS, 128, 256), F32),
            pltpu.VMEM((SEQ, 128, HEADS * HALF), F32),
            pltpu.VMEM((SEQ, HEADS * HALF, 128), BF16),
        ],
    )(place, near, far, asks, keys, values)
    return (latent, frame_heads.reshape(1, 1, SEQ * HALF, WIDE))


def solution(mesh):
    placed = (
        P("clip", None, "seq", None, None),
        P(),
        P(),
        P(),
        P(),
        P(),
        P(),
        P(),
        P("clip", None),
        P("clip", None),
        P(("clip", "seq"), None),
    )
    return jax.shard_map(
        shards,
        mesh=mesh,
        in_specs=placed,
        out_specs=(P("clip", None, "seq", None, None), P("clip", "seq", None, None)),
        check_vma=False,
    )
```

time: 135 us -> 103 us (0.76)
  starting transfers between devices: 51.2 us -> 30.7 us
  blocking collectives: 0 us -> 13.4 us
  waiting for transfers between devices: 35.8 us -> 26.2 us
  Pallas kernels: 36.7 us -> 28.9 us
  local copies, waits for them, and re-layouts: 8.77 us -> 1.79 us
    all_to_all x0 -> x1, blocking collectives: none -> 13.4 us  [exchange(): return lax.all_to_all(stats, 'seq', 0, 0, tiled=True)]
    ppermute x6, starting transfers between devices: 15.6 us -> 4.1 us  [the longest x3 2.14 us: neighbours(): far = lax.ppermute(far, 'seq', NEXT_PAIRS)]
    pallas_call x8, Pallas kernels: 36.7 us -> 28.9 us  [run(): kernel(*(pltpu.with_memory_space_constraint(x, pltpu.HBM) if spec is HBM...]
    all_to_all x3 -> x2, starting transfers between devices: 22.9 us -> 15.2 us  [exchange(): return lax.all_to_all(stats, 'seq', 0, 0, tiled=True)]
    unnamed x39 -> x7, local copies, waits for them, and re-layouts: 7.96 us -> 0.97 us
    all_to_all x3 -> x2, waiting for transfers between devices: 17.8 us -> 10.9 us  [exchange(): return lax.all_to_all(stats, 'seq', 0, 0, tiled=True)]
    ppermute x10 -> x9, waiting for transfers between devices: 18 us -> 15.3 us  [swap(): return lax.ppermute(values, axis, [(i, i ^ bits) for i in range(count)])]
    ppermute x10 -> x9, starting transfers between devices: 12.6 us -> 11.4 us  [swap(): return lax.ppermute(values, axis, [(i, i ^ bits) for i in range(count)])]
  transfers between devices with their start and end apart: 19 -> 17, of which waited for: 10 -> 7; matrix products, arithmetic and copies ran while one was open for 2% -> 3% of each run, Pallas kernels for 1% -> 11%
where the time goes in v2:
time: 103 us
  starting transfers between devices  30.7 us (30%)
  Pallas kernels  28.9 us (28%)
  waiting for transfers between devices  26.2 us (25%)
  blocking collectives  13.4 us (13%)
  local copies, waits for them, and re-layouts  1.79 us (2%)
  other arithmetic  1.14 us (1%)
    pallas_call x8, Pallas kernels, run(): kernel(*(pltpu.with_memory_space_constraint(x, pltpu.HBM) if spec is HBM...  28.9 us
    ppermute x9, waiting for transfers between devices, swap(): return lax.ppermute(values, axis, [(i, i ^ bits) for i in range(count)])  15.3 us
    all_to_all x2, starting transfers between devices, exchange(): return lax.all_to_all(stats, 'seq', 0, 0, tiled=True)  15.2 us
    all_to_all x1, blocking collectives, exchange(): return lax.all_to_all(stats, 'seq', 0, 0, tiled=True)  13.4 us
    ppermute x9, starting transfers between devices, swap(): return lax.ppermute(values, axis, [(i, i ^ bits) for i in range(count)])  11.4 us
    all_to_all x2, waiting for transfers between devices, exchange(): return lax.all_to_all(stats, 'seq', 0, 0, tiled=True)  10.9 us
    ppermute x3, starting transfers between devices, neighbours(): far = lax.ppermute(far, 'seq', NEXT_PAIRS)  2.14 us
  transfers between devices with their start and end apart: 17, of which 7 were waited for; matrix products, arithmetic and copies ran while one was open for 3% of the time, Pallas kernels for 11%

profile of v2, /device:TPU:1, one launch (start us, length us, event | category | flops | bytes accessed | tf_op | source)
XLA Modules:
  0.0 102.9 jit_solution(313095363034890761)
XLA Ops:
  0.6 2.2 %collective-permute-start.1 = (bf16[36,3072]{1,0:T(8,128)(2,1)}, bf16[36,3072]{1,0:T(8,128)(2,1)S(1)}, u32[]{:S(2)}, u32[]{:S(2)}) collective-permute-start(bf16[36,3072]{1,0:T(8,128)(2,1)} %param.21), channel_id=1, source_target_pairs={{0,32},{16,48},{32,0},{48,16},{64,96},{80,112},{96,64},{112,80},{1... | collective-permute-start | bytes 663560 | tf_op jit(solution)/shard_map/ppermute | solution.py:441
  2.8 2.4 %split_kernel.1 = (bf16[1024,256]{1,0:T(8,128)(2,1)S(1)}, bf16[512,256]{1,0:T(8,128)(2,1)S(1)}, bf16[512,256]{1,0:T(8,128)(2,1)S(1)}, f32[16,1,128]{2,1,0:T(1,12...) custom-call(s32[1]{0:T(128)} %bitcast.place_ref, bf16[16,2,32,256]{3,2,1,0:T(8,128)(2,1)} %bitcast.33, ...), custom_call_target="tpu_custom_call" | custom-call | bytes 1048576 | tf_op jit(solution)/shard_map/split_kernel/pallas_call | solution.py:433
  5.2 1.7 %collective-permute-start = (f32[2,3072]{1,0:T(2,128)S(1)}, f32[2,3072]{1,0:T(2,128)S(1)}, u32[]{:S(2)}, u32[]{:S(2)}) collective-permute-start(f32[2,3072]{1,0:T(2,128)S(1)} %get-tuple-element.35.own_mods_ref), channel_id=1, source_target_pairs={{0,16},{16,0},{32,48},{48,32},{64,80},{80,64},{96,112},{112,96},{1... | collective-permute-start | bytes 73736 | tf_op jit(solution)/shard_map/ppermute | solution.py:441
  7.0 8.6 %all-to-all-start = ((f32[16,1,128]{2,1,0:T(1,128)}), f32[16,1,128]{2,1,0:T(1,128)S(1)}, u32[]{:S(2)}, u32[]{:S(2)}) async-start(f32[16,1,128]{2,1,0:T(1,128)} %get-tuple-element.34), calls=%async_computation | async-start | bytes 16384 | tf_op jit(solution)/shard_map/all_to_all | solution.py:454
  15.7 1.6 %collective-permute-start.3 = (bf16[512,256]{1,0:T(8,128)(2,1)S(1)}, bf16[512,256]{1,0:T(8,128)(2,1)S(1)}, u32[]{:S(2)}, u32[]{:S(2)}) collective-permute-start(bf16[512,256]{1,0:T(8,128)(2,1)S(1)} %get-tuple-element.39), channel_id=1, source_target_pairs={{0,15},{1,2},{2,1},{3,4},{4,3},{5,6},{6,5},{7,8},{8,7},{9,10},{10,... | collective-permute-start | bytes 786440 | tf_op jit(solution)/shard_map/ppermute | solution.py:449
  17.3 5.1 %all-to-all-done.stats_ref = f32[16,1,128]{2,1,0:T(1,128)S(1)} async-done(((f32[16,1,128]{2,1,0:T(1,128)}), f32[16,1,128]{2,1,0:T(1,128)S(1)}, u32[]{:S(2)}, u32[]{:S(2)}) %all-to-all-start) | async-done | bytes 8224 | tf_op jit(solution)/shard_map/all_to_all | solution.py:454
  22.4 1.0 pad_maximum_fusion.1.here_ref
  23.4 2.7 %collective-permute-start.4 = (bf16[2,36,3072]{2,1,0:T(8,128)(2,1)S(1)}, bf16[2,36,3072]{2,1,0:T(8,128)(2,1)S(1)}, u32[]{:S(2)}, u32[]{:S(2)}) collective-permute-start(bf16[2,36,3072]{2,1,0:T(8,128)(2,1)S(1)} %pad_maximum_fusion.1.here_ref), channel_id=1, source_target_pairs={{0,64},{16,80},{32,96},{48,112},{64,0},{80,16},{96,32},{112,48},{1... | collective-permute-start | bytes 1327112 | tf_op jit(solution)/shard_map/ppermute | solution.py:441
  26.2 7.7 %first_kernel.1 = (bf16[1024,256]{1,0:T(8,128)(2,1)}, f32[8,256]{1,0:T(8,128)S(1)}, bf16[528,256]{1,0:T(8,128)(2,1)}, bf16[528,256]{1,0:T(8,128)(2,1)S(1)}, f32[16,1,128]{2,1,0:T(1,128)}) custom-call(s32[1]{0:T(128)} %bitcast.place_ref, f32[16,1,128]{2,1,0:T(1,128)S(1)} %all-to-all-done.stats_ref, bf16[1024,256]{1,0:T(8,128)(2,1)S(1)} %get-tuple-element.37.rows_ref.feat_ref, ...), custom_call_target="tpu_custom_call" | custom-call | flops 3623878656 | bytes 5242880 | tf_op jit(solution)/shard_map/first_kernel/pallas_call | solution.py:433
  33.9 1.0 collective-permute-start.5
  35.2 6.7 %all-to-all-start.1 = ((f32[16,1,128]{2,1,0:T(1,128)}), f32[16,1,128]{2,1,0:T(1,128)S(1)}, u32[]{:S(2)}, u32[]{:S(2)}) async-start(f32[16,1,128]{2,1,0:T(1,128)} %get-tuple-element.41), calls=%async_computation.1 | async-start | bytes 16384 | tf_op jit(solution)/shard_map/all_to_all | solution.py:454
  43.1 5.8 %all-to-all-done.1.stats_ref = f32[16,1,128]{2,1,0:T(1,128)S(1)} async-done(((f32[16,1,128]{2,1,0:T(1,128)}), f32[16,1,128]{2,1,0:T(1,128)S(1)}, u32[]{:S(2)}, u32[]{:S(2)}) %all-to-all-start.1) | async-done | bytes 8224 | tf_op jit(solution)/shard_map/all_to_all | solution.py:454
  48.9 7.6 %second_kernel.1 = (bf16[1024,256]{1,0:T(8,128)(2,1)S(1)}, bf16[512,256]{1,0:T(8,128)(2,1)S(1)}, bf16[512,256]{1,0:T(8,128)(2,1)S(1)}, f32[16,1,128]{2,1,0:T(1,128)S(1)}) custom-call(s32[1]{0:T(128)} %bitcast.place_ref, f32[16,1,128]{2,1,0:T(1,128)S(1)} %all-to-all-done.1.stats_ref, bf16[1024,256]{1,0:T(8,128)(2,1)} %get-tuple-element.49.hidden_hbm, ...), custom_call_target="tpu_custom_call" | custom-call | flops 3623878656 | bytes 6291456 | tf_op jit(solution)/shard_map/second_kernel/pallas_call | solution.py:433
  57.5 13.4 %all_to_all.15.stats_ref = f32[16,1,128]{2,1,0:T(1,128)S(1)} all-to-all(f32[16,1,128]{2,1,0:T(1,128)S(1)} %get-tuple-element.53), channel_id=1, replica_groups=mesh['clip'=8,'seq'=16] {'seq'}, dimensions={0} | all-to-all | bytes 16384 | tf_op jit(solution)/shard_map/all_to_all | solution.py:454
  70.8 3.8 %third_kernel.1 = (f32[256,64]{1,0:T(8,128)S(1)}, bf16[432,128]{1,0:T(8,128)(2,1)S(1)}) custom-call(s32[1]{0:T(128)} %bitcast.place_ref, f32[16,1,128]{2,1,0:T(1,128)S(1)} %all_to_all.15.stats_ref, bf16[1024,256]{1,0:T(8,128)(2,1)S(1)} %get-tuple-element.54.rows_ref, bf16[512,256]{1,0:T(8,128)(2,1)S(1)} %collective-permute-done.7.near_ref, ...), custom_call_target="tpu_custom_call" | custom-call | flops 1811939328 | bytes 4194304 | tf_op jit(solution)/shard_map/third_kernel/pallas_call | solution.py:433
  75.8 4.3 %collective-permute-done.10 = bf16[432,128]{1,0:T(8,128)(2,1)S(1)} collective-permute-done((bf16[432,128]{1,0:T(8,128)(2,1)S(1)}, bf16[432,128]{1,0:T(8,128)(2,1)S(1)}, u32[]{:S(2)}, u32[]{:S(2)}) %collective-permute-start.10) | collective-permute-done | bytes 110624 | tf_op jit(solution)/shard_map/ppermute | solution.py:441
  81.7 1.8 %collective-permute-start.13 = (bf16[2,432,128]{2,1,0:T(8,128)(2,1)S(1)}, bf16[2,432,128]{2,1,0:T(8,128)(2,1)S(1)}, u32[]{:S(2)}, u32[]{:S(2)}) collective-permute-start(bf16[2,432,128]{2,1,0:T(8,128)(2,1)S(1)} %get-tuple-element.69), channel_id=1, source_target_pairs={{0,6},{1,7},{2,4},{3,5},{4,2},{5,3},{6,0},{7,1},{8,14},{9,15},{10,... | collective-permute-start | bytes 663560 | tf_op jit(solution)/shard_map/ppermute | solution.py:441
  83.5 3.6 %collective-permute-done.12 = bf16[2,432,128]{2,1,0:T(8,128)(2,1)S(1)} collective-permute-done((bf16[2,432,128]{2,1,0:T(8,128)(2,1)S(1)}, bf16[2,432,128]{2,1,0:T(8,128)(2,1)S(1)}, u32[]{:S(2)}, u32[]{:S(2)}) %collective-permute-start.12) | collective-permute-done | bytes 221216 | tf_op jit(solution)/shard_map/ppermute | solution.py:441
  87.1 3.2 %collective-permute-done.11 = bf16[2,432,128]{2,1,0:T(8,128)(2,1)S(1)} collective-permute-done((bf16[2,432,128]{2,1,0:T(8,128)(2,1)S(1)}, bf16[2,432,128]{2,1,0:T(8,128)(2,1)S(1)}, u32[]{:S(2)}, u32[]{:S(2)}) %collective-permute-start.11) | collective-permute-done | bytes 221216 | tf_op jit(solution)/shard_map/ppermute | solution.py:441
  90.4 3.0 %collective-permute-done.13 = bf16[2,432,128]{2,1,0:T(8,128)(2,1)S(1)} collective-permute-done((bf16[2,432,128]{2,1,0:T(8,128)(2,1)S(1)}, bf16[2,432,128]{2,1,0:T(8,128)(2,1)S(1)}, u32[]{:S(2)}, u32[]{:S(2)}) %collective-permute-start.13) | collective-permute-done | bytes 221216 | tf_op jit(solution)/shard_map/ppermute | solution.py:441
  93.5 1.1 %collective-permute-start.14 = (bf16[8,432,128]{2,1,0:T(8,128)(2,1)S(1)}, bf16[8,432,128]{2,1,0:T(8,128)(2,1)S(1)}, u32[]{:S(2)}, u32[]{:S(2)}) collective-permute-start(bf16[8,432,128]{2,1,0:T(8,128)(2,1)S(1)} %bitcast.24), channel_id=1, source_target_pairs={{0,1},{1,0},{2,3},{3,2},{4,5},{5,4},{6,7},{7,6},{8,9},{9,8},{10,11... | collective-permute-start | bytes 2654216 | tf_op jit(solution)/shard_map/ppermute | solution.py:441
  95.6 1.1 %collective-permute-done.14.far_ref = bf16[8,432,128]{2,1,0:T(8,128)(2,1)S(1)} collective-permute-done((bf16[8,432,128]{2,1,0:T(8,128)(2,1)S(1)}, bf16[8,432,128]{2,1,0:T(8,128)(2,1)S(1)}, u32[]{:S(2)}, u32[]{:S(2)}) %collective-permute-start.14) | collective-permute-done | bytes 884768 | tf_op jit(solution)/shard_map/ppermute | solution.py:441
  96.7 1.6 %sort_kernel.1 = (bf16[1536,256]{1,0:T(8,128)(2,1)S(1)}, bf16[1536,512]{1,0:T(8,128)(2,1)S(1)}, bf16[1536,512]{1,0:T(8,128)(2,1)S(1)}) custom-call(s32[1]{0:T(128)} %bitcast.place_ref, s32[1]{0:T(128)} %bitcast.18.clip_ref, bf16[8,432,128]{2,1,0:T(8,128)(2,1)S(1)} %bitcast.25, bf16[8,432,128]{2,1,0:T(8,128)(2,1)S(1)} %collective-permute-done.14.far_ref), custom_call_target="tpu_custom_call" | custom-call | tf_op jit(solution)/shard_map/sort_kernel/pallas_call | solution.py:433
  98.3 4.6 %attend_kernel.1 = bf16[256,1536]{1,0:T(8,128)(2,1)} custom-call(s32[1]{0:T(128)} %bitcast.place_ref, bf16[8,432,128]{2,1,0:T(8,128)(2,1)S(1)} %bitcast.26, bf16[8,432,128]{2,1,0:T(8,128)(2,1)S(1)} %collective-permute-done.14.far_ref, bf16[1536,256]{1,0:T(8,128)(2,1)S(1)} %get-tuple-element.63.asks_ref, bf16[1536,512]{1,0:T(8,128)(2,1)S(1)} %get-tuple-element.64.keys_ref, ...), custom_call_target="tpu_custom_call" | custom-call | tf_op jit(solution)/shard_map/attend_kernel/pallas_call | solution.py:433
  (33 shorter events, 6.5 us)
Async XLA Ops:
  0.6 21.8 %collective-permute-start.1 = (bf16[36,3072]{1,0:T(8,128)(2,1)}, bf16[36,3072]{1,0:T(8,128)(2,1)S(1)}, u32[]{:S(2)}, u32[]{:S(2)}) collective-permute-start(bf16[36,3072]{1,0:T(8,128)(2,1)} %param.21), channel_id=1, source_target_pairs={{0,32},{16,48},{32,0},{48,16},{64,96},{80,112},{96,64},{112,80},{1... | collective-permute-start | bytes 663560 | tf_op jit(solution)/shard_map/ppermute | solution.py:441
  5.2 17.2 %collective-permute-start = (f32[2,3072]{1,0:T(2,128)S(1)}, f32[2,3072]{1,0:T(2,128)S(1)}, u32[]{:S(2)}, u32[]{:S(2)}) collective-permute-start(f32[2,3072]{1,0:T(2,128)S(1)} %get-tuple-element.35.own_mods_ref), channel_id=1, source_target_pairs={{0,16},{16,0},{32,48},{48,32},{64,80},{80,64},{96,112},{112,96},{1... | collective-permute-start | bytes 73736 | tf_op jit(solution)/shard_map/ppermute | solution.py:441
  7.0 15.5 %all-to-all-start = ((f32[16,1,128]{2,1,0:T(1,128)}), f32[16,1,128]{2,1,0:T(1,128)S(1)}, u32[]{:S(2)}, u32[]{:S(2)}) async-start(f32[16,1,128]{2,1,0:T(1,128)} %get-tuple-element.34), calls=%async_computation | async-start | bytes 16384 | tf_op jit(solution)/shard_map/all_to_all | solution.py:454
  15.5 10.6 %collective-permute-start.2 = (bf16[512,256]{1,0:T(8,128)(2,1)S(1)}, bf16[512,256]{1,0:T(8,128)(2,1)S(1)}, u32[]{:S(2)}, u32[]{:S(2)}) collective-permute-start(bf16[512,256]{1,0:T(8,128)(2,1)S(1)} %get-tuple-element.38), channel_id=1, source_target_pairs={{0,1},{1,0},{2,3},{3,2},{4,5},{5,4},{6,7},{7,6},{8,9},{9,8},{10,11... | collective-permute-start | bytes 786440 | tf_op jit(solution)/shard_map/ppermute | solution.py:450
  15.7 10.5 %collective-permute-start.3 = (bf16[512,256]{1,0:T(8,128)(2,1)S(1)}, bf16[512,256]{1,0:T(8,128)(2,1)S(1)}, u32[]{:S(2)}, u32[]{:S(2)}) collective-permute-start(bf16[512,256]{1,0:T(8,128)(2,1)S(1)} %get-tuple-element.39), channel_id=1, source_target_pairs={{0,15},{1,2},{2,1},{3,4},{4,3},{5,6},{6,5},{7,8},{8,7},{9,10},{10,... | collective-permute-start | bytes 786440 | tf_op jit(solution)/shard_map/ppermute | solution.py:449
  23.4 18.8 %collective-permute-start.4 = (bf16[2,36,3072]{2,1,0:T(8,128)(2,1)S(1)}, bf16[2,36,3072]{2,1,0:T(8,128)(2,1)S(1)}, u32[]{:S(2)}, u32[]{:S(2)}) collective-permute-start(bf16[2,36,3072]{2,1,0:T(8,128)(2,1)S(1)} %pad_maximum_fusion.1.here_ref), channel_id=1, source_target_pairs={{0,64},{16,80},{32,96},{48,112},{64,0},{80,16},{96,32},{112,48},{1... | collective-permute-start | bytes 1327112 | tf_op jit(solution)/shard_map/ppermute | solution.py:441
  26.1 15.7 %copy-start = (bf16[64,3072]{1,0:T(8,128)(2,1)S(1)}, bf16[64,3072]{1,0:T(8,128)(2,1)}, u32[]{:S(2)}) copy-start(bf16[64,3072]{1,0:T(8,128)(2,1)} %embed_ref.1) | copy-start | bytes 1179652
  26.2 15.7 %copy-start.1 = (f32[3072]{0:T(1024)S(1)}, f32[3072]{0:T(1024)}, u32[]{:S(2)}) copy-start(f32[3072]{0:T(1024)} %param.18) | copy-start | bytes 36868
  33.9 14.9 %collective-permute-start.5 = (bf16[528,256]{1,0:T(8,128)(2,1)}, bf16[528,256]{1,0:T(8,128)(2,1)S(1)}, u32[]{:S(2)}, u32[]{:S(2)}) collective-permute-start(bf16[528,256]{1,0:T(8,128)(2,1)} %get-tuple-element.51), channel_id=1, source_target_pairs={{0,1},{1,0},{2,3},{3,2},{4,5},{5,4},{6,7},{7,6},{8,9},{9,8},{10,11... | collective-permute-start | bytes 811016 | tf_op jit(solution)/shard_map/ppermute | solution.py:450
  34.9 13.9 %collective-permute-start.6 = (bf16[528,256]{1,0:T(8,128)(2,1)S(1)}, bf16[528,256]{1,0:T(8,128)(2,1)}, u32[]{:S(2)}, u32[]{:S(2)}) collective-permute-start(bf16[528,256]{1,0:T(8,128)(2,1)S(1)} %get-tuple-element.52), channel_id=1, source_target_pairs={{0,15},{1,2},{2,1},{3,4},{4,3},{5,6},{6,5},{7,8},{8,7},{9,10},{10,... | collective-permute-start | bytes 811016 | tf_op jit(solution)/shard_map/ppermute | solution.py:449
  35.2 13.7 %all-to-all-start.1 = ((f32[16,1,128]{2,1,0:T(1,128)}), f32[16,1,128]{2,1,0:T(1,128)S(1)}, u32[]{:S(2)}, u32[]{:S(2)}) async-start(f32[16,1,128]{2,1,0:T(1,128)} %get-tuple-element.41), calls=%async_computation.1 | async-start | bytes 16384 | tf_op jit(solution)/shard_map/all_to_all | solution.py:454
  48.9 22.0 %copy-start.2 = (bf16[3,3,3,256,16]{3,4,2,1,0:T(8,128)(2,1)S(1)}, bf16[3,3,3,256,16]{3,4,2,1,0:T(8,128)(2,1)}, u32[]{:S(2)}) copy-start(bf16[3,3,3,256,16]{3,4,2,1,0:T(8,128)(2,1)} %param.14) | copy-start | bytes 663556
  56.4 14.4 %collective-permute-start.7 = (bf16[512,256]{1,0:T(8,128)(2,1)S(1)}, bf16[512,256]{1,0:T(8,128)(2,1)S(1)}, u32[]{:S(2)}, u32[]{:S(2)}) collective-permute-start(bf16[512,256]{1,0:T(8,128)(2,1)S(1)} %get-tuple-element.55), channel_id=1, source_target_pairs={{0,1},{1,0},{2,3},{3,2},{4,5},{5,4},{6,7},{7,6},{8,9},{9,8},{10,11... | collective-permute-start | bytes 786440 | tf_op jit(solution)/shard_map/ppermute | solution.py:450
  57.2 13.6 %collective-permute-start.8 = (bf16[512,256]{1,0:T(8,128)(2,1)S(1)}, bf16[512,256]{1,0:T(8,128)(2,1)S(1)}, u32[]{:S(2)}, u32[]{:S(2)}) collective-permute-start(bf16[512,256]{1,0:T(8,128)(2,1)S(1)} %get-tuple-element.56), channel_id=1, source_target_pairs={{0,15},{1,2},{2,1},{3,4},{4,3},{5,6},{6,5},{7,8},{8,7},{9,10},{10,... | collective-permute-start | bytes 786440 | tf_op jit(solution)/shard_map/ppermute | solution.py:449
  57.5 13.4 %collective-permute-start.9 = (bf16[144,128]{1,0:T(8,128)(2,1)S(1)}, bf16[144,128]{1,0:T(8,128)(2,1)S(1)}, u32[]{:S(2)}, u32[]{:S(2)}) collective-permute-start(bf16[144,128]{1,0:T(8,128)(2,1)S(1)} %get-tuple-element.58), channel_id=1, source_target_pairs={{0,16},{16,0},{32,48},{48,32},{64,80},{80,64},{96,112},{112,96},{1... | collective-permute-start | bytes 110600 | tf_op jit(solution)/shard_map/ppermute | solution.py:441
  74.7 5.5 %collective-permute-start.10 = (bf16[432,128]{1,0:T(8,128)(2,1)S(1)}, bf16[432,128]{1,0:T(8,128)(2,1)S(1)}, u32[]{:S(2)}, u32[]{:S(2)}) collective-permute-start(bf16[432,128]{1,0:T(8,128)(2,1)S(1)} %get-tuple-element.59), channel_id=1, source_target_pairs={{0,8},{1,9},{2,10},{3,11},{4,12},{5,13},{6,14},{7,15},{8,0},{9,1},... | collective-permute-start | bytes 331784 | tf_op jit(solution)/shard_map/ppermute | solution.py:441
  80.2 7.0 %collective-permute-start.12 = (bf16[2,432,128]{2,1,0:T(8,128)(2,1)S(1)}, bf16[2,432,128]{2,1,0:T(8,128)(2,1)S(1)}, u32[]{:S(2)}, u32[]{:S(2)}) collective-permute-start(bf16[2,432,128]{2,1,0:T(8,128)(2,1)S(1)} %get-tuple-element.69), channel_id=1, source_target_pairs={{0,4},{1,5},{2,6},{3,7},{4,0},{5,1},{6,2},{7,3},{8,12},{9,13},{10,... | collective-permute-start | bytes 663560 | tf_op jit(solution)/shard_map/ppermute | solution.py:441
  81.2 9.2 %collective-permute-start.11 = (bf16[2,432,128]{2,1,0:T(8,128)(2,1)S(1)}, bf16[2,432,128]{2,1,0:T(8,128)(2,1)S(1)}, u32[]{:S(2)}, u32[]{:S(2)}) collective-permute-start(bf16[2,432,128]{2,1,0:T(8,128)(2,1)S(1)} %get-tuple-element.69), channel_id=1, source_target_pairs={{0,2},{1,3},{2,0},{3,1},{4,6},{5,7},{6,4},{7,5},{8,10},{9,11},{10,... | collective-permute-start | bytes 663560 | tf_op jit(solution)/shard_map/ppermute | solution.py:441
  81.7 11.6 %collective-permute-start.13 = (bf16[2,432,128]{2,1,0:T(8,128)(2,1)S(1)}, bf16[2,432,128]{2,1,0:T(8,128)(2,1)S(1)}, u32[]{:S(2)}, u32[]{:S(2)}) collective-permute-start(bf16[2,432,128]{2,1,0:T(8,128)(2,1)S(1)} %get-tuple-element.69), channel_id=1, source_target_pairs={{0,6},{1,7},{2,4},{3,5},{4,2},{5,3},{6,0},{7,1},{8,14},{9,15},{10,... | collective-permute-start | bytes 663560 | tf_op jit(solution)/shard_map/ppermute | solution.py:441
  93.5 3.1 %collective-permute-start.14 = (bf16[8,432,128]{2,1,0:T(8,128)(2,1)S(1)}, bf16[8,432,128]{2,1,0:T(8,128)(2,1)S(1)}, u32[]{:S(2)}, u32[]{:S(2)}) collective-permute-start(bf16[8,432,128]{2,1,0:T(8,128)(2,1)S(1)} %bitcast.24), channel_id=1, source_target_pairs={{0,1},{1,0},{2,3},{3,2},{4,5},{5,4},{6,7},{7,6},{8,9},{9,8},{10,11... | collective-permute-start | bytes 2654216 | tf_op jit(solution)/shard_map/ppermute | solution.py:441

commit v3 on v2

--- a/solution.py
+++ b/solution.py
@@ -66,13 +66,9 @@
     return out
 
 
-def write_stats(cells, stats_ref):
-    count = cells.shape[0]
-    mean_c = jnp.sum(cells, axis=0, keepdims=True) * (1.0 / count)
+def write_stats(mean_c, square_c, count, stats_ref):
     same = one_hot((iota((C, C), 0) >> 3) == (iota((C, C), 1) >> 3))
     mean_g = exact_dot(rows8(mean_c), same)[0:1] * (1.0 / 8)
-    off = cells - mean_c
-    square_c = jnp.sum(off * off, axis=0, keepdims=True)
     gap = mean_c - mean_g
     square_c = square_c + count * (gap * gap)
     lane = iota((C, 128), 1)
@@ -130,7 +126,9 @@
                     part = wide[side, pl.ds(base, HALF, stride=2)]
                     rows_ref[at : at + HALF, side * 128 : (side + 1) * 128] = part.astype(BF16)
     own_rows(place_ref, rows_ref, near_ref, far_ref)
-    write_stats(cells, stats_ref)
+    mean = jnp.sum(cells, axis=0, keepdims=True) * (1.0 / CELLS)
+    off = cells - mean
+    write_stats(mean, jnp.sum(off * off, axis=0, keepdims=True), CELLS, stats_ref)
 
 
 def fill_window(place_ref, stats_ref, rows_ref, near_ref, far_ref, norms_ref, layer, window, centers=None, load=None):
@@ -173,29 +171,75 @@
                 )
 
 
-def convolve(window, weight):
-    total = None
-    for tap in range(27):
-        p, q, r = tap // 9, tap // 3 % 3, tap % 3
-        cells = window[q : q + 2, p : p + FRAMES, r : r + 2].reshape(CELLS, C)
-        term = dot(cells, weight[tap])
-        total = term if total is None else total + term
-    return total
+TILE = 256
+
+
+def start_weights(source, weight, sems):
+    copies = [
+        pltpu.make_async_copy(source.at[9 * p : 9 * p + 9], weight.at[9 * p : 9 * p + 9], sems.at[p])
+        for p in range(3)
+    ]
+    for copy in copies:
+        copy.start()
+    return copies
+
+
+def convolve(window, weight, copies, total, finish):
+    for p in range(3):
+        copies[p].wait()
+        for tile in range(CELLS // TILE):
+            row, frame = tile * TILE // ROW, tile * TILE % ROW // 32
+            part = None
+            for q in range(3):
+                for r in range(3):
+                    at = frame + p
+                    cells = window[q + row, at : at + TILE // 32, r : r + 2].reshape(TILE, C)
+                    term = dot(cells, weight[9 * p + 3 * q + r])
+                    part = term if part is None else part + term
+            rows = slice(tile * TILE, (tile + 1) * TILE)
+            if p > 0:
+                part = part + total[rows]
+            if p < 2:
+                total[rows] = part
+            else:
+                finish(rows, part)
+
+
+class Moments:
+    def __init__(self):
+        self.center = self.first = self.second = None
+
+    def add(self, tile):
+        if self.center is None:
+            self.center = jnp.sum(tile, axis=0, keepdims=True) * (1.0 / TILE)
+        off = tile - self.center
+        first = jnp.sum(off, axis=0, keepdims=True)
+        second = jnp.sum(off * off, axis=0, keepdims=True)
+        self.first = first if self.first is None else self.first + first
+        self.second = second if self.second is None else self.second + second
+        return off
+
+    def write(self, stats_ref):
+        gap = self.first * (1.0 / CELLS)
+        square = jnp.maximum(self.second - self.first * gap, 0.0)
+        write_stats(self.center + gap, square, CELLS, stats_ref)
 
 
 def first_kernel(
     place_ref, stats_ref, rows_ref, near_ref, far_ref, norms_ref, weight_hbm,
-    hidden_hbm, center_ref, near_out, far_out, stats_out, window, weight, hidden_ref, sems,
+    hidden_hbm, center_ref, near_out, far_out, stats_out, window, weight, total, hidden_ref, sems,
 ):
-    copy = pltpu.make_async_copy(weight_hbm, weight, sems.at[0])
+    copies = start_weights(weight_hbm, weight, sems)
+    fill_window(place_ref, stats_ref, rows_ref, near_ref, far_ref, norms_ref, 0, window)
+    moments = Moments()
+
+    def finish(rows, tile):
+        hidden_ref[rows] = moments.add(tile).astype(BF16)
+
+    convolve(window, weight, copies, total, finish)
+    copy = pltpu.make_async_copy(hidden_ref, hidden_hbm, sems.at[3])
     copy.start()
-    fill_window(place_ref, stats_ref, rows_ref, near_ref, far_ref, norms_ref, 0, window)
-    copy.wait()
-    hidden = convolve(window, weight)
-    center = jnp.sum(hidden, axis=0, keepdims=True) * (1.0 / CELLS)
-    hidden_ref[...] = (hidden - center).astype(BF16)
-    copy = pltpu.make_async_copy(hidden_ref, hidden_hbm, sems.at[1])
-    copy.start()
+    center = moments.center
     center_ref[...] = jnp.broadcast_to(center, (8, C))
     high = center.astype(BF16).astype(F32)
     mid = (center - high).astype(BF16).astype(F32)
@@ -204,27 +248,31 @@
     own_rows(place_ref, hidden_ref, near_out.at[0:ROW], far_out.at[0:ROW])
     near_out[ROW : ROW + 16] = terms.astype(BF16)
     far_out[ROW : ROW + 16] = terms.astype(BF16)
-    write_stats(hidden, stats_out)
+    moments.write(stats_out)
     copy.wait()
 
 
 def second_kernel(
     place_ref, stats_ref, hidden_hbm, center_ref, near_ref, far_ref, norms_ref, feat_ref, weight_hbm,
-    block_ref, near_out, far_out, stats_out, window, weight, hidden_ref, sems,
+    block_ref, near_out, far_out, stats_out, window, weight, total, hidden_ref, sems,
 ):
-    load = pltpu.make_async_copy(hidden_hbm, hidden_ref, sems.at[1])
+    load = pltpu.make_async_copy(hidden_hbm, hidden_ref, sems.at[3])
     load.start()
-    copy = pltpu.make_async_copy(weight_hbm, weight, sems.at[0])
-    copy.start()
+    copies = start_weights(weight_hbm, weight, sems)
     own = center_ref[0:1]
     centers = [jnp.sum(ref[ROW : ROW + 16].astype(F32), axis=0, keepdims=True) for ref in (near_ref, far_ref)]
     centers += [own, own]
     fill_window(place_ref, stats_ref, hidden_ref, near_ref, far_ref, norms_ref, 1, window, centers, load)
-    copy.wait()
-    block = (convolve(window, weight) + feat_ref[...].astype(F32)).astype(BF16)
-    block_ref[...] = block
+    moments = Moments()
+
+    def finish(rows, tile):
+        block = (tile + feat_ref[rows].astype(F32)).astype(BF16)
+        block_ref[rows] = block
+        moments.add(block.astype(F32))
+
+    convolve(window, weight, copies, total, finish)
     own_rows(place_ref, block_ref, near_out, far_out)
-    write_stats(block.astype(F32), stats_out)
+    moments.write(stats_out)
 
 
 def column_to_row(column):
@@ -278,6 +326,26 @@
     parcel_ref[288:432] = other_ref[...]
 
 
+def latent_kernel(patches_ref, latent_ref):
+    n = FRAMES * HALF
+    patches = patches_ref[...]
+    turned = jnp.transpose(jnp.concatenate([patches, jnp.zeros_like(patches)], axis=1))
+    out = None
+    for dw in range(2):
+        rows = jnp.concatenate([turned[(2 * dh + dw) * LAT : (2 * dh + dw + 1) * LAT] for dh in range(2)], axis=0)
+        high = rows.astype(BF16).astype(F32)
+        mid = (rows - high).astype(BF16).astype(F32)
+        parts = jnp.concatenate([high, mid, rows - high - mid], axis=0).astype(BF16)
+        column = iota((n, 2 * n), 1)
+        spread = one_hot(column == iota((n, 2 * n), 0) * 2 + dw)
+        term = dot(parts, spread)
+        term = term[0:32] + term[32:64] + term[64:96]
+        out = term if out is None else out + term
+    for frame in range(FRAMES):
+        for dh in range(2):
+            latent_ref[frame, dh] = out[dh * LAT : (dh + 1) * LAT, frame * 32 : (frame + 1) * 32]
+
+
 def embed_kernel(embed_ref, bias_ref, embed_out, bias_out):
     embed = embed_ref[...].astype(F32)
     embed = embed - jnp.mean(embed, axis=1, keepdims=True)
@@ -330,7 +398,7 @@
     seq, clip = place_ref[0], clip_ref[0]
     for j in range(SEQ):
         source = (near_ref, far_ref)[j & 1]
-        loose[j] = source[j >> 1, 144:432].astype(F32)
+        loose[j] = source[(j >> 1) & 3, j >> 3, 144:432].astype(F32)
         for k in range(CLIPS):
             at = ((clip ^ (2 * (k & 3) + (k >> 2))) * SEQ + (seq ^ j)) * QROWS
             wide[pl.ds(at, QROWS)] = loose[j, k * QROWS : (k + 1) * QROWS]
@@ -353,7 +421,7 @@
 
 def attend_kernel(place_ref, near_ref, far_ref, asks_ref, keys_ref, values_ref, out_ref, queries, mixed, scores, weights):
     seq = place_ref[0]
-    blocks = [(near_ref, far_ref)[j & 1].at[j >> 1] for j in range(SEQ)]
+    blocks = [(near_ref, far_ref)[j & 1].at[(j >> 1) & 3, j >> 3] for j in range(SEQ)]
     lane = iota((128, 128), 1)
     pick = one_hot(iota((8, 128), 1) == iota((8, 128), 0) + seq * 8)
     twin = pl.ds(pl.multiple_of((seq >> 1) * 16, 16), 16)
@@ -458,8 +526,7 @@
     over = swap(block, "seq", 8, SEQ)
     over, beside = lax.optimization_barrier((over, beside))
     pair = jnp.stack([block, over])
-    others = [swap(pair, "seq", bits, SEQ) for bits in (2, 4, 6)]
-    near = jnp.stack([pair] + others, axis=1).reshape((8,) + block.shape)
+    near = jnp.stack([pair] + [swap(pair, "seq", bits, SEQ) for bits in (2, 4, 6)])
     return near, swap(near, "seq", 1, SEQ), beside
 
 
@@ -516,7 +583,7 @@
         first_kernel,
         [cells, shape(8, C, dtype=F32), long_row, long_row, stats],
         [SMEM] + [VMEM] * 5 + [HBM],
-        [WINDOW, WEIGHT, pltpu.VMEM((CELLS, C), BF16), DMA((2,))],
+        [WINDOW, WEIGHT, pltpu.VMEM((CELLS, C), F32), pltpu.VMEM((CELLS, C), BF16), DMA((4,))],
         CONV_FLOPS,
         5 << 20,
         first_out=HBM,
@@ -541,7 +608,7 @@
         second_kernel,
         [cells, row, row, stats],
         [SMEM, VMEM, HBM] + [VMEM] * 5 + [HBM],
-        [WINDOW, WEIGHT, pltpu.VMEM((CELLS, C), BF16), DMA((2,))],
+        [WINDOW, WEIGHT, pltpu.VMEM((CELLS, C), F32), pltpu.VMEM((CELLS, C), BF16), DMA((4,))],
         CONV_FLOPS,
         6 << 20,
     )(place, stats1, hidden, center, near, far, norms, rows_f, second_conv.reshape(taps, C, C))
@@ -558,8 +625,7 @@
         place, stats2, block, near, far, norms,
         out_conv.transpose(0, 1, 2, 4, 3).reshape(taps, LAT, C), embed, bias, own, other,
     )
-    latent = patches.reshape(FRAMES, HALF, 2, 2, LAT).transpose(0, 2, 1, 3, 4)
-    latent = latent.reshape(1, FRAMES, 2, 2 * HALF, LAT)
+    latent = call(latent_kernel, shape(FRAMES, 2, LAT, 2 * HALF, dtype=F32), [VMEM])(patches)
     near, far, latent = gather_seq(parcel, latent)
     asks, keys, values = call(
         sort_kernel,
@@ -578,6 +644,7 @@
             pltpu.VMEM((SEQ, HEADS * HALF, 128), BF16),
         ],
     )(place, near, far, asks, keys, values)
+    latent = latent.transpose(0, 1, 3, 2).reshape(1, FRAMES, 2, 2 * HALF, LAT)
     return (latent, frame_heads.reshape(1, 1, SEQ * HALF, WIDE))
 
 

time: 103 us -> 102 us (level)
  local copies, waits for them, and re-layouts: 1.79 us -> 0.01 us
    pallas_call x8 -> x9, Pallas kernels: 28.9 us -> 28.4 us  [run(): kernel(*(pltpu.with_memory_space_constraint(x, pltpu.HBM) if spec is HBM...]
  transfers between devices with their start and end apart: 17 -> 17, of which waited for: 7 -> 7; matrix products, arithmetic and copies ran while one was open for 3% -> 1% of each run, Pallas kernels for 11% -> 11%
where the time goes in v3:
time: 102 us; the launch traced here: 101 us
  starting transfers between devices  30.7 us (30%)
  Pallas kernels  28.4 us (28%)
  waiting for transfers between devices  26.9 us (26%)
  blocking collectives  13.4 us (13%)
  other arithmetic  1.14 us (1%)
    pallas_call x9, Pallas kernels, run(): kernel(*(pltpu.with_memory_space_constraint(x, pltpu.HBM) if spec is HBM...  28.4 us
    ppermute x9, waiting for transfers between devices, swap(): return lax.ppermute(values, axis, [(i, i ^ bits) for i in range(count)])  15.9 us
    all_to_all x2, starting transfers between devices, exchange(): return lax.all_to_all(stats, 'seq', 0, 0, tiled=True)  15.2 us
    all_to_all x1, blocking collectives, exchange(): return lax.all_to_all(stats, 'seq', 0, 0, tiled=True)  13.4 us
    ppermute x9, starting transfers between devices, swap(): return lax.ppermute(values, axis, [(i, i ^ bits) for i in range(count)])  11.4 us
    all_to_all x2, waiting for transfers between devices, exchange(): return lax.all_to_all(stats, 'seq', 0, 0, tiled=True)  10.9 us
    ppermute x3, starting transfers between devices, neighbours(): far = lax.ppermute(far, 'seq', NEXT_PAIRS)  2.14 us
  transfers between devices with their start and end apart: 17, of which 7 were waited for; matrix products, arithmetic and copies ran while one was open for 1% of the time, Pallas kernels for 11%

profile of v3, /device:TPU:1, one launch (start us, length us, event | category | flops | bytes accessed | tf_op | source)
XLA Modules:
  0.0 101.2 jit_solution(17869389448439467964)
XLA Ops:
  0.6 2.2 %collective-permute-start.1 = (bf16[36,3072]{1,0:T(8,128)(2,1)}, bf16[36,3072]{1,0:T(8,128)(2,1)S(1)}, u32[]{:S(2)}, u32[]{:S(2)}) collective-permute-start(bf16[36,3072]{1,0:T(8,128)(2,1)} %param.21), channel_id=1, source_target_pairs={{0,32},{16,48},{32,0},{48,16},{64,96},{80,112},{96,64},{112,80},{1... | collective-permute-start | bytes 663560 | tf_op jit(solution)/shard_map/ppermute | solution.py:509
  2.8 2.4 %split_kernel.1 = (bf16[1024,256]{1,0:T(8,128)(2,1)S(1)}, bf16[512,256]{1,0:T(8,128)(2,1)S(1)}, bf16[512,256]{1,0:T(8,128)(2,1)S(1)}, f32[16,1,128]{2,1,0:T(1,12...) custom-call(s32[1]{0:T(128)} %bitcast.place_ref, bf16[16,2,32,256]{3,2,1,0:T(8,128)(2,1)} %bitcast.26, ...), custom_call_target="tpu_custom_call" | custom-call | bytes 1048576 | tf_op jit(solution)/shard_map/split_kernel/pallas_call | solution.py:501
  5.2 1.7 %collective-permute-start = (f32[2,3072]{1,0:T(2,128)S(1)}, f32[2,3072]{1,0:T(2,128)S(1)}, u32[]{:S(2)}, u32[]{:S(2)}) collective-permute-start(f32[2,3072]{1,0:T(2,128)S(1)} %get-tuple-element.35.own_mods_ref), channel_id=1, source_target_pairs={{0,16},{16,0},{32,48},{48,32},{64,80},{80,64},{96,112},{112,96},{1... | collective-permute-start | bytes 73736 | tf_op jit(solution)/shard_map/ppermute | solution.py:509
  6.9 8.6 %all-to-all-start = ((f32[16,1,128]{2,1,0:T(1,128)}), f32[16,1,128]{2,1,0:T(1,128)S(1)}, u32[]{:S(2)}, u32[]{:S(2)}) async-start(f32[16,1,128]{2,1,0:T(1,128)} %get-tuple-element.34), calls=%async_computation | async-start | bytes 16384 | tf_op jit(solution)/shard_map/all_to_all | solution.py:522
  15.7 1.6 %collective-permute-start.3 = (bf16[512,256]{1,0:T(8,128)(2,1)S(1)}, bf16[512,256]{1,0:T(8,128)(2,1)S(1)}, u32[]{:S(2)}, u32[]{:S(2)}) collective-permute-start(bf16[512,256]{1,0:T(8,128)(2,1)S(1)} %get-tuple-element.39), channel_id=1, source_target_pairs={{0,15},{1,2},{2,1},{3,4},{4,3},{5,6},{6,5},{7,8},{8,7},{9,10},{10,... | collective-permute-start | bytes 786440 | tf_op jit(solution)/shard_map/ppermute | solution.py:517
  17.3 5.1 %all-to-all-done.stats_ref = f32[16,1,128]{2,1,0:T(1,128)S(1)} async-done(((f32[16,1,128]{2,1,0:T(1,128)}), f32[16,1,128]{2,1,0:T(1,128)S(1)}, u32[]{:S(2)}, u32[]{:S(2)}) %all-to-all-start) | async-done | bytes 8224 | tf_op jit(solution)/shard_map/all_to_all | solution.py:522
  23.4 2.7 %collective-permute-start.4 = (bf16[2,36,3072]{2,1,0:T(8,128)(2,1)S(1)}, bf16[2,36,3072]{2,1,0:T(8,128)(2,1)S(1)}, u32[]{:S(2)}, u32[]{:S(2)}) collective-permute-start(bf16[2,36,3072]{2,1,0:T(8,128)(2,1)S(1)} %pad_maximum_fusion.1.here_ref), channel_id=1, source_target_pairs={{0,64},{16,80},{32,96},{48,112},{64,0},{80,16},{96,32},{112,48},{1... | collective-permute-start | bytes 1327112 | tf_op jit(solution)/shard_map/ppermute | solution.py:509
  26.2 6.9 %first_kernel.1 = (bf16[1024,256]{1,0:T(8,128)(2,1)}, f32[8,256]{1,0:T(8,128)S(1)}, bf16[528,256]{1,0:T(8,128)(2,1)}, bf16[528,256]{1,0:T(8,128)(2,1)S(1)}, f32[16,1,128]{2,1,0:T(1,128)}) custom-call(s32[1]{0:T(128)} %bitcast.place_ref, f32[16,1,128]{2,1,0:T(1,128)S(1)} %all-to-all-done.stats_ref, bf16[1024,256]{1,0:T(8,128)(2,1)S(1)} %get-tuple-element.37.rows_ref.feat_ref, ...), custom_call_target="tpu_custom_call" | custom-call | flops 3623878656 | bytes 5242880 | tf_op jit(solution)/shard_map/first_kernel/pallas_call | solution.py:501
  33.1 1.0 %collective-permute-start.5 = (bf16[528,256]{1,0:T(8,128)(2,1)}, bf16[528,256]{1,0:T(8,128)(2,1)S(1)}, u32[]{:S(2)}, u32[]{:S(2)}) collective-permute-start(bf16[528,256]{1,0:T(8,128)(2,1)} %get-tuple-element.51), channel_id=1, source_target_pairs={{0,1},{1,0},{2,3},{3,2},{4,5},{5,4},{6,7},{7,6},{8,9},{9,8},{10,11... | collective-permute-start | bytes 811016 | tf_op jit(solution)/shard_map/ppermute | solution.py:518
  34.4 6.7 %all-to-all-start.1 = ((f32[16,1,128]{2,1,0:T(1,128)}), f32[16,1,128]{2,1,0:T(1,128)S(1)}, u32[]{:S(2)}, u32[]{:S(2)}) async-start(f32[16,1,128]{2,1,0:T(1,128)} %get-tuple-element.41), calls=%async_computation.1 | async-start | bytes 16384 | tf_op jit(solution)/shard_map/all_to_all | solution.py:522
  42.2 5.8 %all-to-all-done.1.stats_ref = f32[16,1,128]{2,1,0:T(1,128)S(1)} async-done(((f32[16,1,128]{2,1,0:T(1,128)}), f32[16,1,128]{2,1,0:T(1,128)S(1)}, u32[]{:S(2)}, u32[]{:S(2)}) %all-to-all-start.1) | async-done | bytes 8224 | tf_op jit(solution)/shard_map/all_to_all | solution.py:522
  48.0 6.8 %second_kernel.1 = (bf16[1024,256]{1,0:T(8,128)(2,1)S(1)}, bf16[512,256]{1,0:T(8,128)(2,1)S(1)}, bf16[512,256]{1,0:T(8,128)(2,1)S(1)}, f32[16,1,128]{2,1,0:T(1,128)S(1)}) custom-call(s32[1]{0:T(128)} %bitcast.place_ref, f32[16,1,128]{2,1,0:T(1,128)S(1)} %all-to-all-done.1.stats_ref, bf16[1024,256]{1,0:T(8,128)(2,1)} %get-tuple-element.49.hidden_hbm, ...), custom_call_target="tpu_custom_call" | custom-call | flops 3623878656 | bytes 6291456 | tf_op jit(solution)/shard_map/second_kernel/pallas_call | solution.py:501
  55.9 13.4 %all_to_all.15.stats_ref = f32[16,1,128]{2,1,0:T(1,128)S(1)} all-to-all(f32[16,1,128]{2,1,0:T(1,128)S(1)} %get-tuple-element.53), channel_id=1, replica_groups=mesh['clip'=8,'seq'=16] {'seq'}, dimensions={0} | all-to-all | bytes 16384 | tf_op jit(solution)/shard_map/all_to_all | solution.py:522
  69.2 3.8 %third_kernel.1 = (f32[256,64]{1,0:T(8,128)S(1)}, bf16[432,128]{1,0:T(8,128)(2,1)S(1)}) custom-call(s32[1]{0:T(128)} %bitcast.place_ref, f32[16,1,128]{2,1,0:T(1,128)S(1)} %all_to_all.15.stats_ref, bf16[1024,256]{1,0:T(8,128)(2,1)S(1)} %get-tuple-element.54.rows_ref, bf16[512,256]{1,0:T(8,128)(2,1)S(1)} %collective-permute-done.7.near_ref, ...), custom_call_target="tpu_custom_call" | custom-call | flops 1811939328 | bytes 4194304 | tf_op jit(solution)/shard_map/third_kernel/pallas_call | solution.py:501
  73.4 1.1 %latent_kernel.1 = f32[16,2,16,32]{3,2,1,0:T(8,128)} custom-call(f32[256,64]{1,0:T(8,128)S(1)} %get-tuple-element.60.patches_ref), custom_call_target="tpu_custom_call" | custom-call | tf_op jit(solution)/shard_map/latent_kernel/pallas_call | solution.py:501
  74.5 4.0 %collective-permute-done.10 = bf16[432,128]{1,0:T(8,128)(2,1)S(1)} collective-permute-done((bf16[432,128]{1,0:T(8,128)(2,1)S(1)}, bf16[432,128]{1,0:T(8,128)(2,1)S(1)}, u32[]{:S(2)}, u32[]{:S(2)}) %collective-permute-start.10) | collective-permute-done | bytes 110624 | tf_op jit(solution)/shard_map/ppermute | solution.py:509
  80.1 1.8 %collective-permute-start.13 = (bf16[2,432,128]{2,1,0:T(8,128)(2,1)S(1)}, bf16[2,432,128]{2,1,0:T(8,128)(2,1)S(1)}, u32[]{:S(2)}, u32[]{:S(2)}) collective-permute-start(bf16[2,432,128]{2,1,0:T(8,128)(2,1)S(1)} %get-tuple-element.67), channel_id=1, source_target_pairs={{0,6},{1,7},{2,4},{3,5},{4,2},{5,3},{6,0},{7,1},{8,14},{9,15},{10,... | collective-permute-start | bytes 663560 | tf_op jit(solution)/shard_map/ppermute | solution.py:509
  81.9 3.6 %collective-permute-done.12 = bf16[2,432,128]{2,1,0:T(8,128)(2,1)S(1)} collective-permute-done((bf16[2,432,128]{2,1,0:T(8,128)(2,1)S(1)}, bf16[2,432,128]{2,1,0:T(8,128)(2,1)S(1)}, u32[]{:S(2)}, u32[]{:S(2)}) %collective-permute-start.12) | collective-permute-done | bytes 221216 | tf_op jit(solution)/shard_map/ppermute | solution.py:509
  85.5 3.2 %collective-permute-done.11 = bf16[2,432,128]{2,1,0:T(8,128)(2,1)S(1)} collective-permute-done((bf16[2,432,128]{2,1,0:T(8,128)(2,1)S(1)}, bf16[2,432,128]{2,1,0:T(8,128)(2,1)S(1)}, u32[]{:S(2)}, u32[]{:S(2)}) %collective-permute-start.11) | collective-permute-done | bytes 221216 | tf_op jit(solution)/shard_map/ppermute | solution.py:509
  88.8 3.0 %collective-permute-done.13 = bf16[2,432,128]{2,1,0:T(8,128)(2,1)S(1)} collective-permute-done((bf16[2,432,128]{2,1,0:T(8,128)(2,1)S(1)}, bf16[2,432,128]{2,1,0:T(8,128)(2,1)S(1)}, u32[]{:S(2)}, u32[]{:S(2)}) %collective-permute-start.13) | collective-permute-done | bytes 221216 | tf_op jit(solution)/shard_map/ppermute | solution.py:509
  91.9 1.1 %collective-permute-start.14 = (bf16[4,2,432,128]{3,2,1,0:T(8,128)(2,1)S(1)}, bf16[4,2,432,128]{3,2,1,0:T(8,128)(2,1)S(1)}, u32[]{:S(2)}, u32[]{:S(2)}) collective-permute-start(bf16[4,2,432,128]{3,2,1,0:T(8,128)(2,1)S(1)} %pad_maximum_fusion.near_ref), channel_id=1, source_target_pairs={{0,1},{1,0},{2,3},{3,2},{4,5},{5,4},{6,7},{7,6},{8,9},{9,8},{10,11... | collective-permute-start | bytes 2654216 | tf_op jit(solution)/shard_map/ppermute | solution.py:509
  93.0 2.1 %collective-permute-done.14.far_ref = bf16[4,2,432,128]{3,2,1,0:T(8,128)(2,1)S(1)} collective-permute-done((bf16[4,2,432,128]{3,2,1,0:T(8,128)(2,1)S(1)}, bf16[4,2,432,128]{3,2,1,0:T(8,128)(2,1)S(1)}, u32[]{:S(2)}, u32[]{:S(2)}) %collective-permute-start.14) | collective-permute-done | bytes 884768 | tf_op jit(solution)/shard_map/ppermute | solution.py:509
  95.0 1.6 %sort_kernel.1 = (bf16[1536,256]{1,0:T(8,128)(2,1)S(1)}, bf16[1536,512]{1,0:T(8,128)(2,1)S(1)}, bf16[1536,512]{1,0:T(8,128)(2,1)S(1)}) custom-call(s32[1]{0:T(128)} %bitcast.place_ref, s32[1]{0:T(128)} %bitcast.17.clip_ref, bf16[4,2,432,128]{3,2,1,0:T(8,128)(2,1)S(1)} %pad_maximum_fusion.near_ref, bf16[4,2,432,128]{3,2,1,0:T(8,128)(2,1)S(1)} %collective-permute-done.14.far_ref), custom_call_target="tpu_custom_call" | custom-call | tf_op jit(solution)/shard_map/sort_kernel/pallas_call | solution.py:501
  96.7 4.6 %attend_kernel.1 = bf16[256,1536]{1,0:T(8,128)(2,1)} custom-call(s32[1]{0:T(128)} %bitcast.place_ref, bf16[4,2,432,128]{3,2,1,0:T(8,128)(2,1)S(1)} %pad_maximum_fusion.near_ref, bf16[4,2,432,128]{3,2,1,0:T(8,128)(2,1)S(1)} %collective-permute-done.14.far_ref, bf16[1536,256]{1,0:T(8,128)(2,1)S(1)} %get-tuple-element.63.asks_ref, ...), custom_call_target="tpu_custom_call" | custom-call | tf_op jit(solution)/shard_map/attend_kernel/pallas_call | solution.py:501
  (29 shorter events, 5.7 us)
Async XLA Ops:
  0.6 21.8 %collective-permute-start.1 = (bf16[36,3072]{1,0:T(8,128)(2,1)}, bf16[36,3072]{1,0:T(8,128)(2,1)S(1)}, u32[]{:S(2)}, u32[]{:S(2)}) collective-permute-start(bf16[36,3072]{1,0:T(8,128)(2,1)} %param.21), channel_id=1, source_target_pairs={{0,32},{16,48},{32,0},{48,16},{64,96},{80,112},{96,64},{112,80},{1... | collective-permute-start | bytes 663560 | tf_op jit(solution)/shard_map/ppermute | solution.py:509
  5.2 17.2 %collective-permute-start = (f32[2,3072]{1,0:T(2,128)S(1)}, f32[2,3072]{1,0:T(2,128)S(1)}, u32[]{:S(2)}, u32[]{:S(2)}) collective-permute-start(f32[2,3072]{1,0:T(2,128)S(1)} %get-tuple-element.35.own_mods_ref), channel_id=1, source_target_pairs={{0,16},{16,0},{32,48},{48,32},{64,80},{80,64},{96,112},{112,96},{1... | collective-permute-start | bytes 73736 | tf_op jit(solution)/shard_map/ppermute | solution.py:509
  6.9 15.5 %all-to-all-start = ((f32[16,1,128]{2,1,0:T(1,128)}), f32[16,1,128]{2,1,0:T(1,128)S(1)}, u32[]{:S(2)}, u32[]{:S(2)}) async-start(f32[16,1,128]{2,1,0:T(1,128)} %get-tuple-element.34), calls=%async_computation | async-start | bytes 16384 | tf_op jit(solution)/shard_map/all_to_all | solution.py:522
  15.5 10.6 %collective-permute-start.2 = (bf16[512,256]{1,0:T(8,128)(2,1)S(1)}, bf16[512,256]{1,0:T(8,128)(2,1)S(1)}, u32[]{:S(2)}, u32[]{:S(2)}) collective-permute-start(bf16[512,256]{1,0:T(8,128)(2,1)S(1)} %get-tuple-element.38), channel_id=1, source_target_pairs={{0,1},{1,0},{2,3},{3,2},{4,5},{5,4},{6,7},{7,6},{8,9},{9,8},{10,11... | collective-permute-start | bytes 786440 | tf_op jit(solution)/shard_map/ppermute | solution.py:518
  15.7 10.5 %collective-permute-start.3 = (bf16[512,256]{1,0:T(8,128)(2,1)S(1)}, bf16[512,256]{1,0:T(8,128)(2,1)S(1)}, u32[]{:S(2)}, u32[]{:S(2)}) collective-permute-start(bf16[512,256]{1,0:T(8,128)(2,1)S(1)} %get-tuple-element.39), channel_id=1, source_target_pairs={{0,15},{1,2},{2,1},{3,4},{4,3},{5,6},{6,5},{7,8},{8,7},{9,10},{10,... | collective-permute-start | bytes 786440 | tf_op jit(solution)/shard_map/ppermute | solution.py:517
  23.4 17.9 %collective-permute-start.4 = (bf16[2,36,3072]{2,1,0:T(8,128)(2,1)S(1)}, bf16[2,36,3072]{2,1,0:T(8,128)(2,1)S(1)}, u32[]{:S(2)}, u32[]{:S(2)}) collective-permute-start(bf16[2,36,3072]{2,1,0:T(8,128)(2,1)S(1)} %pad_maximum_fusion.1.here_ref), channel_id=1, source_target_pairs={{0,64},{16,80},{32,96},{48,112},{64,0},{80,16},{96,32},{112,48},{1... | collective-permute-start | bytes 1327112 | tf_op jit(solution)/shard_map/ppermute | solution.py:509
  26.1 14.9 %copy-start = (bf16[64,3072]{1,0:T(8,128)(2,1)S(1)}, bf16[64,3072]{1,0:T(8,128)(2,1)}, u32[]{:S(2)}) copy-start(bf16[64,3072]{1,0:T(8,128)(2,1)} %embed_ref.1) | copy-start | bytes 1179652
  26.2 14.9 %copy-start.1 = (f32[3072]{0:T(1024)S(1)}, f32[3072]{0:T(1024)}, u32[]{:S(2)}) copy-start(f32[3072]{0:T(1024)} %param.18) | copy-start | bytes 36868
  33.1 14.9 %collective-permute-start.5 = (bf16[528,256]{1,0:T(8,128)(2,1)}, bf16[528,256]{1,0:T(8,128)(2,1)S(1)}, u32[]{:S(2)}, u32[]{:S(2)}) collective-permute-start(bf16[528,256]{1,0:T(8,128)(2,1)} %get-tuple-element.51), channel_id=1, source_target_pairs={{0,1},{1,0},{2,3},{3,2},{4,5},{5,4},{6,7},{7,6},{8,9},{9,8},{10,11... | collective-permute-start | bytes 811016 | tf_op jit(solution)/shard_map/ppermute | solution.py:518
  34.1 13.9 %collective-permute-start.6 = (bf16[528,256]{1,0:T(8,128)(2,1)S(1)}, bf16[528,256]{1,0:T(8,128)(2,1)}, u32[]{:S(2)}, u32[]{:S(2)}) collective-permute-start(bf16[528,256]{1,0:T(8,128)(2,1)S(1)} %get-tuple-element.52), channel_id=1, source_target_pairs={{0,15},{1,2},{2,1},{3,4},{4,3},{5,6},{6,5},{7,8},{8,7},{9,10},{10,... | collective-permute-start | bytes 811016 | tf_op jit(solution)/shard_map/ppermute | solution.py:517
  34.4 13.7 %all-to-all-start.1 = ((f32[16,1,128]{2,1,0:T(1,128)}), f32[16,1,128]{2,1,0:T(1,128)S(1)}, u32[]{:S(2)}, u32[]{:S(2)}) async-start(f32[16,1,128]{2,1,0:T(1,128)} %get-tuple-element.41), calls=%async_computation.1 | async-start | bytes 16384 | tf_op jit(solution)/shard_map/all_to_all | solution.py:522
  48.0 21.2 %copy-start.2 = (bf16[3,3,3,256,16]{3,4,2,1,0:T(8,128)(2,1)S(1)}, bf16[3,3,3,256,16]{3,4,2,1,0:T(8,128)(2,1)}, u32[]{:S(2)}) copy-start(bf16[3,3,3,256,16]{3,4,2,1,0:T(8,128)(2,1)} %param.14) | copy-start | bytes 663556
  54.8 14.4 %collective-permute-start.7 = (bf16[512,256]{1,0:T(8,128)(2,1)S(1)}, bf16[512,256]{1,0:T(8,128)(2,1)S(1)}, u32[]{:S(2)}, u32[]{:S(2)}) collective-permute-start(bf16[512,256]{1,0:T(8,128)(2,1)S(1)} %get-tuple-element.55), channel_id=1, source_target_pairs={{0,1},{1,0},{2,3},{3,2},{4,5},{5,4},{6,7},{7,6},{8,9},{9,8},{10,11... | collective-permute-start | bytes 786440 | tf_op jit(solution)/shard_map/ppermute | solution.py:518
  55.6 13.6 %collective-permute-start.8 = (bf16[512,256]{1,0:T(8,128)(2,1)S(1)}, bf16[512,256]{1,0:T(8,128)(2,1)S(1)}, u32[]{:S(2)}, u32[]{:S(2)}) collective-permute-start(bf16[512,256]{1,0:T(8,128)(2,1)S(1)} %get-tuple-element.56), channel_id=1, source_target_pairs={{0,15},{1,2},{2,1},{3,4},{4,3},{5,6},{6,5},{7,8},{8,7},{9,10},{10,... | collective-permute-start | bytes 786440 | tf_op jit(solution)/shard_map/ppermute | solution.py:517
  55.9 13.4 %collective-permute-start.9 = (bf16[144,128]{1,0:T(8,128)(2,1)S(1)}, bf16[144,128]{1,0:T(8,128)(2,1)S(1)}, u32[]{:S(2)}, u32[]{:S(2)}) collective-permute-start(bf16[144,128]{1,0:T(8,128)(2,1)S(1)} %get-tuple-element.58), channel_id=1, source_target_pairs={{0,16},{16,0},{32,48},{48,32},{64,80},{80,64},{96,112},{112,96},{1... | collective-permute-start | bytes 110600 | tf_op jit(solution)/shard_map/ppermute | solution.py:509
  73.1 5.5 %collective-permute-start.10 = (bf16[432,128]{1,0:T(8,128)(2,1)S(1)}, bf16[432,128]{1,0:T(8,128)(2,1)S(1)}, u32[]{:S(2)}, u32[]{:S(2)}) collective-permute-start(bf16[432,128]{1,0:T(8,128)(2,1)S(1)} %get-tuple-element.59), channel_id=1, source_target_pairs={{0,8},{1,9},{2,10},{3,11},{4,12},{5,13},{6,14},{7,15},{8,0},{9,1},... | collective-permute-start | bytes 331784 | tf_op jit(solution)/shard_map/ppermute | solution.py:509
  78.6 7.0 %collective-permute-start.12 = (bf16[2,432,128]{2,1,0:T(8,128)(2,1)S(1)}, bf16[2,432,128]{2,1,0:T(8,128)(2,1)S(1)}, u32[]{:S(2)}, u32[]{:S(2)}) collective-permute-start(bf16[2,432,128]{2,1,0:T(8,128)(2,1)S(1)} %get-tuple-element.67), channel_id=1, source_target_pairs={{0,4},{1,5},{2,6},{3,7},{4,0},{5,1},{6,2},{7,3},{8,12},{9,13},{10,... | collective-permute-start | bytes 663560 | tf_op jit(solution)/shard_map/ppermute | solution.py:509
  79.6 9.2 %collective-permute-start.11 = (bf16[2,432,128]{2,1,0:T(8,128)(2,1)S(1)}, bf16[2,432,128]{2,1,0:T(8,128)(2,1)S(1)}, u32[]{:S(2)}, u32[]{:S(2)}) collective-permute-start(bf16[2,432,128]{2,1,0:T(8,128)(2,1)S(1)} %get-tuple-element.67), channel_id=1, source_target_pairs={{0,2},{1,3},{2,0},{3,1},{4,6},{5,7},{6,4},{7,5},{8,10},{9,11},{10,... | collective-permute-start | bytes 663560 | tf_op jit(solution)/shard_map/ppermute | solution.py:509
  80.1 11.6 %collective-permute-start.13 = (bf16[2,432,128]{2,1,0:T(8,128)(2,1)S(1)}, bf16[2,432,128]{2,1,0:T(8,128)(2,1)S(1)}, u32[]{:S(2)}, u32[]{:S(2)}) collective-permute-start(bf16[2,432,128]{2,1,0:T(8,128)(2,1)S(1)} %get-tuple-element.67), channel_id=1, source_target_pairs={{0,6},{1,7},{2,4},{3,5},{4,2},{5,3},{6,0},{7,1},{8,14},{9,15},{10,... | collective-permute-start | bytes 663560 | tf_op jit(solution)/shard_map/ppermute | solution.py:509
  91.9 3.1 %collective-permute-start.14 = (bf16[4,2,432,128]{3,2,1,0:T(8,128)(2,1)S(1)}, bf16[4,2,432,128]{3,2,1,0:T(8,128)(2,1)S(1)}, u32[]{:S(2)}, u32[]{:S(2)}) collective-permute-start(bf16[4,2,432,128]{3,2,1,0:T(8,128)(2,1)S(1)} %pad_maximum_fusion.near_ref), channel_id=1, source_target_pairs={{0,1},{1,0},{2,3},{3,2},{4,5},{5,4},{6,7},{7,6},{8,9},{9,8},{10,11... | collective-permute-start | bytes 2654216 | tf_op jit(solution)/shard_map/ppermute | solution.py:509

commit v4 on v3

--- a/solution.py
+++ b/solution.py
@@ -282,7 +282,7 @@
 
 def third_kernel(
     place_ref, stats_ref, rows_ref, near_ref, far_ref, norms_ref, weight_ref, embed_ref, bias_ref,
-    own_ref, other_ref, patches_ref, parcel_ref, window, weight,
+    own_ref, other_ref, patches_ref, parcel_ref, window, weight, folds,
 ):
     n = FRAMES * HALF
     for p in range(3):
@@ -322,8 +322,17 @@
         lines = jnp.where(line == 2 * side, high, lines)
         lines = jnp.where(line == 2 * side + 1, each - high, lines)
     parcel_ref[128:144] = lines.astype(BF16)
-    parcel_ref[144:288] = own_ref[...]
-    parcel_ref[288:432] = other_ref[...]
+    own, other = own_ref[...].astype(F32), other_ref[...].astype(F32)
+    lane = iota((4 * QROWS, 128), 1)
+    parcel_ref[144:288] = jnp.where(lane < 64, own, pltpu.roll(other, 64, 1)).astype(BF16)
+    folds[0 : 4 * QROWS] = own
+    folds[4 * QROWS : 8 * QROWS] = other
+    folds[8 * QROWS :] = jnp.zeros((8, 128), F32)
+    lane = iota((40, 128), 1)
+    ends = jnp.zeros((40, 128), F32)
+    for i in range(8):
+        ends = jnp.where((lane >> 3) == i, pltpu.roll(folds[i * QROWS : i * QROWS + 40], (8 * i + 64) % 128, 1), ends)
+    parcel_ref[288:336] = jnp.concatenate([ends, jnp.zeros((8, 128), F32)], axis=0).astype(BF16)
 
 
 def latent_kernel(patches_ref, latent_ref):
@@ -396,12 +405,17 @@
 
 def sort_kernel(place_ref, clip_ref, near_ref, far_ref, asks_ref, keys_ref, values_ref, loose, wide):
     seq, clip = place_ref[0], clip_ref[0]
+    spot = iota((40, 128), 1)
     for j in range(SEQ):
         source = (near_ref, far_ref)[j & 1]
-        loose[j] = source[(j >> 1) & 3, j >> 3, 144:432].astype(F32)
+        loose[j] = source[(j >> 1) & 3, j >> 3, 144:336].astype(F32)
         for k in range(CLIPS):
             at = ((clip ^ (2 * (k & 3) + (k >> 2))) * SEQ + (seq ^ j)) * QROWS
-            wide[pl.ds(at, QROWS)] = loose[j, k * QROWS : (k + 1) * QROWS]
+            block = loose[j, (k & 3) * QROWS : (k & 3) * QROWS + 40]
+            block = pltpu.roll(block, 64, 1) if k >> 2 else block
+            ends = pltpu.roll(loose[j, 144:184], (64 - 8 * k) % 128, 1)
+            block = jnp.where(spot < 64, block, jnp.where(spot < 69, ends, 0.0))
+            wide[pl.ds(at, QROWS)] = block[:QROWS]
     lane = iota((WIDE, 128), 1)
     rows = wide[0:WIDE]
     asks_ref[:, 0:128] = rows.astype(BF16)
@@ -616,9 +630,9 @@
     stats2 = exchange(stats2)
     patches, parcel = call(
         third_kernel,
-        [shape(FRAMES * HALF, 4 * LAT, dtype=F32), shape(432, 128)],
+        [shape(FRAMES * HALF, 4 * LAT, dtype=F32), shape(336, 128)],
         [SMEM] + [VMEM] * 10,
-        [WINDOW, pltpu.VMEM((48, 4 * LAT, C), BF16)],
+        [WINDOW, pltpu.VMEM((48, 4 * LAT, C), BF16), pltpu.VMEM((8 * QROWS + 8, 128), F32)],
         CONV_FLOPS // 2,
         4 << 20,
     )(
@@ -631,7 +645,7 @@
         sort_kernel,
         [shape(WIDE, 256), shape(WIDE, 512), shape(WIDE, 512)],
         [SMEM] * 2 + [VMEM] * 2,
-        [pltpu.VMEM((SEQ, 8 * QROWS, 128), F32), pltpu.VMEM((3 * WIDE, 128), F32)],
+        [pltpu.VMEM((SEQ, 192, 128), F32), pltpu.VMEM((3 * WIDE, 128), F32)],
     )(place, clip, near, far)
     frame_heads = call(
         attend_kernel,

time: 102 us -> 98.8 us (0.969)
  waiting for transfers between devices: 26.9 us -> 23.1 us
    ppermute x9, waiting for transfers between devices: 15.9 us -> 12.2 us  [swap(): return lax.ppermute(values, axis, [(i, i ^ bits) for i in range(count)])]
  transfers between devices with their start and end apart: 17 -> 17, of which waited for: 7 -> 7; matrix products, arithmetic and copies ran while one was open for 1% -> 1% of each run, Pallas kernels for 11% -> 12%
where the time goes in v4:
time: 98.8 us; the launch traced here: 98.5 us
  starting transfers between devices  31.5 us (32%)
  Pallas kernels  28.7 us (29%)
  waiting for transfers between devices  23.1 us (23%)
  blocking collectives  13.4 us (14%)
  other arithmetic  1.11 us (1%)
    pallas_call x9, Pallas kernels, run(): kernel(*(pltpu.with_memory_space_constraint(x, pltpu.HBM) if spec is HBM...  28.7 us
    all_to_all x2, starting transfers between devices, exchange(): return lax.all_to_all(stats, 'seq', 0, 0, tiled=True)  15.2 us
    all_to_all x1, blocking collectives, exchange(): return lax.all_to_all(stats, 'seq', 0, 0, tiled=True)  13.4 us
    ppermute x9, starting transfers between devices, swap(): return lax.ppermute(values, axis, [(i, i ^ bits) for i in range(count)])  12.2 us
    ppermute x9, waiting for transfers between devices, swap(): return lax.ppermute(values, axis, [(i, i ^ bits) for i in range(count)])  12.2 us
    all_to_all x2, waiting for transfers between devices, exchange(): return lax.all_to_all(stats, 'seq', 0, 0, tiled=True)  10.9 us
    ppermute x3, starting transfers between devices, neighbours(): far = lax.ppermute(far, 'seq', NEXT_PAIRS)  2.14 us
  transfers between devices with their start and end apart: 17, of which 7 were waited for; matrix products, arithmetic and copies ran while one was open for 1% of the time, Pallas kernels for 12%

profile of v4, /device:TPU:1, one launch (start us, length us, event | category | flops | bytes accessed | tf_op | source)
XLA Modules:
  0.0 98.5 jit_solution(7135973680656556626)
XLA Ops:
  0.6 2.2 %collective-permute-start.1 = (bf16[36,3072]{1,0:T(8,128)(2,1)}, bf16[36,3072]{1,0:T(8,128)(2,1)S(1)}, u32[]{:S(2)}, u32[]{:S(2)}) collective-permute-start(bf16[36,3072]{1,0:T(8,128)(2,1)} %param.21), channel_id=1, source_target_pairs={{0,32},{16,48},{32,0},{48,16},{64,96},{80,112},{96,64},{112,80},{1... | collective-permute-start | bytes 663560 | tf_op jit(solution)/shard_map/ppermute | solution.py:523
  2.8 2.4 %split_kernel.1 = (bf16[1024,256]{1,0:T(8,128)(2,1)S(1)}, bf16[512,256]{1,0:T(8,128)(2,1)S(1)}, bf16[512,256]{1,0:T(8,128)(2,1)S(1)}, f32[16,1,128]{2,1,0:T(1,12...) custom-call(s32[1]{0:T(128)} %bitcast.place_ref, bf16[16,2,32,256]{3,2,1,0:T(8,128)(2,1)} %bitcast.26, ...), custom_call_target="tpu_custom_call" | custom-call | bytes 1048576 | tf_op jit(solution)/shard_map/split_kernel/pallas_call | solution.py:515
  5.2 1.7 %collective-permute-start = (f32[2,3072]{1,0:T(2,128)S(1)}, f32[2,3072]{1,0:T(2,128)S(1)}, u32[]{:S(2)}, u32[]{:S(2)}) collective-permute-start(f32[2,3072]{1,0:T(2,128)S(1)} %get-tuple-element.35.own_mods_ref), channel_id=1, source_target_pairs={{0,16},{16,0},{32,48},{48,32},{64,80},{80,64},{96,112},{112,96},{1... | collective-permute-start | bytes 73736 | tf_op jit(solution)/shard_map/ppermute | solution.py:523
  6.9 8.6 %all-to-all-start = ((f32[16,1,128]{2,1,0:T(1,128)}), f32[16,1,128]{2,1,0:T(1,128)S(1)}, u32[]{:S(2)}, u32[]{:S(2)}) async-start(f32[16,1,128]{2,1,0:T(1,128)} %get-tuple-element.34), calls=%async_computation | async-start | bytes 16384 | tf_op jit(solution)/shard_map/all_to_all | solution.py:536
  15.7 1.6 %collective-permute-start.3 = (bf16[512,256]{1,0:T(8,128)(2,1)S(1)}, bf16[512,256]{1,0:T(8,128)(2,1)S(1)}, u32[]{:S(2)}, u32[]{:S(2)}) collective-permute-start(bf16[512,256]{1,0:T(8,128)(2,1)S(1)} %get-tuple-element.39), channel_id=1, source_target_pairs={{0,15},{1,2},{2,1},{3,4},{4,3},{5,6},{6,5},{7,8},{8,7},{9,10},{10,... | collective-permute-start | bytes 786440 | tf_op jit(solution)/shard_map/ppermute | solution.py:531
  17.3 5.1 %all-to-all-done.stats_ref = f32[16,1,128]{2,1,0:T(1,128)S(1)} async-done(((f32[16,1,128]{2,1,0:T(1,128)}), f32[16,1,128]{2,1,0:T(1,128)S(1)}, u32[]{:S(2)}, u32[]{:S(2)}) %all-to-all-start) | async-done | bytes 8224 | tf_op jit(solution)/shard_map/all_to_all | solution.py:536
  23.4 2.7 %collective-permute-start.4 = (bf16[2,36,3072]{2,1,0:T(8,128)(2,1)S(1)}, bf16[2,36,3072]{2,1,0:T(8,128)(2,1)S(1)}, u32[]{:S(2)}, u32[]{:S(2)}) collective-permute-start(bf16[2,36,3072]{2,1,0:T(8,128)(2,1)S(1)} %pad_maximum_fusion.1.here_ref), channel_id=1, source_target_pairs={{0,64},{16,80},{32,96},{48,112},{64,0},{80,16},{96,32},{112,48},{1... | collective-permute-start | bytes 1327112 | tf_op jit(solution)/shard_map/ppermute | solution.py:523
  26.2 6.9 %first_kernel.1 = (bf16[1024,256]{1,0:T(8,128)(2,1)}, f32[8,256]{1,0:T(8,128)S(1)}, bf16[528,256]{1,0:T(8,128)(2,1)}, bf16[528,256]{1,0:T(8,128)(2,1)S(1)}, f32[16,1,128]{2,1,0:T(1,128)}) custom-call(s32[1]{0:T(128)} %bitcast.place_ref, f32[16,1,128]{2,1,0:T(1,128)S(1)} %all-to-all-done.stats_ref, bf16[1024,256]{1,0:T(8,128)(2,1)S(1)} %get-tuple-element.37.rows_ref.feat_ref, ...), custom_call_target="tpu_custom_call" | custom-call | flops 3623878656 | bytes 5242880 | tf_op jit(solution)/shard_map/first_kernel/pallas_call | solution.py:515
  33.1 1.0 %collective-permute-start.5 = (bf16[528,256]{1,0:T(8,128)(2,1)}, bf16[528,256]{1,0:T(8,128)(2,1)S(1)}, u32[]{:S(2)}, u32[]{:S(2)}) collective-permute-start(bf16[528,256]{1,0:T(8,128)(2,1)} %get-tuple-element.51), channel_id=1, source_target_pairs={{0,1},{1,0},{2,3},{3,2},{4,5},{5,4},{6,7},{7,6},{8,9},{9,8},{10,11... | collective-permute-start | bytes 811016 | tf_op jit(solution)/shard_map/ppermute | solution.py:532
  34.4 6.7 %all-to-all-start.1 = ((f32[16,1,128]{2,1,0:T(1,128)}), f32[16,1,128]{2,1,0:T(1,128)S(1)}, u32[]{:S(2)}, u32[]{:S(2)}) async-start(f32[16,1,128]{2,1,0:T(1,128)} %get-tuple-element.41), calls=%async_computation.1 | async-start | bytes 16384 | tf_op jit(solution)/shard_map/all_to_all | solution.py:536
  42.2 5.8 %all-to-all-done.1.stats_ref = f32[16,1,128]{2,1,0:T(1,128)S(1)} async-done(((f32[16,1,128]{2,1,0:T(1,128)}), f32[16,1,128]{2,1,0:T(1,128)S(1)}, u32[]{:S(2)}, u32[]{:S(2)}) %all-to-all-start.1) | async-done | bytes 8224 | tf_op jit(solution)/shard_map/all_to_all | solution.py:536
  48.0 6.8 %second_kernel.1 = (bf16[1024,256]{1,0:T(8,128)(2,1)S(1)}, bf16[512,256]{1,0:T(8,128)(2,1)S(1)}, bf16[512,256]{1,0:T(8,128)(2,1)S(1)}, f32[16,1,128]{2,1,0:T(1,128)S(1)}) custom-call(s32[1]{0:T(128)} %bitcast.place_ref, f32[16,1,128]{2,1,0:T(1,128)S(1)} %all-to-all-done.1.stats_ref, bf16[1024,256]{1,0:T(8,128)(2,1)} %get-tuple-element.49.hidden_hbm, ...), custom_call_target="tpu_custom_call" | custom-call | flops 3623878656 | bytes 6291456 | tf_op jit(solution)/shard_map/second_kernel/pallas_call | solution.py:515
  55.9 13.4 %all_to_all.15.stats_ref = f32[16,1,128]{2,1,0:T(1,128)S(1)} all-to-all(f32[16,1,128]{2,1,0:T(1,128)S(1)} %get-tuple-element.53), channel_id=1, replica_groups=mesh['clip'=8,'seq'=16] {'seq'}, dimensions={0} | all-to-all | bytes 16384 | tf_op jit(solution)/shard_map/all_to_all | solution.py:536
  69.2 3.8 %third_kernel.1 = (f32[256,64]{1,0:T(8,128)S(1)}, bf16[336,128]{1,0:T(8,128)(2,1)S(1)}) custom-call(s32[1]{0:T(128)} %bitcast.place_ref, f32[16,1,128]{2,1,0:T(1,128)S(1)} %all_to_all.15.stats_ref, bf16[1024,256]{1,0:T(8,128)(2,1)S(1)} %get-tuple-element.54.rows_ref, bf16[512,256]{1,0:T(8,128)(2,1)S(1)} %collective-permute-done.7.near_ref, ...), custom_call_target="tpu_custom_call" | custom-call | flops 1811939328 | bytes 4194304 | tf_op jit(solution)/shard_map/third_kernel/pallas_call | solution.py:515
  73.4 1.1 %latent_kernel.1 = f32[16,2,16,32]{3,2,1,0:T(8,128)} custom-call(f32[256,64]{1,0:T(8,128)S(1)} %get-tuple-element.60.patches_ref), custom_call_target="tpu_custom_call" | custom-call | tf_op jit(solution)/shard_map/latent_kernel/pallas_call | solution.py:515
  74.5 3.5 %collective-permute-done.10 = bf16[336,128]{1,0:T(8,128)(2,1)S(1)} collective-permute-done((bf16[336,128]{1,0:T(8,128)(2,1)S(1)}, bf16[336,128]{1,0:T(8,128)(2,1)S(1)}, u32[]{:S(2)}, u32[]{:S(2)}) %collective-permute-start.10) | collective-permute-done | bytes 86048 | tf_op jit(solution)/shard_map/ppermute | solution.py:523
  79.6 1.8 %collective-permute-start.13 = (bf16[2,336,128]{2,1,0:T(8,128)(2,1)S(1)}, bf16[2,336,128]{2,1,0:T(8,128)(2,1)S(1)}, u32[]{:S(2)}, u32[]{:S(2)}) collective-permute-start(bf16[2,336,128]{2,1,0:T(8,128)(2,1)S(1)} %get-tuple-element.67), channel_id=1, source_target_pairs={{0,6},{1,7},{2,4},{3,5},{4,2},{5,3},{6,0},{7,1},{8,14},{9,15},{10,... | collective-permute-start | bytes 516104 | tf_op jit(solution)/shard_map/ppermute | solution.py:523
  81.3 2.6 %collective-permute-done.12 = bf16[2,336,128]{2,1,0:T(8,128)(2,1)S(1)} collective-permute-done((bf16[2,336,128]{2,1,0:T(8,128)(2,1)S(1)}, bf16[2,336,128]{2,1,0:T(8,128)(2,1)S(1)}, u32[]{:S(2)}, u32[]{:S(2)}) %collective-permute-start.12) | collective-permute-done | bytes 172064 | tf_op jit(solution)/shard_map/ppermute | solution.py:523
  83.9 1.9 %collective-permute-done.11 = bf16[2,336,128]{2,1,0:T(8,128)(2,1)S(1)} collective-permute-done((bf16[2,336,128]{2,1,0:T(8,128)(2,1)S(1)}, bf16[2,336,128]{2,1,0:T(8,128)(2,1)S(1)}, u32[]{:S(2)}, u32[]{:S(2)}) %collective-permute-start.11) | collective-permute-done | bytes 172064 | tf_op jit(solution)/shard_map/ppermute | solution.py:523
  85.8 2.4 %collective-permute-done.13 = bf16[2,336,128]{2,1,0:T(8,128)(2,1)S(1)} collective-permute-done((bf16[2,336,128]{2,1,0:T(8,128)(2,1)S(1)}, bf16[2,336,128]{2,1,0:T(8,128)(2,1)S(1)}, u32[]{:S(2)}, u32[]{:S(2)}) %collective-permute-start.13) | collective-permute-done | bytes 172064 | tf_op jit(solution)/shard_map/ppermute | solution.py:523
  88.3 1.9 %collective-permute-start.14 = (bf16[4,2,336,128]{3,2,1,0:T(8,128)(2,1)S(1)}, bf16[4,2,336,128]{3,2,1,0:T(8,128)(2,1)S(1)}, u32[]{:S(2)}, u32[]{:S(2)}) collective-permute-start(bf16[4,2,336,128]{3,2,1,0:T(8,128)(2,1)S(1)} %pad_maximum_fusion.near_ref), channel_id=1, source_target_pairs={{0,1},{1,0},{2,3},{3,2},{4,5},{5,4},{6,7},{7,6},{8,9},{9,8},{10,11... | collective-permute-start | bytes 2064392 | tf_op jit(solution)/shard_map/ppermute | solution.py:523
  90.2 1.8 %collective-permute-done.14.far_ref = bf16[4,2,336,128]{3,2,1,0:T(8,128)(2,1)S(1)} collective-permute-done((bf16[4,2,336,128]{3,2,1,0:T(8,128)(2,1)S(1)}, bf16[4,2,336,128]{3,2,1,0:T(8,128)(2,1)S(1)}, u32[]{:S(2)}, u32[]{:S(2)}) %collective-permute-start.14) | collective-permute-done | bytes 688160 | tf_op jit(solution)/shard_map/ppermute | solution.py:523
  92.0 1.9 %sort_kernel.1 = (bf16[1536,256]{1,0:T(8,128)(2,1)S(1)}, bf16[1536,512]{1,0:T(8,128)(2,1)S(1)}, bf16[1536,512]{1,0:T(8,128)(2,1)S(1)}) custom-call(s32[1]{0:T(128)} %bitcast.place_ref, s32[1]{0:T(128)} %bitcast.17.clip_ref, bf16[4,2,336,128]{3,2,1,0:T(8,128)(2,1)S(1)} %pad_maximum_fusion.near_ref, bf16[4,2,336,128]{3,2,1,0:T(8,128)(2,1)S(1)} %collective-permute-done.14.far_ref), custom_call_target="tpu_custom_call" | custom-call | tf_op jit(solution)/shard_map/sort_kernel/pallas_call | solution.py:515
  93.9 4.6 %attend_kernel.1 = bf16[256,1536]{1,0:T(8,128)(2,1)} custom-call(s32[1]{0:T(128)} %bitcast.place_ref, bf16[4,2,336,128]{3,2,1,0:T(8,128)(2,1)S(1)} %pad_maximum_fusion.near_ref, bf16[4,2,336,128]{3,2,1,0:T(8,128)(2,1)S(1)} %collective-permute-done.14.far_ref, bf16[1536,256]{1,0:T(8,128)(2,1)S(1)} %get-tuple-element.63.asks_ref, ...), custom_call_target="tpu_custom_call" | custom-call | tf_op jit(solution)/shard_map/attend_kernel/pallas_call | solution.py:515
  (29 shorter events, 5.7 us)
Async XLA Ops:
  0.6 21.8 %collective-permute-start.1 = (bf16[36,3072]{1,0:T(8,128)(2,1)}, bf16[36,3072]{1,0:T(8,128)(2,1)S(1)}, u32[]{:S(2)}, u32[]{:S(2)}) collective-permute-start(bf16[36,3072]{1,0:T(8,128)(2,1)} %param.21), channel_id=1, source_target_pairs={{0,32},{16,48},{32,0},{48,16},{64,96},{80,112},{96,64},{112,80},{1... | collective-permute-start | bytes 663560 | tf_op jit(solution)/shard_map/ppermute | solution.py:523
  5.2 17.2 %collective-permute-start = (f32[2,3072]{1,0:T(2,128)S(1)}, f32[2,3072]{1,0:T(2,128)S(1)}, u32[]{:S(2)}, u32[]{:S(2)}) collective-permute-start(f32[2,3072]{1,0:T(2,128)S(1)} %get-tuple-element.35.own_mods_ref), channel_id=1, source_target_pairs={{0,16},{16,0},{32,48},{48,32},{64,80},{80,64},{96,112},{112,96},{1... | collective-permute-start | bytes 73736 | tf_op jit(solution)/shard_map/ppermute | solution.py:523
  6.9 15.5 %all-to-all-start = ((f32[16,1,128]{2,1,0:T(1,128)}), f32[16,1,128]{2,1,0:T(1,128)S(1)}, u32[]{:S(2)}, u32[]{:S(2)}) async-start(f32[16,1,128]{2,1,0:T(1,128)} %get-tuple-element.34), calls=%async_computation | async-start | bytes 16384 | tf_op jit(solution)/shard_map/all_to_all | solution.py:536
  15.5 10.6 %collective-permute-start.2 = (bf16[512,256]{1,0:T(8,128)(2,1)S(1)}, bf16[512,256]{1,0:T(8,128)(2,1)S(1)}, u32[]{:S(2)}, u32[]{:S(2)}) collective-permute-start(bf16[512,256]{1,0:T(8,128)(2,1)S(1)} %get-tuple-element.38), channel_id=1, source_target_pairs={{0,1},{1,0},{2,3},{3,2},{4,5},{5,4},{6,7},{7,6},{8,9},{9,8},{10,11... | collective-permute-start | bytes 786440 | tf_op jit(solution)/shard_map/ppermute | solution.py:532
  15.7 10.5 %collective-permute-start.3 = (bf16[512,256]{1,0:T(8,128)(2,1)S(1)}, bf16[512,256]{1,0:T(8,128)(2,1)S(1)}, u32[]{:S(2)}, u32[]{:S(2)}) collective-permute-start(bf16[512,256]{1,0:T(8,128)(2,1)S(1)} %get-tuple-element.39), channel_id=1, source_target_pairs={{0,15},{1,2},{2,1},{3,4},{4,3},{5,6},{6,5},{7,8},{8,7},{9,10},{10,... | collective-permute-start | bytes 786440 | tf_op jit(solution)/shard_map/ppermute | solution.py:531
  23.4 17.9 %collective-permute-start.4 = (bf16[2,36,3072]{2,1,0:T(8,128)(2,1)S(1)}, bf16[2,36,3072]{2,1,0:T(8,128)(2,1)S(1)}, u32[]{:S(2)}, u32[]{:S(2)}) collective-permute-start(bf16[2,36,3072]{2,1,0:T(8,128)(2,1)S(1)} %pad_maximum_fusion.1.here_ref), channel_id=1, source_target_pairs={{0,64},{16,80},{32,96},{48,112},{64,0},{80,16},{96,32},{112,48},{1... | collective-permute-start | bytes 1327112 | tf_op jit(solution)/shard_map/ppermute | solution.py:523
  26.1 14.9 %copy-start = (bf16[64,3072]{1,0:T(8,128)(2,1)S(1)}, bf16[64,3072]{1,0:T(8,128)(2,1)}, u32[]{:S(2)}) copy-start(bf16[64,3072]{1,0:T(8,128)(2,1)} %embed_ref.1) | copy-start | bytes 1179652
  26.2 14.9 %copy-start.1 = (f32[3072]{0:T(1024)S(1)}, f32[3072]{0:T(1024)}, u32[]{:S(2)}) copy-start(f32[3072]{0:T(1024)} %param.18) | copy-start | bytes 36868
  33.1 14.9 %collective-permute-start.5 = (bf16[528,256]{1,0:T(8,128)(2,1)}, bf16[528,256]{1,0:T(8,128)(2,1)S(1)}, u32[]{:S(2)}, u32[]{:S(2)}) collective-permute-start(bf16[528,256]{1,0:T(8,128)(2,1)} %get-tuple-element.51), channel_id=1, source_target_pairs={{0,1},{1,0},{2,3},{3,2},{4,5},{5,4},{6,7},{7,6},{8,9},{9,8},{10,11... | collective-permute-start | bytes 811016 | tf_op jit(solution)/shard_map/ppermute | solution.py:532
  34.1 13.9 %collective-permute-start.6 = (bf16[528,256]{1,0:T(8,128)(2,1)S(1)}, bf16[528,256]{1,0:T(8,128)(2,1)}, u32[]{:S(2)}, u32[]{:S(2)}) collective-permute-start(bf16[528,256]{1,0:T(8,128)(2,1)S(1)} %get-tuple-element.52), channel_id=1, source_target_pairs={{0,15},{1,2},{2,1},{3,4},{4,3},{5,6},{6,5},{7,8},{8,7},{9,10},{10,... | collective-permute-start | bytes 811016 | tf_op jit(solution)/shard_map/ppermute | solution.py:531
  34.4 13.7 %all-to-all-start.1 = ((f32[16,1,128]{2,1,0:T(1,128)}), f32[16,1,128]{2,1,0:T(1,128)S(1)}, u32[]{:S(2)}, u32[]{:S(2)}) async-start(f32[16,1,128]{2,1,0:T(1,128)} %get-tuple-element.41), calls=%async_computation.1 | async-start | bytes 16384 | tf_op jit(solution)/shard_map/all_to_all | solution.py:536
  48.0 21.2 %copy-start.2 = (bf16[3,3,3,256,16]{3,4,2,1,0:T(8,128)(2,1)S(1)}, bf16[3,3,3,256,16]{3,4,2,1,0:T(8,128)(2,1)}, u32[]{:S(2)}) copy-start(bf16[3,3,3,256,16]{3,4,2,1,0:T(8,128)(2,1)} %param.14) | copy-start | bytes 663556
  54.8 14.4 %collective-permute-start.7 = (bf16[512,256]{1,0:T(8,128)(2,1)S(1)}, bf16[512,256]{1,0:T(8,128)(2,1)S(1)}, u32[]{:S(2)}, u32[]{:S(2)}) collective-permute-start(bf16[512,256]{1,0:T(8,128)(2,1)S(1)} %get-tuple-element.55), channel_id=1, source_target_pairs={{0,1},{1,0},{2,3},{3,2},{4,5},{5,4},{6,7},{7,6},{8,9},{9,8},{10,11... | collective-permute-start | bytes 786440 | tf_op jit(solution)/shard_map/ppermute | solution.py:532
  55.6 13.6 %collective-permute-start.8 = (bf16[512,256]{1,0:T(8,128)(2,1)S(1)}, bf16[512,256]{1,0:T(8,128)(2,1)S(1)}, u32[]{:S(2)}, u32[]{:S(2)}) collective-permute-start(bf16[512,256]{1,0:T(8,128)(2,1)S(1)} %get-tuple-element.56), channel_id=1, source_target_pairs={{0,15},{1,2},{2,1},{3,4},{4,3},{5,6},{6,5},{7,8},{8,7},{9,10},{10,... | collective-permute-start | bytes 786440 | tf_op jit(solution)/shard_map/ppermute | solution.py:531
  55.9 13.4 %collective-permute-start.9 = (bf16[144,128]{1,0:T(8,128)(2,1)S(1)}, bf16[144,128]{1,0:T(8,128)(2,1)S(1)}, u32[]{:S(2)}, u32[]{:S(2)}) collective-permute-start(bf16[144,128]{1,0:T(8,128)(2,1)S(1)} %get-tuple-element.58), channel_id=1, source_target_pairs={{0,16},{16,0},{32,48},{48,32},{64,80},{80,64},{96,112},{112,96},{1... | collective-permute-start | bytes 110600 | tf_op jit(solution)/shard_map/ppermute | solution.py:523
  73.1 4.9 %collective-permute-start.10 = (bf16[336,128]{1,0:T(8,128)(2,1)S(1)}, bf16[336,128]{1,0:T(8,128)(2,1)S(1)}, u32[]{:S(2)}, u32[]{:S(2)}) collective-permute-start(bf16[336,128]{1,0:T(8,128)(2,1)S(1)} %get-tuple-element.59), channel_id=1, source_target_pairs={{0,8},{1,9},{2,10},{3,11},{4,12},{5,13},{6,14},{7,15},{8,0},{9,1},... | collective-permute-start | bytes 258056 | tf_op jit(solution)/shard_map/ppermute | solution.py:523
  78.0 5.9 %collective-permute-start.12 = (bf16[2,336,128]{2,1,0:T(8,128)(2,1)S(1)}, bf16[2,336,128]{2,1,0:T(8,128)(2,1)S(1)}, u32[]{:S(2)}, u32[]{:S(2)}) collective-permute-start(bf16[2,336,128]{2,1,0:T(8,128)(2,1)S(1)} %get-tuple-element.67), channel_id=1, source_target_pairs={{0,4},{1,5},{2,6},{3,7},{4,0},{5,1},{6,2},{7,3},{8,12},{9,13},{10,... | collective-permute-start | bytes 516104 | tf_op jit(solution)/shard_map/ppermute | solution.py:523
  79.0 6.8 %collective-permute-start.11 = (bf16[2,336,128]{2,1,0:T(8,128)(2,1)S(1)}, bf16[2,336,128]{2,1,0:T(8,128)(2,1)S(1)}, u32[]{:S(2)}, u32[]{:S(2)}) collective-permute-start(bf16[2,336,128]{2,1,0:T(8,128)(2,1)S(1)} %get-tuple-element.67), channel_id=1, source_target_pairs={{0,2},{1,3},{2,0},{3,1},{4,6},{5,7},{6,4},{7,5},{8,10},{9,11},{10,... | collective-permute-start | bytes 516104 | tf_op jit(solution)/shard_map/ppermute | solution.py:523
  79.6 8.7 %collective-permute-start.13 = (bf16[2,336,128]{2,1,0:T(8,128)(2,1)S(1)}, bf16[2,336,128]{2,1,0:T(8,128)(2,1)S(1)}, u32[]{:S(2)}, u32[]{:S(2)}) collective-permute-start(bf16[2,336,128]{2,1,0:T(8,128)(2,1)S(1)} %get-tuple-element.67), channel_id=1, source_target_pairs={{0,6},{1,7},{2,4},{3,5},{4,2},{5,3},{6,0},{7,1},{8,14},{9,15},{10,... | collective-permute-start | bytes 516104 | tf_op jit(solution)/shard_map/ppermute | solution.py:523
  88.3 3.7 %collective-permute-start.14 = (bf16[4,2,336,128]{3,2,1,0:T(8,128)(2,1)S(1)}, bf16[4,2,336,128]{3,2,1,0:T(8,128)(2,1)S(1)}, u32[]{:S(2)}, u32[]{:S(2)}) collective-permute-start(bf16[4,2,336,128]{3,2,1,0:T(8,128)(2,1)S(1)} %pad_maximum_fusion.near_ref), channel_id=1, source_target_pairs={{0,1},{1,0},{2,3},{3,2},{4,5},{5,4},{6,7},{7,6},{8,9},{9,8},{10,11... | collective-permute-start | bytes 2064392 | tf_op jit(solution)/shard_map/ppermute | solution.py:523

commit v5 on v4

--- a/solution.py
+++ b/solution.py
@@ -355,28 +355,26 @@
             latent_ref[frame, dh] = out[dh * LAT : (dh + 1) * LAT, frame * 32 : (frame + 1) * 32]
 
 
-def embed_kernel(embed_ref, bias_ref, embed_out, bias_out):
+def fold_kernel(
+    w0_ref, w1_ref, w2_ref, w3_ref, embed_ref, bias_ref, own_mods_ref, mods_ref,
+    own_ref, other_ref, embed_out, bias_out, stacked, wide,
+):
     embed = embed_ref[...].astype(F32)
     embed = embed - jnp.mean(embed, axis=1, keepdims=True)
     high = embed.astype(BF16)
     embed_out[0:64] = high
     embed_out[64:128] = (embed - high.astype(F32)).astype(BF16)
-    bias = bias_ref[...]
-    bias_out[...] = jnp.broadcast_to(bias - jnp.mean(bias, axis=1, keepdims=True), (8, D))
-
-
-def fold_kernel(
-    here_ref, there_ref, embed_ref, bias_ref, own_mods_ref, mods_ref, own_ref, other_ref, stacked, wide,
-):
+    center = bias_ref[...] - jnp.mean(bias_ref[...], axis=1, keepdims=True)
+    bias_out[...] = jnp.broadcast_to(center, (8, D))
     for i in range(4):
-        stacked[i * QPAD : i * QPAD + QROWS] = (here_ref, there_ref)[i >> 1][i & 1]
-        stacked[i * QPAD + QROWS : (i + 1) * QPAD] = jnp.zeros((QPAD - QROWS, D), BF16)
-    embed = embed_ref[0:64].astype(F32) + embed_ref[64:128].astype(F32)
+        block = (w0_ref, w1_ref, w2_ref, w3_ref)[i][...].astype(F32)
+        block = jnp.concatenate([block, jnp.zeros((QPAD - QROWS, D), F32)], axis=0)
+        stacked[i * QPAD : (i + 1) * QPAD] = block.astype(BF16)
     row = iota((64, D), 0)
     sides = []
     for mod_ref in (own_mods_ref, mods_ref):
         scale, shift = 1.0 + mod_ref[0:1], mod_ref[1:2]
-        bias = bias_ref[0:1] * scale
+        bias = center * scale
         bias_high = bias.astype(BF16).astype(F32)
         shift_high = shift.astype(BF16).astype(F32)
         ends = jnp.where(row == 0, bias_high, jnp.where(row == 1, bias - bias_high, 0.0))
@@ -591,8 +589,8 @@
     mods = swap(own_mods, "clip", 1, CLIPS)
     stats0 = exchange(stats0)
     stats0, mods, beside = lax.optimization_barrier((stats0, mods, beside))
-    here = jnp.stack([qkv_weight, beside])
-    there = swap(here, "clip", 4, CLIPS)
+    stats0, mine = lax.optimization_barrier((stats0, qkv_weight))
+    rows = [qkv_weight, beside] + [swap(mine, "clip", bits, CLIPS) for bits in (4, 6)]
     hidden, center, near_h, far_h, stats1 = call(
         first_kernel,
         [cells, shape(8, C, dtype=F32), long_row, long_row, stats],
@@ -604,19 +602,8 @@
     )(place, stats0, rows_f, near, far, norms, first_conv.reshape(taps, C, C))
     near, far = neighbours(near_h, far_h)
 
-    embed, bias = call(embed_kernel, [shape(128, D), shape(8, D, dtype=F32)], [VMEM] * 2)(
-        embed_weight, embed_bias.reshape(1, D)
-    )
-    folded = shape(4 * QROWS, 128)
-    own, other = call(
-        fold_kernel,
-        [folded, folded],
-        [VMEM] * 6,
-        [pltpu.VMEM((4 * QPAD, D), BF16), pltpu.VMEM((4 * QROWS, 128), F32)],
-    )(here, there, embed, bias, own_mods, mods)
     stats1 = exchange(stats1)
-    stats1, own, other = lax.optimization_barrier((stats1, own, other))
-    other = swap(other, "clip", 1, CLIPS)
+    stats1, *rows = lax.optimization_barrier((stats1, *rows))
 
     block, near_b, far_b, stats2 = call(
         second_kernel,
@@ -627,6 +614,15 @@
         6 << 20,
     )(place, stats1, hidden, center, near, far, norms, rows_f, second_conv.reshape(taps, C, C))
     near, far = neighbours(near_b, far_b)
+    stats2, *rows = lax.optimization_barrier((stats2, *rows))
+    folded = shape(4 * QROWS, 128)
+    own, other, embed, bias = call(
+        fold_kernel,
+        [folded, folded, shape(128, D), shape(8, D, dtype=F32)],
+        [VMEM] * 8,
+        [pltpu.VMEM((4 * QPAD, D), BF16), pltpu.VMEM((4 * QROWS, 128), F32)],
+    )(*rows, embed_weight, embed_bias.reshape(1, D), own_mods, mods)
+    other = swap(other, "clip", 1, CLIPS)
     stats2 = exchange(stats2)
     patches, parcel = call(
         third_kernel,

time: 98.8 us -> 97.5 us (0.987)
  blocking collectives: 13.4 us -> 41.2 us
  starting transfers between devices: 31.5 us -> 16.7 us
  waiting for transfers between devices: 23.1 us -> 12.2 us
  Pallas kernels: 28.7 us -> 26.3 us
  other arithmetic: 1.11 us -> 0.11 us
    all_to_all x1 -> x3, blocking collectives: 13.4 us -> 41.2 us  [exchange(): return lax.all_to_all(stats, 'seq', 0, 0, tiled=True)]
    all_to_all x2 -> x0, starting transfers between devices: 15.2 us -> none  [exchange(): return lax.all_to_all(stats, 'seq', 0, 0, tiled=True)]
    all_to_all x2 -> x0, waiting for transfers between devices: 10.9 us -> none  [exchange(): return lax.all_to_all(stats, 'seq', 0, 0, tiled=True)]
    pallas_call x9 -> x8, Pallas kernels: 28.7 us -> 26.3 us  [run(): kernel(*(pltpu.with_memory_space_constraint(x, pltpu.HBM) if spec is HBM...]
    ppermute x3, starting transfers between devices: 1.95 us -> 3 us  [neighbours(): return (lax.ppermute(near, 'seq', CHIP_PAIRS), far)]
    another operation x1 -> x0, other arithmetic: 1 us -> none  [shards(): here = jnp.stack([qkv_weight, beside])]
    ppermute x9 -> x10, starting transfers between devices: 12.2 us -> 11.9 us  [swap(): return lax.ppermute(values, axis, [(i, i ^ bits) for i in range(count)])]
    ppermute x9 -> x10, waiting for transfers between devices: 12.2 us -> 12.2 us  [swap(): return lax.ppermute(values, axis, [(i, i ^ bits) for i in range(count)])]
  transfers between devices with their start and end apart: 17 -> 16, of which waited for: 7 -> 5; matrix products, arithmetic and copies ran while one was open for 1% -> 0% of each run, Pallas kernels for 12% -> 2%
where the time goes in v5:
time: 97.5 us; the launch traced here: 97.3 us
  blocking collectives  41.2 us (42%)
  Pallas kernels  26.3 us (27%)
  starting transfers between devices  16.7 us (17%)
  waiting for transfers between devices  12.2 us (13%)
    all_to_all x3, blocking collectives, exchange(): return lax.all_to_all(stats, 'seq', 0, 0, tiled=True)  41.2 us
    pallas_call x8, Pallas kernels, run(): kernel(*(pltpu.with_memory_space_constraint(x, pltpu.HBM) if spec is HBM...  26.3 us
    ppermute x10, waiting for transfers between devices, swap(): return lax.ppermute(values, axis, [(i, i ^ bits) for i in range(count)])  12.2 us
    ppermute x10, starting transfers between devices, swap(): return lax.ppermute(values, axis, [(i, i ^ bits) for i in range(count)])  11.9 us
    ppermute x3, starting transfers between devices, neighbours(): return (lax.ppermute(near, 'seq', CHIP_PAIRS), far)  3 us
  transfers between devices with their start and end apart: 16, of which 5 were waited for; matrix products, arithmetic and copies ran while one was open for 0% of the time, Pallas kernels for 2%

profile of v5, /device:TPU:1, one launch (start us, length us, event | category | flops | bytes accessed | tf_op | source)
XLA Modules:
  0.0 97.3 jit_solution(17009894816709073478)
XLA Ops:
  0.6 1.8 %split_kernel.1 = (bf16[1024,256]{1,0:T(8,128)(2,1)S(1)}, bf16[512,256]{1,0:T(8,128)(2,1)S(1)}, bf16[512,256]{1,0:T(8,128)(2,1)S(1)}, f32[16,1,128]{2,1,0:T(1,12...) custom-call(s32[1]{0:T(128)} %bitcast.place_ref, bf16[16,2,32,256]{3,2,1,0:T(8,128)(2,1)} %bitcast.24, ...), custom_call_target="tpu_custom_call" | custom-call | bytes 1048576 | tf_op jit(solution)/shard_map/split_kernel/pallas_call | solution.py:513
  2.4 1.5 %collective-permute-start.2 = (bf16[512,256]{1,0:T(8,128)(2,1)S(1)}, bf16[512,256]{1,0:T(8,128)(2,1)S(1)}, u32[]{:S(2)}, u32[]{:S(2)}) collective-permute-start(bf16[512,256]{1,0:T(8,128)(2,1)S(1)} %get-tuple-element.48), channel_id=1, source_target_pairs={{0,1},{1,0},{2,3},{3,2},{4,5},{5,4},{6,7},{7,6},{8,9},{9,8},{10,11... | collective-permute-start | bytes 786440 | tf_op jit(solution)/shard_map/ppermute | solution.py:530
  3.9 1.3 %collective-permute-start.3 = (bf16[512,256]{1,0:T(8,128)(2,1)S(1)}, bf16[512,256]{1,0:T(8,128)(2,1)S(1)}, u32[]{:S(2)}, u32[]{:S(2)}) collective-permute-start(bf16[512,256]{1,0:T(8,128)(2,1)S(1)} %get-tuple-element.49), channel_id=1, source_target_pairs={{0,15},{1,2},{2,1},{3,4},{4,3},{5,6},{6,5},{7,8},{8,7},{9,10},{10,... | collective-permute-start | bytes 786440 | tf_op jit(solution)/shard_map/ppermute | solution.py:529
  5.2 1.3 %collective-permute-start.1 = (bf16[36,3072]{1,0:T(8,128)(2,1)}, bf16[36,3072]{1,0:T(8,128)(2,1)S(1)}, u32[]{:S(2)}, u32[]{:S(2)}) collective-permute-start(bf16[36,3072]{1,0:T(8,128)(2,1)} %w0_ref), channel_id=1, source_target_pairs={{0,32},{16,48},{32,0},{48,16},{64,96},{80,112},{96,64},{112,80},{1... | collective-permute-start | bytes 663560 | tf_op jit(solution)/shard_map/ppermute | solution.py:521
  6.5 1.6 %collective-permute-start = (f32[2,3072]{1,0:T(2,128)S(1)}, f32[2,3072]{1,0:T(2,128)S(1)}, u32[]{:S(2)}, u32[]{:S(2)}) collective-permute-start(f32[2,3072]{1,0:T(2,128)S(1)} %get-tuple-element.44.own_mods_ref), channel_id=1, source_target_pairs={{0,16},{16,0},{32,48},{48,32},{64,80},{80,64},{96,112},{112,96},{1... | collective-permute-start | bytes 73736 | tf_op jit(solution)/shard_map/ppermute | solution.py:521
  8.1 14.1 %all_to_all.15.stats_ref = f32[16,1,128]{2,1,0:T(1,128)S(1)} all-to-all(f32[16,1,128]{2,1,0:T(1,128)S(1)} %get-tuple-element.43), channel_id=1, replica_groups=mesh['clip'=8,'seq'=16] {'seq'}, dimensions={0} | all-to-all | bytes 16384 | tf_op jit(solution)/shard_map/all_to_all | solution.py:534
  22.3 6.2 %first_kernel.1 = (bf16[1024,256]{1,0:T(8,128)(2,1)}, f32[8,256]{1,0:T(8,128)S(1)}, bf16[528,256]{1,0:T(8,128)(2,1)S(1)}, bf16[528,256]{1,0:T(8,128)(2,1)S(1)}, f32[16,1,128]{2,1,0:T(1,128)S(1)}) custom-call(s32[1]{0:T(128)} %bitcast.place_ref, f32[16,1,128]{2,1,0:T(1,128)S(1)} %all_to_all.15.stats_ref, ...), custom_call_target="tpu_custom_call" | custom-call | flops 3623878656 | bytes 5242880 | tf_op jit(solution)/shard_map/first_kernel/pallas_call | solution.py:513
  29.5 1.9 %collective-permute-start.5 = (bf16[36,3072]{1,0:T(8,128)(2,1)S(1)}, bf16[36,3072]{1,0:T(8,128)(2,1)S(1)}, u32[]{:S(2)}, u32[]{:S(2)}) collective-permute-start(bf16[36,3072]{1,0:T(8,128)(2,1)S(1)} %copy-done.1), channel_id=1, source_target_pairs={{0,96},{16,112},{32,64},{48,80},{64,32},{80,48},{96,0},{112,16},{1... | collective-permute-start | bytes 663560 | tf_op jit(solution)/shard_map/ppermute | solution.py:521
  32.2 13.2 %all_to_all.16.stats_ref = f32[16,1,128]{2,1,0:T(1,128)S(1)} all-to-all(f32[16,1,128]{2,1,0:T(1,128)S(1)} %get-tuple-element.51), channel_id=1, replica_groups=mesh['clip'=8,'seq'=16] {'seq'}, dimensions={0} | all-to-all | bytes 16384 | tf_op jit(solution)/shard_map/all_to_all | solution.py:534
  45.5 5.9 %second_kernel.1 = (bf16[1024,256]{1,0:T(8,128)(2,1)S(1)}, bf16[512,256]{1,0:T(8,128)(2,1)S(1)}, bf16[512,256]{1,0:T(8,128)(2,1)S(1)}, f32[16,1,128]{2,1,0:T(1,128)S(1)}) custom-call(s32[1]{0:T(128)} %bitcast.place_ref, f32[16,1,128]{2,1,0:T(1,128)S(1)} %all_to_all.16.stats_ref, bf16[1024,256]{1,0:T(8,128)(2,1)} %get-tuple-element.55.hidden_hbm, ...), custom_call_target="tpu_custom_call" | custom-call | flops 3623878656 | bytes 6291456 | tf_op jit(solution)/shard_map/second_kernel/pallas_call | solution.py:513
  52.4 1.0 %fold_kernel.1 = (bf16[144,128]{1,0:T(8,128)(2,1)S(1)}, bf16[144,128]{1,0:T(8,128)(2,1)S(1)}, bf16[128,3072]{1,0:T(8,128)(2,1)S(1)}, f32[8,3072]{1,0:T(8,128)S(1)}) custom-call(bf16[36,3072]{1,0:T(8,128)(2,1)S(1)} %copy-done.1, bf16[36,3072]{1,0:T(8,128)(2,1)S(1)} %collective-permute-done.1.w1_ref, bf16[36,3072]{1,0:T(8,128)(2,1)S(1)} %collective-permute-done.4.w2_ref, ...), custom_call_target="tpu_custom_call" | custom-call | tf_op jit(solution)/shard_map/fold_kernel/pallas_call | solution.py:513
  54.1 13.9 %all_to_all.17.stats_ref = f32[16,1,128]{2,1,0:T(1,128)S(1)} all-to-all(f32[16,1,128]{2,1,0:T(1,128)S(1)} %get-tuple-element.64), channel_id=1, replica_groups=mesh['clip'=8,'seq'=16] {'seq'}, dimensions={0} | all-to-all | bytes 16384 | tf_op jit(solution)/shard_map/all_to_all | solution.py:534
  68.0 3.8 %third_kernel.1 = (f32[256,64]{1,0:T(8,128)S(1)}, bf16[336,128]{1,0:T(8,128)(2,1)S(1)}) custom-call(s32[1]{0:T(128)} %bitcast.place_ref, f32[16,1,128]{2,1,0:T(1,128)S(1)} %all_to_all.17.stats_ref, bf16[1024,256]{1,0:T(8,128)(2,1)S(1)} %get-tuple-element.65.rows_ref, bf16[512,256]{1,0:T(8,128)(2,1)S(1)} %collective-permute-done.8.near_ref, ...), custom_call_target="tpu_custom_call" | custom-call | flops 1811939328 | bytes 4194304 | tf_op jit(solution)/shard_map/third_kernel/pallas_call | solution.py:513
  72.2 1.1 %latent_kernel.1 = f32[16,2,16,32]{3,2,1,0:T(8,128)} custom-call(f32[256,64]{1,0:T(8,128)S(1)} %get-tuple-element.78.patches_ref), custom_call_target="tpu_custom_call" | custom-call | tf_op jit(solution)/shard_map/latent_kernel/pallas_call | solution.py:513
  73.3 3.5 %collective-permute-done.11 = bf16[336,128]{1,0:T(8,128)(2,1)S(1)} collective-permute-done((bf16[336,128]{1,0:T(8,128)(2,1)S(1)}, bf16[336,128]{1,0:T(8,128)(2,1)S(1)}, u32[]{:S(2)}, u32[]{:S(2)}) %collective-permute-start.11) | collective-permute-done | bytes 86048 | tf_op jit(solution)/shard_map/ppermute | solution.py:521
  76.8 1.0 %collective-permute-start.13 = (bf16[2,336,128]{2,1,0:T(8,128)(2,1)S(1)}, bf16[2,336,128]{2,1,0:T(8,128)(2,1)S(1)}, u32[]{:S(2)}, u32[]{:S(2)}) collective-permute-start(bf16[2,336,128]{2,1,0:T(8,128)(2,1)S(1)} %get-tuple-element.85), channel_id=1, source_target_pairs={{0,4},{1,5},{2,6},{3,7},{4,0},{5,1},{6,2},{7,3},{8,12},{9,13},{10,... | collective-permute-start | bytes 516104 | tf_op jit(solution)/shard_map/ppermute | solution.py:521
  78.3 1.8 %collective-permute-start.14 = (bf16[2,336,128]{2,1,0:T(8,128)(2,1)S(1)}, bf16[2,336,128]{2,1,0:T(8,128)(2,1)S(1)}, u32[]{:S(2)}, u32[]{:S(2)}) collective-permute-start(bf16[2,336,128]{2,1,0:T(8,128)(2,1)S(1)} %get-tuple-element.85), channel_id=1, source_target_pairs={{0,6},{1,7},{2,4},{3,5},{4,2},{5,3},{6,0},{7,1},{8,14},{9,15},{10,... | collective-permute-start | bytes 516104 | tf_op jit(solution)/shard_map/ppermute | solution.py:521
  80.1 2.6 %collective-permute-done.13 = bf16[2,336,128]{2,1,0:T(8,128)(2,1)S(1)} collective-permute-done((bf16[2,336,128]{2,1,0:T(8,128)(2,1)S(1)}, bf16[2,336,128]{2,1,0:T(8,128)(2,1)S(1)}, u32[]{:S(2)}, u32[]{:S(2)}) %collective-permute-start.13) | collective-permute-done | bytes 172064 | tf_op jit(solution)/shard_map/ppermute | solution.py:521
  82.7 1.9 %collective-permute-done.12 = bf16[2,336,128]{2,1,0:T(8,128)(2,1)S(1)} collective-permute-done((bf16[2,336,128]{2,1,0:T(8,128)(2,1)S(1)}, bf16[2,336,128]{2,1,0:T(8,128)(2,1)S(1)}, u32[]{:S(2)}, u32[]{:S(2)}) %collective-permute-start.12) | collective-permute-done | bytes 172064 | tf_op jit(solution)/shard_map/ppermute | solution.py:521
  84.6 2.4 %collective-permute-done.14 = bf16[2,336,128]{2,1,0:T(8,128)(2,1)S(1)} collective-permute-done((bf16[2,336,128]{2,1,0:T(8,128)(2,1)S(1)}, bf16[2,336,128]{2,1,0:T(8,128)(2,1)S(1)}, u32[]{:S(2)}, u32[]{:S(2)}) %collective-permute-start.14) | collective-permute-done | bytes 172064 | tf_op jit(solution)/shard_map/ppermute | solution.py:521
  87.1 1.9 %collective-permute-start.15 = (bf16[4,2,336,128]{3,2,1,0:T(8,128)(2,1)S(1)}, bf16[4,2,336,128]{3,2,1,0:T(8,128)(2,1)S(1)}, u32[]{:S(2)}, u32[]{:S(2)}) collective-permute-start(bf16[4,2,336,128]{3,2,1,0:T(8,128)(2,1)S(1)} %pad_maximum_fusion.near_ref), channel_id=1, source_target_pairs={{0,1},{1,0},{2,3},{3,2},{4,5},{5,4},{6,7},{7,6},{8,9},{9,8},{10,11... | collective-permute-start | bytes 2064392 | tf_op jit(solution)/shard_map/ppermute | solution.py:521
  89.0 1.8 %collective-permute-done.15.far_ref = bf16[4,2,336,128]{3,2,1,0:T(8,128)(2,1)S(1)} collective-permute-done((bf16[4,2,336,128]{3,2,1,0:T(8,128)(2,1)S(1)}, bf16[4,2,336,128]{3,2,1,0:T(8,128)(2,1)S(1)}, u32[]{:S(2)}, u32[]{:S(2)}) %collective-permute-start.15) | collective-permute-done | bytes 688160 | tf_op jit(solution)/shard_map/ppermute | solution.py:521
  90.8 1.9 %sort_kernel.1 = (bf16[1536,256]{1,0:T(8,128)(2,1)S(1)}, bf16[1536,512]{1,0:T(8,128)(2,1)S(1)}, bf16[1536,512]{1,0:T(8,128)(2,1)S(1)}) custom-call(s32[1]{0:T(128)} %bitcast.place_ref, s32[1]{0:T(128)} %bitcast.15.clip_ref, bf16[4,2,336,128]{3,2,1,0:T(8,128)(2,1)S(1)} %pad_maximum_fusion.near_ref, bf16[4,2,336,128]{3,2,1,0:T(8,128)(2,1)S(1)} %collective-permute-done.15.far_ref), custom_call_target="tpu_custom_call" | custom-call | tf_op jit(solution)/shard_map/sort_kernel/pallas_call | solution.py:513
  92.7 4.6 %attend_kernel.1 = bf16[256,1536]{1,0:T(8,128)(2,1)} custom-call(s32[1]{0:T(128)} %bitcast.place_ref, bf16[4,2,336,128]{3,2,1,0:T(8,128)(2,1)S(1)} %pad_maximum_fusion.near_ref, bf16[4,2,336,128]{3,2,1,0:T(8,128)(2,1)S(1)} %collective-permute-done.15.far_ref, bf16[1536,256]{1,0:T(8,128)(2,1)S(1)} %get-tuple-element.81.asks_ref, ...), custom_call_target="tpu_custom_call" | custom-call | tf_op jit(solution)/shard_map/attend_kernel/pallas_call | solution.py:513
  (29 shorter events, 4.6 us)
Async XLA Ops:
  2.4 19.9 %collective-permute-start.2 = (bf16[512,256]{1,0:T(8,128)(2,1)S(1)}, bf16[512,256]{1,0:T(8,128)(2,1)S(1)}, u32[]{:S(2)}, u32[]{:S(2)}) collective-permute-start(bf16[512,256]{1,0:T(8,128)(2,1)S(1)} %get-tuple-element.48), channel_id=1, source_target_pairs={{0,1},{1,0},{2,3},{3,2},{4,5},{5,4},{6,7},{7,6},{8,9},{9,8},{10,11... | collective-permute-start | bytes 786440 | tf_op jit(solution)/shard_map/ppermute | solution.py:530
  3.9 18.4 %collective-permute-start.3 = (bf16[512,256]{1,0:T(8,128)(2,1)S(1)}, bf16[512,256]{1,0:T(8,128)(2,1)S(1)}, u32[]{:S(2)}, u32[]{:S(2)}) collective-permute-start(bf16[512,256]{1,0:T(8,128)(2,1)S(1)} %get-tuple-element.49), channel_id=1, source_target_pairs={{0,15},{1,2},{2,1},{3,4},{4,3},{5,6},{6,5},{7,8},{8,7},{9,10},{10,... | collective-permute-start | bytes 786440 | tf_op jit(solution)/shard_map/ppermute | solution.py:529
  5.2 17.1 %collective-permute-start.1 = (bf16[36,3072]{1,0:T(8,128)(2,1)}, bf16[36,3072]{1,0:T(8,128)(2,1)S(1)}, u32[]{:S(2)}, u32[]{:S(2)}) collective-permute-start(bf16[36,3072]{1,0:T(8,128)(2,1)} %w0_ref), channel_id=1, source_target_pairs={{0,32},{16,48},{32,0},{48,16},{64,96},{80,112},{96,64},{112,80},{1... | collective-permute-start | bytes 663560 | tf_op jit(solution)/shard_map/ppermute | solution.py:521
  6.5 15.8 %collective-permute-start = (f32[2,3072]{1,0:T(2,128)S(1)}, f32[2,3072]{1,0:T(2,128)S(1)}, u32[]{:S(2)}, u32[]{:S(2)}) collective-permute-start(f32[2,3072]{1,0:T(2,128)S(1)} %get-tuple-element.44.own_mods_ref), channel_id=1, source_target_pairs={{0,16},{16,0},{32,48},{48,32},{64,80},{80,64},{96,112},{112,96},{1... | collective-permute-start | bytes 73736 | tf_op jit(solution)/shard_map/ppermute | solution.py:521
  22.3 7.2 %copy-start.1 = (bf16[36,3072]{1,0:T(8,128)(2,1)S(1)}, bf16[36,3072]{1,0:T(8,128)(2,1)}, u32[]{:S(2)}) copy-start(bf16[36,3072]{1,0:T(8,128)(2,1)} %w0_ref) | copy-start | bytes 663556
  28.5 16.9 %collective-permute-start.6 = (bf16[528,256]{1,0:T(8,128)(2,1)S(1)}, bf16[528,256]{1,0:T(8,128)(2,1)S(1)}, u32[]{:S(2)}, u32[]{:S(2)}) collective-permute-start(bf16[528,256]{1,0:T(8,128)(2,1)S(1)} %get-tuple-element.57), channel_id=1, source_target_pairs={{0,1},{1,0},{2,3},{3,2},{4,5},{5,4},{6,7},{7,6},{8,9},{9,8},{10,11... | collective-permute-start | bytes 811016 | tf_op jit(solution)/shard_map/ppermute | solution.py:530
  29.3 16.2 %collective-permute-start.7 = (bf16[528,256]{1,0:T(8,128)(2,1)S(1)}, bf16[528,256]{1,0:T(8,128)(2,1)S(1)}, u32[]{:S(2)}, u32[]{:S(2)}) collective-permute-start(bf16[528,256]{1,0:T(8,128)(2,1)S(1)} %get-tuple-element.58), channel_id=1, source_target_pairs={{0,15},{1,2},{2,1},{3,4},{4,3},{5,6},{6,5},{7,8},{8,7},{9,10},{10,... | collective-permute-start | bytes 811016 | tf_op jit(solution)/shard_map/ppermute | solution.py:529
  29.5 15.9 %collective-permute-start.5 = (bf16[36,3072]{1,0:T(8,128)(2,1)S(1)}, bf16[36,3072]{1,0:T(8,128)(2,1)S(1)}, u32[]{:S(2)}, u32[]{:S(2)}) collective-permute-start(bf16[36,3072]{1,0:T(8,128)(2,1)S(1)} %copy-done.1), channel_id=1, source_target_pairs={{0,96},{16,112},{32,64},{48,80},{64,32},{80,48},{96,0},{112,16},{1... | collective-permute-start | bytes 663560 | tf_op jit(solution)/shard_map/ppermute | solution.py:521
  31.4 14.0 %collective-permute-start.4 = (bf16[36,3072]{1,0:T(8,128)(2,1)S(1)}, bf16[36,3072]{1,0:T(8,128)(2,1)S(1)}, u32[]{:S(2)}, u32[]{:S(2)}) collective-permute-start(bf16[36,3072]{1,0:T(8,128)(2,1)S(1)} %copy-done.1), channel_id=1, source_target_pairs={{0,64},{16,80},{32,96},{48,112},{64,0},{80,16},{96,32},{112,48},{1... | collective-permute-start | bytes 663560 | tf_op jit(solution)/shard_map/ppermute | solution.py:521
  45.4 6.9 %copy-start = (bf16[64,3072]{1,0:T(8,128)(2,1)S(1)}, bf16[64,3072]{1,0:T(8,128)(2,1)}, u32[]{:S(2)}) copy-start(bf16[64,3072]{1,0:T(8,128)(2,1)} %embed_ref.1) | copy-start | bytes 1179652
  45.5 6.9 %copy-start.2 = (f32[3072]{0:T(1024)S(1)}, f32[3072]{0:T(1024)}, u32[]{:S(2)}) copy-start(f32[3072]{0:T(1024)} %param.18) | copy-start | bytes 36868
  45.5 22.5 %copy-start.3 = (bf16[3,3,3,256,16]{3,4,2,1,0:T(8,128)(2,1)S(1)}, bf16[3,3,3,256,16]{3,4,2,1,0:T(8,128)(2,1)}, u32[]{:S(2)}) copy-start(bf16[3,3,3,256,16]{3,4,2,1,0:T(8,128)(2,1)} %param.14) | copy-start | bytes 663556
  51.4 16.7 %collective-permute-start.8 = (bf16[512,256]{1,0:T(8,128)(2,1)S(1)}, bf16[512,256]{1,0:T(8,128)(2,1)S(1)}, u32[]{:S(2)}, u32[]{:S(2)}) collective-permute-start(bf16[512,256]{1,0:T(8,128)(2,1)S(1)} %get-tuple-element.66), channel_id=1, source_target_pairs={{0,1},{1,0},{2,3},{3,2},{4,5},{5,4},{6,7},{7,6},{8,9},{9,8},{10,11... | collective-permute-start | bytes 786440 | tf_op jit(solution)/shard_map/ppermute | solution.py:530
  52.1 15.9 %collective-permute-start.9 = (bf16[512,256]{1,0:T(8,128)(2,1)S(1)}, bf16[512,256]{1,0:T(8,128)(2,1)S(1)}, u32[]{:S(2)}, u32[]{:S(2)}) collective-permute-start(bf16[512,256]{1,0:T(8,128)(2,1)S(1)} %get-tuple-element.67), channel_id=1, source_target_pairs={{0,15},{1,2},{2,1},{3,4},{4,3},{5,6},{6,5},{7,8},{8,7},{9,10},{10,... | collective-permute-start | bytes 786440 | tf_op jit(solution)/shard_map/ppermute | solution.py:529
  53.4 14.6 %collective-permute-start.10 = (bf16[144,128]{1,0:T(8,128)(2,1)S(1)}, bf16[144,128]{1,0:T(8,128)(2,1)S(1)}, u32[]{:S(2)}, u32[]{:S(2)}) collective-permute-start(bf16[144,128]{1,0:T(8,128)(2,1)S(1)} %get-tuple-element.76), channel_id=1, source_target_pairs={{0,16},{16,0},{32,48},{48,32},{64,80},{80,64},{96,112},{112,96},{1... | collective-permute-start | bytes 110600 | tf_op jit(solution)/shard_map/ppermute | solution.py:521
  71.8 4.9 %collective-permute-start.11 = (bf16[336,128]{1,0:T(8,128)(2,1)S(1)}, bf16[336,128]{1,0:T(8,128)(2,1)S(1)}, u32[]{:S(2)}, u32[]{:S(2)}) collective-permute-start(bf16[336,128]{1,0:T(8,128)(2,1)S(1)} %get-tuple-element.77), channel_id=1, source_target_pairs={{0,8},{1,9},{2,10},{3,11},{4,12},{5,13},{6,14},{7,15},{8,0},{9,1},... | collective-permute-start | bytes 258056 | tf_op jit(solution)/shard_map/ppermute | solution.py:521
  76.8 5.9 %collective-permute-start.13 = (bf16[2,336,128]{2,1,0:T(8,128)(2,1)S(1)}, bf16[2,336,128]{2,1,0:T(8,128)(2,1)S(1)}, u32[]{:S(2)}, u32[]{:S(2)}) collective-permute-start(bf16[2,336,128]{2,1,0:T(8,128)(2,1)S(1)} %get-tuple-element.85), channel_id=1, source_target_pairs={{0,4},{1,5},{2,6},{3,7},{4,0},{5,1},{6,2},{7,3},{8,12},{9,13},{10,... | collective-permute-start | bytes 516104 | tf_op jit(solution)/shard_map/ppermute | solution.py:521
  77.8 6.8 %collective-permute-start.12 = (bf16[2,336,128]{2,1,0:T(8,128)(2,1)S(1)}, bf16[2,336,128]{2,1,0:T(8,128)(2,1)S(1)}, u32[]{:S(2)}, u32[]{:S(2)}) collective-permute-start(bf16[2,336,128]{2,1,0:T(8,128)(2,1)S(1)} %get-tuple-element.85), channel_id=1, source_target_pairs={{0,2},{1,3},{2,0},{3,1},{4,6},{5,7},{6,4},{7,5},{8,10},{9,11},{10,... | collective-permute-start | bytes 516104 | tf_op jit(solution)/shard_map/ppermute | solution.py:521
  78.3 8.7 %collective-permute-start.14 = (bf16[2,336,128]{2,1,0:T(8,128)(2,1)S(1)}, bf16[2,336,128]{2,1,0:T(8,128)(2,1)S(1)}, u32[]{:S(2)}, u32[]{:S(2)}) collective-permute-start(bf16[2,336,128]{2,1,0:T(8,128)(2,1)S(1)} %get-tuple-element.85), channel_id=1, source_target_pairs={{0,6},{1,7},{2,4},{3,5},{4,2},{5,3},{6,0},{7,1},{8,14},{9,15},{10,... | collective-permute-start | bytes 516104 | tf_op jit(solution)/shard_map/ppermute | solution.py:521
  87.1 3.7 %collective-permute-start.15 = (bf16[4,2,336,128]{3,2,1,0:T(8,128)(2,1)S(1)}, bf16[4,2,336,128]{3,2,1,0:T(8,128)(2,1)S(1)}, u32[]{:S(2)}, u32[]{:S(2)}) collective-permute-start(bf16[4,2,336,128]{3,2,1,0:T(8,128)(2,1)S(1)} %pad_maximum_fusion.near_ref), channel_id=1, source_target_pairs={{0,1},{1,0},{2,3},{3,2},{4,5},{5,4},{6,7},{7,6},{8,9},{9,8},{10,11... | collective-permute-start | bytes 2064392 | tf_op jit(solution)/shard_map/ppermute | solution.py:521

commit v6 on v5

--- a/solution.py
+++ b/solution.py
@@ -566,7 +566,6 @@
     stats = shape(SEQ, 1, 128, dtype=F32)
     taps = 27
 
-    beside = swap(qkv_weight, "clip", 2, CLIPS)
     cells = shape(CELLS, C)
     long_row = shape(ROW + 16, C)
     rows_f, near, far, stats0, norms, own_mods = call(
@@ -588,9 +587,9 @@
     near, far = neighbours(near, far)
     mods = swap(own_mods, "clip", 1, CLIPS)
     stats0 = exchange(stats0)
-    stats0, mods, beside = lax.optimization_barrier((stats0, mods, beside))
+    stats0, mods = lax.optimization_barrier((stats0, mods))
     stats0, mine = lax.optimization_barrier((stats0, qkv_weight))
-    rows = [qkv_weight, beside] + [swap(mine, "clip", bits, CLIPS) for bits in (4, 6)]
+    rows = [qkv_weight] + [swap(mine, "clip", bits, CLIPS) for bits in (2, 4, 6)]
     hidden, center, near_h, far_h, stats1 = call(
         first_kernel,
         [cells, shape(8, C, dtype=F32), long_row, long_row, stats],

time: 97.5 us -> 97.4 us (level)
  blocking collectives: 41.2 us -> 27.8 us
  waiting for transfers between devices: 12.2 us -> 19.1 us
  starting transfers between devices: 16.7 us -> 22.5 us
    all_to_all x3 -> x2, blocking collectives: 41.2 us -> 27.8 us  [exchange(): return lax.all_to_all(stats, 'seq', 0, 0, tiled=True)]
    all_to_all x0 -> x1, starting transfers between devices: none -> 6.48 us  [exchange(): return lax.all_to_all(stats, 'seq', 0, 0, tiled=True)]
    ppermute x10, waiting for transfers between devices: 12.2 us -> 15.8 us  [swap(): return lax.ppermute(values, axis, [(i, i ^ bits) for i in range(count)])]
    all_to_all x0 -> x1, waiting for transfers between devices: none -> 3.3 us  [exchange(): return lax.all_to_all(stats, 'seq', 0, 0, tiled=True)]
  transfers between devices with their start and end apart: 16 -> 17, of which waited for: 5 -> 8; matrix products, arithmetic and copies ran while one was open for 0% -> 0% of each run, Pallas kernels for 2% -> 2%
where the time goes in v6:
time: 97.4 us; the launch traced here: 97.1 us
  blocking collectives  27.8 us (29%)
  Pallas kernels  26.9 us (28%)
  starting transfers between devices  22.5 us (23%)
  waiting for transfers between devices  19.1 us (20%)
    all_to_all x2, blocking collectives, exchange(): return lax.all_to_all(stats, 'seq', 0, 0, tiled=True)  27.8 us
    pallas_call x8, Pallas kernels, run(): kernel(*(pltpu.with_memory_space_constraint(x, pltpu.HBM) if spec is HBM...  26.9 us
    ppermute x10, waiting for transfers between devices, swap(): return lax.ppermute(values, axis, [(i, i ^ bits) for i in range(count)])  15.8 us
    ppermute x10, starting transfers between devices, swap(): return lax.ppermute(values, axis, [(i, i ^ bits) for i in range(count)])  11.2 us
    all_to_all x1, starting transfers between devices, exchange(): return lax.all_to_all(stats, 'seq', 0, 0, tiled=True)  6.48 us
    all_to_all x1, waiting for transfers between devices, exchange(): return lax.all_to_all(stats, 'seq', 0, 0, tiled=True)  3.3 us
    ppermute x3, starting transfers between devices, neighbours(): return (lax.ppermute(near, 'seq', CHIP_PAIRS), far)  2.99 us
  transfers between devices with their start and end apart: 17, of which 8 were waited for; matrix products, arithmetic and copies ran while one was open for 0% of the time, Pallas kernels for 2%

profile of v6, /device:TPU:1, one launch (start us, length us, event | category | flops | bytes accessed | tf_op | source)
XLA Modules:
  0.0 97.1 jit_solution(8830050757597097994)
XLA Ops:
  0.6 1.8 %split_kernel.1 = (bf16[1024,256]{1,0:T(8,128)(2,1)S(1)}, bf16[512,256]{1,0:T(8,128)(2,1)S(1)}, bf16[512,256]{1,0:T(8,128)(2,1)S(1)}, f32[16,1,128]{2,1,0:T(1,12...) custom-call(s32[1]{0:T(128)} %bitcast.place_ref, bf16[16,2,32,256]{3,2,1,0:T(8,128)(2,1)} %bitcast.24, ...), custom_call_target="tpu_custom_call" | custom-call | bytes 1048576 | tf_op jit(solution)/shard_map/split_kernel/pallas_call | solution.py:513
  2.4 1.5 %collective-permute-start.1 = (bf16[512,256]{1,0:T(8,128)(2,1)S(1)}, bf16[512,256]{1,0:T(8,128)(2,1)S(1)}, u32[]{:S(2)}, u32[]{:S(2)}) collective-permute-start(bf16[512,256]{1,0:T(8,128)(2,1)S(1)} %get-tuple-element.47), channel_id=1, source_target_pairs={{0,1},{1,0},{2,3},{3,2},{4,5},{5,4},{6,7},{7,6},{8,9},{9,8},{10,11... | collective-permute-start | bytes 786440 | tf_op jit(solution)/shard_map/ppermute | solution.py:530
  3.9 1.3 %collective-permute-start.2 = (bf16[512,256]{1,0:T(8,128)(2,1)S(1)}, bf16[512,256]{1,0:T(8,128)(2,1)S(1)}, u32[]{:S(2)}, u32[]{:S(2)}) collective-permute-start(bf16[512,256]{1,0:T(8,128)(2,1)S(1)} %get-tuple-element.48), channel_id=1, source_target_pairs={{0,15},{1,2},{2,1},{3,4},{4,3},{5,6},{6,5},{7,8},{8,7},{9,10},{10,... | collective-permute-start | bytes 786440 | tf_op jit(solution)/shard_map/ppermute | solution.py:529
  5.2 1.6 %collective-permute-start = (f32[2,3072]{1,0:T(2,128)S(1)}, f32[2,3072]{1,0:T(2,128)S(1)}, u32[]{:S(2)}, u32[]{:S(2)}) collective-permute-start(f32[2,3072]{1,0:T(2,128)S(1)} %get-tuple-element.43.own_mods_ref), channel_id=1, source_target_pairs={{0,16},{16,0},{32,48},{48,32},{64,80},{80,64},{96,112},{112,96},{1... | collective-permute-start | bytes 73736 | tf_op jit(solution)/shard_map/ppermute | solution.py:521
  6.8 13.9 %all_to_all.15.stats_ref = f32[16,1,128]{2,1,0:T(1,128)S(1)} all-to-all(f32[16,1,128]{2,1,0:T(1,128)S(1)} %get-tuple-element.42), channel_id=1, replica_groups=mesh['clip'=8,'seq'=16] {'seq'}, dimensions={0} | all-to-all | bytes 16384 | tf_op jit(solution)/shard_map/all_to_all | solution.py:534
  20.8 6.8 %first_kernel.1 = (bf16[1024,256]{1,0:T(8,128)(2,1)}, f32[8,256]{1,0:T(8,128)S(1)}, bf16[528,256]{1,0:T(8,128)(2,1)S(1)}, bf16[528,256]{1,0:T(8,128)(2,1)S(1)}, f32[16,1,128]{2,1,0:T(1,128)}) custom-call(s32[1]{0:T(128)} %bitcast.place_ref, f32[16,1,128]{2,1,0:T(1,128)S(1)} %all_to_all.15.stats_ref, ...), custom_call_target="tpu_custom_call" | custom-call | flops 3623878656 | bytes 5242880 | tf_op jit(solution)/shard_map/first_kernel/pallas_call | solution.py:513
  28.6 2.7 %collective-permute-start.5 = (bf16[36,3072]{1,0:T(8,128)(2,1)S(1)}, bf16[36,3072]{1,0:T(8,128)(2,1)S(1)}, u32[]{:S(2)}, u32[]{:S(2)}) collective-permute-start(bf16[36,3072]{1,0:T(8,128)(2,1)S(1)} %copy-done.1), channel_id=1, source_target_pairs={{0,96},{16,112},{32,64},{48,80},{64,32},{80,48},{96,0},{112,16},{1... | collective-permute-start | bytes 663560 | tf_op jit(solution)/shard_map/ppermute | solution.py:521
  31.9 6.5 %all-to-all-start.1 = ((f32[16,1,128]{2,1,0:T(1,128)}), f32[16,1,128]{2,1,0:T(1,128)S(1)}, u32[]{:S(2)}, u32[]{:S(2)}) async-start(f32[16,1,128]{2,1,0:T(1,128)} %get-tuple-element.50), calls=%async_computation.1 | async-start | bytes 16384 | tf_op jit(solution)/shard_map/all_to_all | solution.py:534
  38.4 3.5 %collective-permute-done.5.w3_ref = bf16[36,3072]{1,0:T(8,128)(2,1)S(1)} collective-permute-done((bf16[36,3072]{1,0:T(8,128)(2,1)S(1)}, bf16[36,3072]{1,0:T(8,128)(2,1)S(1)}, u32[]{:S(2)}, u32[]{:S(2)}) %collective-permute-start.5) | collective-permute-done | bytes 221216 | tf_op jit(solution)/shard_map/ppermute | solution.py:521
  42.0 3.3 %all-to-all-done.1.stats_ref = f32[16,1,128]{2,1,0:T(1,128)S(1)} async-done(((f32[16,1,128]{2,1,0:T(1,128)}), f32[16,1,128]{2,1,0:T(1,128)S(1)}, u32[]{:S(2)}, u32[]{:S(2)}) %all-to-all-start.1) | async-done | bytes 8224 | tf_op jit(solution)/shard_map/all_to_all | solution.py:534
  45.3 5.9 %second_kernel.1 = (bf16[1024,256]{1,0:T(8,128)(2,1)S(1)}, bf16[512,256]{1,0:T(8,128)(2,1)S(1)}, bf16[512,256]{1,0:T(8,128)(2,1)S(1)}, f32[16,1,128]{2,1,0:T(1,128)S(1)}) custom-call(s32[1]{0:T(128)} %bitcast.place_ref, f32[16,1,128]{2,1,0:T(1,128)S(1)} %all-to-all-done.1.stats_ref, bf16[1024,256]{1,0:T(8,128)(2,1)} %get-tuple-element.53.hidden_hbm, ...), custom_call_target="tpu_custom_call" | custom-call | flops 3623878656 | bytes 6291456 | tf_op jit(solution)/shard_map/second_kernel/pallas_call | solution.py:513
  52.2 1.0 %fold_kernel.1 = (bf16[144,128]{1,0:T(8,128)(2,1)S(1)}, bf16[144,128]{1,0:T(8,128)(2,1)S(1)}, bf16[128,3072]{1,0:T(8,128)(2,1)S(1)}, f32[8,3072]{1,0:T(8,128)S(1)}) custom-call(bf16[36,3072]{1,0:T(8,128)(2,1)S(1)} %copy-done.1, bf16[36,3072]{1,0:T(8,128)(2,1)S(1)} %collective-permute-done.3.w1_ref, bf16[36,3072]{1,0:T(8,128)(2,1)S(1)} %collective-permute-done.4.w2_ref, ...), custom_call_target="tpu_custom_call" | custom-call | tf_op jit(solution)/shard_map/fold_kernel/pallas_call | solution.py:513
  53.9 13.9 %all_to_all.16.stats_ref = f32[16,1,128]{2,1,0:T(1,128)S(1)} all-to-all(f32[16,1,128]{2,1,0:T(1,128)S(1)} %get-tuple-element.62), channel_id=1, replica_groups=mesh['clip'=8,'seq'=16] {'seq'}, dimensions={0} | all-to-all | bytes 16384 | tf_op jit(solution)/shard_map/all_to_all | solution.py:534
  67.8 3.8 %third_kernel.1 = (f32[256,64]{1,0:T(8,128)S(1)}, bf16[336,128]{1,0:T(8,128)(2,1)S(1)}) custom-call(s32[1]{0:T(128)} %bitcast.place_ref, f32[16,1,128]{2,1,0:T(1,128)S(1)} %all_to_all.16.stats_ref, bf16[1024,256]{1,0:T(8,128)(2,1)S(1)} %get-tuple-element.63.rows_ref, bf16[512,256]{1,0:T(8,128)(2,1)S(1)} %collective-permute-done.8.near_ref, ...), custom_call_target="tpu_custom_call" | custom-call | flops 1811939328 | bytes 4194304 | tf_op jit(solution)/shard_map/third_kernel/pallas_call | solution.py:513
  72.0 1.1 %latent_kernel.1 = f32[16,2,16,32]{3,2,1,0:T(8,128)} custom-call(f32[256,64]{1,0:T(8,128)S(1)} %get-tuple-element.76.patches_ref), custom_call_target="tpu_custom_call" | custom-call | tf_op jit(solution)/shard_map/latent_kernel/pallas_call | solution.py:513
  73.1 3.5 %collective-permute-done.11 = bf16[336,128]{1,0:T(8,128)(2,1)S(1)} collective-permute-done((bf16[336,128]{1,0:T(8,128)(2,1)S(1)}, bf16[336,128]{1,0:T(8,128)(2,1)S(1)}, u32[]{:S(2)}, u32[]{:S(2)}) %collective-permute-start.11) | collective-permute-done | bytes 86048 | tf_op jit(solution)/shard_map/ppermute | solution.py:521
  78.1 1.8 %collective-permute-start.14 = (bf16[2,336,128]{2,1,0:T(8,128)(2,1)S(1)}, bf16[2,336,128]{2,1,0:T(8,128)(2,1)S(1)}, u32[]{:S(2)}, u32[]{:S(2)}) collective-permute-start(bf16[2,336,128]{2,1,0:T(8,128)(2,1)S(1)} %get-tuple-element.83), channel_id=1, source_target_pairs={{0,6},{1,7},{2,4},{3,5},{4,2},{5,3},{6,0},{7,1},{8,14},{9,15},{10,... | collective-permute-start | bytes 516104 | tf_op jit(solution)/shard_map/ppermute | solution.py:521
  79.9 2.6 %collective-permute-done.13 = bf16[2,336,128]{2,1,0:T(8,128)(2,1)S(1)} collective-permute-done((bf16[2,336,128]{2,1,0:T(8,128)(2,1)S(1)}, bf16[2,336,128]{2,1,0:T(8,128)(2,1)S(1)}, u32[]{:S(2)}, u32[]{:S(2)}) %collective-permute-start.13) | collective-permute-done | bytes 172064 | tf_op jit(solution)/shard_map/ppermute | solution.py:521
  82.5 1.9 %collective-permute-done.12 = bf16[2,336,128]{2,1,0:T(8,128)(2,1)S(1)} collective-permute-done((bf16[2,336,128]{2,1,0:T(8,128)(2,1)S(1)}, bf16[2,336,128]{2,1,0:T(8,128)(2,1)S(1)}, u32[]{:S(2)}, u32[]{:S(2)}) %collective-permute-start.12) | collective-permute-done | bytes 172064 | tf_op jit(solution)/shard_map/ppermute | solution.py:521
  84.4 2.4 %collective-permute-done.14 = bf16[2,336,128]{2,1,0:T(8,128)(2,1)S(1)} collective-permute-done((bf16[2,336,128]{2,1,0:T(8,128)(2,1)S(1)}, bf16[2,336,128]{2,1,0:T(8,128)(2,1)S(1)}, u32[]{:S(2)}, u32[]{:S(2)}) %collective-permute-start.14) | collective-permute-done | bytes 172064 | tf_op jit(solution)/shard_map/ppermute | solution.py:521
  86.9 1.9 %collective-permute-start.15 = (bf16[4,2,336,128]{3,2,1,0:T(8,128)(2,1)S(1)}, bf16[4,2,336,128]{3,2,1,0:T(8,128)(2,1)S(1)}, u32[]{:S(2)}, u32[]{:S(2)}) collective-permute-start(bf16[4,2,336,128]{3,2,1,0:T(8,128)(2,1)S(1)} %pad_maximum_fusion.near_ref), channel_id=1, source_target_pairs={{0,1},{1,0},{2,3},{3,2},{4,5},{5,4},{6,7},{7,6},{8,9},{9,8},{10,11... | collective-permute-start | bytes 2064392 | tf_op jit(solution)/shard_map/ppermute | solution.py:521
  88.8 1.8 %collective-permute-done.15.far_ref = bf16[4,2,336,128]{3,2,1,0:T(8,128)(2,1)S(1)} collective-permute-done((bf16[4,2,336,128]{3,2,1,0:T(8,128)(2,1)S(1)}, bf16[4,2,336,128]{3,2,1,0:T(8,128)(2,1)S(1)}, u32[]{:S(2)}, u32[]{:S(2)}) %collective-permute-start.15) | collective-permute-done | bytes 688160 | tf_op jit(solution)/shard_map/ppermute | solution.py:521
  90.6 1.9 %sort_kernel.1 = (bf16[1536,256]{1,0:T(8,128)(2,1)S(1)}, bf16[1536,512]{1,0:T(8,128)(2,1)S(1)}, bf16[1536,512]{1,0:T(8,128)(2,1)S(1)}) custom-call(s32[1]{0:T(128)} %bitcast.place_ref, s32[1]{0:T(128)} %bitcast.15.clip_ref, bf16[4,2,336,128]{3,2,1,0:T(8,128)(2,1)S(1)} %pad_maximum_fusion.near_ref, bf16[4,2,336,128]{3,2,1,0:T(8,128)(2,1)S(1)} %collective-permute-done.15.far_ref), custom_call_target="tpu_custom_call" | custom-call | tf_op jit(solution)/shard_map/sort_kernel/pallas_call | solution.py:513
  92.5 4.6 %attend_kernel.1 = bf16[256,1536]{1,0:T(8,128)(2,1)} custom-call(s32[1]{0:T(128)} %bitcast.place_ref, bf16[4,2,336,128]{3,2,1,0:T(8,128)(2,1)S(1)} %pad_maximum_fusion.near_ref, bf16[4,2,336,128]{3,2,1,0:T(8,128)(2,1)S(1)} %collective-permute-done.15.far_ref, bf16[1536,256]{1,0:T(8,128)(2,1)S(1)} %get-tuple-element.79.asks_ref, ...), custom_call_target="tpu_custom_call" | custom-call | tf_op jit(solution)/shard_map/attend_kernel/pallas_call | solution.py:513
  (30 shorter events, 5.5 us)
Async XLA Ops:
  2.4 18.3 %collective-permute-start.1 = (bf16[512,256]{1,0:T(8,128)(2,1)S(1)}, bf16[512,256]{1,0:T(8,128)(2,1)S(1)}, u32[]{:S(2)}, u32[]{:S(2)}) collective-permute-start(bf16[512,256]{1,0:T(8,128)(2,1)S(1)} %get-tuple-element.47), channel_id=1, source_target_pairs={{0,1},{1,0},{2,3},{3,2},{4,5},{5,4},{6,7},{7,6},{8,9},{9,8},{10,11... | collective-permute-start | bytes 786440 | tf_op jit(solution)/shard_map/ppermute | solution.py:530
  3.9 16.8 %collective-permute-start.2 = (bf16[512,256]{1,0:T(8,128)(2,1)S(1)}, bf16[512,256]{1,0:T(8,128)(2,1)S(1)}, u32[]{:S(2)}, u32[]{:S(2)}) collective-permute-start(bf16[512,256]{1,0:T(8,128)(2,1)S(1)} %get-tuple-element.48), channel_id=1, source_target_pairs={{0,15},{1,2},{2,1},{3,4},{4,3},{5,6},{6,5},{7,8},{8,7},{9,10},{10,... | collective-permute-start | bytes 786440 | tf_op jit(solution)/shard_map/ppermute | solution.py:529
  5.2 15.6 %collective-permute-start = (f32[2,3072]{1,0:T(2,128)S(1)}, f32[2,3072]{1,0:T(2,128)S(1)}, u32[]{:S(2)}, u32[]{:S(2)}) collective-permute-start(f32[2,3072]{1,0:T(2,128)S(1)} %get-tuple-element.43.own_mods_ref), channel_id=1, source_target_pairs={{0,16},{16,0},{32,48},{48,32},{64,80},{80,64},{96,112},{112,96},{1... | collective-permute-start | bytes 73736 | tf_op jit(solution)/shard_map/ppermute | solution.py:521
  20.8 7.8 %copy-start.1 = (bf16[36,3072]{1,0:T(8,128)(2,1)S(1)}, bf16[36,3072]{1,0:T(8,128)(2,1)}, u32[]{:S(2)}) copy-start(bf16[36,3072]{1,0:T(8,128)(2,1)} %w0_ref) | copy-start | bytes 663556
  27.6 17.7 %collective-permute-start.6 = (bf16[528,256]{1,0:T(8,128)(2,1)S(1)}, bf16[528,256]{1,0:T(8,128)(2,1)S(1)}, u32[]{:S(2)}, u32[]{:S(2)}) collective-permute-start(bf16[528,256]{1,0:T(8,128)(2,1)S(1)} %get-tuple-element.55), channel_id=1, source_target_pairs={{0,1},{1,0},{2,3},{3,2},{4,5},{5,4},{6,7},{7,6},{8,9},{9,8},{10,11... | collective-permute-start | bytes 811016 | tf_op jit(solution)/shard_map/ppermute | solution.py:530
  28.3 17.0 %collective-permute-start.7 = (bf16[528,256]{1,0:T(8,128)(2,1)S(1)}, bf16[528,256]{1,0:T(8,128)(2,1)S(1)}, u32[]{:S(2)}, u32[]{:S(2)}) collective-permute-start(bf16[528,256]{1,0:T(8,128)(2,1)S(1)} %get-tuple-element.56), channel_id=1, source_target_pairs={{0,15},{1,2},{2,1},{3,4},{4,3},{5,6},{6,5},{7,8},{8,7},{9,10},{10,... | collective-permute-start | bytes 811016 | tf_op jit(solution)/shard_map/ppermute | solution.py:529
  28.6 13.3 %collective-permute-start.5 = (bf16[36,3072]{1,0:T(8,128)(2,1)S(1)}, bf16[36,3072]{1,0:T(8,128)(2,1)S(1)}, u32[]{:S(2)}, u32[]{:S(2)}) collective-permute-start(bf16[36,3072]{1,0:T(8,128)(2,1)S(1)} %copy-done.1), channel_id=1, source_target_pairs={{0,96},{16,112},{32,64},{48,80},{64,32},{80,48},{96,0},{112,16},{1... | collective-permute-start | bytes 663560 | tf_op jit(solution)/shard_map/ppermute | solution.py:521
  31.3 10.6 %collective-permute-start.4 = (bf16[36,3072]{1,0:T(8,128)(2,1)S(1)}, bf16[36,3072]{1,0:T(8,128)(2,1)S(1)}, u32[]{:S(2)}, u32[]{:S(2)}) collective-permute-start(bf16[36,3072]{1,0:T(8,128)(2,1)S(1)} %copy-done.1), channel_id=1, source_target_pairs={{0,64},{16,80},{32,96},{48,112},{64,0},{80,16},{96,32},{112,48},{1... | collective-permute-start | bytes 663560 | tf_op jit(solution)/shard_map/ppermute | solution.py:521
  31.7 10.3 %collective-permute-start.3 = (bf16[36,3072]{1,0:T(8,128)(2,1)S(1)}, bf16[36,3072]{1,0:T(8,128)(2,1)S(1)}, u32[]{:S(2)}, u32[]{:S(2)}) collective-permute-start(bf16[36,3072]{1,0:T(8,128)(2,1)S(1)} %copy-done.1), channel_id=1, source_target_pairs={{0,32},{16,48},{32,0},{48,16},{64,96},{80,112},{96,64},{112,80},{1... | collective-permute-start | bytes 663560 | tf_op jit(solution)/shard_map/ppermute | solution.py:521
  31.9 13.4 %all-to-all-start.1 = ((f32[16,1,128]{2,1,0:T(1,128)}), f32[16,1,128]{2,1,0:T(1,128)S(1)}, u32[]{:S(2)}, u32[]{:S(2)}) async-start(f32[16,1,128]{2,1,0:T(1,128)} %get-tuple-element.50), calls=%async_computation.1 | async-start | bytes 16384 | tf_op jit(solution)/shard_map/all_to_all | solution.py:534
  45.3 6.9 %copy-start = (bf16[64,3072]{1,0:T(8,128)(2,1)S(1)}, bf16[64,3072]{1,0:T(8,128)(2,1)}, u32[]{:S(2)}) copy-start(bf16[64,3072]{1,0:T(8,128)(2,1)} %embed_ref.1) | copy-start | bytes 1179652
  45.3 6.9 %copy-start.2 = (f32[3072]{0:T(1024)S(1)}, f32[3072]{0:T(1024)}, u32[]{:S(2)}) copy-start(f32[3072]{0:T(1024)} %param.18) | copy-start | bytes 36868
  45.3 22.5 %copy-start.3 = (bf16[3,3,3,256,16]{3,4,2,1,0:T(8,128)(2,1)S(1)}, bf16[3,3,3,256,16]{3,4,2,1,0:T(8,128)(2,1)}, u32[]{:S(2)}) copy-start(bf16[3,3,3,256,16]{3,4,2,1,0:T(8,128)(2,1)} %param.14) | copy-start | bytes 663556
  51.2 16.6 %collective-permute-start.8 = (bf16[512,256]{1,0:T(8,128)(2,1)S(1)}, bf16[512,256]{1,0:T(8,128)(2,1)S(1)}, u32[]{:S(2)}, u32[]{:S(2)}) collective-permute-start(bf16[512,256]{1,0:T(8,128)(2,1)S(1)} %get-tuple-element.64), channel_id=1, source_target_pairs={{0,1},{1,0},{2,3},{3,2},{4,5},{5,4},{6,7},{7,6},{8,9},{9,8},{10,11... | collective-permute-start | bytes 786440 | tf_op jit(solution)/shard_map/ppermute | solution.py:530
  52.0 15.8 %collective-permute-start.9 = (bf16[512,256]{1,0:T(8,128)(2,1)S(1)}, bf16[512,256]{1,0:T(8,128)(2,1)S(1)}, u32[]{:S(2)}, u32[]{:S(2)}) collective-permute-start(bf16[512,256]{1,0:T(8,128)(2,1)S(1)} %get-tuple-element.65), channel_id=1, source_target_pairs={{0,15},{1,2},{2,1},{3,4},{4,3},{5,6},{6,5},{7,8},{8,7},{9,10},{10,... | collective-permute-start | bytes 786440 | tf_op jit(solution)/shard_map/ppermute | solution.py:529
  53.2 14.6 %collective-permute-start.10 = (bf16[144,128]{1,0:T(8,128)(2,1)S(1)}, bf16[144,128]{1,0:T(8,128)(2,1)S(1)}, u32[]{:S(2)}, u32[]{:S(2)}) collective-permute-start(bf16[144,128]{1,0:T(8,128)(2,1)S(1)} %get-tuple-element.74), channel_id=1, source_target_pairs={{0,16},{16,0},{32,48},{48,32},{64,80},{80,64},{96,112},{112,96},{1... | collective-permute-start | bytes 110600 | tf_op jit(solution)/shard_map/ppermute | solution.py:521
  71.6 4.9 %collective-permute-start.11 = (bf16[336,128]{1,0:T(8,128)(2,1)S(1)}, bf16[336,128]{1,0:T(8,128)(2,1)S(1)}, u32[]{:S(2)}, u32[]{:S(2)}) collective-permute-start(bf16[336,128]{1,0:T(8,128)(2,1)S(1)} %get-tuple-element.75), channel_id=1, source_target_pairs={{0,8},{1,9},{2,10},{3,11},{4,12},{5,13},{6,14},{7,15},{8,0},{9,1},... | collective-permute-start | bytes 258056 | tf_op jit(solution)/shard_map/ppermute | solution.py:521
  76.6 5.9 %collective-permute-start.13 = (bf16[2,336,128]{2,1,0:T(8,128)(2,1)S(1)}, bf16[2,336,128]{2,1,0:T(8,128)(2,1)S(1)}, u32[]{:S(2)}, u32[]{:S(2)}) collective-permute-start(bf16[2,336,128]{2,1,0:T(8,128)(2,1)S(1)} %get-tuple-element.83), channel_id=1, source_target_pairs={{0,4},{1,5},{2,6},{3,7},{4,0},{5,1},{6,2},{7,3},{8,12},{9,13},{10,... | collective-permute-start | bytes 516104 | tf_op jit(solution)/shard_map/ppermute | solution.py:521
  77.5 6.8 %collective-permute-start.12 = (bf16[2,336,128]{2,1,0:T(8,128)(2,1)S(1)}, bf16[2,336,128]{2,1,0:T(8,128)(2,1)S(1)}, u32[]{:S(2)}, u32[]{:S(2)}) collective-permute-start(bf16[2,336,128]{2,1,0:T(8,128)(2,1)S(1)} %get-tuple-element.83), channel_id=1, source_target_pairs={{0,2},{1,3},{2,0},{3,1},{4,6},{5,7},{6,4},{7,5},{8,10},{9,11},{10,... | collective-permute-start | bytes 516104 | tf_op jit(solution)/shard_map/ppermute | solution.py:521
  78.1 8.7 %collective-permute-start.14 = (bf16[2,336,128]{2,1,0:T(8,128)(2,1)S(1)}, bf16[2,336,128]{2,1,0:T(8,128)(2,1)S(1)}, u32[]{:S(2)}, u32[]{:S(2)}) collective-permute-start(bf16[2,336,128]{2,1,0:T(8,128)(2,1)S(1)} %get-tuple-element.83), channel_id=1, source_target_pairs={{0,6},{1,7},{2,4},{3,5},{4,2},{5,3},{6,0},{7,1},{8,14},{9,15},{10,... | collective-permute-start | bytes 516104 | tf_op jit(solution)/shard_map/ppermute | solution.py:521
  86.9 3.7 %collective-permute-start.15 = (bf16[4,2,336,128]{3,2,1,0:T(8,128)(2,1)S(1)}, bf16[4,2,336,128]{3,2,1,0:T(8,128)(2,1)S(1)}, u32[]{:S(2)}, u32[]{:S(2)}) collective-permute-start(bf16[4,2,336,128]{3,2,1,0:T(8,128)(2,1)S(1)} %pad_maximum_fusion.near_ref), channel_id=1, source_target_pairs={{0,1},{1,0},{2,3},{3,2},{4,5},{5,4},{6,7},{7,6},{8,9},{9,8},{10,11... | collective-permute-start | bytes 2064392 | tf_op jit(solution)/shard_map/ppermute | solution.py:521

commit v7 on v6

--- a/solution.py
+++ b/solution.py
@@ -401,12 +401,12 @@
 WIDE = HEADS * HDIM
 
 
-def sort_kernel(place_ref, clip_ref, near_ref, far_ref, asks_ref, keys_ref, values_ref, loose, wide):
+def sort_kernel(place_ref, clip_ref, *refs):
+    asks_ref, keys_ref, values_ref, loose, wide = refs[8:]
     seq, clip = place_ref[0], clip_ref[0]
     spot = iota((40, 128), 1)
     for j in range(SEQ):
-        source = (near_ref, far_ref)[j & 1]
-        loose[j] = source[(j >> 1) & 3, j >> 3, 144:336].astype(F32)
+        loose[j] = refs[4 * (j & 1) + ((j >> 1) & 3)][j >> 3, 144:336].astype(F32)
         for k in range(CLIPS):
             at = ((clip ^ (2 * (k & 3) + (k >> 2))) * SEQ + (seq ^ j)) * QROWS
             block = loose[j, (k & 3) * QROWS : (k & 3) * QROWS + 40]
@@ -431,9 +431,10 @@
             target[:, 256 * side + 128 : 256 * side + 256] = extra.astype(BF16)
 
 
-def attend_kernel(place_ref, near_ref, far_ref, asks_ref, keys_ref, values_ref, out_ref, queries, mixed, scores, weights):
+def attend_kernel(place_ref, *refs):
+    asks_ref, keys_ref, values_ref, out_ref, queries, mixed, scores, weights = refs[8:]
     seq = place_ref[0]
-    blocks = [(near_ref, far_ref)[j & 1].at[(j >> 1) & 3, j >> 3] for j in range(SEQ)]
+    blocks = [refs[4 * (j & 1) + ((j >> 1) & 3)].at[j >> 3] for j in range(SEQ)]
     lane = iota((128, 128), 1)
     pick = one_hot(iota((8, 128), 1) == iota((8, 128), 0) + seq * 8)
     twin = pl.ds(pl.multiple_of((seq >> 1) * 16, 16), 16)
@@ -538,8 +539,8 @@
     over = swap(block, "seq", 8, SEQ)
     over, beside = lax.optimization_barrier((over, beside))
     pair = jnp.stack([block, over])
-    near = jnp.stack([pair] + [swap(pair, "seq", bits, SEQ) for bits in (2, 4, 6)])
-    return near, swap(near, "seq", 1, SEQ), beside
+    near = [pair] + [swap(pair, "seq", bits, SEQ) for bits in (2, 4, 6)]
+    return near + [swap(x, "seq", 1, SEQ) for x in near], beside
 
 
 WINDOW = pltpu.VMEM((4, FRAMES + 2, 4, HALF, C), BF16)
@@ -635,24 +636,24 @@
         out_conv.transpose(0, 1, 2, 4, 3).reshape(taps, LAT, C), embed, bias, own, other,
     )
     latent = call(latent_kernel, shape(FRAMES, 2, LAT, 2 * HALF, dtype=F32), [VMEM])(patches)
-    near, far, latent = gather_seq(parcel, latent)
+    parcels, latent = gather_seq(parcel, latent)
     asks, keys, values = call(
         sort_kernel,
         [shape(WIDE, 256), shape(WIDE, 512), shape(WIDE, 512)],
-        [SMEM] * 2 + [VMEM] * 2,
+        [SMEM] * 2 + [VMEM] * 8,
         [pltpu.VMEM((SEQ, 192, 128), F32), pltpu.VMEM((3 * WIDE, 128), F32)],
-    )(place, clip, near, far)
+    )(place, clip, *parcels)
     frame_heads = call(
         attend_kernel,
         shape(SEQ * HALF, WIDE),
-        [SMEM] + [VMEM] * 5,
+        [SMEM] + [VMEM] * 11,
         [
             pltpu.VMEM((SEQ, HEADS, HALF, 256), BF16),
             pltpu.VMEM((2, HEADS, 128, 256), F32),
             pltpu.VMEM((SEQ, 128, HEADS * HALF), F32),
             pltpu.VMEM((SEQ, HEADS * HALF, 128), BF16),
         ],
-    )(place, near, far, asks, keys, values)
+    )(place, *parcels, asks, keys, values)
     latent = latent.transpose(0, 1, 3, 2).reshape(1, FRAMES, 2, 2 * HALF, LAT)
     return (latent, frame_heads.reshape(1, 1, SEQ * HALF, WIDE))
 

time: 97.4 us -> 96.8 us (level)
  waiting for transfers between devices: 19.1 us -> 14 us
  starting transfers between devices: 22.5 us -> 27.1 us
    ppermute x10 -> x13, waiting for transfers between devices: 15.8 us -> 10.7 us  [swap(): return lax.ppermute(values, axis, [(i, i ^ bits) for i in range(count)])]
    ppermute x10 -> x13, starting transfers between devices: 11.2 us -> 15.9 us  [swap(): return lax.ppermute(values, axis, [(i, i ^ bits) for i in range(count)])]
  transfers between devices with their start and end apart: 17 -> 20, of which waited for: 8 -> 8; matrix products, arithmetic and copies ran while one was open for 0% -> 0% of each run, Pallas kernels for 2% -> 2%
where the time goes in v7:
time: 96.8 us; the launch traced here: 96.5 us
  blocking collectives  27.8 us (29%)
  starting transfers between devices  27.1 us (28%)
  Pallas kernels  26.9 us (28%)
  waiting for transfers between devices  14 us (14%)
    all_to_all x2, blocking collectives, exchange(): return lax.all_to_all(stats, 'seq', 0, 0, tiled=True)  27.8 us
    pallas_call x8, Pallas kernels, run(): kernel(*(pltpu.with_memory_space_constraint(x, pltpu.HBM) if spec is HBM...  26.9 us
    ppermute x13, starting transfers between devices, swap(): return lax.ppermute(values, axis, [(i, i ^ bits) for i in range(count)])  15.9 us
    ppermute x13, waiting for transfers between devices, swap(): return lax.ppermute(values, axis, [(i, i ^ bits) for i in range(count)])  10.7 us
    all_to_all x1, starting transfers between devices, exchange(): return lax.all_to_all(stats, 'seq', 0, 0, tiled=True)  6.48 us
    all_to_all x1, waiting for transfers between devices, exchange(): return lax.all_to_all(stats, 'seq', 0, 0, tiled=True)  3.3 us
    ppermute x3, starting transfers between devices, neighbours(): return (lax.ppermute(near, 'seq', CHIP_PAIRS), far)  2.99 us
  transfers between devices with their start and end apart: 20, of which 8 were waited for; matrix products, arithmetic and copies ran while one was open for 0% of the time, Pallas kernels for 2%

profile of v7, /device:TPU:1, one launch (start us, length us, event | category | flops | bytes accessed | tf_op | source)
XLA Modules:
  0.0 96.5 jit_solution(5482924114699114017)
XLA Ops:
  0.6 1.8 %split_kernel.1 = (bf16[1024,256]{1,0:T(8,128)(2,1)S(1)}, bf16[512,256]{1,0:T(8,128)(2,1)S(1)}, bf16[512,256]{1,0:T(8,128)(2,1)S(1)}, f32[16,1,128]{2,1,0:T(1,12...) custom-call(s32[1]{0:T(128)} %bitcast.place_ref, bf16[16,2,32,256]{3,2,1,0:T(8,128)(2,1)} %bitcast.19, ...), custom_call_target="tpu_custom_call" | custom-call | bytes 1048576 | tf_op jit(solution)/shard_map/split_kernel/pallas_call | solution.py:514
  2.4 1.5 %collective-permute-start.1 = (bf16[512,256]{1,0:T(8,128)(2,1)S(1)}, bf16[512,256]{1,0:T(8,128)(2,1)S(1)}, u32[]{:S(2)}, u32[]{:S(2)}) collective-permute-start(bf16[512,256]{1,0:T(8,128)(2,1)S(1)} %get-tuple-element.47), channel_id=1, source_target_pairs={{0,1},{1,0},{2,3},{3,2},{4,5},{5,4},{6,7},{7,6},{8,9},{9,8},{10,11... | collective-permute-start | bytes 786440 | tf_op jit(solution)/shard_map/ppermute | solution.py:531
  3.9 1.3 %collective-permute-start.2 = (bf16[512,256]{1,0:T(8,128)(2,1)S(1)}, bf16[512,256]{1,0:T(8,128)(2,1)S(1)}, u32[]{:S(2)}, u32[]{:S(2)}) collective-permute-start(bf16[512,256]{1,0:T(8,128)(2,1)S(1)} %get-tuple-element.48), channel_id=1, source_target_pairs={{0,15},{1,2},{2,1},{3,4},{4,3},{5,6},{6,5},{7,8},{8,7},{9,10},{10,... | collective-permute-start | bytes 786440 | tf_op jit(solution)/shard_map/ppermute | solution.py:530
  5.2 1.6 %collective-permute-start = (f32[2,3072]{1,0:T(2,128)S(1)}, f32[2,3072]{1,0:T(2,128)S(1)}, u32[]{:S(2)}, u32[]{:S(2)}) collective-permute-start(f32[2,3072]{1,0:T(2,128)S(1)} %get-tuple-element.43.own_mods_ref), channel_id=1, source_target_pairs={{0,16},{16,0},{32,48},{48,32},{64,80},{80,64},{96,112},{112,96},{1... | collective-permute-start | bytes 73736 | tf_op jit(solution)/shard_map/ppermute | solution.py:522
  6.8 13.9 %all_to_all.15.stats_ref = f32[16,1,128]{2,1,0:T(1,128)S(1)} all-to-all(f32[16,1,128]{2,1,0:T(1,128)S(1)} %get-tuple-element.42), channel_id=1, replica_groups=mesh['clip'=8,'seq'=16] {'seq'}, dimensions={0} | all-to-all | bytes 16384 | tf_op jit(solution)/shard_map/all_to_all | solution.py:535
  20.8 6.8 %first_kernel.1 = (bf16[1024,256]{1,0:T(8,128)(2,1)}, f32[8,256]{1,0:T(8,128)S(1)}, bf16[528,256]{1,0:T(8,128)(2,1)S(1)}, bf16[528,256]{1,0:T(8,128)(2,1)S(1)}, f32[16,1,128]{2,1,0:T(1,128)}) custom-call(s32[1]{0:T(128)} %bitcast.place_ref, f32[16,1,128]{2,1,0:T(1,128)S(1)} %all_to_all.15.stats_ref, ...), custom_call_target="tpu_custom_call" | custom-call | flops 3623878656 | bytes 5242880 | tf_op jit(solution)/shard_map/first_kernel/pallas_call | solution.py:514
  28.6 2.7 %collective-permute-start.5 = (bf16[36,3072]{1,0:T(8,128)(2,1)S(1)}, bf16[36,3072]{1,0:T(8,128)(2,1)S(1)}, u32[]{:S(2)}, u32[]{:S(2)}) collective-permute-start(bf16[36,3072]{1,0:T(8,128)(2,1)S(1)} %copy-done.1), channel_id=1, source_target_pairs={{0,96},{16,112},{32,64},{48,80},{64,32},{80,48},{96,0},{112,16},{1... | collective-permute-start | bytes 663560 | tf_op jit(solution)/shard_map/ppermute | solution.py:522
  31.9 6.5 %all-to-all-start.1 = ((f32[16,1,128]{2,1,0:T(1,128)}), f32[16,1,128]{2,1,0:T(1,128)S(1)}, u32[]{:S(2)}, u32[]{:S(2)}) async-start(f32[16,1,128]{2,1,0:T(1,128)} %get-tuple-element.50), calls=%async_computation.1 | async-start | bytes 16384 | tf_op jit(solution)/shard_map/all_to_all | solution.py:535
  38.4 3.5 %collective-permute-done.5.w3_ref = bf16[36,3072]{1,0:T(8,128)(2,1)S(1)} collective-permute-done((bf16[36,3072]{1,0:T(8,128)(2,1)S(1)}, bf16[36,3072]{1,0:T(8,128)(2,1)S(1)}, u32[]{:S(2)}, u32[]{:S(2)}) %collective-permute-start.5) | collective-permute-done | bytes 221216 | tf_op jit(solution)/shard_map/ppermute | solution.py:522
  42.0 3.3 %all-to-all-done.1.stats_ref = f32[16,1,128]{2,1,0:T(1,128)S(1)} async-done(((f32[16,1,128]{2,1,0:T(1,128)}), f32[16,1,128]{2,1,0:T(1,128)S(1)}, u32[]{:S(2)}, u32[]{:S(2)}) %all-to-all-start.1) | async-done | bytes 8224 | tf_op jit(solution)/shard_map/all_to_all | solution.py:535
  45.3 5.9 %second_kernel.1 = (bf16[1024,256]{1,0:T(8,128)(2,1)S(1)}, bf16[512,256]{1,0:T(8,128)(2,1)S(1)}, bf16[512,256]{1,0:T(8,128)(2,1)S(1)}, f32[16,1,128]{2,1,0:T(1,128)S(1)}) custom-call(s32[1]{0:T(128)} %bitcast.place_ref, f32[16,1,128]{2,1,0:T(1,128)S(1)} %all-to-all-done.1.stats_ref, bf16[1024,256]{1,0:T(8,128)(2,1)} %get-tuple-element.53.hidden_hbm, ...), custom_call_target="tpu_custom_call" | custom-call | flops 3623878656 | bytes 6291456 | tf_op jit(solution)/shard_map/second_kernel/pallas_call | solution.py:514
  52.2 1.0 %fold_kernel.1 = (bf16[144,128]{1,0:T(8,128)(2,1)S(1)}, bf16[144,128]{1,0:T(8,128)(2,1)S(1)}, bf16[128,3072]{1,0:T(8,128)(2,1)S(1)}, f32[8,3072]{1,0:T(8,128)S(1)}) custom-call(bf16[36,3072]{1,0:T(8,128)(2,1)S(1)} %copy-done.1, bf16[36,3072]{1,0:T(8,128)(2,1)S(1)} %collective-permute-done.3.w1_ref, bf16[36,3072]{1,0:T(8,128)(2,1)S(1)} %collective-permute-done.4.w2_ref, ...), custom_call_target="tpu_custom_call" | custom-call | tf_op jit(solution)/shard_map/fold_kernel/pallas_call | solution.py:514
  53.9 13.9 %all_to_all.16.stats_ref = f32[16,1,128]{2,1,0:T(1,128)S(1)} all-to-all(f32[16,1,128]{2,1,0:T(1,128)S(1)} %get-tuple-element.62), channel_id=1, replica_groups=mesh['clip'=8,'seq'=16] {'seq'}, dimensions={0} | all-to-all | bytes 16384 | tf_op jit(solution)/shard_map/all_to_all | solution.py:535
  67.8 3.8 %third_kernel.1 = (f32[256,64]{1,0:T(8,128)S(1)}, bf16[336,128]{1,0:T(8,128)(2,1)S(1)}) custom-call(s32[1]{0:T(128)} %bitcast.place_ref, f32[16,1,128]{2,1,0:T(1,128)S(1)} %all_to_all.16.stats_ref, bf16[1024,256]{1,0:T(8,128)(2,1)S(1)} %get-tuple-element.63.rows_ref, bf16[512,256]{1,0:T(8,128)(2,1)S(1)} %collective-permute-done.8.near_ref, ...), custom_call_target="tpu_custom_call" | custom-call | flops 1811939328 | bytes 4194304 | tf_op jit(solution)/shard_map/third_kernel/pallas_call | solution.py:514
  72.0 1.1 %latent_kernel.1 = f32[16,2,16,32]{3,2,1,0:T(8,128)} custom-call(f32[256,64]{1,0:T(8,128)S(1)} %get-tuple-element.76.patches_ref), custom_call_target="tpu_custom_call" | custom-call | tf_op jit(solution)/shard_map/latent_kernel/pallas_call | solution.py:514
  73.1 3.5 %collective-permute-done.11 = bf16[336,128]{1,0:T(8,128)(2,1)S(1)} collective-permute-done((bf16[336,128]{1,0:T(8,128)(2,1)S(1)}, bf16[336,128]{1,0:T(8,128)(2,1)S(1)}, u32[]{:S(2)}, u32[]{:S(2)}) %collective-permute-start.11) | collective-permute-done | bytes 86048 | tf_op jit(solution)/shard_map/ppermute | solution.py:522
  76.6 1.0 %collective-permute-start.14 = (bf16[2,336,128]{2,1,0:T(8,128)(2,1)S(1)}, bf16[2,336,128]{2,1,0:T(8,128)(2,1)S(1)}, u32[]{:S(2)}, u32[]{:S(2)}) collective-permute-start(bf16[2,336,128]{2,1,0:T(8,128)(2,1)S(1)} %pad_maximum_fusion.refs_0_), channel_id=1, source_target_pairs={{0,6},{1,7},{2,4},{3,5},{4,2},{5,3},{6,0},{7,1},{8,14},{9,15},{10,... | collective-permute-start | bytes 516104 | tf_op jit(solution)/shard_map/ppermute | solution.py:522
  77.5 1.2 %collective-permute-start.13 = (bf16[2,336,128]{2,1,0:T(8,128)(2,1)S(1)}, bf16[2,336,128]{2,1,0:T(8,128)(2,1)S(1)}, u32[]{:S(2)}, u32[]{:S(2)}) collective-permute-start(bf16[2,336,128]{2,1,0:T(8,128)(2,1)S(1)} %pad_maximum_fusion.refs_0_), channel_id=1, source_target_pairs={{0,4},{1,5},{2,6},{3,7},{4,0},{5,1},{6,2},{7,3},{8,12},{9,13},{10,... | collective-permute-start | bytes 516104 | tf_op jit(solution)/shard_map/ppermute | solution.py:522
  78.7 1.2 %collective-permute-start.12 = (bf16[2,336,128]{2,1,0:T(8,128)(2,1)S(1)}, bf16[2,336,128]{2,1,0:T(8,128)(2,1)S(1)}, u32[]{:S(2)}, u32[]{:S(2)}) collective-permute-start(bf16[2,336,128]{2,1,0:T(8,128)(2,1)S(1)} %pad_maximum_fusion.refs_0_), channel_id=1, source_target_pairs={{0,2},{1,3},{2,0},{3,1},{4,6},{5,7},{6,4},{7,5},{8,10},{9,11},{10,... | collective-permute-start | bytes 516104 | tf_op jit(solution)/shard_map/ppermute | solution.py:522
  79.9 2.7 %collective-permute-start.15 = (bf16[2,336,128]{2,1,0:T(8,128)(2,1)S(1)}, bf16[2,336,128]{2,1,0:T(8,128)(2,1)S(1)}, u32[]{:S(2)}, u32[]{:S(2)}) collective-permute-start(bf16[2,336,128]{2,1,0:T(8,128)(2,1)S(1)} %pad_maximum_fusion.refs_0_), channel_id=1, source_target_pairs={{0,1},{1,0},{2,3},{3,2},{4,5},{5,4},{6,7},{7,6},{8,9},{9,8},{10,11... | collective-permute-start | bytes 516104 | tf_op jit(solution)/shard_map/ppermute | solution.py:522
  82.6 2.5 %collective-permute-done.14.refs_3_ = bf16[2,336,128]{2,1,0:T(8,128)(2,1)S(1)} collective-permute-done((bf16[2,336,128]{2,1,0:T(8,128)(2,1)S(1)}, bf16[2,336,128]{2,1,0:T(8,128)(2,1)S(1)}, u32[]{:S(2)}, u32[]{:S(2)}) %collective-permute-start.14) | collective-permute-done | bytes 172064 | tf_op jit(solution)/shard_map/ppermute | solution.py:522
  85.1 3.3 %collective-permute-start.18 = (bf16[2,336,128]{2,1,0:T(8,128)(2,1)S(1)}, bf16[2,336,128]{2,1,0:T(8,128)(2,1)S(1)}, u32[]{:S(2)}, u32[]{:S(2)}) collective-permute-start(bf16[2,336,128]{2,1,0:T(8,128)(2,1)S(1)} %collective-permute-done.14.refs_3_), channel_id=1, source_target_pairs={{0,1},{1,0},{2,3},{3,2},{4,5},{5,4},{6,7},{7,6},{8,9},{9,8},{10,11... | collective-permute-start | bytes 516104 | tf_op jit(solution)/shard_map/ppermute | solution.py:522
  90.0 1.9 %sort_kernel.1 = (bf16[1536,256]{1,0:T(8,128)(2,1)S(1)}, bf16[1536,512]{1,0:T(8,128)(2,1)S(1)}, bf16[1536,512]{1,0:T(8,128)(2,1)S(1)}) custom-call(s32[1]{0:T(128)} %bitcast.place_ref, s32[1]{0:T(128)} %bitcast.11.clip_ref, bf16[2,336,128]{2,1,0:T(8,128)(2,1)S(1)} %pad_maximum_fusion.refs_0_, bf16[2,336,128]{2,1,0:T(8,128)(2,1)S(1)} %collective-permute-done.12.refs_1_, ...), custom_call_target="tpu_custom_call" | custom-call | tf_op jit(solution)/shard_map/sort_kernel/pallas_call | solution.py:514
  91.9 4.6 %attend_kernel.1 = bf16[256,1536]{1,0:T(8,128)(2,1)} custom-call(s32[1]{0:T(128)} %bitcast.place_ref, bf16[2,336,128]{2,1,0:T(8,128)(2,1)S(1)} %pad_maximum_fusion.refs_0_, bf16[2,336,128]{2,1,0:T(8,128)(2,1)S(1)} %collective-permute-done.12.refs_1_, bf16[2,336,128]{2,1,0:T(8,128)(2,1)S(1)} %collective-permute-done.13.refs_2_, ...), custom_call_target="tpu_custom_call" | custom-call | tf_op jit(solution)/shard_map/attend_kernel/pallas_call | solution.py:514
  (35 shorter events, 5.5 us)
Async XLA Ops:
  2.4 18.3 %collective-permute-start.1 = (bf16[512,256]{1,0:T(8,128)(2,1)S(1)}, bf16[512,256]{1,0:T(8,128)(2,1)S(1)}, u32[]{:S(2)}, u32[]{:S(2)}) collective-permute-start(bf16[512,256]{1,0:T(8,128)(2,1)S(1)} %get-tuple-element.47), channel_id=1, source_target_pairs={{0,1},{1,0},{2,3},{3,2},{4,5},{5,4},{6,7},{7,6},{8,9},{9,8},{10,11... | collective-permute-start | bytes 786440 | tf_op jit(solution)/shard_map/ppermute | solution.py:531
  3.9 16.8 %collective-permute-start.2 = (bf16[512,256]{1,0:T(8,128)(2,1)S(1)}, bf16[512,256]{1,0:T(8,128)(2,1)S(1)}, u32[]{:S(2)}, u32[]{:S(2)}) collective-permute-start(bf16[512,256]{1,0:T(8,128)(2,1)S(1)} %get-tuple-element.48), channel_id=1, source_target_pairs={{0,15},{1,2},{2,1},{3,4},{4,3},{5,6},{6,5},{7,8},{8,7},{9,10},{10,... | collective-permute-start | bytes 786440 | tf_op jit(solution)/shard_map/ppermute | solution.py:530
  5.2 15.6 %collective-permute-start = (f32[2,3072]{1,0:T(2,128)S(1)}, f32[2,3072]{1,0:T(2,128)S(1)}, u32[]{:S(2)}, u32[]{:S(2)}) collective-permute-start(f32[2,3072]{1,0:T(2,128)S(1)} %get-tuple-element.43.own_mods_ref), channel_id=1, source_target_pairs={{0,16},{16,0},{32,48},{48,32},{64,80},{80,64},{96,112},{112,96},{1... | collective-permute-start | bytes 73736 | tf_op jit(solution)/shard_map/ppermute | solution.py:522
  20.8 7.8 %copy-start.1 = (bf16[36,3072]{1,0:T(8,128)(2,1)S(1)}, bf16[36,3072]{1,0:T(8,128)(2,1)}, u32[]{:S(2)}) copy-start(bf16[36,3072]{1,0:T(8,128)(2,1)} %w0_ref) | copy-start | bytes 663556
  27.6 17.7 %collective-permute-start.6 = (bf16[528,256]{1,0:T(8,128)(2,1)S(1)}, bf16[528,256]{1,0:T(8,128)(2,1)S(1)}, u32[]{:S(2)}, u32[]{:S(2)}) collective-permute-start(bf16[528,256]{1,0:T(8,128)(2,1)S(1)} %get-tuple-element.55), channel_id=1, source_target_pairs={{0,1},{1,0},{2,3},{3,2},{4,5},{5,4},{6,7},{7,6},{8,9},{9,8},{10,11... | collective-permute-start | bytes 811016 | tf_op jit(solution)/shard_map/ppermute | solution.py:531
  28.3 17.0 %collective-permute-start.7 = (bf16[528,256]{1,0:T(8,128)(2,1)S(1)}, bf16[528,256]{1,0:T(8,128)(2,1)S(1)}, u32[]{:S(2)}, u32[]{:S(2)}) collective-permute-start(bf16[528,256]{1,0:T(8,128)(2,1)S(1)} %get-tuple-element.56), channel_id=1, source_target_pairs={{0,15},{1,2},{2,1},{3,4},{4,3},{5,6},{6,5},{7,8},{8,7},{9,10},{10,... | collective-permute-start | bytes 811016 | tf_op jit(solution)/shard_map/ppermute | solution.py:530
  28.6 13.3 %collective-permute-start.5 = (bf16[36,3072]{1,0:T(8,128)(2,1)S(1)}, bf16[36,3072]{1,0:T(8,128)(2,1)S(1)}, u32[]{:S(2)}, u32[]{:S(2)}) collective-permute-start(bf16[36,3072]{1,0:T(8,128)(2,1)S(1)} %copy-done.1), channel_id=1, source_target_pairs={{0,96},{16,112},{32,64},{48,80},{64,32},{80,48},{96,0},{112,16},{1... | collective-permute-start | bytes 663560 | tf_op jit(solution)/shard_map/ppermute | solution.py:522
  31.3 10.6 %collective-permute-start.4 = (bf16[36,3072]{1,0:T(8,128)(2,1)S(1)}, bf16[36,3072]{1,0:T(8,128)(2,1)S(1)}, u32[]{:S(2)}, u32[]{:S(2)}) collective-permute-start(bf16[36,3072]{1,0:T(8,128)(2,1)S(1)} %copy-done.1), channel_id=1, source_target_pairs={{0,64},{16,80},{32,96},{48,112},{64,0},{80,16},{96,32},{112,48},{1... | collective-permute-start | bytes 663560 | tf_op jit(solution)/shard_map/ppermute | solution.py:522
  31.7 10.3 %collective-permute-start.3 = (bf16[36,3072]{1,0:T(8,128)(2,1)S(1)}, bf16[36,3072]{1,0:T(8,128)(2,1)S(1)}, u32[]{:S(2)}, u32[]{:S(2)}) collective-permute-start(bf16[36,3072]{1,0:T(8,128)(2,1)S(1)} %copy-done.1), channel_id=1, source_target_pairs={{0,32},{16,48},{32,0},{48,16},{64,96},{80,112},{96,64},{112,80},{1... | collective-permute-start | bytes 663560 | tf_op jit(solution)/shard_map/ppermute | solution.py:522
  31.9 13.4 %all-to-all-start.1 = ((f32[16,1,128]{2,1,0:T(1,128)}), f32[16,1,128]{2,1,0:T(1,128)S(1)}, u32[]{:S(2)}, u32[]{:S(2)}) async-start(f32[16,1,128]{2,1,0:T(1,128)} %get-tuple-element.50), calls=%async_computation.1 | async-start | bytes 16384 | tf_op jit(solution)/shard_map/all_to_all | solution.py:535
  45.3 6.9 %copy-start = (bf16[64,3072]{1,0:T(8,128)(2,1)S(1)}, bf16[64,3072]{1,0:T(8,128)(2,1)}, u32[]{:S(2)}) copy-start(bf16[64,3072]{1,0:T(8,128)(2,1)} %embed_ref.1) | copy-start | bytes 1179652
  45.3 6.9 %copy-start.2 = (f32[3072]{0:T(1024)S(1)}, f32[3072]{0:T(1024)}, u32[]{:S(2)}) copy-start(f32[3072]{0:T(1024)} %param.18) | copy-start | bytes 36868
  45.3 22.5 %copy-start.3 = (bf16[3,3,3,256,16]{3,4,2,1,0:T(8,128)(2,1)S(1)}, bf16[3,3,3,256,16]{3,4,2,1,0:T(8,128)(2,1)}, u32[]{:S(2)}) copy-start(bf16[3,3,3,256,16]{3,4,2,1,0:T(8,128)(2,1)} %param.14) | copy-start | bytes 663556
  51.2 16.6 %collective-permute-start.8 = (bf16[512,256]{1,0:T(8,128)(2,1)S(1)}, bf16[512,256]{1,0:T(8,128)(2,1)S(1)}, u32[]{:S(2)}, u32[]{:S(2)}) collective-permute-start(bf16[512,256]{1,0:T(8,128)(2,1)S(1)} %get-tuple-element.64), channel_id=1, source_target_pairs={{0,1},{1,0},{2,3},{3,2},{4,5},{5,4},{6,7},{7,6},{8,9},{9,8},{10,11... | collective-permute-start | bytes 786440 | tf_op jit(solution)/shard_map/ppermute | solution.py:531
  52.0 15.8 %collective-permute-start.9 = (bf16[512,256]{1,0:T(8,128)(2,1)S(1)}, bf16[512,256]{1,0:T(8,128)(2,1)S(1)}, u32[]{:S(2)}, u32[]{:S(2)}) collective-permute-start(bf16[512,256]{1,0:T(8,128)(2,1)S(1)} %get-tuple-element.65), channel_id=1, source_target_pairs={{0,15},{1,2},{2,1},{3,4},{4,3},{5,6},{6,5},{7,8},{8,7},{9,10},{10,... | collective-permute-start | bytes 786440 | tf_op jit(solution)/shard_map/ppermute | solution.py:530
  53.2 14.6 %collective-permute-start.10 = (bf16[144,128]{1,0:T(8,128)(2,1)S(1)}, bf16[144,128]{1,0:T(8,128)(2,1)S(1)}, u32[]{:S(2)}, u32[]{:S(2)}) collective-permute-start(bf16[144,128]{1,0:T(8,128)(2,1)S(1)} %get-tuple-element.74), channel_id=1, source_target_pairs={{0,16},{16,0},{32,48},{48,32},{64,80},{80,64},{96,112},{112,96},{1... | collective-permute-start | bytes 110600 | tf_op jit(solution)/shard_map/ppermute | solution.py:522
  71.6 4.9 %collective-permute-start.11 = (bf16[336,128]{1,0:T(8,128)(2,1)S(1)}, bf16[336,128]{1,0:T(8,128)(2,1)S(1)}, u32[]{:S(2)}, u32[]{:S(2)}) collective-permute-start(bf16[336,128]{1,0:T(8,128)(2,1)S(1)} %get-tuple-element.75), channel_id=1, source_target_pairs={{0,8},{1,9},{2,10},{3,11},{4,12},{5,13},{6,14},{7,15},{8,0},{9,1},... | collective-permute-start | bytes 258056 | tf_op jit(solution)/shard_map/ppermute | solution.py:522
  76.6 8.5 %collective-permute-start.14 = (bf16[2,336,128]{2,1,0:T(8,128)(2,1)S(1)}, bf16[2,336,128]{2,1,0:T(8,128)(2,1)S(1)}, u32[]{:S(2)}, u32[]{:S(2)}) collective-permute-start(bf16[2,336,128]{2,1,0:T(8,128)(2,1)S(1)} %pad_maximum_fusion.refs_0_), channel_id=1, source_target_pairs={{0,6},{1,7},{2,4},{3,5},{4,2},{5,3},{6,0},{7,1},{8,14},{9,15},{10,... | collective-permute-start | bytes 516104 | tf_op jit(solution)/shard_map/ppermute | solution.py:522
  77.5 10.8 %collective-permute-start.13 = (bf16[2,336,128]{2,1,0:T(8,128)(2,1)S(1)}, bf16[2,336,128]{2,1,0:T(8,128)(2,1)S(1)}, u32[]{:S(2)}, u32[]{:S(2)}) collective-permute-start(bf16[2,336,128]{2,1,0:T(8,128)(2,1)S(1)} %pad_maximum_fusion.refs_0_), channel_id=1, source_target_pairs={{0,4},{1,5},{2,6},{3,7},{4,0},{5,1},{6,2},{7,3},{8,12},{9,13},{10,... | collective-permute-start | bytes 516104 | tf_op jit(solution)/shard_map/ppermute | solution.py:522
  78.7 9.6 %collective-permute-start.12 = (bf16[2,336,128]{2,1,0:T(8,128)(2,1)S(1)}, bf16[2,336,128]{2,1,0:T(8,128)(2,1)S(1)}, u32[]{:S(2)}, u32[]{:S(2)}) collective-permute-start(bf16[2,336,128]{2,1,0:T(8,128)(2,1)S(1)} %pad_maximum_fusion.refs_0_), channel_id=1, source_target_pairs={{0,2},{1,3},{2,0},{3,1},{4,6},{5,7},{6,4},{7,5},{8,10},{9,11},{10,... | collective-permute-start | bytes 516104 | tf_op jit(solution)/shard_map/ppermute | solution.py:522
  79.9 9.0 %collective-permute-start.15 = (bf16[2,336,128]{2,1,0:T(8,128)(2,1)S(1)}, bf16[2,336,128]{2,1,0:T(8,128)(2,1)S(1)}, u32[]{:S(2)}, u32[]{:S(2)}) collective-permute-start(bf16[2,336,128]{2,1,0:T(8,128)(2,1)S(1)} %pad_maximum_fusion.refs_0_), channel_id=1, source_target_pairs={{0,1},{1,0},{2,3},{3,2},{4,5},{5,4},{6,7},{7,6},{8,9},{9,8},{10,11... | collective-permute-start | bytes 516104 | tf_op jit(solution)/shard_map/ppermute | solution.py:522
  85.1 4.3 %collective-permute-start.18 = (bf16[2,336,128]{2,1,0:T(8,128)(2,1)S(1)}, bf16[2,336,128]{2,1,0:T(8,128)(2,1)S(1)}, u32[]{:S(2)}, u32[]{:S(2)}) collective-permute-start(bf16[2,336,128]{2,1,0:T(8,128)(2,1)S(1)} %collective-permute-done.14.refs_3_), channel_id=1, source_target_pairs={{0,1},{1,0},{2,3},{3,2},{4,5},{5,4},{6,7},{7,6},{8,9},{9,8},{10,11... | collective-permute-start | bytes 516104 | tf_op jit(solution)/shard_map/ppermute | solution.py:522
  88.3 1.4 %collective-permute-start.17 = (bf16[2,336,128]{2,1,0:T(8,128)(2,1)S(1)}, bf16[2,336,128]{2,1,0:T(8,128)(2,1)S(1)}, u32[]{:S(2)}, u32[]{:S(2)}) collective-permute-start(bf16[2,336,128]{2,1,0:T(8,128)(2,1)S(1)} %collective-permute-done.13.refs_2_), channel_id=1, source_target_pairs={{0,1},{1,0},{2,3},{3,2},{4,5},{5,4},{6,7},{7,6},{8,9},{9,8},{10,11... | collective-permute-start | bytes 516104 | tf_op jit(solution)/shard_map/ppermute | solution.py:522
  88.3 1.6 %collective-permute-start.16 = (bf16[2,336,128]{2,1,0:T(8,128)(2,1)S(1)}, bf16[2,336,128]{2,1,0:T(8,128)(2,1)S(1)}, u32[]{:S(2)}, u32[]{:S(2)}) collective-permute-start(bf16[2,336,128]{2,1,0:T(8,128)(2,1)S(1)} %collective-permute-done.12.refs_1_), channel_id=1, source_target_pairs={{0,1},{1,0},{2,3},{3,2},{4,5},{5,4},{6,7},{7,6},{8,9},{9,8},{10,11... | collective-permute-start | bytes 516104 | tf_op jit(solution)/shard_map/ppermute | solution.py:522

commit v8 on v7

--- a/solution.py
+++ b/solution.py
@@ -307,8 +307,13 @@
                 patches = term if patches is None else patches + term
     patches_ref[...] = patches
     rounded = patches.astype(BF16)
-    embedded = dot(jnp.concatenate([rounded, rounded], axis=1), embed_ref[...]) + bias_ref[0:1]
-    spread = jnp.sum(embedded * embedded, axis=1, keepdims=True) * (1.0 / D)
+    twice = jnp.concatenate([rounded, rounded], axis=1)
+    spread = jnp.zeros((n, 128), F32)
+    for at in range(0, D, C):
+        embedded = dot(twice, embed_ref[:, at : at + C]) + bias_ref[0:1, at : at + C]
+        embedded = embedded * embedded
+        spread = spread + (embedded[:, 0:128] + embedded[:, 128:256])
+    spread = jnp.sum(spread, axis=1, keepdims=True) * (1.0 / D)
     rstd = lax.rsqrt(spread + EPS)
     scaled = (rounded.astype(F32) * rstd).reshape(FRAMES, 2, 8, 64)
     rstd = jnp.broadcast_to(rstd, (n, 128)).reshape(FRAMES, 2, 8, 128)
@@ -401,7 +406,7 @@
 WIDE = HEADS * HDIM
 
 
-def sort_kernel(place_ref, clip_ref, *refs):
+def sort_folds(place_ref, clip_ref, *refs):
     asks_ref, keys_ref, values_ref, loose, wide = refs[8:]
     seq, clip = place_ref[0], clip_ref[0]
     spot = iota((40, 128), 1)
@@ -431,8 +436,9 @@
             target[:, 256 * side + 128 : 256 * side + 256] = extra.astype(BF16)
 
 
-def attend_kernel(place_ref, *refs):
-    asks_ref, keys_ref, values_ref, out_ref, queries, mixed, scores, weights = refs[8:]
+def attend_kernel(place_ref, clip_ref, *refs):
+    out_ref, asks_ref, keys_ref, values_ref, loose, wide, queries, mixed, scores, weights = refs[8:]
+    sort_folds(place_ref, clip_ref, *refs[:8], asks_ref, keys_ref, values_ref, loose, wide)
     seq = place_ref[0]
     blocks = [refs[4 * (j & 1) + ((j >> 1) & 3)].at[j >> 3] for j in range(SEQ)]
     lane = iota((128, 128), 1)
@@ -637,23 +643,22 @@
     )
     latent = call(latent_kernel, shape(FRAMES, 2, LAT, 2 * HALF, dtype=F32), [VMEM])(patches)
     parcels, latent = gather_seq(parcel, latent)
-    asks, keys, values = call(
-        sort_kernel,
-        [shape(WIDE, 256), shape(WIDE, 512), shape(WIDE, 512)],
-        [SMEM] * 2 + [VMEM] * 8,
-        [pltpu.VMEM((SEQ, 192, 128), F32), pltpu.VMEM((3 * WIDE, 128), F32)],
-    )(place, clip, *parcels)
     frame_heads = call(
         attend_kernel,
         shape(SEQ * HALF, WIDE),
-        [SMEM] + [VMEM] * 11,
+        [SMEM] * 2 + [VMEM] * 8,
         [
+            pltpu.VMEM((WIDE, 256), BF16),
+            pltpu.VMEM((WIDE, 512), BF16),
+            pltpu.VMEM((WIDE, 512), BF16),
+            pltpu.VMEM((SEQ, 192, 128), F32),
+            pltpu.VMEM((3 * WIDE, 128), F32),
             pltpu.VMEM((SEQ, HEADS, HALF, 256), BF16),
             pltpu.VMEM((2, HEADS, 128, 256), F32),
             pltpu.VMEM((SEQ, 128, HEADS * HALF), F32),
             pltpu.VMEM((SEQ, HEADS * HALF, 128), BF16),
         ],
-    )(place, *parcels, asks, keys, values)
+    )(place, clip, *parcels)
     latent = latent.transpose(0, 1, 3, 2).reshape(1, FRAMES, 2, 2 * HALF, LAT)
     return (latent, frame_heads.reshape(1, 1, SEQ * HALF, WIDE))
 

time: 96.8 us -> 95.9 us (level)
    pallas_call x8 -> x7, Pallas kernels: 26.9 us -> 26 us  [run(): kernel(*(pltpu.with_memory_space_constraint(x, pltpu.HBM) if spec is HBM...]
where the time goes in v8:
time: 95.9 us; the launch traced here: 95.6 us
  blocking collectives  27.8 us (29%)
  starting transfers between devices  27.1 us (28%)
  Pallas kernels  26 us (27%)
  waiting for transfers between devices  14 us (15%)
    all_to_all x2, blocking collectives, exchange(): return lax.all_to_all(stats, 'seq', 0, 0, tiled=True)  27.8 us
    pallas_call x7, Pallas kernels, run(): kernel(*(pltpu.with_memory_space_constraint(x, pltpu.HBM) if spec is HBM...  26 us
    ppermute x13, starting transfers between devices, swap(): return lax.ppermute(values, axis, [(i, i ^ bits) for i in range(count)])  15.9 us
    ppermute x13, waiting for transfers between devices, swap(): return lax.ppermute(values, axis, [(i, i ^ bits) for i in range(count)])  10.7 us
    all_to_all x1, starting transfers between devices, exchange(): return lax.all_to_all(stats, 'seq', 0, 0, tiled=True)  6.48 us
    all_to_all x1, waiting for transfers between devices, exchange(): return lax.all_to_all(stats, 'seq', 0, 0, tiled=True)  3.3 us
    ppermute x3, starting transfers between devices, neighbours(): return (lax.ppermute(near, 'seq', CHIP_PAIRS), far)  2.99 us
  transfers between devices with their start and end apart: 20, of which 8 were waited for; matrix products, arithmetic and copies ran while one was open for 0% of the time, Pallas kernels for 2%

profile of v8, /device:TPU:1, one launch (start us, length us, event | category | flops | bytes accessed | tf_op | source)
XLA Modules:
  0.0 95.6 jit_solution(8087375719971570599)
XLA Ops:
  0.6 1.8 %split_kernel.1 = (bf16[1024,256]{1,0:T(8,128)(2,1)S(1)}, bf16[512,256]{1,0:T(8,128)(2,1)S(1)}, bf16[512,256]{1,0:T(8,128)(2,1)S(1)}, f32[16,1,128]{2,1,0:T(1,12...) custom-call(s32[1]{0:T(128)} %bitcast.place_ref, bf16[16,2,32,256]{3,2,1,0:T(8,128)(2,1)} %bitcast.19, ...), custom_call_target="tpu_custom_call" | custom-call | bytes 1048576 | tf_op jit(solution)/shard_map/split_kernel/pallas_call | solution.py:520
  2.4 1.5 %collective-permute-start.1 = (bf16[512,256]{1,0:T(8,128)(2,1)S(1)}, bf16[512,256]{1,0:T(8,128)(2,1)S(1)}, u32[]{:S(2)}, u32[]{:S(2)}) collective-permute-start(bf16[512,256]{1,0:T(8,128)(2,1)S(1)} %get-tuple-element.44), channel_id=1, source_target_pairs={{0,1},{1,0},{2,3},{3,2},{4,5},{5,4},{6,7},{7,6},{8,9},{9,8},{10,11... | collective-permute-start | bytes 786440 | tf_op jit(solution)/shard_map/ppermute | solution.py:537
  3.9 1.3 %collective-permute-start.2 = (bf16[512,256]{1,0:T(8,128)(2,1)S(1)}, bf16[512,256]{1,0:T(8,128)(2,1)S(1)}, u32[]{:S(2)}, u32[]{:S(2)}) collective-permute-start(bf16[512,256]{1,0:T(8,128)(2,1)S(1)} %get-tuple-element.45), channel_id=1, source_target_pairs={{0,15},{1,2},{2,1},{3,4},{4,3},{5,6},{6,5},{7,8},{8,7},{9,10},{10,... | collective-permute-start | bytes 786440 | tf_op jit(solution)/shard_map/ppermute | solution.py:536
  5.2 1.6 %collective-permute-start = (f32[2,3072]{1,0:T(2,128)S(1)}, f32[2,3072]{1,0:T(2,128)S(1)}, u32[]{:S(2)}, u32[]{:S(2)}) collective-permute-start(f32[2,3072]{1,0:T(2,128)S(1)} %get-tuple-element.40.own_mods_ref), channel_id=1, source_target_pairs={{0,16},{16,0},{32,48},{48,32},{64,80},{80,64},{96,112},{112,96},{1... | collective-permute-start | bytes 73736 | tf_op jit(solution)/shard_map/ppermute | solution.py:528
  6.8 13.9 %all_to_all.15.stats_ref = f32[16,1,128]{2,1,0:T(1,128)S(1)} all-to-all(f32[16,1,128]{2,1,0:T(1,128)S(1)} %get-tuple-element.39), channel_id=1, replica_groups=mesh['clip'=8,'seq'=16] {'seq'}, dimensions={0} | all-to-all | bytes 16384 | tf_op jit(solution)/shard_map/all_to_all | solution.py:541
  20.8 6.8 %first_kernel.1 = (bf16[1024,256]{1,0:T(8,128)(2,1)}, f32[8,256]{1,0:T(8,128)S(1)}, bf16[528,256]{1,0:T(8,128)(2,1)S(1)}, bf16[528,256]{1,0:T(8,128)(2,1)S(1)}, f32[16,1,128]{2,1,0:T(1,128)}) custom-call(s32[1]{0:T(128)} %bitcast.place_ref, f32[16,1,128]{2,1,0:T(1,128)S(1)} %all_to_all.15.stats_ref, ...), custom_call_target="tpu_custom_call" | custom-call | flops 3623878656 | bytes 5242880 | tf_op jit(solution)/shard_map/first_kernel/pallas_call | solution.py:520
  27.6 0.7 collective-permute-start.6
  28.6 2.7 %collective-permute-start.5 = (bf16[36,3072]{1,0:T(8,128)(2,1)S(1)}, bf16[36,3072]{1,0:T(8,128)(2,1)S(1)}, u32[]{:S(2)}, u32[]{:S(2)}) collective-permute-start(bf16[36,3072]{1,0:T(8,128)(2,1)S(1)} %copy-done.1), channel_id=1, source_target_pairs={{0,96},{16,112},{32,64},{48,80},{64,32},{80,48},{96,0},{112,16},{1... | collective-permute-start | bytes 663560 | tf_op jit(solution)/shard_map/ppermute | solution.py:528
  31.9 6.5 %all-to-all-start.1 = ((f32[16,1,128]{2,1,0:T(1,128)}), f32[16,1,128]{2,1,0:T(1,128)S(1)}, u32[]{:S(2)}, u32[]{:S(2)}) async-start(f32[16,1,128]{2,1,0:T(1,128)} %get-tuple-element.47), calls=%async_computation.1 | async-start | bytes 16384 | tf_op jit(solution)/shard_map/all_to_all | solution.py:541
  38.4 3.5 %collective-permute-done.5.w3_ref = bf16[36,3072]{1,0:T(8,128)(2,1)S(1)} collective-permute-done((bf16[36,3072]{1,0:T(8,128)(2,1)S(1)}, bf16[36,3072]{1,0:T(8,128)(2,1)S(1)}, u32[]{:S(2)}, u32[]{:S(2)}) %collective-permute-start.5) | collective-permute-done | bytes 221216 | tf_op jit(solution)/shard_map/ppermute | solution.py:528
  42.0 3.3 %all-to-all-done.1.stats_ref = f32[16,1,128]{2,1,0:T(1,128)S(1)} async-done(((f32[16,1,128]{2,1,0:T(1,128)}), f32[16,1,128]{2,1,0:T(1,128)S(1)}, u32[]{:S(2)}, u32[]{:S(2)}) %all-to-all-start.1) | async-done | bytes 8224 | tf_op jit(solution)/shard_map/all_to_all | solution.py:541
  45.3 5.9 %second_kernel.1 = (bf16[1024,256]{1,0:T(8,128)(2,1)S(1)}, bf16[512,256]{1,0:T(8,128)(2,1)S(1)}, bf16[512,256]{1,0:T(8,128)(2,1)S(1)}, f32[16,1,128]{2,1,0:T(1,128)S(1)}) custom-call(s32[1]{0:T(128)} %bitcast.place_ref, f32[16,1,128]{2,1,0:T(1,128)S(1)} %all-to-all-done.1.stats_ref, bf16[1024,256]{1,0:T(8,128)(2,1)} %get-tuple-element.50.hidden_hbm, ...), custom_call_target="tpu_custom_call" | custom-call | flops 3623878656 | bytes 6291456 | tf_op jit(solution)/shard_map/second_kernel/pallas_call | solution.py:520
  52.2 1.0 %fold_kernel.1 = (bf16[144,128]{1,0:T(8,128)(2,1)S(1)}, bf16[144,128]{1,0:T(8,128)(2,1)S(1)}, bf16[128,3072]{1,0:T(8,128)(2,1)S(1)}, f32[8,3072]{1,0:T(8,128)S(1)}) custom-call(bf16[36,3072]{1,0:T(8,128)(2,1)S(1)} %copy-done.1, bf16[36,3072]{1,0:T(8,128)(2,1)S(1)} %collective-permute-done.3.w1_ref, bf16[36,3072]{1,0:T(8,128)(2,1)S(1)} %collective-permute-done.4.w2_ref, ...), custom_call_target="tpu_custom_call" | custom-call | tf_op jit(solution)/shard_map/fold_kernel/pallas_call | solution.py:520
  53.9 13.9 %all_to_all.16.stats_ref = f32[16,1,128]{2,1,0:T(1,128)S(1)} all-to-all(f32[16,1,128]{2,1,0:T(1,128)S(1)} %get-tuple-element.59), channel_id=1, replica_groups=mesh['clip'=8,'seq'=16] {'seq'}, dimensions={0} | all-to-all | bytes 16384 | tf_op jit(solution)/shard_map/all_to_all | solution.py:541
  67.8 3.8 %third_kernel.1 = (f32[256,64]{1,0:T(8,128)S(1)}, bf16[336,128]{1,0:T(8,128)(2,1)S(1)}) custom-call(s32[1]{0:T(128)} %bitcast.place_ref, f32[16,1,128]{2,1,0:T(1,128)S(1)} %all_to_all.16.stats_ref, bf16[1024,256]{1,0:T(8,128)(2,1)S(1)} %get-tuple-element.60.rows_ref, bf16[512,256]{1,0:T(8,128)(2,1)S(1)} %collective-permute-done.8.near_ref, ...), custom_call_target="tpu_custom_call" | custom-call | flops 1811939328 | bytes 4194304 | tf_op jit(solution)/shard_map/third_kernel/pallas_call | solution.py:520
  72.0 1.1 %latent_kernel.1 = f32[16,2,16,32]{3,2,1,0:T(8,128)} custom-call(f32[256,64]{1,0:T(8,128)S(1)} %get-tuple-element.73.patches_ref), custom_call_target="tpu_custom_call" | custom-call | tf_op jit(solution)/shard_map/latent_kernel/pallas_call | solution.py:520
  73.1 3.5 %collective-permute-done.11 = bf16[336,128]{1,0:T(8,128)(2,1)S(1)} collective-permute-done((bf16[336,128]{1,0:T(8,128)(2,1)S(1)}, bf16[336,128]{1,0:T(8,128)(2,1)S(1)}, u32[]{:S(2)}, u32[]{:S(2)}) %collective-permute-start.11) | collective-permute-done | bytes 86048 | tf_op jit(solution)/shard_map/ppermute | solution.py:528
  76.6 1.0 %collective-permute-start.14 = (bf16[2,336,128]{2,1,0:T(8,128)(2,1)S(1)}, bf16[2,336,128]{2,1,0:T(8,128)(2,1)S(1)}, u32[]{:S(2)}, u32[]{:S(2)}) collective-permute-start(bf16[2,336,128]{2,1,0:T(8,128)(2,1)S(1)} %pad_maximum_fusion.refs_0_), channel_id=1, source_target_pairs={{0,6},{1,7},{2,4},{3,5},{4,2},{5,3},{6,0},{7,1},{8,14},{9,15},{10,... | collective-permute-start | bytes 516104 | tf_op jit(solution)/shard_map/ppermute | solution.py:528
  77.5 1.2 %collective-permute-start.13 = (bf16[2,336,128]{2,1,0:T(8,128)(2,1)S(1)}, bf16[2,336,128]{2,1,0:T(8,128)(2,1)S(1)}, u32[]{:S(2)}, u32[]{:S(2)}) collective-permute-start(bf16[2,336,128]{2,1,0:T(8,128)(2,1)S(1)} %pad_maximum_fusion.refs_0_), channel_id=1, source_target_pairs={{0,4},{1,5},{2,6},{3,7},{4,0},{5,1},{6,2},{7,3},{8,12},{9,13},{10,... | collective-permute-start | bytes 516104 | tf_op jit(solution)/shard_map/ppermute | solution.py:528
  78.7 1.2 %collective-permute-start.12 = (bf16[2,336,128]{2,1,0:T(8,128)(2,1)S(1)}, bf16[2,336,128]{2,1,0:T(8,128)(2,1)S(1)}, u32[]{:S(2)}, u32[]{:S(2)}) collective-permute-start(bf16[2,336,128]{2,1,0:T(8,128)(2,1)S(1)} %pad_maximum_fusion.refs_0_), channel_id=1, source_target_pairs={{0,2},{1,3},{2,0},{3,1},{4,6},{5,7},{6,4},{7,5},{8,10},{9,11},{10,... | collective-permute-start | bytes 516104 | tf_op jit(solution)/shard_map/ppermute | solution.py:528
  79.9 2.7 %collective-permute-start.15 = (bf16[2,336,128]{2,1,0:T(8,128)(2,1)S(1)}, bf16[2,336,128]{2,1,0:T(8,128)(2,1)S(1)}, u32[]{:S(2)}, u32[]{:S(2)}) collective-permute-start(bf16[2,336,128]{2,1,0:T(8,128)(2,1)S(1)} %pad_maximum_fusion.refs_0_), channel_id=1, source_target_pairs={{0,1},{1,0},{2,3},{3,2},{4,5},{5,4},{6,7},{7,6},{8,9},{9,8},{10,11... | collective-permute-start | bytes 516104 | tf_op jit(solution)/shard_map/ppermute | solution.py:528
  82.6 2.5 %collective-permute-done.14.refs_3_ = bf16[2,336,128]{2,1,0:T(8,128)(2,1)S(1)} collective-permute-done((bf16[2,336,128]{2,1,0:T(8,128)(2,1)S(1)}, bf16[2,336,128]{2,1,0:T(8,128)(2,1)S(1)}, u32[]{:S(2)}, u32[]{:S(2)}) %collective-permute-start.14) | collective-permute-done | bytes 172064 | tf_op jit(solution)/shard_map/ppermute | solution.py:528
  85.1 3.3 %collective-permute-start.18 = (bf16[2,336,128]{2,1,0:T(8,128)(2,1)S(1)}, bf16[2,336,128]{2,1,0:T(8,128)(2,1)S(1)}, u32[]{:S(2)}, u32[]{:S(2)}) collective-permute-start(bf16[2,336,128]{2,1,0:T(8,128)(2,1)S(1)} %collective-permute-done.14.refs_3_), channel_id=1, source_target_pairs={{0,1},{1,0},{2,3},{3,2},{4,5},{5,4},{6,7},{7,6},{8,9},{9,8},{10,11... | collective-permute-start | bytes 516104 | tf_op jit(solution)/shard_map/ppermute | solution.py:528
  90.0 5.6 %attend_kernel.1 = bf16[256,1536]{1,0:T(8,128)(2,1)} custom-call(s32[1]{0:T(128)} %bitcast.place_ref, s32[1]{0:T(128)} %bitcast.9.clip_ref, bf16[2,336,128]{2,1,0:T(8,128)(2,1)S(1)} %pad_maximum_fusion.refs_0_, bf16[2,336,128]{2,1,0:T(8,128)(2,1)S(1)} %collective-permute-done.12.refs_1_, bf16[2,336,128]{2,1,0:T(8,128)(2,1)S(1)} %collective-permute-done.13.refs_2_, ...), custom_call_target="tpu_custom_call" | custom-call | tf_op jit(solution)/shard_map/attend_kernel/pallas_call | solution.py:520
  (34 shorter events, 4.7 us)
Async XLA Ops:
  2.4 18.3 %collective-permute-start.1 = (bf16[512,256]{1,0:T(8,128)(2,1)S(1)}, bf16[512,256]{1,0:T(8,128)(2,1)S(1)}, u32[]{:S(2)}, u32[]{:S(2)}) collective-permute-start(bf16[512,256]{1,0:T(8,128)(2,1)S(1)} %get-tuple-element.44), channel_id=1, source_target_pairs={{0,1},{1,0},{2,3},{3,2},{4,5},{5,4},{6,7},{7,6},{8,9},{9,8},{10,11... | collective-permute-start | bytes 786440 | tf_op jit(solution)/shard_map/ppermute | solution.py:537
  3.9 16.8 %collective-permute-start.2 = (bf16[512,256]{1,0:T(8,128)(2,1)S(1)}, bf16[512,256]{1,0:T(8,128)(2,1)S(1)}, u32[]{:S(2)}, u32[]{:S(2)}) collective-permute-start(bf16[512,256]{1,0:T(8,128)(2,1)S(1)} %get-tuple-element.45), channel_id=1, source_target_pairs={{0,15},{1,2},{2,1},{3,4},{4,3},{5,6},{6,5},{7,8},{8,7},{9,10},{10,... | collective-permute-start | bytes 786440 | tf_op jit(solution)/shard_map/ppermute | solution.py:536
  5.2 15.6 %collective-permute-start = (f32[2,3072]{1,0:T(2,128)S(1)}, f32[2,3072]{1,0:T(2,128)S(1)}, u32[]{:S(2)}, u32[]{:S(2)}) collective-permute-start(f32[2,3072]{1,0:T(2,128)S(1)} %get-tuple-element.40.own_mods_ref), channel_id=1, source_target_pairs={{0,16},{16,0},{32,48},{48,32},{64,80},{80,64},{96,112},{112,96},{1... | collective-permute-start | bytes 73736 | tf_op jit(solution)/shard_map/ppermute | solution.py:528
  20.8 7.8 %copy-start.1 = (bf16[36,3072]{1,0:T(8,128)(2,1)S(1)}, bf16[36,3072]{1,0:T(8,128)(2,1)}, u32[]{:S(2)}) copy-start(bf16[36,3072]{1,0:T(8,128)(2,1)} %w0_ref) | copy-start | bytes 663556
  27.6 17.7 %collective-permute-start.6 = (bf16[528,256]{1,0:T(8,128)(2,1)S(1)}, bf16[528,256]{1,0:T(8,128)(2,1)S(1)}, u32[]{:S(2)}, u32[]{:S(2)}) collective-permute-start(bf16[528,256]{1,0:T(8,128)(2,1)S(1)} %get-tuple-element.52), channel_id=1, source_target_pairs={{0,1},{1,0},{2,3},{3,2},{4,5},{5,4},{6,7},{7,6},{8,9},{9,8},{10,11... | collective-permute-start | bytes 811016 | tf_op jit(solution)/shard_map/ppermute | solution.py:537
  28.3 17.0 %collective-permute-start.7 = (bf16[528,256]{1,0:T(8,128)(2,1)S(1)}, bf16[528,256]{1,0:T(8,128)(2,1)S(1)}, u32[]{:S(2)}, u32[]{:S(2)}) collective-permute-start(bf16[528,256]{1,0:T(8,128)(2,1)S(1)} %get-tuple-element.53), channel_id=1, source_target_pairs={{0,15},{1,2},{2,1},{3,4},{4,3},{5,6},{6,5},{7,8},{8,7},{9,10},{10,... | collective-permute-start | bytes 811016 | tf_op jit(solution)/shard_map/ppermute | solution.py:536
  28.6 13.3 %collective-permute-start.5 = (bf16[36,3072]{1,0:T(8,128)(2,1)S(1)}, bf16[36,3072]{1,0:T(8,128)(2,1)S(1)}, u32[]{:S(2)}, u32[]{:S(2)}) collective-permute-start(bf16[36,3072]{1,0:T(8,128)(2,1)S(1)} %copy-done.1), channel_id=1, source_target_pairs={{0,96},{16,112},{32,64},{48,80},{64,32},{80,48},{96,0},{112,16},{1... | collective-permute-start | bytes 663560 | tf_op jit(solution)/shard_map/ppermute | solution.py:528
  31.3 10.6 %collective-permute-start.4 = (bf16[36,3072]{1,0:T(8,128)(2,1)S(1)}, bf16[36,3072]{1,0:T(8,128)(2,1)S(1)}, u32[]{:S(2)}, u32[]{:S(2)}) collective-permute-start(bf16[36,3072]{1,0:T(8,128)(2,1)S(1)} %copy-done.1), channel_id=1, source_target_pairs={{0,64},{16,80},{32,96},{48,112},{64,0},{80,16},{96,32},{112,48},{1... | collective-permute-start | bytes 663560 | tf_op jit(solution)/shard_map/ppermute | solution.py:528
  31.7 10.3 %collective-permute-start.3 = (bf16[36,3072]{1,0:T(8,128)(2,1)S(1)}, bf16[36,3072]{1,0:T(8,128)(2,1)S(1)}, u32[]{:S(2)}, u32[]{:S(2)}) collective-permute-start(bf16[36,3072]{1,0:T(8,128)(2,1)S(1)} %copy-done.1), channel_id=1, source_target_pairs={{0,32},{16,48},{32,0},{48,16},{64,96},{80,112},{96,64},{112,80},{1... | collective-permute-start | bytes 663560 | tf_op jit(solution)/shard_map/ppermute | solution.py:528
  31.9 13.4 %all-to-all-start.1 = ((f32[16,1,128]{2,1,0:T(1,128)}), f32[16,1,128]{2,1,0:T(1,128)S(1)}, u32[]{:S(2)}, u32[]{:S(2)}) async-start(f32[16,1,128]{2,1,0:T(1,128)} %get-tuple-element.47), calls=%async_computation.1 | async-start | bytes 16384 | tf_op jit(solution)/shard_map/all_to_all | solution.py:541
  45.3 6.9 %copy-start = (bf16[64,3072]{1,0:T(8,128)(2,1)S(1)}, bf16[64,3072]{1,0:T(8,128)(2,1)}, u32[]{:S(2)}) copy-start(bf16[64,3072]{1,0:T(8,128)(2,1)} %embed_ref.1) | copy-start | bytes 1179652
  45.3 6.9 %copy-start.2 = (f32[3072]{0:T(1024)S(1)}, f32[3072]{0:T(1024)}, u32[]{:S(2)}) copy-start(f32[3072]{0:T(1024)} %param.18) | copy-start | bytes 36868
  45.3 22.5 %copy-start.3 = (bf16[3,3,3,256,16]{3,4,2,1,0:T(8,128)(2,1)S(1)}, bf16[3,3,3,256,16]{3,4,2,1,0:T(8,128)(2,1)}, u32[]{:S(2)}) copy-start(bf16[3,3,3,256,16]{3,4,2,1,0:T(8,128)(2,1)} %param.14) | copy-start | bytes 663556
  51.2 16.6 %collective-permute-start.8 = (bf16[512,256]{1,0:T(8,128)(2,1)S(1)}, bf16[512,256]{1,0:T(8,128)(2,1)S(1)}, u32[]{:S(2)}, u32[]{:S(2)}) collective-permute-start(bf16[512,256]{1,0:T(8,128)(2,1)S(1)} %get-tuple-element.61), channel_id=1, source_target_pairs={{0,1},{1,0},{2,3},{3,2},{4,5},{5,4},{6,7},{7,6},{8,9},{9,8},{10,11... | collective-permute-start | bytes 786440 | tf_op jit(solution)/shard_map/ppermute | solution.py:537
  52.0 15.8 %collective-permute-start.9 = (bf16[512,256]{1,0:T(8,128)(2,1)S(1)}, bf16[512,256]{1,0:T(8,128)(2,1)S(1)}, u32[]{:S(2)}, u32[]{:S(2)}) collective-permute-start(bf16[512,256]{1,0:T(8,128)(2,1)S(1)} %get-tuple-element.62), channel_id=1, source_target_pairs={{0,15},{1,2},{2,1},{3,4},{4,3},{5,6},{6,5},{7,8},{8,7},{9,10},{10,... | collective-permute-start | bytes 786440 | tf_op jit(solution)/shard_map/ppermute | solution.py:536
  53.2 14.6 %collective-permute-start.10 = (bf16[144,128]{1,0:T(8,128)(2,1)S(1)}, bf16[144,128]{1,0:T(8,128)(2,1)S(1)}, u32[]{:S(2)}, u32[]{:S(2)}) collective-permute-start(bf16[144,128]{1,0:T(8,128)(2,1)S(1)} %get-tuple-element.71), channel_id=1, source_target_pairs={{0,16},{16,0},{32,48},{48,32},{64,80},{80,64},{96,112},{112,96},{1... | collective-permute-start | bytes 110600 | tf_op jit(solution)/shard_map/ppermute | solution.py:528
  71.6 4.9 %collective-permute-start.11 = (bf16[336,128]{1,0:T(8,128)(2,1)S(1)}, bf16[336,128]{1,0:T(8,128)(2,1)S(1)}, u32[]{:S(2)}, u32[]{:S(2)}) collective-permute-start(bf16[336,128]{1,0:T(8,128)(2,1)S(1)} %get-tuple-element.72), channel_id=1, source_target_pairs={{0,8},{1,9},{2,10},{3,11},{4,12},{5,13},{6,14},{7,15},{8,0},{9,1},... | collective-permute-start | bytes 258056 | tf_op jit(solution)/shard_map/ppermute | solution.py:528
  76.6 8.5 %collective-permute-start.14 = (bf16[2,336,128]{2,1,0:T(8,128)(2,1)S(1)}, bf16[2,336,128]{2,1,0:T(8,128)(2,1)S(1)}, u32[]{:S(2)}, u32[]{:S(2)}) collective-permute-start(bf16[2,336,128]{2,1,0:T(8,128)(2,1)S(1)} %pad_maximum_fusion.refs_0_), channel_id=1, source_target_pairs={{0,6},{1,7},{2,4},{3,5},{4,2},{5,3},{6,0},{7,1},{8,14},{9,15},{10,... | collective-permute-start | bytes 516104 | tf_op jit(solution)/shard_map/ppermute | solution.py:528
  77.5 10.8 %collective-permute-start.13 = (bf16[2,336,128]{2,1,0:T(8,128)(2,1)S(1)}, bf16[2,336,128]{2,1,0:T(8,128)(2,1)S(1)}, u32[]{:S(2)}, u32[]{:S(2)}) collective-permute-start(bf16[2,336,128]{2,1,0:T(8,128)(2,1)S(1)} %pad_maximum_fusion.refs_0_), channel_id=1, source_target_pairs={{0,4},{1,5},{2,6},{3,7},{4,0},{5,1},{6,2},{7,3},{8,12},{9,13},{10,... | collective-permute-start | bytes 516104 | tf_op jit(solution)/shard_map/ppermute | solution.py:528
  78.7 9.6 %collective-permute-start.12 = (bf16[2,336,128]{2,1,0:T(8,128)(2,1)S(1)}, bf16[2,336,128]{2,1,0:T(8,128)(2,1)S(1)}, u32[]{:S(2)}, u32[]{:S(2)}) collective-permute-start(bf16[2,336,128]{2,1,0:T(8,128)(2,1)S(1)} %pad_maximum_fusion.refs_0_), channel_id=1, source_target_pairs={{0,2},{1,3},{2,0},{3,1},{4,6},{5,7},{6,4},{7,5},{8,10},{9,11},{10,... | collective-permute-start | bytes 516104 | tf_op jit(solution)/shard_map/ppermute | solution.py:528
  79.9 9.0 %collective-permute-start.15 = (bf16[2,336,128]{2,1,0:T(8,128)(2,1)S(1)}, bf16[2,336,128]{2,1,0:T(8,128)(2,1)S(1)}, u32[]{:S(2)}, u32[]{:S(2)}) collective-permute-start(bf16[2,336,128]{2,1,0:T(8,128)(2,1)S(1)} %pad_maximum_fusion.refs_0_), channel_id=1, source_target_pairs={{0,1},{1,0},{2,3},{3,2},{4,5},{5,4},{6,7},{7,6},{8,9},{9,8},{10,11... | collective-permute-start | bytes 516104 | tf_op jit(solution)/shard_map/ppermute | solution.py:528
  85.1 4.3 %collective-permute-start.18 = (bf16[2,336,128]{2,1,0:T(8,128)(2,1)S(1)}, bf16[2,336,128]{2,1,0:T(8,128)(2,1)S(1)}, u32[]{:S(2)}, u32[]{:S(2)}) collective-permute-start(bf16[2,336,128]{2,1,0:T(8,128)(2,1)S(1)} %collective-permute-done.14.refs_3_), channel_id=1, source_target_pairs={{0,1},{1,0},{2,3},{3,2},{4,5},{5,4},{6,7},{7,6},{8,9},{9,8},{10,11... | collective-permute-start | bytes 516104 | tf_op jit(solution)/shard_map/ppermute | solution.py:528
  88.3 1.4 %collective-permute-start.17 = (bf16[2,336,128]{2,1,0:T(8,128)(2,1)S(1)}, bf16[2,336,128]{2,1,0:T(8,128)(2,1)S(1)}, u32[]{:S(2)}, u32[]{:S(2)}) collective-permute-start(bf16[2,336,128]{2,1,0:T(8,128)(2,1)S(1)} %collective-permute-done.13.refs_2_), channel_id=1, source_target_pairs={{0,1},{1,0},{2,3},{3,2},{4,5},{5,4},{6,7},{7,6},{8,9},{9,8},{10,11... | collective-permute-start | bytes 516104 | tf_op jit(solution)/shard_map/ppermute | solution.py:528
  88.3 1.6 %collective-permute-start.16 = (bf16[2,336,128]{2,1,0:T(8,128)(2,1)S(1)}, bf16[2,336,128]{2,1,0:T(8,128)(2,1)S(1)}, u32[]{:S(2)}, u32[]{:S(2)}) collective-permute-start(bf16[2,336,128]{2,1,0:T(8,128)(2,1)S(1)} %collective-permute-done.12.refs_1_), channel_id=1, source_target_pairs={{0,1},{1,0},{2,3},{3,2},{4,5},{5,4},{6,7},{7,6},{8,9},{9,8},{10,11... | collective-permute-start | bytes 516104 | tf_op jit(solution)/shard_map/ppermute | solution.py:528

commit v9 on v8

--- a/solution.py
+++ b/solution.py
@@ -254,11 +254,17 @@
 
 def second_kernel(
     place_ref, stats_ref, hidden_hbm, center_ref, near_ref, far_ref, norms_ref, feat_ref, weight_hbm,
-    block_ref, near_out, far_out, stats_out, window, weight, total, hidden_ref, sems,
+    w0_ref, w1_ref, w2_ref, w3_ref, embed_ref, bias_ref, own_mods_ref, mods_ref,
+    block_ref, near_out, far_out, stats_out, own_out, other_out, embed_out, bias_out,
+    window, weight, total, hidden_ref, sems, stacked, wide,
 ):
     load = pltpu.make_async_copy(hidden_hbm, hidden_ref, sems.at[3])
     load.start()
     copies = start_weights(weight_hbm, weight, sems)
+    fold_kernel(
+        w0_ref, w1_ref, w2_ref, w3_ref, embed_ref, bias_ref, own_mods_ref, mods_ref,
+        own_out, other_out, embed_out, bias_out, stacked, wide,
+    )
     own = center_ref[0:1]
     centers = [jnp.sum(ref[ROW : ROW + 16].astype(F32), axis=0, keepdims=True) for ref in (near_ref, far_ref)]
     centers += [own, own]
@@ -611,23 +617,19 @@
     stats1 = exchange(stats1)
     stats1, *rows = lax.optimization_barrier((stats1, *rows))
 
-    block, near_b, far_b, stats2 = call(
+    folded = shape(4 * QROWS, 128)
+    block, near_b, far_b, stats2, own, other, embed, bias = call(
         second_kernel,
-        [cells, row, row, stats],
-        [SMEM, VMEM, HBM] + [VMEM] * 5 + [HBM],
-        [WINDOW, WEIGHT, pltpu.VMEM((CELLS, C), F32), pltpu.VMEM((CELLS, C), BF16), DMA((4,))],
+        [cells, row, row, stats, folded, folded, shape(128, D), shape(8, D, dtype=F32)],
+        [SMEM, VMEM, HBM] + [VMEM] * 5 + [HBM] + [VMEM] * 8,
+        [WINDOW, WEIGHT, pltpu.VMEM((CELLS, C), F32), pltpu.VMEM((CELLS, C), BF16), DMA((4,)),
+            pltpu.VMEM((4 * QPAD, D), BF16), pltpu.VMEM((4 * QROWS, 128), F32),
+        ],
         CONV_FLOPS,
         6 << 20,
-    )(place, stats1, hidden, center, near, far, norms, rows_f, second_conv.reshape(taps, C, C))
+    )(place, stats1, hidden, center, near, far, norms, rows_f, second_conv.reshape(taps, C, C), *rows, embed_weight, embed_bias.reshape(1, D), own_mods, mods)
     near, far = neighbours(near_b, far_b)
     stats2, *rows = lax.optimization_barrier((stats2, *rows))
-    folded = shape(4 * QROWS, 128)
-    own, other, embed, bias = call(
-        fold_kernel,
-        [folded, folded, shape(128, D), shape(8, D, dtype=F32)],
-        [VMEM] * 8,
-        [pltpu.VMEM((4 * QPAD, D), BF16), pltpu.VMEM((4 * QROWS, 128), F32)],
-    )(*rows, embed_weight, embed_bias.reshape(1, D), own_mods, mods)
     other = swap(other, "clip", 1, CLIPS)
     stats2 = exchange(stats2)
     patches, parcel = call(

time: 95.9 us -> 98.3 us (1.025)
  Pallas kernels: 26 us -> 28.4 us
    pallas_call x7 -> x6, Pallas kernels: 26 us -> 28.4 us  [run(): kernel(*(pltpu.with_memory_space_constraint(x, pltpu.HBM) if spec is HBM...]
  transfers between devices with their start and end apart: 20 -> 20, of which waited for: 8 -> 8; matrix products, arithmetic and copies ran while one was open for 0% -> 0% of each run, Pallas kernels for 2% -> 1%
where the time goes in v9:
time: 98.3 us; the launch traced here: 98 us
  Pallas kernels  28.4 us (29%)
  blocking collectives  27.8 us (28%)
  starting transfers between devices  27.1 us (28%)
  waiting for transfers between devices  14 us (14%)
    pallas_call x6, Pallas kernels, run(): kernel(*(pltpu.with_memory_space_constraint(x, pltpu.HBM) if spec is HBM...  28.4 us
    all_to_all x2, blocking collectives, exchange(): return lax.all_to_all(stats, 'seq', 0, 0, tiled=True)  27.8 us
    ppermute x13, starting transfers between devices, swap(): return lax.ppermute(values, axis, [(i, i ^ bits) for i in range(count)])  15.8 us
    ppermute x13, waiting for transfers between devices, swap(): return lax.ppermute(values, axis, [(i, i ^ bits) for i in range(count)])  10.7 us
    all_to_all x1, starting transfers between devices, exchange(): return lax.all_to_all(stats, 'seq', 0, 0, tiled=True)  6.48 us
    all_to_all x1, waiting for transfers between devices, exchange(): return lax.all_to_all(stats, 'seq', 0, 0, tiled=True)  3.3 us
    ppermute x3, starting transfers between devices, neighbours(): return (lax.ppermute(near, 'seq', CHIP_PAIRS), far)  3 us
  transfers between devices with their start and end apart: 20, of which 8 were waited for; matrix products, arithmetic and copies ran while one was open for 0% of the time, Pallas kernels for 1%

profile of v9, /device:TPU:1, one launch (start us, length us, event | category | flops | bytes accessed | tf_op | source)
XLA Modules:
  0.0 98.0 jit_solution(11625146647951549197)
XLA Ops:
  0.6 1.8 %split_kernel.1 = (bf16[1024,256]{1,0:T(8,128)(2,1)S(1)}, bf16[512,256]{1,0:T(8,128)(2,1)S(1)}, bf16[512,256]{1,0:T(8,128)(2,1)S(1)}, f32[16,1,128]{2,1,0:T(1,12...) custom-call(s32[1]{0:T(128)} %bitcast.place_ref, bf16[16,2,32,256]{3,2,1,0:T(8,128)(2,1)} %bitcast.19, ...), custom_call_target="tpu_custom_call" | custom-call | bytes 1048576 | tf_op jit(solution)/shard_map/split_kernel/pallas_call | solution.py:526
  2.4 1.5 %collective-permute-start.1 = (bf16[512,256]{1,0:T(8,128)(2,1)S(1)}, bf16[512,256]{1,0:T(8,128)(2,1)S(1)}, u32[]{:S(2)}, u32[]{:S(2)}) collective-permute-start(bf16[512,256]{1,0:T(8,128)(2,1)S(1)} %get-tuple-element.40), channel_id=1, source_target_pairs={{0,1},{1,0},{2,3},{3,2},{4,5},{5,4},{6,7},{7,6},{8,9},{9,8},{10,11... | collective-permute-start | bytes 786440 | tf_op jit(solution)/shard_map/ppermute | solution.py:543
  3.9 1.3 %collective-permute-start.2 = (bf16[512,256]{1,0:T(8,128)(2,1)S(1)}, bf16[512,256]{1,0:T(8,128)(2,1)S(1)}, u32[]{:S(2)}, u32[]{:S(2)}) collective-permute-start(bf16[512,256]{1,0:T(8,128)(2,1)S(1)} %get-tuple-element.41), channel_id=1, source_target_pairs={{0,15},{1,2},{2,1},{3,4},{4,3},{5,6},{6,5},{7,8},{8,7},{9,10},{10,... | collective-permute-start | bytes 786440 | tf_op jit(solution)/shard_map/ppermute | solution.py:542
  5.2 1.6 %collective-permute-start = (f32[2,3072]{1,0:T(2,128)S(1)}, f32[2,3072]{1,0:T(2,128)S(1)}, u32[]{:S(2)}, u32[]{:S(2)}) collective-permute-start(f32[2,3072]{1,0:T(2,128)S(1)} %get-tuple-element.36.own_mods_ref), channel_id=1, source_target_pairs={{0,16},{16,0},{32,48},{48,32},{64,80},{80,64},{96,112},{112,96},{1... | collective-permute-start | bytes 73736 | tf_op jit(solution)/shard_map/ppermute | solution.py:534
  6.8 13.9 %all_to_all.15.stats_ref = f32[16,1,128]{2,1,0:T(1,128)S(1)} all-to-all(f32[16,1,128]{2,1,0:T(1,128)S(1)} %get-tuple-element.35), channel_id=1, replica_groups=mesh['clip'=8,'seq'=16] {'seq'}, dimensions={0} | all-to-all | bytes 16384 | tf_op jit(solution)/shard_map/all_to_all | solution.py:547
  20.8 6.8 %first_kernel.1 = (bf16[1024,256]{1,0:T(8,128)(2,1)}, f32[8,256]{1,0:T(8,128)S(1)}, bf16[528,256]{1,0:T(8,128)(2,1)S(1)}, bf16[528,256]{1,0:T(8,128)(2,1)S(1)}, f32[16,1,128]{2,1,0:T(1,128)}) custom-call(s32[1]{0:T(128)} %bitcast.place_ref, f32[16,1,128]{2,1,0:T(1,128)S(1)} %all_to_all.15.stats_ref, ...), custom_call_target="tpu_custom_call" | custom-call | flops 3623878656 | bytes 5242880 | tf_op jit(solution)/shard_map/first_kernel/pallas_call | solution.py:526
  27.6 0.7 collective-permute-start.6
  28.7 2.7 %collective-permute-start.5 = (bf16[36,3072]{1,0:T(8,128)(2,1)S(1)}, bf16[36,3072]{1,0:T(8,128)(2,1)S(1)}, u32[]{:S(2)}, u32[]{:S(2)}) collective-permute-start(bf16[36,3072]{1,0:T(8,128)(2,1)S(1)} %copy-done.1), channel_id=1, source_target_pairs={{0,96},{16,112},{32,64},{48,80},{64,32},{80,48},{96,0},{112,16},{1... | collective-permute-start | bytes 663560 | tf_op jit(solution)/shard_map/ppermute | solution.py:534
  32.0 6.5 %all-to-all-start.1 = ((f32[16,1,128]{2,1,0:T(1,128)}), f32[16,1,128]{2,1,0:T(1,128)S(1)}, u32[]{:S(2)}, u32[]{:S(2)}) async-start(f32[16,1,128]{2,1,0:T(1,128)} %get-tuple-element.43), calls=%async_computation.1 | async-start | bytes 16384 | tf_op jit(solution)/shard_map/all_to_all | solution.py:547
  38.4 3.5 %collective-permute-done.5.w3_ref = bf16[36,3072]{1,0:T(8,128)(2,1)S(1)} collective-permute-done((bf16[36,3072]{1,0:T(8,128)(2,1)S(1)}, bf16[36,3072]{1,0:T(8,128)(2,1)S(1)}, u32[]{:S(2)}, u32[]{:S(2)}) %collective-permute-start.5) | collective-permute-done | bytes 221216 | tf_op jit(solution)/shard_map/ppermute | solution.py:534
  42.1 3.3 %all-to-all-done.1.stats_ref = f32[16,1,128]{2,1,0:T(1,128)S(1)} async-done(((f32[16,1,128]{2,1,0:T(1,128)}), f32[16,1,128]{2,1,0:T(1,128)S(1)}, u32[]{:S(2)}, u32[]{:S(2)}) %all-to-all-start.1) | async-done | bytes 8224 | tf_op jit(solution)/shard_map/all_to_all | solution.py:547
  45.4 9.2 %second_kernel.1 = (bf16[1024,256]{1,0:T(8,128)(2,1)S(1)}, bf16[512,256]{1,0:T(8,128)(2,1)S(1)}, bf16[512,256]{1,0:T(8,128)(2,1)S(1)}, f32[16,1,128]{2,1,0:T(1,1...) custom-call(s32[1]{0:T(128)} %bitcast.place_ref, ...), custom_call_target="tpu_custom_call" | custom-call | flops 3623878656 | bytes 6291456 | tf_op jit(solution)/shard_map/second_kernel/pallas_call | solution.py:526
  54.6 0.7 collective-permute-start.8
  56.3 13.9 %all_to_all.16.stats_ref = f32[16,1,128]{2,1,0:T(1,128)S(1)} all-to-all(f32[16,1,128]{2,1,0:T(1,128)S(1)} %get-tuple-element.56), channel_id=1, replica_groups=mesh['clip'=8,'seq'=16] {'seq'}, dimensions={0} | all-to-all | bytes 16384 | tf_op jit(solution)/shard_map/all_to_all | solution.py:547
  70.2 3.8 %third_kernel.1 = (f32[256,64]{1,0:T(8,128)S(1)}, bf16[336,128]{1,0:T(8,128)(2,1)S(1)}) custom-call(s32[1]{0:T(128)} %bitcast.place_ref, f32[16,1,128]{2,1,0:T(1,128)S(1)} %all_to_all.16.stats_ref, bf16[1024,256]{1,0:T(8,128)(2,1)S(1)} %get-tuple-element.57.rows_ref, bf16[512,256]{1,0:T(8,128)(2,1)S(1)} %collective-permute-done.8.near_ref, ...), custom_call_target="tpu_custom_call" | custom-call | flops 1811939328 | bytes 4194304 | tf_op jit(solution)/shard_map/third_kernel/pallas_call | solution.py:526
  74.3 1.1 %latent_kernel.1 = f32[16,2,16,32]{3,2,1,0:T(8,128)} custom-call(f32[256,64]{1,0:T(8,128)S(1)} %get-tuple-element.65.patches_ref), custom_call_target="tpu_custom_call" | custom-call | tf_op jit(solution)/shard_map/latent_kernel/pallas_call | solution.py:526
  75.4 3.5 %collective-permute-done.11 = bf16[336,128]{1,0:T(8,128)(2,1)S(1)} collective-permute-done((bf16[336,128]{1,0:T(8,128)(2,1)S(1)}, bf16[336,128]{1,0:T(8,128)(2,1)S(1)}, u32[]{:S(2)}, u32[]{:S(2)}) %collective-permute-start.11) | collective-permute-done | bytes 86048 | tf_op jit(solution)/shard_map/ppermute | solution.py:534
  78.9 1.0 %collective-permute-start.14 = (bf16[2,336,128]{2,1,0:T(8,128)(2,1)S(1)}, bf16[2,336,128]{2,1,0:T(8,128)(2,1)S(1)}, u32[]{:S(2)}, u32[]{:S(2)}) collective-permute-start(bf16[2,336,128]{2,1,0:T(8,128)(2,1)S(1)} %pad_maximum_fusion.refs_0_), channel_id=1, source_target_pairs={{0,6},{1,7},{2,4},{3,5},{4,2},{5,3},{6,0},{7,1},{8,14},{9,15},{10,... | collective-permute-start | bytes 516104 | tf_op jit(solution)/shard_map/ppermute | solution.py:534
  79.9 1.2 %collective-permute-start.13 = (bf16[2,336,128]{2,1,0:T(8,128)(2,1)S(1)}, bf16[2,336,128]{2,1,0:T(8,128)(2,1)S(1)}, u32[]{:S(2)}, u32[]{:S(2)}) collective-permute-start(bf16[2,336,128]{2,1,0:T(8,128)(2,1)S(1)} %pad_maximum_fusion.refs_0_), channel_id=1, source_target_pairs={{0,4},{1,5},{2,6},{3,7},{4,0},{5,1},{6,2},{7,3},{8,12},{9,13},{10,... | collective-permute-start | bytes 516104 | tf_op jit(solution)/shard_map/ppermute | solution.py:534
  81.1 1.2 %collective-permute-start.12 = (bf16[2,336,128]{2,1,0:T(8,128)(2,1)S(1)}, bf16[2,336,128]{2,1,0:T(8,128)(2,1)S(1)}, u32[]{:S(2)}, u32[]{:S(2)}) collective-permute-start(bf16[2,336,128]{2,1,0:T(8,128)(2,1)S(1)} %pad_maximum_fusion.refs_0_), channel_id=1, source_target_pairs={{0,2},{1,3},{2,0},{3,1},{4,6},{5,7},{6,4},{7,5},{8,10},{9,11},{10,... | collective-permute-start | bytes 516104 | tf_op jit(solution)/shard_map/ppermute | solution.py:534
  82.2 2.7 %collective-permute-start.15 = (bf16[2,336,128]{2,1,0:T(8,128)(2,1)S(1)}, bf16[2,336,128]{2,1,0:T(8,128)(2,1)S(1)}, u32[]{:S(2)}, u32[]{:S(2)}) collective-permute-start(bf16[2,336,128]{2,1,0:T(8,128)(2,1)S(1)} %pad_maximum_fusion.refs_0_), channel_id=1, source_target_pairs={{0,1},{1,0},{2,3},{3,2},{4,5},{5,4},{6,7},{7,6},{8,9},{9,8},{10,11... | collective-permute-start | bytes 516104 | tf_op jit(solution)/shard_map/ppermute | solution.py:534
  84.9 2.5 %collective-permute-done.14.refs_3_ = bf16[2,336,128]{2,1,0:T(8,128)(2,1)S(1)} collective-permute-done((bf16[2,336,128]{2,1,0:T(8,128)(2,1)S(1)}, bf16[2,336,128]{2,1,0:T(8,128)(2,1)S(1)}, u32[]{:S(2)}, u32[]{:S(2)}) %collective-permute-start.14) | collective-permute-done | bytes 172064 | tf_op jit(solution)/shard_map/ppermute | solution.py:534
  87.4 3.3 %collective-permute-start.18 = (bf16[2,336,128]{2,1,0:T(8,128)(2,1)S(1)}, bf16[2,336,128]{2,1,0:T(8,128)(2,1)S(1)}, u32[]{:S(2)}, u32[]{:S(2)}) collective-permute-start(bf16[2,336,128]{2,1,0:T(8,128)(2,1)S(1)} %collective-permute-done.14.refs_3_), channel_id=1, source_target_pairs={{0,1},{1,0},{2,3},{3,2},{4,5},{5,4},{6,7},{7,6},{8,9},{9,8},{10,11... | collective-permute-start | bytes 516104 | tf_op jit(solution)/shard_map/ppermute | solution.py:534
  92.4 5.6 %attend_kernel.1 = bf16[256,1536]{1,0:T(8,128)(2,1)} custom-call(s32[1]{0:T(128)} %bitcast.place_ref, s32[1]{0:T(128)} %bitcast.9.clip_ref, bf16[2,336,128]{2,1,0:T(8,128)(2,1)S(1)} %pad_maximum_fusion.refs_0_, bf16[2,336,128]{2,1,0:T(8,128)(2,1)S(1)} %collective-permute-done.12.refs_1_, bf16[2,336,128]{2,1,0:T(8,128)(2,1)S(1)} %collective-permute-done.13.refs_2_, ...), custom_call_target="tpu_custom_call" | custom-call | tf_op jit(solution)/shard_map/attend_kernel/pallas_call | solution.py:526
  (33 shorter events, 4.0 us)
Async XLA Ops:
  2.4 18.3 %collective-permute-start.1 = (bf16[512,256]{1,0:T(8,128)(2,1)S(1)}, bf16[512,256]{1,0:T(8,128)(2,1)S(1)}, u32[]{:S(2)}, u32[]{:S(2)}) collective-permute-start(bf16[512,256]{1,0:T(8,128)(2,1)S(1)} %get-tuple-element.40), channel_id=1, source_target_pairs={{0,1},{1,0},{2,3},{3,2},{4,5},{5,4},{6,7},{7,6},{8,9},{9,8},{10,11... | collective-permute-start | bytes 786440 | tf_op jit(solution)/shard_map/ppermute | solution.py:543
  3.9 16.8 %collective-permute-start.2 = (bf16[512,256]{1,0:T(8,128)(2,1)S(1)}, bf16[512,256]{1,0:T(8,128)(2,1)S(1)}, u32[]{:S(2)}, u32[]{:S(2)}) collective-permute-start(bf16[512,256]{1,0:T(8,128)(2,1)S(1)} %get-tuple-element.41), channel_id=1, source_target_pairs={{0,15},{1,2},{2,1},{3,4},{4,3},{5,6},{6,5},{7,8},{8,7},{9,10},{10,... | collective-permute-start | bytes 786440 | tf_op jit(solution)/shard_map/ppermute | solution.py:542
  5.2 15.6 %collective-permute-start = (f32[2,3072]{1,0:T(2,128)S(1)}, f32[2,3072]{1,0:T(2,128)S(1)}, u32[]{:S(2)}, u32[]{:S(2)}) collective-permute-start(f32[2,3072]{1,0:T(2,128)S(1)} %get-tuple-element.36.own_mods_ref), channel_id=1, source_target_pairs={{0,16},{16,0},{32,48},{48,32},{64,80},{80,64},{96,112},{112,96},{1... | collective-permute-start | bytes 73736 | tf_op jit(solution)/shard_map/ppermute | solution.py:534
  20.8 7.9 %copy-start.1 = (bf16[36,3072]{1,0:T(8,128)(2,1)S(1)}, bf16[36,3072]{1,0:T(8,128)(2,1)}, u32[]{:S(2)}) copy-start(bf16[36,3072]{1,0:T(8,128)(2,1)} %w0_ref) | copy-start | bytes 663556
  20.8 24.6 %copy-start = (bf16[64,3072]{1,0:T(8,128)(2,1)S(1)}, bf16[64,3072]{1,0:T(8,128)(2,1)}, u32[]{:S(2)}) copy-start(bf16[64,3072]{1,0:T(8,128)(2,1)} %embed_ref.1) | copy-start | bytes 1179652
  20.8 24.6 %copy-start.3 = (f32[3072]{0:T(1024)S(1)}, f32[3072]{0:T(1024)}, u32[]{:S(2)}) copy-start(f32[3072]{0:T(1024)} %param.18) | copy-start | bytes 36868
  27.6 17.7 %collective-permute-start.6 = (bf16[528,256]{1,0:T(8,128)(2,1)S(1)}, bf16[528,256]{1,0:T(8,128)(2,1)S(1)}, u32[]{:S(2)}, u32[]{:S(2)}) collective-permute-start(bf16[528,256]{1,0:T(8,128)(2,1)S(1)} %get-tuple-element.48), channel_id=1, source_target_pairs={{0,1},{1,0},{2,3},{3,2},{4,5},{5,4},{6,7},{7,6},{8,9},{9,8},{10,11... | collective-permute-start | bytes 811016 | tf_op jit(solution)/shard_map/ppermute | solution.py:543
  28.4 17.0 %collective-permute-start.7 = (bf16[528,256]{1,0:T(8,128)(2,1)S(1)}, bf16[528,256]{1,0:T(8,128)(2,1)S(1)}, u32[]{:S(2)}, u32[]{:S(2)}) collective-permute-start(bf16[528,256]{1,0:T(8,128)(2,1)S(1)} %get-tuple-element.49), channel_id=1, source_target_pairs={{0,15},{1,2},{2,1},{3,4},{4,3},{5,6},{6,5},{7,8},{8,7},{9,10},{10,... | collective-permute-start | bytes 811016 | tf_op jit(solution)/shard_map/ppermute | solution.py:542
  28.7 13.3 %collective-permute-start.5 = (bf16[36,3072]{1,0:T(8,128)(2,1)S(1)}, bf16[36,3072]{1,0:T(8,128)(2,1)S(1)}, u32[]{:S(2)}, u32[]{:S(2)}) collective-permute-start(bf16[36,3072]{1,0:T(8,128)(2,1)S(1)} %copy-done.1), channel_id=1, source_target_pairs={{0,96},{16,112},{32,64},{48,80},{64,32},{80,48},{96,0},{112,16},{1... | collective-permute-start | bytes 663560 | tf_op jit(solution)/shard_map/ppermute | solution.py:534
  31.4 10.6 %collective-permute-start.4 = (bf16[36,3072]{1,0:T(8,128)(2,1)S(1)}, bf16[36,3072]{1,0:T(8,128)(2,1)S(1)}, u32[]{:S(2)}, u32[]{:S(2)}) collective-permute-start(bf16[36,3072]{1,0:T(8,128)(2,1)S(1)} %copy-done.1), channel_id=1, source_target_pairs={{0,64},{16,80},{32,96},{48,112},{64,0},{80,16},{96,32},{112,48},{1... | collective-permute-start | bytes 663560 | tf_op jit(solution)/shard_map/ppermute | solution.py:534
  31.7 10.3 %collective-permute-start.3 = (bf16[36,3072]{1,0:T(8,128)(2,1)S(1)}, bf16[36,3072]{1,0:T(8,128)(2,1)S(1)}, u32[]{:S(2)}, u32[]{:S(2)}) collective-permute-start(bf16[36,3072]{1,0:T(8,128)(2,1)S(1)} %copy-done.1), channel_id=1, source_target_pairs={{0,32},{16,48},{32,0},{48,16},{64,96},{80,112},{96,64},{112,80},{1... | collective-permute-start | bytes 663560 | tf_op jit(solution)/shard_map/ppermute | solution.py:534
  32.0 13.4 %all-to-all-start.1 = ((f32[16,1,128]{2,1,0:T(1,128)}), f32[16,1,128]{2,1,0:T(1,128)S(1)}, u32[]{:S(2)}, u32[]{:S(2)}) async-start(f32[16,1,128]{2,1,0:T(1,128)} %get-tuple-element.43), calls=%async_computation.1 | async-start | bytes 16384 | tf_op jit(solution)/shard_map/all_to_all | solution.py:547
  45.4 24.8 %copy-start.2 = (bf16[3,3,3,256,16]{3,4,2,1,0:T(8,128)(2,1)S(1)}, bf16[3,3,3,256,16]{3,4,2,1,0:T(8,128)(2,1)}, u32[]{:S(2)}) copy-start(bf16[3,3,3,256,16]{3,4,2,1,0:T(8,128)(2,1)} %param.14) | copy-start | bytes 663556
  54.6 15.5 %collective-permute-start.8 = (bf16[512,256]{1,0:T(8,128)(2,1)S(1)}, bf16[512,256]{1,0:T(8,128)(2,1)S(1)}, u32[]{:S(2)}, u32[]{:S(2)}) collective-permute-start(bf16[512,256]{1,0:T(8,128)(2,1)S(1)} %get-tuple-element.58), channel_id=1, source_target_pairs={{0,1},{1,0},{2,3},{3,2},{4,5},{5,4},{6,7},{7,6},{8,9},{9,8},{10,11... | collective-permute-start | bytes 786440 | tf_op jit(solution)/shard_map/ppermute | solution.py:543
  55.4 14.7 %collective-permute-start.9 = (bf16[512,256]{1,0:T(8,128)(2,1)S(1)}, bf16[512,256]{1,0:T(8,128)(2,1)S(1)}, u32[]{:S(2)}, u32[]{:S(2)}) collective-permute-start(bf16[512,256]{1,0:T(8,128)(2,1)S(1)} %get-tuple-element.59), channel_id=1, source_target_pairs={{0,15},{1,2},{2,1},{3,4},{4,3},{5,6},{6,5},{7,8},{8,7},{9,10},{10,... | collective-permute-start | bytes 786440 | tf_op jit(solution)/shard_map/ppermute | solution.py:542
  55.7 14.5 %collective-permute-start.10 = (bf16[144,128]{1,0:T(8,128)(2,1)S(1)}, bf16[144,128]{1,0:T(8,128)(2,1)S(1)}, u32[]{:S(2)}, u32[]{:S(2)}) collective-permute-start(bf16[144,128]{1,0:T(8,128)(2,1)S(1)} %get-tuple-element.63), channel_id=1, source_target_pairs={{0,16},{16,0},{32,48},{48,32},{64,80},{80,64},{96,112},{112,96},{1... | collective-permute-start | bytes 110600 | tf_op jit(solution)/shard_map/ppermute | solution.py:534
  74.0 4.9 %collective-permute-start.11 = (bf16[336,128]{1,0:T(8,128)(2,1)S(1)}, bf16[336,128]{1,0:T(8,128)(2,1)S(1)}, u32[]{:S(2)}, u32[]{:S(2)}) collective-permute-start(bf16[336,128]{1,0:T(8,128)(2,1)S(1)} %get-tuple-element.64), channel_id=1, source_target_pairs={{0,8},{1,9},{2,10},{3,11},{4,12},{5,13},{6,14},{7,15},{8,0},{9,1},... | collective-permute-start | bytes 258056 | tf_op jit(solution)/shard_map/ppermute | solution.py:534
  78.9 8.5 %collective-permute-start.14 = (bf16[2,336,128]{2,1,0:T(8,128)(2,1)S(1)}, bf16[2,336,128]{2,1,0:T(8,128)(2,1)S(1)}, u32[]{:S(2)}, u32[]{:S(2)}) collective-permute-start(bf16[2,336,128]{2,1,0:T(8,128)(2,1)S(1)} %pad_maximum_fusion.refs_0_), channel_id=1, source_target_pairs={{0,6},{1,7},{2,4},{3,5},{4,2},{5,3},{6,0},{7,1},{8,14},{9,15},{10,... | collective-permute-start | bytes 516104 | tf_op jit(solution)/shard_map/ppermute | solution.py:534
  79.9 10.8 %collective-permute-start.13 = (bf16[2,336,128]{2,1,0:T(8,128)(2,1)S(1)}, bf16[2,336,128]{2,1,0:T(8,128)(2,1)S(1)}, u32[]{:S(2)}, u32[]{:S(2)}) collective-permute-start(bf16[2,336,128]{2,1,0:T(8,128)(2,1)S(1)} %pad_maximum_fusion.refs_0_), channel_id=1, source_target_pairs={{0,4},{1,5},{2,6},{3,7},{4,0},{5,1},{6,2},{7,3},{8,12},{9,13},{10,... | collective-permute-start | bytes 516104 | tf_op jit(solution)/shard_map/ppermute | solution.py:534
  81.1 9.6 %collective-permute-start.12 = (bf16[2,336,128]{2,1,0:T(8,128)(2,1)S(1)}, bf16[2,336,128]{2,1,0:T(8,128)(2,1)S(1)}, u32[]{:S(2)}, u32[]{:S(2)}) collective-permute-start(bf16[2,336,128]{2,1,0:T(8,128)(2,1)S(1)} %pad_maximum_fusion.refs_0_), channel_id=1, source_target_pairs={{0,2},{1,3},{2,0},{3,1},{4,6},{5,7},{6,4},{7,5},{8,10},{9,11},{10,... | collective-permute-start | bytes 516104 | tf_op jit(solution)/shard_map/ppermute | solution.py:534
  82.2 9.0 %collective-permute-start.15 = (bf16[2,336,128]{2,1,0:T(8,128)(2,1)S(1)}, bf16[2,336,128]{2,1,0:T(8,128)(2,1)S(1)}, u32[]{:S(2)}, u32[]{:S(2)}) collective-permute-start(bf16[2,336,128]{2,1,0:T(8,128)(2,1)S(1)} %pad_maximum_fusion.refs_0_), channel_id=1, source_target_pairs={{0,1},{1,0},{2,3},{3,2},{4,5},{5,4},{6,7},{7,6},{8,9},{9,8},{10,11... | collective-permute-start | bytes 516104 | tf_op jit(solution)/shard_map/ppermute | solution.py:534
  87.4 4.3 %collective-permute-start.18 = (bf16[2,336,128]{2,1,0:T(8,128)(2,1)S(1)}, bf16[2,336,128]{2,1,0:T(8,128)(2,1)S(1)}, u32[]{:S(2)}, u32[]{:S(2)}) collective-permute-start(bf16[2,336,128]{2,1,0:T(8,128)(2,1)S(1)} %collective-permute-done.14.refs_3_), channel_id=1, source_target_pairs={{0,1},{1,0},{2,3},{3,2},{4,5},{5,4},{6,7},{7,6},{8,9},{9,8},{10,11... | collective-permute-start | bytes 516104 | tf_op jit(solution)/shard_map/ppermute | solution.py:534
  90.7 1.4 %collective-permute-start.17 = (bf16[2,336,128]{2,1,0:T(8,128)(2,1)S(1)}, bf16[2,336,128]{2,1,0:T(8,128)(2,1)S(1)}, u32[]{:S(2)}, u32[]{:S(2)}) collective-permute-start(bf16[2,336,128]{2,1,0:T(8,128)(2,1)S(1)} %collective-permute-done.13.refs_2_), channel_id=1, source_target_pairs={{0,1},{1,0},{2,3},{3,2},{4,5},{5,4},{6,7},{7,6},{8,9},{9,8},{10,11... | collective-permute-start | bytes 516104 | tf_op jit(solution)/shard_map/ppermute | solution.py:534
  90.7 1.7 %collective-permute-start.16 = (bf16[2,336,128]{2,1,0:T(8,128)(2,1)S(1)}, bf16[2,336,128]{2,1,0:T(8,128)(2,1)S(1)}, u32[]{:S(2)}, u32[]{:S(2)}) collective-permute-start(bf16[2,336,128]{2,1,0:T(8,128)(2,1)S(1)} %collective-permute-done.12.refs_1_), channel_id=1, source_target_pairs={{0,1},{1,0},{2,3},{3,2},{4,5},{5,4},{6,7},{7,6},{8,9},{9,8},{10,11... | collective-permute-start | bytes 516104 | tf_op jit(solution)/shard_map/ppermute | solution.py:534
